TPU v7x, 32 devices: a whole 2x2x4 slice. The times are simulated.
32 devices in a mesh: seq: 8 (over z, x), mp: 4 (over y, core).
Axes of the slice: x: 2, y: 2, z: 4, core: 2. Of those that a mesh axis runs over, the one named last changes fastest.
Arguments:
- span_pairs: bfloat16 [4096, 2, 896], P('seq', None, 'mp'), may hold values from -6 to 6
- dec_queries: bfloat16 [4096, 2048], P('seq', 'mp'), may hold values from -6 to 6
- database: float32 [16, 128, 896], P('seq'), may hold values from -6 to 6
- nbr_index: int32 [64, 2], P('seq'), may hold values from 0 to 1
- nbr_host: int32 [64, 2], P('seq'), may hold values from 0 to 7, as said below
- enc_gain: float32 [896], replicated, may hold values from 0.25 to 1.75
- enc_query: bfloat16 [896, 896], P(None, 'mp'), may hold values from -0.1875 to 0.1875
- enc_out: bfloat16 [896, 896], P('mp'), may hold values from -0.1875 to 0.1875
- ffn_gain: float32 [896], replicated, may hold values from 0.25 to 1.75
- ffn_up: bfloat16 [896, 1792], P(None, 'mp'), may hold values from -0.1875 to 0.1875
- ffn_down: bfloat16 [1792, 896], P('mp'), may hold values from -0.125 to 0.125
- dec_kv: bfloat16 [896, 2, 2048], P(None, None, 'mp'), may hold values from -0.1875 to 0.1875
Outputs:
- attended: float32 [4096, 2048], P('seq', 'mp')
Inputs may be any that keep to these rules, and one draw needn't show every extreme that they name: `nbr_host`: the 16 neighbours of the spans of one seq index name each host at most 2 times, and some host exactly 2 times. Over all spans every host is named exactly 16 times.
All inputs are finite; a program needn't handle non-finite values.
Results may differ from a plain program's by a relative error of at most 0.019.
Values may be sent and summed in bfloat16 or wider, within the bound.
No kernel may reach another device: no remote copies, remote signals or barrier semaphores. Data moves between devices by JAX's collectives and lax.ppermute only.
A program may use at most 128 MiB of HBM per device.

v0:
```python
import jax
import jax.numpy as jnp
from jax import lax
from jax.sharding import PartitionSpec as P

HEAD_DIM = 128
EHEAD_DIM = 112
SPAN = 64
NBL = 128
NEIGH = 2
CH_DEV = 8


def passed_along(array, axis, by):
    length = lax.axis_size(axis)
    pairs = [(i, i + by) for i in range(length) if 0 <= i + by < length]
    return lax.ppermute(array, axis, pairs)


def rms_scale(values, gain):
    return values * lax.rsqrt(jnp.mean(values * values, axis=-1, keepdims=True) + 1e-06) * gain


def on_device(
    span_pairs,
    dec_queries,
    database,
    nbr_index,
    nbr_host,
    enc_gain,
    enc_query,
    enc_out,
    ffn_gain,
    ffn_up,
    ffn_down,
    dec_kv,
):
    seq_size = lax.axis_size("seq")
    lanes = lax.axis_size("mp")
    lane_index = lax.axis_index("mp")
    local_count = NEIGH * CH_DEV
    slot_cap = (local_count + seq_size - 1) // seq_size
    slot_count = seq_size * slot_cap
    width = database.shape[2]
    enc_width = span_pairs.shape[2]
    enc_heads = enc_width // EHEAD_DIM
    enc_scale = float(EHEAD_DIM) ** (-0.5)
    dec_scale = float(HEAD_DIM) ** (-0.5)
    kv_local = span_pairs.reshape(CH_DEV, SPAN, 2, enc_width)
    hosts = nbr_host.reshape(local_count)
    codes = nbr_index.reshape(local_count) + 1
    order = jnp.arange(local_count)
    earlier = (hosts[:, None] == hosts[None, :]) & (order[None, :] < order[:, None])
    ranks = jnp.sum(earlier.astype(jnp.int32), axis=1)
    target = hosts * slot_cap + ranks
    place = jnp.arange(slot_count)[:, None] == target[None, :]
    place_bf = place.astype(jnp.bfloat16).reshape(slot_count, CH_DEV, NEIGH)
    outgoing = jnp.einsum(
        "pmk,mtce->ptce", place_bf, kv_local, preferred_element_type=jnp.float32
    ).astype(jnp.bfloat16)
    out_codes = jnp.sum(place.astype(jnp.int32) * codes[None, :], axis=1)
    incoming, in_codes = (
        lax.all_to_all(
            outgoing.reshape(seq_size, slot_cap, SPAN, 2, enc_width),
            "seq",
            split_axis=0,
            concat_axis=0,
            tiled=True,
        ),
        lax.all_to_all(
            out_codes.reshape(seq_size, slot_cap), "seq", split_axis=0, concat_axis=0, tiled=True
        ),
    )
    in_codes = in_codes.reshape(slot_count)
    live = in_codes > 0
    slot_rank = jnp.cumsum(live.astype(jnp.int32)) - 1
    pick = live[None, :] & (slot_rank[None, :] == jnp.arange(local_count)[:, None])
    pick_bf = pick.astype(jnp.bfloat16)
    packed_kv = jnp.einsum(
        "ap,ptce->atce",
        pick_bf,
        incoming.reshape(slot_count, SPAN, 2, enc_width),
        preferred_element_type=jnp.float32,
    ).astype(jnp.bfloat16)
    packed_codes = jnp.sum(pick.astype(jnp.int32) * in_codes[None, :], axis=1)
    packed_entry = jnp.maximum(packed_codes - 1, 0)
    neighbours = jnp.swapaxes(jnp.take(database, packed_entry, axis=0), 0, 1)
    normed = rms_scale(neighbours, enc_gain).astype(jnp.bfloat16)
    query = (
        jnp.einsum("rae,ef->raf", normed, enc_query, preferred_element_type=jnp.float32) * enc_scale
    ).astype(jnp.bfloat16)
    query = query.reshape(NBL, local_count, enc_heads, EHEAD_DIM)
    keys = packed_kv[:, :, 0].reshape(local_count, SPAN, enc_heads, EHEAD_DIM)
    values = packed_kv[:, :, 1].reshape(local_count, SPAN, enc_heads, EHEAD_DIM)
    scores = jnp.einsum("rahd,akhd->ahrk", query, keys, preferred_element_type=jnp.float32)
    weights = jax.nn.softmax(scores, axis=-1).astype(jnp.bfloat16)
    enc_attended = jnp.einsum(
        "ahrk,akhd->rahd", weights, values, preferred_element_type=jnp.float32
    )
    enc_attended = enc_attended.astype(jnp.bfloat16).reshape(NBL, local_count, enc_width)
    partial_value = jnp.einsum(
        "raf,fe->rae", enc_attended, enc_out, preferred_element_type=jnp.float32
    )
    row_count = NBL // lanes
    row_start = lane_index * row_count
    mixed = lax.psum_scatter(
        partial_value.astype(jnp.bfloat16), "mp", scatter_dimension=0, tiled=True
    ).astype(jnp.float32)
    resid = lax.dynamic_slice_in_dim(neighbours, row_start, row_count, 0) + mixed
    up_full, down_full = (
        lax.all_gather(ffn_up, "mp", axis=1, tiled=True),
        lax.all_gather(ffn_down, "mp", axis=0, tiled=True),
    )
    unit_width = ffn_up.shape[1]
    inner = rms_scale(resid, ffn_gain).astype(jnp.bfloat16)
    units = jax.nn.gelu(
        jnp.einsum("rae,ef->raf", inner, up_full, preferred_element_type=jnp.float32)
    ).astype(jnp.bfloat16)
    units = units.reshape(row_count, local_count, lanes, unit_width)
    down_terms = jnp.einsum(
        "ragf,gfe->rage",
        units,
        down_full.reshape(lanes, unit_width, width),
        preferred_element_type=jnp.float32,
    )
    down_terms = down_terms.astype(jnp.bfloat16).astype(jnp.float32)
    encoded = (resid + jnp.sum(down_terms, axis=2)).astype(jnp.bfloat16)
    returning = jnp.einsum(
        "ap,rae->pre", pick_bf, encoded, preferred_element_type=jnp.float32
    ).astype(jnp.bfloat16)
    answers = lax.all_to_all(
        returning.reshape(seq_size, slot_cap, row_count, width),
        "seq",
        split_axis=0,
        concat_axis=0,
        tiled=True,
    )
    mine = jnp.einsum(
        "pmk,pre->mkre",
        place_bf,
        answers.reshape(slot_count, row_count, width),
        preferred_element_type=jnp.float32,
    ).astype(jnp.bfloat16)
    previous = passed_along(mine[CH_DEV - 1], "seq", 1)
    used = jnp.concatenate([previous[None], mine[: CH_DEV - 1]], axis=0)
    dec_width = dec_kv.shape[2]
    dec_heads = dec_width // HEAD_DIM
    dec_pairs = jnp.einsum(
        "mkre,ecd->mkrcd",
        lax.all_gather(used, "mp", axis=2, tiled=True),
        dec_kv,
        preferred_element_type=jnp.float32,
    ).astype(jnp.bfloat16)
    dec_keys = dec_pairs[:, :, :, 0].reshape(CH_DEV, NEIGH * NBL, dec_heads, HEAD_DIM)
    dec_values = dec_pairs[:, :, :, 1].reshape(CH_DEV, NEIGH * NBL, dec_heads, HEAD_DIM)
    dec_q = (dec_queries.astype(jnp.float32) * dec_scale).astype(jnp.bfloat16)
    dec_q = dec_q.reshape(CH_DEV, SPAN, dec_heads, HEAD_DIM)
    dec_scores = jnp.einsum("mqhd,mkhd->mhqk", dec_q, dec_keys, preferred_element_type=jnp.float32)
    dec_weights = jax.nn.softmax(dec_scores, axis=-1).astype(jnp.bfloat16)
    result = jnp.einsum(
        "mhqk,mkhd->mqhd", dec_weights, dec_values, preferred_element_type=jnp.float32
    )
    return result.reshape(CH_DEV * SPAN, dec_width)


def solution(mesh):
    placed = (
        P("seq", None, "mp"),
        P("seq", "mp"),
        P("seq", None, None),
        P("seq", None),
        P("seq", None),
        P(),
        P(None, "mp"),
        P("mp", None),
        P(),
        P(None, "mp"),
        P("mp", None),
        P(None, None, "mp"),
    )
    return jax.shard_map(
        on_device, mesh=mesh, in_specs=placed, out_specs=P("seq", "mp"), check_vma=False
    )
```

profile of v0, /device:TPU:0, one launch (start us, length us, event | category | flops | bytes accessed | tf_op | source)
XLA Modules:
  0.0 292.3 jit_solution(199352800378488206)
XLA Ops:
  9.3 7.3 %all-to-all-start = ((s32[8,1,2]{2,1,0:T(1,128)}), s32[8,1,2]{2,1,0:T(1,128)S(1)}, u32[]{:S(2)}, u32[]{:S(2)}) async-start(s32[8,1,2]{2,1,0:T(1,128)} %bitcast.3), calls=%async_computation | async-start | bytes 8192 | tf_op jit(solution)/shard_map/all_to_all | solution.py:70
  19.9 3.0 %copy.104 = bf16[8,2,64,2,224]{4,1,3,2,0:T(2,128)(2,1)} copy(bf16[8,2,64,2,224]{4,1,0,3,2:T(2,128)(2,1)} %reshape.183) | data formatting | bytes 1835008 | tf_op jit(solution)/shard_map/reshape | solution.py:64
  23.0 5.9 %all-to-all-start.1 = ((bf16[8,2,64,2,224]{4,1,3,2,0:T(2,128)(2,1)}), bf16[8,2,64,2,224]{4,1,3,2,0:T(2,128)(2,1)}, u32[]{:S(2)}, u32[]{:S(2)}) async-start(bf16[8,2,64,2,224]{4,1,3,2,0:T(2,128)(2,1)} %copy.104), calls=%async_computation.1 | async-start | bytes 2097152 | tf_op jit(solution)/shard_map/all_to_all | solution.py:63
  30.6 4.0 %gather_fusion = f32[16,128,896]{2,1,0:T(8,128)} fusion(f32[2,128,896]{2,1,0:T(8,128)S(1)} %copy-done.1, s32[1024]{0:T(1024)S(1)} %pad_clamp_fusion), kind=kCustom, calls=%fused_computation | custom fusion | bytes 14680128 | tf_op jit(solution)/shard_map/jit(_take)/gather | solution.py:87
  34.6 4.0 %fusion.2 = (f32[128,16]{0,1:T(8,128)S(1)}, f32[16,128,896]{2,1,0:T(8,128)S(1)}) fusion(f32[16,128,896]{2,1,0:T(8,128)} %gather_fusion, pred[16]{0:T(512)(128)(4,1)S(1)} %broadcast_compare_fusion), kind=kLoop, calls=%fused_computation.5 | loop fusion | flops 5502976 | bytes 14688272 | tf_op jit(solution)/shard_map/reduce_sum | solution.py:21
  38.6 2.9 %copy-done.2 = f32[16,128,896]{2,1,0:T(8,128)} copy-done((f32[16,128,896]{2,1,0:T(8,128)}, f32[16,128,896]{2,1,0:T(8,128)S(1)}, u32[]{:S(2)}) %copy-start.2) | copy-done | bytes 7340056
  41.6 2.4 multiply_convert_fusion.1
  44.0 10.4 %all-to-all-done.1 = bf16[8,2,64,2,224]{4,1,3,2,0:T(2,128)(2,1)} async-done(((bf16[8,2,64,2,224]{4,1,3,2,0:T(2,128)(2,1)}), bf16[8,2,64,2,224]{4,1,3,2,0:T(2,128)(2,1)}, u32[]{:S(2)}, u32[]{:S(2)}) %all-to-all-start.1) | async-done | bytes 917536 | tf_op jit(solution)/shard_map/all_to_all | solution.py:63
  54.4 2.4 copy.105
  65.7 2.3 convolution_convert_fusion.5
  68.0 4.1 %convolution_convert_fusion = bf16[128,16,896]{2,0,1:T(8,128)(2,1)} fusion(bf16[128,16,224]{0,2,1:T(8,128)(2,1)S(1)} %bitcast.113, bf16[224,896]{1,0:T(8,128)(2,1)} %param.19), kind=kOutput, calls=%fused_computation.27 | convolution fusion | flops 823918592 | bytes 4988928 | tf_op jit(solution)/shard_map/raf,fe->rae/dot_general | solution.py:101
  73.8 38.5 %reduce-scatter.2.cloned.1.call-done = bf16[32,16,896]{2,0,1:T(8,128)(2,1)} async-done(((bf16[128,16,896]{2,0,1:T(8,128)(2,1)}), bf16[32,16,896]{2,0,1:T(8,128)(2,1)}) %reduce-scatter.2.cloned.1.call-update) | async-done | bytes 917520 | tf_op jit(solution)/shard_map/reduce_scatter | solution.py:106
  112.3 2.2 multiply_reduce_fusion
  114.5 2.7 multiply_convert_fusion
  117.3 25.6 %all-gather.4.cloned.1.call-done = bf16[896,1792]{0,1:T(8,128)(2,1)} async-done(((bf16[896,448]{0,1:T(8,128)(2,1)}), bf16[896,1792]{0,1:T(8,128)(2,1)}) %all-gather.4.cloned.1.call-update) | async-done | bytes 3211280 | tf_op jit(solution)/shard_map/all_gather | solution.py:111
  142.9 6.1 %fusion.12 = bf16[32,16,1792]{2,1,0:T(8,128)(2,1)} fusion(bf16[896,1792]{0,1:T(8,128)(2,1)} %all-gather.4.cloned.1.call-done, bf16[32,16,896]{2,0,1:T(8,128)(2,1)} %multiply_convert_fusion), kind=kOutput, calls=%fused_computation.17 | convolution fusion | flops 1652424704 | bytes 5963776 | tf_op jit(solution)/shard_map/rae,ef->raf/dot_general | solution.py:117
  149.0 6.2 %reshape.187 = bf16[32,16,4,448]{3,2,1,0:T(4,128)(2,1)} reshape(bf16[32,16,1792]{2,1,0:T(8,128)(2,1)} %fusion.12) | data formatting | bytes 3670016 | tf_op jit(solution)/shard_map/reshape | solution.py:119
  155.1 18.3 %all-gather.6.cloned.1.call-done = bf16[1792,896]{1,0:T(8,128)(2,1)} async-done(((bf16[448,896]{1,0:T(8,128)(2,1)}), bf16[1792,896]{1,0:T(8,128)(2,1)}) %all-gather.6.cloned.1.call-update) | async-done | bytes 3211280 | tf_op jit(solution)/shard_map/all_gather | solution.py:112
  173.5 5.0 %convert_reduce_fusion = f32[32,16,896]{2,1,0:T(8,128)S(1)} fusion(bf16[4,448,896,1]{2,1,3,0:T(8,128)(2,1)} %bitcast.117, bf16[32,16,4,448]{3,2,1,0:T(4,128)(2,1)} %reshape.187), kind=kOutput, calls=%fused_computation.8 | convolution fusion | flops 1649213440 | bytes 6881280 | tf_op jit(solution)/shard_map/ragf,gfe->rage/dot_general | solution.py:120
  178.5 2.3 fusion.32
  182.6 1.8 copy.113
  184.4 29.0 %all_to_all.19 = bf16[8,2,32,896]{3,1,2,0:T(2,128)(2,1)S(1)} all-to-all(bf16[8,2,32,896]{3,1,2,0:T(2,128)(2,1)S(1)} %copy.113), channel_id=1, replica_groups=mesh['seq'=8,'mp'=4] {'seq'}, dimensions={0} | all-to-all | bytes 1835008 | tf_op jit(solution)/shard_map/all_to_all | solution.py:131
  214.9 2.5 reshape.211
  218.1 3.0 %collective-permute-start = (bf16[2,32,896]{2,1,0:T(8,128)(2,1)S(1)}, bf16[2,32,896]{2,1,0:T(8,128)(2,1)S(1)}, u32[]{:S(2)}, u32[]{:S(2)}) collective-permute-start(bf16[2,32,896]{2,1,0:T(8,128)(2,1)S(1)} %bitcast.114), channel_id=1, source_target_pairs={{0,4},{4,8},{8,12},{12,16},{16,20},{20,24},{24,28},{1,5},{5,9},{9,... | collective-permute-start | bytes 344072 | tf_op jit(solution)/shard_map/ppermute | solution.py:17
  221.1 2.3 collective-permute-done
  225.3 30.7 %all-gather.8.cloned.1.call-done = bf16[8,2,128,896]{3,0,2,1:T(8,128)(2,1)} async-done(((bf16[8,2,32,896]{3,0,2,1:T(8,128)(2,1)}), bf16[8,2,128,896]{3,0,2,1:T(8,128)(2,1)}) %all-gather.8.cloned.1.call-update) | async-done | bytes 3670032 | tf_op jit(solution)/shard_map/all_gather | solution.py:150
  256.0 6.8 %fusion.23 = bf16[8,2,128,2,512]{4,2,3,1,0:T(8,128)(2,1)S(1)} fusion(bf16[8,2,128,896,1]{3,0,2,1,4:T(8,128)(2,1)} %bitcast.116, bf16[896,2,512,1,1]{2,1,0,4,3:T(2,128)(2,1)S(1)} %bitcast.108), kind=kOutput, calls=%fused_computation.26 | convolution fusion | flops 3760193536 | bytes 9699328 | tf_op jit(solution)/shard_map/mkre,ecd->mkrcd/dot_general | solution.py:148
  262.7 2.4 fusion.70
  265.2 4.0 %reshape_squeeze.15 = bf16[8,256,4,128]{3,2,1,0:T(4,128)(2,1)} reshape(bf16[8,2,128,1,512]{4,2,3,1,0:T(8,128)(2,1)} %get-tuple-element.9) | data formatting | bytes 4194304 | tf_op jit(solution)/shard_map/reshape;squeeze | solution.py:154
  269.2 2.4 fusion.28
  273.6 4.0 %reshape_squeeze.14 = bf16[8,256,4,128]{3,2,1,0:T(4,128)(2,1)} reshape(bf16[8,2,128,1,512]{4,2,3,1,0:T(8,128)(2,1)} %get-tuple-element.10) | data formatting | bytes 4194304 | tf_op jit(solution)/shard_map/reshape;squeeze | solution.py:155
  277.5 6.5 %fusion.37 = f32[8,64,4,128]{3,1,2,0:T(8,128)S(1)} fusion(bf16[8,256,4,128]{3,2,1,0:T(4,128)(2,1)} %reshape_squeeze.14, f32[8,4,64]{2,1,0:T(4,128)S(1)} %fusion.73, f32[8,4,64,256]{3,2,1,0:T(8,128)} %copy-done.3), kind=kOutput, calls=%fused_computation.49 | convolution fusion | flops 135792896 | bytes 5251072 | tf_op jit(solution)/shard_map/mhqk,mkhd->mqhd/dot_general | solution.py:160
  (79 shorter events, 27.9 us)
Async XLA Ops:
  6.5 249.4 %copy-start = (bf16[896,2,512]{2,1,0:T(2,128)(2,1)S(1)}, bf16[896,2,512]{2,1,0:T(2,128)(2,1)}, u32[]{:S(2)}) copy-start(bf16[896,2,512]{2,1,0:T(2,128)(2,1)} %param.23) | copy-start | bytes 5505028
  9.3 13.7 %all-to-all-start = ((s32[8,1,2]{2,1,0:T(1,128)}), s32[8,1,2]{2,1,0:T(1,128)S(1)}, u32[]{:S(2)}, u32[]{:S(2)}) async-start(s32[8,1,2]{2,1,0:T(1,128)} %bitcast.3), calls=%async_computation | async-start | bytes 8192 | tf_op jit(solution)/shard_map/all_to_all | solution.py:70
  19.9 10.7 %copy-start.1 = (f32[2,128,896]{2,1,0:T(8,128)S(1)}, f32[2,128,896]{2,1,0:T(8,128)}, u32[]{:S(2)}) copy-start(f32[2,128,896]{2,1,0:T(8,128)} %param.14) | copy-start | bytes 2752516
  23.0 31.4 %all-to-all-start.1 = ((bf16[8,2,64,2,224]{4,1,3,2,0:T(2,128)(2,1)}), bf16[8,2,64,2,224]{4,1,3,2,0:T(2,128)(2,1)}, u32[]{:S(2)}, u32[]{:S(2)}) async-start(bf16[8,2,64,2,224]{4,1,3,2,0:T(2,128)(2,1)} %copy.104), calls=%async_computation.1 | async-start | bytes 2097152 | tf_op jit(solution)/shard_map/all_to_all | solution.py:63
  28.9 83.4 %reduce-scatter.2.cloned.1.call-start = ((), (), s32[]{:S(2)}) async-start(), calls=%async_computation.4 | async-start | bytes 4587520 | tf_op jit(solution)/shard_map/reduce_scatter | solution.py:106
  34.6 7.0 %copy-start.8 = (bf16[896,224]{0,1:T(8,128)(2,1)S(1)}, bf16[896,224]{0,1:T(8,128)(2,1)}, u32[]{:S(2)}) copy-start(bf16[896,224]{0,1:T(8,128)(2,1)} %param.18) | copy-start | bytes 1204228
  34.6 7.0 %copy-start.9 = (f32[896]{0:T(1024)S(1)}, f32[896]{0:T(1024)}, u32[]{:S(2)}) copy-start(f32[896]{0:T(1024)} %param.17) | copy-start | bytes 10756
  38.6 3.0 %copy-start.2 = (f32[16,128,896]{2,1,0:T(8,128)}, f32[16,128,896]{2,1,0:T(8,128)S(1)}, u32[]{:S(2)}) copy-start(f32[16,128,896]{2,1,0:T(8,128)S(1)} %get-tuple-element.8) | copy-start | bytes 22020100
  60.4 2.4 copy-start.5
  63.2 1.0 copy-start.6
  72.1 42.4 %copy-start.10 = (f32[896]{0:T(1024)S(1)}, f32[896]{0:T(1024)}, u32[]{:S(2)}) copy-start(f32[896]{0:T(1024)} %param.20) | copy-start | bytes 10756
  72.1 70.8 %all-gather.4.cloned.1.call-start = ((), (), s32[]{:S(2)}) async-start(), calls=%async_computation.5 | async-start | bytes 4014080 | tf_op jit(solution)/shard_map/all_gather | solution.py:111
  72.9 100.6 %all-gather.6.cloned.1.call-start = ((), (), s32[]{:S(2)}) async-start(), calls=%async_computation.6 | async-start | bytes 4014080 | tf_op jit(solution)/shard_map/all_gather | solution.py:112
  73.6 182.4 %all-gather.8.cloned.1.call-start = ((), (), s32[]{:S(2)}) async-start(), calls=%async_computation.7 | async-start | bytes 4587520 | tf_op jit(solution)/shard_map/all_gather | solution.py:150
  112.3 2.2 copy-start.4
  217.9 7.2 %copy-start.7 = (bf16[512,512]{1,0:T(8,128)(2,1)S(1)}, bf16[512,512]{1,0:T(8,128)(2,1)}, u32[]{:S(2)}) copy-start(bf16[512,512]{1,0:T(8,128)(2,1)} %param.13) | copy-start | bytes 1572868
  218.1 5.4 %collective-permute-start = (bf16[2,32,896]{2,1,0:T(8,128)(2,1)S(1)}, bf16[2,32,896]{2,1,0:T(8,128)(2,1)S(1)}, u32[]{:S(2)}, u32[]{:S(2)}) collective-permute-start(bf16[2,32,896]{2,1,0:T(8,128)(2,1)S(1)} %bitcast.114), channel_id=1, source_target_pairs={{0,4},{4,8},{8,12},{12,16},{16,20},{20,24},{24,28},{1,5},{5,9},{9,... | collective-permute-start | bytes 344072 | tf_op jit(solution)/shard_map/ppermute | solution.py:17
  271.6 1.3 copy-start.3
Sparse Core Ops, SparseCore 0:
  72.2 40.0 reduce-scatter.1
  113.9 28.8 all-gather.3
  144.5 28.8 all-gather.5
  225.2 30.7 all-gather.7
where the time goes:
time: 293 us; the launch traced here: 292 us
  waiting for transfers between devices  127 us (43%)
  local copies, waits for them, and re-layouts  51.3 us (18%)
  matrix products  39.1 us (13%)
  blocking collectives  29 us (10%)
  starting transfers between devices  16.5 us (6%)
  other arithmetic  15.6 us (5%)
  between operations  13.4 us (5%)
    reduce_scatter x1, waiting for transfers between devices, on_device(): lax.psum_scatter(partial_value.astype(jnp.bfloat16), 'mp', scatter_dimens...  38.5 us
    all_gather x1, waiting for transfers between devices, on_device(): lax.all_gather(used, 'mp', axis=2, tiled=True)  30.7 us
    all_to_all x1, blocking collectives, on_device(): lax.all_to_all(returning.reshape(seq_size, slot_cap, row_count, width), '...  29 us
    all_gather x1, waiting for transfers between devices, on_device(): lax.all_gather(ffn_up, 'mp', axis=1, tiled=True)  25.6 us
    all_gather x1, waiting for transfers between devices, on_device(): lax.all_gather(ffn_down, 'mp', axis=0, tiled=True)  18.3 us
    all_to_all x1, waiting for transfers between devices, on_device(): lax.all_to_all(outgoing.reshape(seq_size, slot_cap, SPAN, 2, enc_width),...  10.4 us
    unnamed x26, local copies, waits for them, and re-layouts  8.45 us
    all_to_all x1, starting transfers between devices, on_device(): lax.all_to_all(out_codes.reshape(seq_size, slot_cap), 'seq', split_axis=0...  7.25 us
  transfers between devices with their start and end apart: 7, of which 7 were waited for; matrix products, arithmetic and copies ran while one was open for 12% of the time, Pallas kernels for 0%

commit v1 on v0

v1 whole, which is shorter than its diff:
```python
import functools

import jax
import jax.numpy as jnp
from jax import lax
from jax.experimental import pallas as pl
from jax.experimental.pallas import tpu as pltpu
from jax.sharding import PartitionSpec as P

HEAD_DIM = 128
EHEAD_DIM = 112
SPAN = 64
NBL = 128
NEIGH = 2
CH_DEV = 8
HALVES = 2
BLOCK = 512
VMEM_LIMIT = 60 * 1024 * 1024

NT = (((1,), (1,)), ((), ()))
NN = (((1,), (0,)), ((), ()))


def mxu(lhs, rhs, dims):
    return lax.dot_general(lhs, rhs, dims, preferred_element_type=jnp.float32)


def rms_scale(values, gain):
    return values * lax.rsqrt(jnp.mean(values * values, axis=-1, keepdims=True) + 1e-06) * gain


def turned(chunk):
    return jnp.concatenate([chunk[:, SPAN:], chunk[:, :SPAN]], axis=1)


def attention_kernel(lanes, blocks, entries, before, seq_index, gain, *refs):
    refs = list(refs)
    db_refs = [refs.pop(0) for _ in range(blocks)]
    near = [[refs.pop(0) for _ in range(2)] for _ in range(lanes // 2)]
    far = [[refs.pop(0) for _ in range(2)] for _ in range(lanes // 2)]
    kv_refs = [refs.pop(0) for _ in range(lanes)]
    resid, nbrs, weights_in, kv_in, held, nbr_sem, piece_sem, out_sem = refs
    per_host = db_refs[0].shape[0] // 2
    part_rows, width = db_refs[0].shape[1:]
    span_rows = NEIGH * part_rows
    pair_rows = 2 * span_rows
    rows = CH_DEV * span_rows
    pad = HEAD_DIM - EHEAD_DIM
    scale = float(EHEAD_DIM) ** (-0.5)
    here = seq_index[0]
    odd = here % 2
    copies = []
    for span in range(CH_DEV):
        for k in range(NEIGH):
            entry = before[k, 0] if span == 0 else entries[k, span - 1]
            host, index = entry // per_host, entry % per_host
            block = (here // 2 - host // 2 + blocks) % blocks
            place = (here + host) % 2 * per_host + index
            spot = nbrs.at[span * NEIGH + k]
            for b in range(blocks):

                @pl.when(block == b)
                def _(b=b, place=place, spot=spot):
                    pltpu.make_async_copy(db_refs[b].at[place], spot, nbr_sem).start()

            copies.append(pltpu.make_async_copy(db_refs[0].at[0], spot, nbr_sem))
    piece_copies = []
    for p, pair in enumerate(near + far):
        mine = [
            pltpu.make_async_copy(ref, weights_in.at[p, i], piece_sem.at[p, i])
            for i, ref in enumerate(pair)
        ]
        mine.append(pltpu.make_async_copy(kv_refs[p], kv_in.at[p], piece_sem.at[p, 2]))
        for copy in mine:
            copy.start()
        piece_copies.append(mine)
    for copy in copies:
        copy.wait()
    lane = lax.broadcasted_iota(jnp.int32, (pair_rows, 2 * SPAN), 1)
    row = lax.broadcasted_iota(jnp.int32, (pair_rows, 2 * SPAN), 0)
    own_lanes = (lane < SPAN) == (row < span_rows)
    rest = jnp.zeros((pad, 2 * SPAN), jnp.bfloat16)
    empty = jnp.zeros((HEAD_DIM, 2 * SPAN), jnp.bfloat16)
    ones = jnp.ones((2 * HEAD_DIM - EHEAD_DIM, 2 * SPAN), jnp.bfloat16)
    weight_rest = jnp.zeros((pad, width), jnp.bfloat16)
    out_copies = []
    for start in range(0, rows, BLOCK):
        blocks_here = range(start // part_rows, (start + BLOCK) // part_rows)
        values = jnp.concatenate([nbrs[i].astype(jnp.float32) for i in blocks_here], axis=0)
        normed = rms_scale(values, gain[...]).astype(jnp.bfloat16)
        total = values
        for p in range(lanes):
            if start == 0:
                for copy in piece_copies[p]:
                    copy.wait()
            first, second = weights_in[p, 0], weights_in[p, 1]
            if p < lanes // 2:
                q_parts = (first[:EHEAD_DIM], first[EHEAD_DIM:])
                out_parts = (second[:EHEAD_DIM], second[EHEAD_DIM:])
            else:
                first, second = (
                    jnp.where(odd == 0, first, second),
                    jnp.where(odd == 0, second, first),
                )
                q_parts = (first[:EHEAD_DIM], second[:EHEAD_DIM])
                out_parts = (first[EHEAD_DIM:], second[EHEAD_DIM:])
            q_w = jnp.concatenate([q_parts[0], weight_rest, q_parts[1], weight_rest], axis=0)
            out_w = jnp.concatenate([out_parts[0], weight_rest, out_parts[1], weight_rest], axis=0)
            query = (mxu(normed, q_w, NT) * scale).astype(jnp.bfloat16)
            scores = []
            for at in range(0, BLOCK, pair_rows):
                tok = (start + at) // pair_rows * 2 * SPAN
                keys = kv_in[p, 0, :, tok : tok + 2 * SPAN]
                keys = jnp.concatenate(
                    [
                        jnp.concatenate([keys[:EHEAD_DIM], rest, empty], axis=0),
                        jnp.concatenate([empty, turned(keys[EHEAD_DIM:]), rest], axis=0),
                    ],
                    axis=1,
                )
                both = mxu(query[at : at + pair_rows], keys, NN)
                scores.append(jnp.where(own_lanes, both[:, : 2 * SPAN], both[:, 2 * SPAN :]))
            scores = jnp.concatenate(scores, axis=0)
            left = lax.broadcasted_iota(jnp.int32, scores.shape, 1) < SPAN
            low = jnp.max(jnp.where(left, scores, -jnp.inf), axis=1, keepdims=True)
            high = jnp.max(jnp.where(left, -jnp.inf, scores), axis=1, keepdims=True)
            weights = jnp.exp(scores - jnp.where(left, low, high)).astype(jnp.bfloat16)
            attended = []
            for at in range(0, BLOCK, pair_rows):
                tok = (start + at) // pair_rows * 2 * SPAN
                part = weights[at : at + pair_rows]
                vals = kv_in[p, 1, :, tok : tok + 2 * SPAN]
                heads = []
                for head in range(2):
                    picked = jnp.where(own_lanes if head == 0 else ~own_lanes, part, jnp.zeros_like(part))
                    of_head = vals[:EHEAD_DIM] if head == 0 else turned(vals[EHEAD_DIM:])
                    mixed = mxu(picked, jnp.concatenate([of_head, ones], axis=0), NT)
                    heads.append((mixed[:, :HEAD_DIM] / mixed[:, HEAD_DIM:]).astype(jnp.bfloat16))
                attended.append(jnp.concatenate(heads, axis=1))
            total = total + mxu(jnp.concatenate(attended, axis=0), out_w, NN)
        held[start : start + BLOCK, :] = total
        copy = pltpu.make_async_copy(
            held.at[pl.ds(start, BLOCK)], resid.at[pl.ds(start, BLOCK)], out_sem.at[start // BLOCK]
        )
        copy.start()
        out_copies.append(copy)
    for copy in out_copies:
        copy.wait()


def ffn_kernel(near, gain, resid, *refs):
    *group_refs, encoded, resid_in, near_in, far_in, resid_sem, near_sem, far_sem = refs
    count = resid.shape[0] // BLOCK
    resid_copies = [
        pltpu.make_async_copy(
            resid.at[pl.ds(i * BLOCK, BLOCK)], resid_in.at[pl.ds(i * BLOCK, BLOCK)], resid_sem.at[i]
        )
        for i in range(count)
    ]
    resid_copies[0].start()
    copies = []
    for i, ref in enumerate(group_refs):
        if i < 2 * near:
            copies.append(pltpu.make_async_copy(ref, near_in.at[i], near_sem.at[i]))
        else:
            j = i - 2 * near
            copies.append(pltpu.make_async_copy(ref, far_in.at[j], far_sem.at[j]))
        copies[-1].start()
    for copy in resid_copies[1:]:
        copy.start()
    half = far_in.shape[1] // 2
    groups = [([2 * i, 2 * i + 1], near_in.at[2 * i], near_in.at[2 * i + 1]) for i in range(near)]
    for j in range(len(group_refs) - 2 * near):
        groups.append(([2 * near + j], far_in.at[j, pl.ds(0, half)], far_in.at[j, pl.ds(half, half)]))
    for i in range(count):
        resid_copies[i].wait()
        total = resid_in[i * BLOCK : (i + 1) * BLOCK, :]
        normed = rms_scale(total, gain[...]).astype(jnp.bfloat16)

        def raised(g):
            if i == 0:
                for c in groups[g][0]:
                    copies[c].wait()
            return mxu(normed, groups[g][1][...], NT)

        ahead = raised(0)
        for g in range(len(groups)):
            units = ahead
            if g + 1 < len(groups):
                ahead = raised(g + 1)
            total = total + mxu(jax.nn.gelu(units).astype(jnp.bfloat16), groups[g][2][...], NN)
        encoded[i * BLOCK : (i + 1) * BLOCK, :] = total.astype(jnp.bfloat16)


def pairs_kernel(encoded, weights, pairs):
    for start in range(0, encoded.shape[0], BLOCK):
        pairs[start : start + BLOCK, :] = mxu(
            encoded[start : start + BLOCK, :], weights[...], NN
        ).astype(jnp.bfloat16)


def decoder_kernel(first, own_pairs, other, weights, queries, out, other_pairs):
    rows = other.shape[0]
    part = rows // CH_DEV
    width = queries.shape[1]
    scale = float(HEAD_DIM) ** (-0.5)
    for start in range(0, rows, BLOCK):
        other_pairs[start : start + BLOCK, :] = mxu(
            other[start : start + BLOCK, :], weights[...], NN
        ).astype(jnp.bfloat16)

    def span_pairs_of(span, col):
        return jnp.concatenate(
            [r[span * part : (span + 1) * part, col : col + HEAD_DIM] for r in (own_pairs, other_pairs)],
            axis=0,
        )

    for head in range(width // HEAD_DIM):
        col = head * HEAD_DIM
        query = (queries[:, col : col + HEAD_DIM].astype(jnp.float32) * scale).astype(jnp.bfloat16)
        scores = jnp.concatenate(
            [
                mxu(query[span * SPAN : (span + 1) * SPAN], span_pairs_of(span, col), NT)
                for span in range(CH_DEV)
            ],
            axis=0,
        )
        weights_f = jnp.exp(scores - jnp.max(scores, axis=1, keepdims=True))
        weights_f = weights_f / jnp.sum(weights_f, axis=1, keepdims=True)
        weights_b = weights_f.astype(jnp.bfloat16)
        for span in range(CH_DEV):
            result = mxu(
                weights_b[span * SPAN : (span + 1) * SPAN], span_pairs_of(span, width + col), NN
            )
            if span == 0:
                result = jnp.where(first[0] == 0, jnp.zeros_like(result), result)
            out[span * SPAN : (span + 1) * SPAN, col : col + HEAD_DIM] = result


def call(body, out_shape, in_specs, name, flops, scratch=(), out="v"):
    spaces = {"s": pltpu.SMEM, "v": pltpu.VMEM, "h": pl.ANY}
    return pl.pallas_call(
        body,
        out_shape=out_shape,
        in_specs=[pl.BlockSpec(memory_space=spaces[c]) for c in in_specs],
        out_specs=pl.BlockSpec(memory_space=spaces[out]),
        scratch_shapes=list(scratch),
        compiler_params=pltpu.CompilerParams(vmem_limit_bytes=VMEM_LIMIT),
        cost_estimate=pl.CostEstimate(flops=flops, bytes_accessed=8_000_000, transcendentals=0),
        name=name,
    )


def on_device(
    span_pairs,
    dec_queries,
    database,
    nbr_index,
    nbr_host,
    enc_gain,
    enc_query,
    enc_out,
    ffn_gain,
    ffn_up,
    ffn_down,
    dec_kv,
):
    seq_size = lax.axis_size("seq")
    lanes = lax.axis_size("mp")
    seq_index = lax.axis_index("seq")
    lane_index = lax.axis_index("mp")
    entries_here, block_rows, width = database.shape
    half_rows = block_rows // HALVES
    rows = CH_DEV * NEIGH * half_rows
    blocks = seq_size // 2
    odd = seq_index % 2
    far_lanes = lanes // 2 - 1

    def core_swap(array):
        return lax.ppermute(array, "mp", [(i, i ^ 1) for i in range(lanes)])

    def lane_step(array, step):
        return lax.ppermute(array, "mp", [(i, (i + 2 * step) % lanes) for i in range(lanes)])

    def seq_swap(array):
        return lax.ppermute(array, "seq", [(i, i ^ 1) for i in range(seq_size)])

    def seq_ring(array):
        return lax.ppermute(array, "seq", [(i, (i + 2) % seq_size) for i in range(seq_size)])

    def next_seq(array):
        return lax.ppermute(array, "seq", [(i, i + 1) for i in range(seq_size - 1)])

    def half_of(arrays):
        return jnp.concatenate(
            [
                lax.dynamic_slice_in_dim(a, odd * (a.shape[0] // 2), a.shape[0] // 2, 0)
                for a in arrays
            ],
            axis=0,
        )

    def after(array, *others):
        return lax.optimization_barrier((array, *others))[0]

    query_t, up_t = enc_query.T, ffn_up.T
    kv_t = jnp.transpose(span_pairs, (1, 2, 0))
    kv_rows, tokens = kv_t.shape[1:]
    kept = tokens - SPAN

    entries = (nbr_host * entries_here + nbr_index).T
    digits = jnp.stack([entries[:, CH_DEV - 1] // 128, entries[:, CH_DEV - 1] % 128], axis=1)
    digits = jnp.broadcast_to(digits[:, :, None], (2, 2, SPAN)).astype(jnp.bfloat16)
    packet = jnp.concatenate([kv_t[:, :, kept:], jnp.pad(digits, ((0, 0), (0, 14), (0, 0)))], axis=1)

    attention_half = half_of((query_t, enc_out))
    attention_far = [lane_step(attention_half, n + 1) for n in range(far_lanes)]
    packet = next_seq(packet)
    database_half = lax.dynamic_slice_in_dim(
        database, (lane_index % HALVES) * half_rows, half_rows, 1
    ).astype(jnp.bfloat16)
    block = jnp.concatenate([database_half, seq_swap(database_half)], axis=0)
    attention_core = (core_swap(query_t), core_swap(enc_out))

    database_blocks = [block]
    for _ in range(blocks - 1):
        database_blocks.append(seq_ring(database_blocks[-1]))

    before = packet[:, kv_rows : kv_rows + 2, 0].astype(jnp.int32)
    before = before[:, :1] * 128 + before[:, 1:]
    kv_t = jnp.concatenate([packet[:, :kv_rows], kv_t[:, :, :kept]], axis=2)

    ffn_half = after(half_of((up_t, ffn_down)), *attention_far)
    ffn_far = [lane_step(ffn_half, n + 1) for n in range(far_lanes)]
    attention_cross = [seq_swap(a) for a in attention_far]
    kv_core = core_swap(kv_t)
    kv_send = after(kv_t, *ffn_far)
    kv_far = [lane_step(kv_send, n + 1) for n in range(far_lanes)]
    ffn_cross = [seq_swap(a) for a in ffn_far]
    up_send, down_send = after((up_t, ffn_down), *attention_cross)
    ffn_core = (core_swap(up_send), core_swap(down_send))

    kv_pieces = [kv_t, kv_core]
    attention_pieces = [query_t, enc_out, *attention_core]
    for straight, crossed, kv in zip(attention_far, attention_cross, kv_far):
        attention_pieces += [straight, crossed, core_swap(straight), core_swap(crossed)]
        kv_pieces += [kv, core_swap(kv)]
    ffn_pieces = [up_t, ffn_down, *ffn_core]
    for piece in ffn_far + ffn_cross:
        ffn_pieces += [piece, core_swap(piece)]

    gemm = 2 * rows * width * width
    here = seq_index.reshape(1).astype(jnp.int32)
    spans_in = CH_DEV * NEIGH
    steps = rows // BLOCK
    dma = pltpu.SemaphoreType.DMA
    resid = call(
        functools.partial(attention_kernel, lanes, blocks),
        jax.ShapeDtypeStruct((rows, width), jnp.float32),
        "sss" + "v" + "h" * (blocks + 3 * lanes),
        "encoder_attention",
        2 * gemm,
        scratch=[
            pltpu.VMEM((spans_in, half_rows, width), jnp.bfloat16),
            pltpu.VMEM((lanes, 2, *enc_out.shape), jnp.bfloat16),
            pltpu.VMEM((lanes, *kv_t.shape), jnp.bfloat16),
            pltpu.VMEM((rows, width), jnp.float32),
            dma,
            dma((lanes, 3)),
            dma((steps,)),
        ],
        out="h",
    )(
        entries,
        before,
        here,
        enc_gain.reshape(1, width),
        *database_blocks,
        *attention_pieces,
        *kv_pieces,
    )
    far_pieces = len(ffn_pieces) - 4
    encoded = call(
        functools.partial(ffn_kernel, 2),
        jax.ShapeDtypeStruct((rows, width), jnp.bfloat16),
        "v" + "h" * (1 + len(ffn_pieces)),
        "encoder_ffn",
        4 * gemm,
        scratch=[
            pltpu.VMEM((rows, width), jnp.float32),
            pltpu.VMEM((4, *ffn_down.shape), jnp.bfloat16),
            pltpu.VMEM((far_pieces, *ffn_down.shape), jnp.bfloat16),
            dma((steps,)),
            dma((4,)),
            dma((far_pieces,)),
        ],
    )(ffn_gain.reshape(1, width), resid, *ffn_pieces)

    other = core_swap(encoded)
    dec_width = dec_kv.shape[2]
    kv_weights = dec_kv.reshape(width, 2 * dec_width)
    pairs_shape = (rows, 2 * dec_width)
    pairs_flops = 2 * rows * width * 2 * dec_width
    own_pairs = call(
        pairs_kernel, jax.ShapeDtypeStruct(pairs_shape, jnp.bfloat16), "vv", "decoder_pairs", pairs_flops
    )(encoded, kv_weights)
    return call(
        decoder_kernel,
        jax.ShapeDtypeStruct(dec_queries.shape, jnp.float32),
        "svvvv",
        "decoder_attention",
        pairs_flops,
        scratch=[pltpu.VMEM(pairs_shape, jnp.bfloat16)],
    )(here, own_pairs, other, kv_weights, dec_queries)


def solution(mesh):
    placed = (
        P("seq", None, "mp"),
        P("seq", "mp"),
        P("seq", None, None),
        P("seq", None),
        P("seq", None),
        P(),
        P(None, "mp"),
        P("mp", None),
        P(),
        P(None, "mp"),
        P("mp", None),
        P(None, None, "mp"),
    )
    return jax.shard_map(
        on_device, mesh=mesh, in_specs=placed, out_specs=P("seq", "mp"), check_vma=False
    )
```

time: 293 us -> 116 us (0.40)
  waiting for transfers between devices: 127 us -> 39.8 us
  Pallas kernels: 0 us -> 46.5 us
  local copies, waits for them, and re-layouts: 51.3 us -> 7.08 us
  matrix products: 39.1 us -> 0 us
  blocking collectives: 29 us -> 0 us
  other arithmetic: 15.6 us -> 1.39 us
  between operations: 13.4 us -> 0.31 us
  starting transfers between devices: 16.5 us -> 19.9 us
    all_gather x3 -> x0, waiting for transfers between devices: 74.6 us -> none  [the longest x1 30.7 us: on_device(): lax.all_gather(used, 'mp', axis=2, tiled=True)]
    pallas_call x0 -> x4, Pallas kernels: none -> 46.5 us  [the longest x1 16.8 us: on_device(): call(functools.partial(attention_kernel, lanes, blocks), jax.ShapeDtypeSt...]
    dot_general x13 -> x0, matrix products: 39.1 us -> none  [the longest x1 6.76 us: on_device(): jnp.einsum('mkre,ecd->mkrcd', lax.all_gather(used, 'mp', axis=2, tiled=Tr...]
    reduce_scatter x1 -> x0, waiting for transfers between devices: 38.5 us -> none  [on_device(): lax.psum_scatter(partial_value.astype(jnp.bfloat16), 'mp', scatter_dimens...]
    ppermute x1 -> x21, waiting for transfers between devices: 2.34 us -> 39.8 us  [the longest x3 18.6 us: seq_ring(): lax.ppermute(array, 'seq', [(i, (i + 2) % seq_size) for i in range(seq_si...]
    all_to_all x1 -> x0, blocking collectives: 29 us -> none  [on_device(): lax.all_to_all(returning.reshape(seq_size, slot_cap, row_count, width), '...]
    ppermute x1 -> x21, starting transfers between devices: 3 us -> 19.9 us  [the longest x3 5.65 us: seq_ring(): lax.ppermute(array, 'seq', [(i, (i + 2) % seq_size) for i in range(seq_si...]
    reshape x9 -> x2, local copies, waits for them, and re-layouts: 18.1 us -> 1.16 us  [the longest x1 0.58 us: on_device(): ffn_gain.reshape(1, width)]
  transfers between devices with their start and end apart: 7 -> 21, of which waited for: 7 -> 9; matrix products, arithmetic and copies ran while one was open for 12% -> 5% of each run, Pallas kernels for 0% -> 20%
where the time goes in v1:
time: 116 us; the launch traced here: 115 us
  Pallas kernels  46.5 us (40%)
  waiting for transfers between devices  39.8 us (34%)
  starting transfers between devices  19.9 us (17%)
  local copies, waits for them, and re-layouts  7.08 us (6%)
  other arithmetic  1.39 us (1%)
    ppermute x3, waiting for transfers between devices, seq_ring(): lax.ppermute(array, 'seq', [(i, (i + 2) % seq_size) for i in range(seq_si...  18.6 us
    pallas_call x1, Pallas kernels, on_device(): call(functools.partial(attention_kernel, lanes, blocks), jax.ShapeDtypeSt...  16.8 us
    pallas_call x1, Pallas kernels, on_device(): call(functools.partial(ffn_kernel, 2), jax.ShapeDtypeStruct((rows, width)...  15.9 us
    ppermute x3, waiting for transfers between devices, seq_swap(): return lax.ppermute(array, 'seq', [(i, i ^ 1) for i in range(seq_size)])  10.7 us
    pallas_call x1, Pallas kernels, on_device(): call(decoder_kernel, jax.ShapeDtypeStruct(dec_queries.shape, jnp.float32)...  8.07 us
    ppermute x3, waiting for transfers between devices, lane_step(): lax.ppermute(array, 'mp', [(i, (i + 2 * step) % lanes) for i in range(lan...  6.43 us
    pallas_call x1, Pallas kernels, on_device(): call(pairs_kernel, jax.ShapeDtypeStruct(pairs_shape, jnp.bfloat16), 'vv',...  5.75 us
    ppermute x3, starting transfers between devices, seq_ring(): lax.ppermute(array, 'seq', [(i, (i + 2) % seq_size) for i in range(seq_si...  5.65 us
  transfers between devices with their start and end apart: 21, of which 9 were waited for; matrix products, arithmetic and copies ran while one was open for 5% of the time, Pallas kernels for 20%

profile of v1, /device:TPU:0, one launch (start us, length us, event | category | flops | bytes accessed | tf_op | source)
XLA Modules:
  0.0 115.0 jit_solution(14701483856605081633)
XLA Ops:
  0.0 1.1 constant_dynamic-slice_fusion.1
  1.1 1.0 dynamic-slice_bitcast_fusion.1
  2.1 3.1 %collective-permute-start.7 = (bf16[224,896]{1,0:T(8,128)(2,1)S(1)}, bf16[224,896]{1,0:T(8,128)(2,1)S(1)}, u32[]{:S(2)}, u32[]{:S(2)}) collective-permute-start(bf16[224,896]{1,0:T(8,128)(2,1)S(1)} %pad_maximum_fusion.3), channel_id=1, source_target_pairs={{0,2},{1,3},{2,0},{3,1},{4,6},{5,7},{6,4},{7,5},{8,10},{9,11},{10,... | collective-permute-start | bytes 1204232 | tf_op jit(solution)/shard_map/ppermute | solution.py:283
  5.2 1.6 %collective-permute-start.1 = (bf16[2,64,896]{2,1,0:T(8,128)(2,1)S(1)}, bf16[2,64,896]{2,1,0:T(8,128)(2,1)S(1)}, u32[]{:S(2)}, u32[]{:S(2)}) collective-permute-start(bf16[2,64,896]{2,1,0:T(8,128)(2,1)S(1)} %dynamic-slice_convert_fusion), channel_id=1, source_target_pairs={{0,4},{4,0},{8,12},{12,8},{16,20},{20,16},{24,28},{28,24},{1,5},{5... | collective-permute-start | bytes 688136 | tf_op jit(solution)/shard_map/ppermute | solution.py:286
  6.8 1.0 constant_dynamic-slice_fusion
  8.0 6.4 %collective-permute-done.7.refs_8_ = bf16[224,896]{1,0:T(8,128)(2,1)S(1)} collective-permute-done((bf16[224,896]{1,0:T(8,128)(2,1)S(1)}, bf16[224,896]{1,0:T(8,128)(2,1)S(1)}, u32[]{:S(2)}, u32[]{:S(2)}) %collective-permute-start.7) | collective-permute-done | bytes 401440 | tf_op jit(solution)/shard_map/ppermute | solution.py:283
  14.5 1.7 %collective-permute-start.12 = (bf16[448,896]{1,0:T(8,128)(2,1)S(1)}, bf16[448,896]{1,0:T(8,128)(2,1)}, u32[]{:S(2)}, u32[]{:S(2)}) collective-permute-start(bf16[448,896]{1,0:T(8,128)(2,1)S(1)} %pad_maximum_fusion), channel_id=1, source_target_pairs={{0,2},{1,3},{2,0},{3,1},{4,6},{5,7},{6,4},{7,5},{8,10},{9,11},{10,... | collective-permute-start | bytes 2408456 | tf_op jit(solution)/shard_map/ppermute | solution.py:283
  16.3 1.6 %collective-permute-start.2 = (bf16[4,64,896]{2,1,0:T(8,128)(2,1)S(1)}, bf16[4,64,896]{2,1,0:T(8,128)(2,1)S(1)}, u32[]{:S(2)}, u32[]{:S(2)}) collective-permute-start(bf16[4,64,896]{2,1,0:T(8,128)(2,1)S(1)} %pad_maximum_fusion.1.refs_0_), channel_id=1, source_target_pairs={{0,8},{4,12},{8,16},{12,20},{16,24},{20,28},{24,0},{28,4},{1,9},{5... | collective-permute-start | bytes 1376264 | tf_op jit(solution)/shard_map/ppermute | solution.py:289
  18.3 3.4 %collective-permute-start = (bf16[2,240,64]{2,1,0:T(8,128)(2,1)S(1)}, bf16[2,240,64]{2,1,0:T(8,128)(2,1)S(1)}, u32[]{:S(2)}, u32[]{:S(2)}) collective-permute-start(bf16[2,240,64]{2,1,0:T(8,128)(2,1)S(1)} %fusion.1), channel_id=1, source_target_pairs={{0,4},{4,8},{8,12},{12,16},{16,20},{20,24},{24,28},{1,5},{5,9},{9,... | collective-permute-start | bytes 184328 | tf_op jit(solution)/shard_map/ppermute | solution.py:292
  21.7 2.4 %collective-permute-done = bf16[2,240,64]{2,1,0:T(8,128)(2,1)S(1)} collective-permute-done((bf16[2,240,64]{2,1,0:T(8,128)(2,1)S(1)}, bf16[2,240,64]{2,1,0:T(8,128)(2,1)S(1)}, u32[]{:S(2)}, u32[]{:S(2)}) %collective-permute-start) | collective-permute-done | bytes 61472 | tf_op jit(solution)/shard_map/ppermute | solution.py:292
  24.1 5.2 %collective-permute-done.2.refs_1_ = bf16[4,64,896]{2,1,0:T(8,128)(2,1)S(1)} collective-permute-done((bf16[4,64,896]{2,1,0:T(8,128)(2,1)S(1)}, bf16[4,64,896]{2,1,0:T(8,128)(2,1)S(1)}, u32[]{:S(2)}, u32[]{:S(2)}) %collective-permute-start.2) | collective-permute-done | bytes 458784 | tf_op jit(solution)/shard_map/ppermute | solution.py:289
  29.3 3.8 %collective-permute-start.3 = (bf16[4,64,896]{2,1,0:T(8,128)(2,1)S(1)}, bf16[4,64,896]{2,1,0:T(8,128)(2,1)S(1)}, u32[]{:S(2)}, u32[]{:S(2)}) collective-permute-start(bf16[4,64,896]{2,1,0:T(8,128)(2,1)S(1)} %collective-permute-done.2.refs_1_), channel_id=1, source_target_pairs={{0,8},{4,12},{8,16},{12,20},{16,24},{20,28},{24,0},{28,4},{1,9},{5... | collective-permute-start | bytes 1376264 | tf_op jit(solution)/shard_map/ppermute | solution.py:289
  33.4 0.5 collective-permute-start.6
  33.9 2.0 %collective-permute-start.18 = (bf16[448,896]{1,0:T(8,128)(2,1)}, bf16[448,896]{1,0:T(8,128)(2,1)}, u32[]{:S(2)}, u32[]{:S(2)}) collective-permute-start(bf16[448,896]{1,0:T(8,128)(2,1)} %collective-permute-done.12.refs_4_), channel_id=1, source_target_pairs={{0,4},{4,0},{8,12},{12,8},{16,20},{20,16},{24,28},{28,24},{1,5},{5... | collective-permute-start | bytes 2408456 | tf_op jit(solution)/shard_map/ppermute | solution.py:286
  35.9 7.5 %collective-permute-done.3.refs_2_ = bf16[4,64,896]{2,1,0:T(8,128)(2,1)S(1)} collective-permute-done((bf16[4,64,896]{2,1,0:T(8,128)(2,1)S(1)}, bf16[4,64,896]{2,1,0:T(8,128)(2,1)S(1)}, u32[]{:S(2)}, u32[]{:S(2)}) %collective-permute-start.3) | collective-permute-done | bytes 458784 | tf_op jit(solution)/shard_map/ppermute | solution.py:289
  43.7 0.5 collective-permute-start.13
  44.2 2.0 %collective-permute-done.8.refs_9_ = bf16[224,896]{1,0:T(8,128)(2,1)S(1)} collective-permute-done((bf16[224,896]{1,0:T(8,128)(2,1)}, bf16[224,896]{1,0:T(8,128)(2,1)S(1)}, u32[]{:S(2)}, u32[]{:S(2)}) %collective-permute-start.8) | collective-permute-done | bytes 401440 | tf_op jit(solution)/shard_map/ppermute | solution.py:286
  46.3 0.5 collective-permute-start.15
  46.8 1.2 %collective-permute-done.10.refs_11_ = bf16[224,896]{1,0:T(8,128)(2,1)S(1)} collective-permute-done((bf16[224,896]{1,0:T(8,128)(2,1)S(1)}, bf16[224,896]{1,0:T(8,128)(2,1)S(1)}, u32[]{:S(2)}, u32[]{:S(2)}) %collective-permute-start.10) | collective-permute-done | bytes 401440 | tf_op jit(solution)/shard_map/ppermute | solution.py:280
  48.1 5.9 %collective-permute-done.4.refs_3_ = bf16[4,64,896]{2,1,0:T(8,128)(2,1)S(1)} collective-permute-done((bf16[4,64,896]{2,1,0:T(8,128)(2,1)S(1)}, bf16[4,64,896]{2,1,0:T(8,128)(2,1)S(1)}, u32[]{:S(2)}, u32[]{:S(2)}) %collective-permute-start.4) | collective-permute-done | bytes 458784 | tf_op jit(solution)/shard_map/ppermute | solution.py:289
  54.0 8.7 %collective-permute-done.18.refs_6_ = bf16[448,896]{1,0:T(8,128)(2,1)} collective-permute-done((bf16[448,896]{1,0:T(8,128)(2,1)}, bf16[448,896]{1,0:T(8,128)(2,1)}, u32[]{:S(2)}, u32[]{:S(2)}) %collective-permute-start.18) | collective-permute-done | bytes 802848 | tf_op jit(solution)/shard_map/ppermute | solution.py:286
  62.7 0.6 collective-permute-start.14
  63.3 0.6 reshape.17.gain
  63.9 0.6 reshape.16.gain
  64.6 0.7 slice_add_fusion.before
  65.2 0.4 collective-permute-done.14.refs_15_
  65.7 0.8 copy-done.18
  66.4 16.8 %encoder_attention.1.resid = f32[1024,896]{1,0:T(8,128)} custom-call(s32[2,8]{1,0:T(2,128)} %copy-done.8, s32[2,1]{1,0:T(2,128)} %slice_add_fusion.before, s32[1]{0:T(128)} %bitcast.seq_index.first, f32[1,896]{1,0:T(1,128)} %reshape.17.gain, bf16[4,64,896]{2,1,0:T(8,128)(2,1)} %copy-done.3, bf16[4,64,896]{2,1,0:T(8,128)(2,1)} %copy-done.13, ...), custom_call_target="tpu_custom_call" | custom-call | flops 3288334336 | bytes 8000000 | tf_op jit(solution)/shard_map/encoder_attention/pallas_call | solution.py:357
  83.3 15.9 %encoder_ffn.1.encoded = bf16[1024,896]{1,0:T(8,128)(2,1)} custom-call(f32[1,896]{1,0:T(1,128)} %reshape.16.gain, f32[1024,896]{1,0:T(8,128)} %encoder_attention.1.resid, bf16[448,896]{1,0:T(8,128)(2,1)} %bitcast.18, bf16[448,896]{1,0:T(8,128)(2,1)} %refs_1_.1, bf16[448,896]{1,0:T(8,128)(2,1)} %collective-permute-done.15.refs_2_, ...), custom_call_target="tpu_custom_call" | custom-call | flops 6576668672 | bytes 8000000 | tf_op jit(solution)/shard_map/encoder_ffn/pallas_call | solution.py:383
  99.4 1.7 %copy.13 = bf16[112,8,2,512]{3,1,2,0:T(8,128)(2,1)} copy(bf16[112,8,2,512]{3,2,1,0:T(2,128)(2,1)S(1)} %bitcast.15) | data formatting | bytes 3670016
  101.1 5.8 %decoder_pairs.1.own_pairs = bf16[1024,1024]{1,0:T(8,128)(2,1)} custom-call(bf16[1024,896]{1,0:T(8,128)(2,1)} %encoder_ffn.1.encoded, bf16[896,1024]{1,0:T(8,128)(2,1)} %bitcast.13), custom_call_target="tpu_custom_call" | custom-call | flops 1879048192 | bytes 8000000 | tf_op jit(solution)/shard_map/decoder_pairs/pallas_call | solution.py:404
  106.9 8.1 %decoder_attention.1 = f32[512,512]{1,0:T(8,128)} custom-call(s32[1]{0:T(128)} %bitcast.seq_index.first, bf16[1024,1024]{1,0:T(8,128)(2,1)} %decoder_pairs.1.own_pairs, bf16[1024,896]{1,0:T(8,128)(2,1)} %collective-permute-done.20.other, bf16[896,1024]{1,0:T(8,128)(2,1)} %bitcast.14, bf16[512,512]{1,0:T(8,128)(2,1)} %queries.1), custom_call_target="tpu_custom_call" | custom-call | flops 1879048192 | bytes 8000000 | tf_op jit(solution)/shard_map/decoder_attention/pallas_call | solution.py:407
  (81 shorter events, 1.8 us)
Async XLA Ops:
  2.1 12.3 %collective-permute-start.7 = (bf16[224,896]{1,0:T(8,128)(2,1)S(1)}, bf16[224,896]{1,0:T(8,128)(2,1)S(1)}, u32[]{:S(2)}, u32[]{:S(2)}) collective-permute-start(bf16[224,896]{1,0:T(8,128)(2,1)S(1)} %pad_maximum_fusion.3), channel_id=1, source_target_pairs={{0,2},{1,3},{2,0},{3,1},{4,6},{5,7},{6,4},{7,5},{8,10},{9,11},{10,... | collective-permute-start | bytes 1204232 | tf_op jit(solution)/shard_map/ppermute | solution.py:283
  5.2 11.0 %collective-permute-start.1 = (bf16[2,64,896]{2,1,0:T(8,128)(2,1)S(1)}, bf16[2,64,896]{2,1,0:T(8,128)(2,1)S(1)}, u32[]{:S(2)}, u32[]{:S(2)}) collective-permute-start(bf16[2,64,896]{2,1,0:T(8,128)(2,1)S(1)} %dynamic-slice_convert_fusion), channel_id=1, source_target_pairs={{0,4},{4,0},{8,12},{12,8},{16,20},{20,16},{24,28},{28,24},{1,5},{5... | collective-permute-start | bytes 688136 | tf_op jit(solution)/shard_map/ppermute | solution.py:286
  6.8 27.1 %collective-permute-start.5 = (bf16[224,896]{1,0:T(8,128)(2,1)S(1)}, bf16[224,896]{1,0:T(8,128)(2,1)}, u32[]{:S(2)}, u32[]{:S(2)}) collective-permute-start(bf16[224,896]{1,0:T(8,128)(2,1)S(1)} %bitcast.21), channel_id=1, source_target_pairs={{0,1},{1,0},{2,3},{3,2},{4,5},{5,4},{6,7},{7,6},{8,9},{9,8},{10,11... | collective-permute-start | bytes 1204232 | tf_op jit(solution)/shard_map/ppermute | solution.py:280
  7.9 25.5 %copy-start.7 = (bf16[224,896]{1,0:T(8,128)(2,1)S(1)}, bf16[224,896]{1,0:T(8,128)(2,1)}, u32[]{:S(2)}) copy-start(bf16[224,896]{1,0:T(8,128)(2,1)} %refs_5_.1) | copy-start | bytes 1204228
  7.9 55.4 %copy-start.9 = (f32[896]{0:T(1024)S(1)}, f32[896]{0:T(1024)}, u32[]{:S(2)}) copy-start(f32[896]{0:T(1024)} %param.17) | copy-start | bytes 10756
  7.9 56.0 %copy-start.10 = (f32[896]{0:T(1024)S(1)}, f32[896]{0:T(1024)}, u32[]{:S(2)}) copy-start(f32[896]{0:T(1024)} %param.20) | copy-start | bytes 10756
  8.0 58.4 %copy-start.8 = (s32[2,8]{1,0:T(2,128)}, s32[2,8]{1,0:T(2,128)S(1)}, u32[]{:S(2)}) copy-start(s32[2,8]{1,0:T(2,128)S(1)} %add_bitcast_fusion.entries) | copy-start | bytes 196
  14.4 18.6 %copy-start.19 = (bf16[224,896]{1,0:T(8,128)(2,1)}, bf16[224,896]{1,0:T(8,128)(2,1)S(1)}, u32[]{:S(2)}) copy-start(bf16[224,896]{1,0:T(8,128)(2,1)S(1)} %collective-permute-done.7.refs_8_) | copy-start | bytes 1204228
  14.5 19.4 %collective-permute-start.12 = (bf16[448,896]{1,0:T(8,128)(2,1)S(1)}, bf16[448,896]{1,0:T(8,128)(2,1)}, u32[]{:S(2)}, u32[]{:S(2)}) collective-permute-start(bf16[448,896]{1,0:T(8,128)(2,1)S(1)} %pad_maximum_fusion), channel_id=1, source_target_pairs={{0,2},{1,3},{2,0},{3,1},{4,6},{5,7},{6,4},{7,5},{8,10},{9,11},{10,... | collective-permute-start | bytes 2408456 | tf_op jit(solution)/shard_map/ppermute | solution.py:283
  16.2 50.2 %copy-start.3 = (bf16[4,64,896]{2,1,0:T(8,128)(2,1)}, bf16[4,64,896]{2,1,0:T(8,128)(2,1)S(1)}, u32[]{:S(2)}) copy-start(bf16[4,64,896]{2,1,0:T(8,128)(2,1)S(1)} %pad_maximum_fusion.1.refs_0_) | copy-start | bytes 1376260
  16.3 13.0 %collective-permute-start.2 = (bf16[4,64,896]{2,1,0:T(8,128)(2,1)S(1)}, bf16[4,64,896]{2,1,0:T(8,128)(2,1)S(1)}, u32[]{:S(2)}, u32[]{:S(2)}) collective-permute-start(bf16[4,64,896]{2,1,0:T(8,128)(2,1)S(1)} %pad_maximum_fusion.1.refs_0_), channel_id=1, source_target_pairs={{0,8},{4,12},{8,16},{12,20},{16,24},{20,28},{24,0},{28,4},{1,9},{5... | collective-permute-start | bytes 1376264 | tf_op jit(solution)/shard_map/ppermute | solution.py:289
  18.3 5.8 %collective-permute-start = (bf16[2,240,64]{2,1,0:T(8,128)(2,1)S(1)}, bf16[2,240,64]{2,1,0:T(8,128)(2,1)S(1)}, u32[]{:S(2)}, u32[]{:S(2)}) collective-permute-start(bf16[2,240,64]{2,1,0:T(8,128)(2,1)S(1)} %fusion.1), channel_id=1, source_target_pairs={{0,4},{4,8},{8,12},{12,16},{16,20},{20,24},{24,28},{1,5},{5,9},{9,... | collective-permute-start | bytes 184328 | tf_op jit(solution)/shard_map/ppermute | solution.py:292
  29.3 37.1 %copy-start.13 = (bf16[4,64,896]{2,1,0:T(8,128)(2,1)}, bf16[4,64,896]{2,1,0:T(8,128)(2,1)S(1)}, u32[]{:S(2)}) copy-start(bf16[4,64,896]{2,1,0:T(8,128)(2,1)S(1)} %collective-permute-done.2.refs_1_) | copy-start | bytes 1376260
  29.3 14.2 %collective-permute-start.3 = (bf16[4,64,896]{2,1,0:T(8,128)(2,1)S(1)}, bf16[4,64,896]{2,1,0:T(8,128)(2,1)S(1)}, u32[]{:S(2)}, u32[]{:S(2)}) collective-permute-start(bf16[4,64,896]{2,1,0:T(8,128)(2,1)S(1)} %collective-permute-done.2.refs_1_), channel_id=1, source_target_pairs={{0,8},{4,12},{8,16},{12,20},{16,24},{20,28},{24,0},{28,4},{1,9},{5... | collective-permute-start | bytes 1376264 | tf_op jit(solution)/shard_map/ppermute | solution.py:289
  33.3 33.1 %copy-start.4 = (bf16[2,224,512]{2,1,0:T(8,128)(2,1)}, bf16[2,224,512]{2,1,0:T(8,128)(2,1)S(1)}, u32[]{:S(2)}) copy-start(bf16[2,224,512]{2,1,0:T(8,128)(2,1)S(1)} %pad_maximum_fusion.2.refs_12_) | copy-start | bytes 1376260
  33.3 10.9 %collective-permute-start.11 = (bf16[2,224,512]{2,1,0:T(8,128)(2,1)S(1)}, bf16[2,224,512]{2,1,0:T(8,128)(2,1)S(1)}, u32[]{:S(2)}, u32[]{:S(2)}) collective-permute-start(bf16[2,224,512]{2,1,0:T(8,128)(2,1)S(1)} %pad_maximum_fusion.2.refs_12_), channel_id=1, source_target_pairs={{0,1},{1,0},{2,3},{3,2},{4,5},{5,4},{6,7},{7,6},{8,9},{9,8},{10,11... | collective-permute-start | bytes 1376264 | tf_op jit(solution)/shard_map/ppermute | solution.py:280
  33.4 10.3 %collective-permute-start.6 = (bf16[224,896]{1,0:T(8,128)(2,1)S(1)}, bf16[224,896]{1,0:T(8,128)(2,1)}, u32[]{:S(2)}, u32[]{:S(2)}) collective-permute-start(bf16[224,896]{1,0:T(8,128)(2,1)S(1)} %copy-done.7), channel_id=1, source_target_pairs={{0,1},{1,0},{2,3},{3,2},{4,5},{5,4},{6,7},{7,6},{8,9},{9,8},{10,11... | collective-permute-start | bytes 1204232 | tf_op jit(solution)/shard_map/ppermute | solution.py:280
  33.9 12.4 %collective-permute-start.8 = (bf16[224,896]{1,0:T(8,128)(2,1)}, bf16[224,896]{1,0:T(8,128)(2,1)S(1)}, u32[]{:S(2)}, u32[]{:S(2)}) collective-permute-start(bf16[224,896]{1,0:T(8,128)(2,1)} %copy-done.19), channel_id=1, source_target_pairs={{0,4},{4,0},{8,12},{12,8},{16,20},{20,16},{24,28},{28,24},{1,5},{5... | collective-permute-start | bytes 1204232 | tf_op jit(solution)/shard_map/ppermute | solution.py:286
  33.9 28.8 %collective-permute-start.18 = (bf16[448,896]{1,0:T(8,128)(2,1)}, bf16[448,896]{1,0:T(8,128)(2,1)}, u32[]{:S(2)}, u32[]{:S(2)}) collective-permute-start(bf16[448,896]{1,0:T(8,128)(2,1)} %collective-permute-done.12.refs_4_), channel_id=1, source_target_pairs={{0,4},{4,0},{8,12},{12,8},{16,20},{20,16},{24,28},{28,24},{1,5},{5... | collective-permute-start | bytes 2408456 | tf_op jit(solution)/shard_map/ppermute | solution.py:286
  43.5 23.0 %copy-start.14 = (bf16[4,64,896]{2,1,0:T(8,128)(2,1)}, bf16[4,64,896]{2,1,0:T(8,128)(2,1)S(1)}, u32[]{:S(2)}) copy-start(bf16[4,64,896]{2,1,0:T(8,128)(2,1)S(1)} %collective-permute-done.3.refs_2_) | copy-start | bytes 1376260
  43.5 10.5 %collective-permute-start.4 = (bf16[4,64,896]{2,1,0:T(8,128)(2,1)S(1)}, bf16[4,64,896]{2,1,0:T(8,128)(2,1)S(1)}, u32[]{:S(2)}, u32[]{:S(2)}) collective-permute-start(bf16[4,64,896]{2,1,0:T(8,128)(2,1)S(1)} %collective-permute-done.3.refs_2_), channel_id=1, source_target_pairs={{0,8},{4,12},{8,16},{12,20},{16,24},{20,28},{24,0},{28,4},{1,9},{5... | collective-permute-start | bytes 1376264 | tf_op jit(solution)/shard_map/ppermute | solution.py:289
  43.7 19.0 %collective-permute-start.13 = (bf16[2,224,512]{2,1,0:T(8,128)(2,1)S(1)}, bf16[2,224,512]{2,1,0:T(8,128)(2,1)S(1)}, u32[]{:S(2)}, u32[]{:S(2)}) collective-permute-start(bf16[2,224,512]{2,1,0:T(8,128)(2,1)S(1)} %pad_maximum_fusion.2.refs_12_), channel_id=1, source_target_pairs={{0,2},{1,3},{2,0},{3,1},{4,6},{5,7},{6,4},{7,5},{8,10},{9,11},{10,... | collective-permute-start | bytes 1376264 | tf_op jit(solution)/shard_map/ppermute | solution.py:283
  44.2 21.0 %copy-start.15 = (bf16[2,224,512]{2,1,0:T(8,128)(2,1)}, bf16[2,224,512]{2,1,0:T(8,128)(2,1)S(1)}, u32[]{:S(2)}) copy-start(bf16[2,224,512]{2,1,0:T(8,128)(2,1)S(1)} %collective-permute-done.11.refs_13_) | copy-start | bytes 1376260
  44.2 2.0 %collective-permute-start.9 = (bf16[224,896]{1,0:T(8,128)(2,1)}, bf16[224,896]{1,0:T(8,128)(2,1)S(1)}, u32[]{:S(2)}, u32[]{:S(2)}) collective-permute-start(bf16[224,896]{1,0:T(8,128)(2,1)} %copy-done.19), channel_id=1, source_target_pairs={{0,1},{1,0},{2,3},{3,2},{4,5},{5,4},{6,7},{7,6},{8,9},{9,8},{10,11... | collective-permute-start | bytes 1204232 | tf_op jit(solution)/shard_map/ppermute | solution.py:280
  46.2 17.6 %copy-start.20 = (bf16[224,896]{1,0:T(8,128)(2,1)}, bf16[224,896]{1,0:T(8,128)(2,1)S(1)}, u32[]{:S(2)}) copy-start(bf16[224,896]{1,0:T(8,128)(2,1)S(1)} %collective-permute-done.8.refs_9_) | copy-start | bytes 1204228
  46.2 1.7 %collective-permute-start.10 = (bf16[224,896]{1,0:T(8,128)(2,1)S(1)}, bf16[224,896]{1,0:T(8,128)(2,1)S(1)}, u32[]{:S(2)}, u32[]{:S(2)}) collective-permute-start(bf16[224,896]{1,0:T(8,128)(2,1)S(1)} %collective-permute-done.8.refs_9_), channel_id=1, source_target_pairs={{0,1},{1,0},{2,3},{3,2},{4,5},{5,4},{6,7},{7,6},{8,9},{9,8},{10,11... | collective-permute-start | bytes 1204232 | tf_op jit(solution)/shard_map/ppermute | solution.py:280
  46.3 37.0 %collective-permute-start.15 = (bf16[448,896]{1,0:T(8,128)(2,1)S(1)}, bf16[448,896]{1,0:T(8,128)(2,1)}, u32[]{:S(2)}, u32[]{:S(2)}) collective-permute-start(bf16[448,896]{1,0:T(8,128)(2,1)S(1)} %bitcast.19), channel_id=1, source_target_pairs={{0,1},{1,0},{2,3},{3,2},{4,5},{5,4},{6,7},{7,6},{8,9},{9,8},{10,11... | collective-permute-start | bytes 2408456 | tf_op jit(solution)/shard_map/ppermute | solution.py:280
  48.0 35.2 %collective-permute-start.16 = (bf16[448,896]{1,0:T(8,128)(2,1)}, bf16[448,896]{1,0:T(8,128)(2,1)}, u32[]{:S(2)}, u32[]{:S(2)}) collective-permute-start(bf16[448,896]{1,0:T(8,128)(2,1)} %refs_1_.1), channel_id=1, source_target_pairs={{0,1},{1,0},{2,3},{3,2},{4,5},{5,4},{6,7},{7,6},{8,9},{9,8},{10,11... | collective-permute-start | bytes 2408456 | tf_op jit(solution)/shard_map/ppermute | solution.py:280
  54.0 29.2 %collective-permute-start.17 = (bf16[448,896]{1,0:T(8,128)(2,1)}, bf16[448,896]{1,0:T(8,128)(2,1)}, u32[]{:S(2)}, u32[]{:S(2)}) collective-permute-start(bf16[448,896]{1,0:T(8,128)(2,1)} %collective-permute-done.12.refs_4_), channel_id=1, source_target_pairs={{0,1},{1,0},{2,3},{3,2},{4,5},{5,4},{6,7},{7,6},{8,9},{9,8},{10,11... | collective-permute-start | bytes 2408456 | tf_op jit(solution)/shard_map/ppermute | solution.py:280
  62.7 20.6 %collective-permute-start.19 = (bf16[448,896]{1,0:T(8,128)(2,1)}, bf16[448,896]{1,0:T(8,128)(2,1)}, u32[]{:S(2)}, u32[]{:S(2)}) collective-permute-start(bf16[448,896]{1,0:T(8,128)(2,1)} %collective-permute-done.18.refs_6_), channel_id=1, source_target_pairs={{0,1},{1,0},{2,3},{3,2},{4,5},{5,4},{6,7},{7,6},{8,9},{9,8},{10,11... | collective-permute-start | bytes 2408456 | tf_op jit(solution)/shard_map/ppermute | solution.py:280
  62.7 2.9 %collective-permute-start.14 = (bf16[2,224,512]{2,1,0:T(8,128)(2,1)S(1)}, bf16[2,224,512]{2,1,0:T(8,128)(2,1)S(1)}, u32[]{:S(2)}, u32[]{:S(2)}) collective-permute-start(bf16[2,224,512]{2,1,0:T(8,128)(2,1)S(1)} %collective-permute-done.13.refs_14_), channel_id=1, source_target_pairs={{0,1},{1,0},{2,3},{3,2},{4,5},{5,4},{6,7},{7,6},{8,9},{9,8},{10,11... | collective-permute-start | bytes 1376264 | tf_op jit(solution)/shard_map/ppermute | solution.py:280
  99.2 7.7 %collective-permute-start.20 = (bf16[1024,896]{1,0:T(8,128)(2,1)}, bf16[1024,896]{1,0:T(8,128)(2,1)}, u32[]{:S(2)}, u32[]{:S(2)}) collective-permute-start(bf16[1024,896]{1,0:T(8,128)(2,1)} %encoder_ffn.1.encoded), channel_id=1, source_target_pairs={{0,1},{1,0},{2,3},{3,2},{4,5},{5,4},{6,7},{7,6},{8,9},{9,8},{10,11... | collective-permute-start | bytes 5505032 | tf_op jit(solution)/shard_map/ppermute | solution.py:280
  (12 other events, 98.3 us)

commit v2 on v1

v2 whole, which is shorter than its diff:
```python
import functools

import jax
import jax.numpy as jnp
from jax import lax
from jax.experimental import pallas as pl
from jax.experimental.pallas import tpu as pltpu
from jax.sharding import PartitionSpec as P

HEAD_DIM = 128
EHEAD_DIM = 112
SPAN = 64
NBL = 128
NEIGH = 2
CH_DEV = 8
HALVES = 2
BLOCK = 512
DIGIT = 128

NT = (((1,), (1,)), ((), ()))
NN = (((1,), (0,)), ((), ()))


def mxu(lhs, rhs, dims):
    return lax.dot_general(lhs, rhs, dims, preferred_element_type=jnp.float32)


def rms_scale(values, gain):
    return values * lax.rsqrt(jnp.mean(values * values, axis=-1, keepdims=True) + 1e-06) * gain


def turned(chunk):
    return jnp.concatenate([chunk[:, SPAN:], chunk[:, :SPAN]], axis=1)


def prepare_kernel(place, host, index, database, query_t, enc_out, up_t, down, kv_t, *refs):
    db_half, attention_half, ffn_half, packet, db_in, kv_in, sems = refs
    per_host, half_rows, width = db_half.shape
    seq, lane = place[0], place[1]
    copies = [
        pltpu.make_async_copy(
            database.at[:, pl.ds(pl.multiple_of(lane % HALVES * half_rows, half_rows), half_rows)],
            db_in,
            sems.at[0],
        ),
        pltpu.make_async_copy(kv_t.at[:, :, pl.ds(kv_t.shape[2] - 2 * SPAN, 2 * SPAN)], kv_in, sems.at[1]),
    ]
    halves = ((query_t, attention_half, 0, seq % 2), (enc_out, attention_half, 1, seq % 2))
    halves += ((up_t, ffn_half, 0, seq // 2 % 2), (down, ffn_half, 1, seq // 2 % 2))
    for i, (source, target, spot, parity) in enumerate(halves):
        count = source.shape[0] // 2
        copies.append(
            pltpu.make_async_copy(
                source.at[pl.ds(pl.multiple_of(parity * count, 16), count)],
                target.at[pl.ds(spot * count, count)],
                sems.at[2 + i],
            )
        )
    for copy in copies:
        copy.start()
    copies[0].wait()
    db_half[...] = db_in[...].astype(jnp.bfloat16)
    copies[1].wait()
    kv_rows = kv_in.shape[1]
    row = lax.broadcasted_iota(jnp.int32, (packet.shape[1] - kv_rows, SPAN), 0)
    for k in range(NEIGH):
        entry = host[k, CH_DEV - 1] * per_host + index[k, CH_DEV - 1]
        digits = jnp.where(row == 0, entry // DIGIT, jnp.where(row == 1, entry % DIGIT, 0))
        packet[k, :kv_rows, :] = kv_in[k][:, SPAN:]
        packet[k, kv_rows:, :] = digits.astype(jnp.float32).astype(jnp.bfloat16)
    for copy in copies[2:]:
        copy.wait()


def gather_kernel(blocks, here, host, index, before, gain, *refs):
    *db_refs, values_out, normed_out, nbrs, sems = refs
    per_host, part_rows, width = db_refs[0].shape
    seq = here[0]
    copies = []
    for i in range(nbrs.shape[0]):
        span, k = i // NEIGH, i % NEIGH
        if span == 0:
            of_host, place = before[k, 0] // per_host, before[k, 0] % per_host
        else:
            of_host, place = host[k, span - 1], index[k, span - 1]
        block = (seq // 2 - of_host // 2 + blocks) % blocks * 2 + (seq + of_host) % 2
        for b in range(2 * blocks):

            @pl.when(block == b)
            def _(b=b, place=place, i=i):
                pltpu.make_async_copy(db_refs[b].at[place], nbrs.at[i], sems.at[i]).start()

        copies.append(pltpu.make_async_copy(db_refs[0].at[0], nbrs.at[i], sems.at[i]))
    for i in range(nbrs.shape[0]):
        copies[i].wait()
        values = nbrs[i].astype(jnp.float32)
        at = slice(i * part_rows, (i + 1) * part_rows)
        values_out[at, :] = values
        normed_out[at, :] = rms_scale(values, gain[...]).astype(jnp.bfloat16)


def attention_kernel(pieces, far, seq_index, before, normed_in, *refs):
    weight_refs, kv_refs, (result,) = refs[: 2 * pieces], refs[2 * pieces : 3 * pieces], refs[3 * pieces :]
    rows, width = before.shape
    span_rows = rows // CH_DEV
    pair_rows = 2 * span_rows
    pad = HEAD_DIM - EHEAD_DIM
    scale = float(EHEAD_DIM) ** (-0.5)
    odd = seq_index[0] % 2
    lane = lax.broadcasted_iota(jnp.int32, (pair_rows, 2 * SPAN), 1)
    row = lax.broadcasted_iota(jnp.int32, (pair_rows, 2 * SPAN), 0)
    own_lanes = (lane < SPAN) == (row < span_rows)
    rest = jnp.zeros((pad, 2 * SPAN), jnp.bfloat16)
    empty = jnp.zeros((HEAD_DIM, 2 * SPAN), jnp.bfloat16)
    ones = jnp.ones((2 * HEAD_DIM - EHEAD_DIM, 2 * SPAN), jnp.bfloat16)
    weight_rest = jnp.zeros((pad, width), jnp.bfloat16)
    for p in range(pieces):
        first, second = weight_refs[2 * p][...], weight_refs[2 * p + 1][...]
        if far:
            first, second = (
                jnp.where(odd == 0, first, second),
                jnp.where(odd == 0, second, first),
            )
            q_parts = (first[:EHEAD_DIM], second[:EHEAD_DIM])
            out_parts = (first[EHEAD_DIM:], second[EHEAD_DIM:])
        else:
            q_parts = (first[:EHEAD_DIM], first[EHEAD_DIM:])
            out_parts = (second[:EHEAD_DIM], second[EHEAD_DIM:])
        q_w = jnp.concatenate([q_parts[0], weight_rest, q_parts[1], weight_rest], axis=0)
        out_w = jnp.concatenate([out_parts[0], weight_rest, out_parts[1], weight_rest], axis=0)
        for start in range(0, rows, BLOCK):
            block = slice(start, start + BLOCK)
            query = (mxu(normed_in[block, :], q_w, NT) * scale).astype(jnp.bfloat16)
            scores = []
            for at in range(0, BLOCK, pair_rows):
                tok = (start + at) // pair_rows * 2 * SPAN
                keys = kv_refs[p][0, :, tok : tok + 2 * SPAN]
                keys = jnp.concatenate(
                    [
                        jnp.concatenate([keys[:EHEAD_DIM], rest, empty], axis=0),
                        jnp.concatenate([empty, turned(keys[EHEAD_DIM:]), rest], axis=0),
                    ],
                    axis=1,
                )
                both = mxu(query[at : at + pair_rows], keys, NN)
                scores.append(jnp.where(own_lanes, both[:, : 2 * SPAN], both[:, 2 * SPAN :]))
            scores = jnp.concatenate(scores, axis=0)
            left = lax.broadcasted_iota(jnp.int32, scores.shape, 1) < SPAN
            low = jnp.max(jnp.where(left, scores, -jnp.inf), axis=1, keepdims=True)
            high = jnp.max(jnp.where(left, -jnp.inf, scores), axis=1, keepdims=True)
            weights = jnp.exp(scores - jnp.where(left, low, high)).astype(jnp.bfloat16)
            attended = []
            for at in range(0, BLOCK, pair_rows):
                tok = (start + at) // pair_rows * 2 * SPAN
                part = weights[at : at + pair_rows]
                vals = kv_refs[p][1, :, tok : tok + 2 * SPAN]
                heads = []
                for head in range(2):
                    picked = jnp.where(own_lanes if head == 0 else ~own_lanes, part, jnp.zeros_like(part))
                    of_head = vals[:EHEAD_DIM] if head == 0 else turned(vals[EHEAD_DIM:])
                    mixed = mxu(picked, jnp.concatenate([of_head, ones], axis=0), NT)
                    heads.append((mixed[:, :HEAD_DIM] / mixed[:, HEAD_DIM:]).astype(jnp.bfloat16))
                attended.append(jnp.concatenate(heads, axis=1))
            so_far = before if p == 0 else result
            result[block, :] = so_far[block, :] + mxu(jnp.concatenate(attended, axis=0), out_w, NN)


def ffn_kernel(far, first, gain, before, *refs):
    if first:
        *group_refs, total, normed = refs
        normed[...] = rms_scale(before[...], gain[...]).astype(jnp.bfloat16)
        result = total
    else:
        normed, *group_refs, result, total = refs
    if far:
        half = group_refs[0].shape[0] // 2
        groups = [(r.at[pl.ds(0, half)], r.at[pl.ds(half, half)]) for r in group_refs]
    else:
        groups = list(zip(group_refs[::2], group_refs[1::2]))
    ahead = mxu(normed[...], groups[0][0][...], NT)
    for g in range(len(groups)):
        units = ahead
        if g + 1 < len(groups):
            ahead = mxu(normed[...], groups[g + 1][0][...], NT)
        added = mxu(jax.nn.gelu(units).astype(jnp.bfloat16), groups[g][1][...], NN)
        added = (before if g == 0 else total)[...] + added
        if g + 1 < len(groups):
            total[...] = added
        else:
            result[...] = added.astype(result.dtype)


def pairs_kernel(encoded, weights, pairs):
    pairs[...] = mxu(encoded[...], weights[...], NN).astype(jnp.bfloat16)


def decoder_kernel(first, own_pairs, other, weights, queries, out, other_pairs):
    rows = other.shape[0]
    part = rows // CH_DEV
    width = queries.shape[1]
    scale = float(HEAD_DIM) ** (-0.5)
    other_pairs[...] = mxu(other[...], weights[...], NN).astype(jnp.bfloat16)

    def span_pairs_of(span, col):
        return jnp.concatenate(
            [r[span * part : (span + 1) * part, col : col + HEAD_DIM] for r in (own_pairs, other_pairs)],
            axis=0,
        )

    for head in range(width // HEAD_DIM):
        col = head * HEAD_DIM
        query = (queries[:, col : col + HEAD_DIM].astype(jnp.float32) * scale).astype(jnp.bfloat16)
        scores = jnp.concatenate(
            [
                mxu(query[span * SPAN : (span + 1) * SPAN], span_pairs_of(span, col), NT)
                for span in range(CH_DEV)
            ],
            axis=0,
        )
        weights_f = jnp.exp(scores - jnp.max(scores, axis=1, keepdims=True))
        weights_f = weights_f / jnp.sum(weights_f, axis=1, keepdims=True)
        weights_b = weights_f.astype(jnp.bfloat16)
        for span in range(CH_DEV):
            result = mxu(
                weights_b[span * SPAN : (span + 1) * SPAN], span_pairs_of(span, width + col), NN
            )
            if span == 0:
                result = jnp.where(first[0] == 0, jnp.zeros_like(result), result)
            out[span * SPAN : (span + 1) * SPAN, col : col + HEAD_DIM] = result


def call(body, out_shape, in_specs, name, flops, vmem_mib, scratch=()):
    spaces = {"s": pltpu.SMEM, "v": pltpu.VMEM, "h": pl.ANY}
    return pl.pallas_call(
        body,
        out_shape=out_shape,
        in_specs=[pl.BlockSpec(memory_space=spaces[c]) for c in in_specs],
        out_specs=jax.tree.map(lambda _: pl.BlockSpec(memory_space=pltpu.VMEM), out_shape),
        scratch_shapes=list(scratch),
        compiler_params=pltpu.CompilerParams(vmem_limit_bytes=vmem_mib * 1024 * 1024),
        cost_estimate=pl.CostEstimate(flops=flops, bytes_accessed=8_000_000, transcendentals=0),
        name=name,
    )


def on_device(
    span_pairs,
    dec_queries,
    database,
    nbr_index,
    nbr_host,
    enc_gain,
    enc_query,
    enc_out,
    ffn_gain,
    ffn_up,
    ffn_down,
    dec_kv,
):
    seq_size = lax.axis_size("seq")
    lanes = lax.axis_size("mp")
    seq_index = lax.axis_index("seq")
    lane_index = lax.axis_index("mp")
    entries_here, block_rows, width = database.shape
    half_rows = block_rows // HALVES
    rows = CH_DEV * NEIGH * half_rows
    blocks = seq_size // 2
    far_lanes = lanes // 2 - 1

    def core_swap(array):
        return lax.ppermute(array, "mp", [(i, i ^ 1) for i in range(lanes)])

    def lane_step(array, step):
        return lax.ppermute(array, "mp", [(i, (i + 2 * step) % lanes) for i in range(lanes)])

    def seq_swap(array):
        return lax.ppermute(array, "seq", [(i, i ^ 1) for i in range(seq_size)])

    def seq_cross(array):
        return lax.ppermute(array, "seq", [(i, i ^ 2) for i in range(seq_size)])

    def seq_ring(array):
        return lax.ppermute(array, "seq", [(i, (i + 2) % seq_size) for i in range(seq_size)])

    def next_seq(array):
        return lax.ppermute(array, "seq", [(i, i + 1) for i in range(seq_size - 1)])

    def after(array, *others):
        return lax.optimization_barrier((array, *others))[0]

    query_t, up_t = enc_query.T, ffn_up.T
    kv_t = jnp.transpose(span_pairs, (1, 2, 0))
    kv_rows, tokens = kv_t.shape[1:]
    kept = tokens - SPAN

    here = seq_index.reshape(1).astype(jnp.int32)
    place = jnp.stack([seq_index, lane_index]).astype(jnp.int32)
    host, index = nbr_host.T, nbr_index.T
    dma = pltpu.SemaphoreType.DMA
    short = functools.partial(jax.ShapeDtypeStruct, dtype=jnp.bfloat16)
    database_half, attention_half, ffn_half, packet = call(
        prepare_kernel,
        (
            short((entries_here, half_rows, width)),
            short(enc_out.shape),
            short(ffn_down.shape),
            short((2, kv_rows + 16, SPAN)),
        ),
        "sss" + "h" * 6,
        "prepare",
        rows * width,
        8,
        scratch=[
            pltpu.VMEM((entries_here, half_rows, width), jnp.float32),
            pltpu.VMEM((2, kv_rows, 2 * SPAN), jnp.bfloat16),
            dma((6,)),
        ],
    )(place, host, index, database, query_t, enc_out, up_t, ffn_down, kv_t)

    attention_far = [lane_step(attention_half, n + 1) for n in range(far_lanes)]
    packet = next_seq(packet)
    database_ring = [database_half]
    for _ in range(blocks - 1):
        database_ring.append(seq_ring(database_ring[-1]))
    database_blocks = []
    for block in database_ring:
        database_blocks += [block, seq_swap(block)]

    dec_width = dec_kv.shape[2]
    kv_weights = dec_kv.reshape(width, 2 * dec_width)
    enc_gain, ffn_gain = enc_gain.reshape(1, width), ffn_gain.reshape(1, width)
    before = packet[:, kv_rows : kv_rows + 2, 0].astype(jnp.int32)
    before = before[:, :1] * DIGIT + before[:, 1:]
    kv_t = jnp.concatenate([packet[:, :kv_rows], kv_t[:, :, :kept]], axis=2)

    near_step = database_ring[min(1, blocks - 1)]
    ffn_far = [
        lane_step(after(ffn_half, packet, near_step, database_blocks[1], *attention_far), n + 1)
        for n in range(far_lanes)
    ]
    attention_core = tuple(core_swap(a) for a in after((query_t, enc_out), database_ring[-1]))
    attention_cross = [seq_swap(after(a, *database_blocks)) for a in attention_far]
    kv_t, kv_weights, enc_gain, ffn_gain, before, *_ = lax.optimization_barrier(
        (kv_t, kv_weights, enc_gain, ffn_gain, before, database_blocks[min(3, 2 * blocks - 1)])
    )
    kv_core = core_swap(kv_t)
    kv_send = after(kv_t, *ffn_far, *database_blocks)
    kv_far = [lane_step(kv_send, n + 1) for n in range(far_lanes)]
    ffn_cross = [seq_cross(a) for a in ffn_far]
    up_send, down_send = after((up_t, ffn_down), *attention_cross)
    ffn_core = (core_swap(up_send), core_swap(down_send))

    gemm = 2 * rows * width * width
    long_rows = jax.ShapeDtypeStruct((rows, width), jnp.float32)
    short_rows = short((rows, width))
    values, normed = call(
        functools.partial(gather_kernel, blocks),
        (long_rows, short_rows),
        "ssssv" + "h" * 2 * blocks,
        "neighbour_rows",
        10 * rows * width,
        16,
        scratch=[
            pltpu.VMEM((CH_DEV * NEIGH, half_rows, width), jnp.bfloat16),
            dma((CH_DEV * NEIGH,)),
        ],
    )(here, host, index, before, enc_gain, *database_blocks)

    def attention(so_far, weights, kv, far):
        return call(
            functools.partial(attention_kernel, len(kv), far),
            long_rows,
            "svv" + "v" * 3 * len(kv),
            "encoder_attention",
            gemm * 2 * len(kv) // lanes,
            24,
        )(here, so_far, normed, *weights, *kv)

    partial_rows = attention(values, (query_t, enc_out, *attention_core), (kv_t, kv_core), False)
    far_weights, far_kv = [], []
    kv_forward = after(tuple(kv_far), partial_rows)
    for straight, crossed, kv, forward in zip(attention_far, attention_cross, kv_far, kv_forward):
        far_weights += [straight, crossed, core_swap(straight), core_swap(crossed)]
        far_kv += [kv, core_swap(forward)]
    resid = attention(partial_rows, far_weights, far_kv, True)

    near_units = (up_t, ffn_down, *ffn_core)
    partial_rows, normed = call(
        functools.partial(ffn_kernel, False, True),
        (long_rows, short_rows),
        "vv" + "v" * len(near_units),
        "encoder_ffn_near",
        2 * gemm,
        30,
    )(ffn_gain, resid, *near_units)
    ffn_cross = after(tuple(ffn_cross), resid)
    far_units = [p for piece in [*ffn_far, *ffn_cross] for p in (piece, core_swap(piece))]
    encoded = call(
        functools.partial(ffn_kernel, True, False),
        short_rows,
        "vvv" + "v" * len(far_units),
        "encoder_ffn_far",
        2 * gemm,
        30,
        scratch=[pltpu.VMEM((rows, width), jnp.float32)],
    )(ffn_gain, partial_rows, normed, *far_units)

    other = core_swap(encoded)
    pairs_shape = (rows, 2 * dec_width)
    pairs_flops = 2 * rows * width * 2 * dec_width
    own_pairs = call(
        pairs_kernel,
        jax.ShapeDtypeStruct(pairs_shape, jnp.bfloat16),
        "vv",
        "decoder_pairs",
        pairs_flops,
        20,
    )(encoded, kv_weights)
    return call(
        decoder_kernel,
        jax.ShapeDtypeStruct(dec_queries.shape, jnp.float32),
        "svvvv",
        "decoder_attention",
        pairs_flops,
        28,
        scratch=[pltpu.VMEM(pairs_shape, jnp.bfloat16)],
    )(here, own_pairs, other, kv_weights, dec_queries)


def solution(mesh):
    placed = (
        P("seq", None, "mp"),
        P("seq", "mp"),
        P("seq", None, None),
        P("seq", None),
        P("seq", None),
        P(),
        P(None, "mp"),
        P("mp", None),
        P(),
        P(None, "mp"),
        P("mp", None),
        P(None, None, "mp"),
    )
    return jax.shard_map(
        on_device, mesh=mesh, in_specs=placed, out_specs=P("seq", "mp"), check_vma=False
    )
```

time: 116 us -> 90.2 us (0.78)
  waiting for transfers between devices: 39.8 us -> 22.8 us
  Pallas kernels: 46.5 us -> 35.8 us
  starting transfers between devices: 19.9 us -> 21.9 us
  local copies, waits for them, and re-layouts: 7.08 us -> 8.53 us
    ppermute x3, waiting for transfers between devices: 18.6 us -> 9.9 us  [seq_ring(): lax.ppermute(array, 'seq', [(i, (i + 2) % seq_size) for i in range(seq_si...]
    ppermute x3, waiting for transfers between devices: 6.43 us -> 0.01 us  [lane_step(): lax.ppermute(array, 'mp', [(i, (i + 2 * step) % lanes) for i in range(lan...]
    unnamed x47 -> x39, local copies, waits for them, and re-layouts: 2.6 us -> 8.51 us
    pallas_call x2 -> x6, Pallas kernels: 32.7 us -> 28.1 us  [the longest x2 10 us: attention(): call(functools.partial(attention_kernel, len(kv), far), long_rows, 'svv'...]
    pallas_call x1, Pallas kernels: 5.75 us -> 2.33 us  [on_device(): call(pairs_kernel, jax.ShapeDtypeStruct(pairs_shape, jnp.bfloat16), 'vv',...]
    dynamic_slice x4 -> x0, local copies, waits for them, and re-layouts: 3.12 us -> none  [half_of(): lax.dynamic_slice_in_dim(a, odd * (a.shape[0] // 2), a.shape[0] // 2, 0)]
    pallas_call x1, Pallas kernels: 8.07 us -> 5.33 us  [on_device(): call(decoder_kernel, jax.ShapeDtypeStruct(dec_queries.shape, jnp.float32)...]
    ppermute x3 -> x5, waiting for transfers between devices: 10.7 us -> 7.98 us  [seq_swap(): return lax.ppermute(array, 'seq', [(i, i ^ 1) for i in range(seq_size)])]
  transfers between devices with their start and end apart: 21 -> 24, of which waited for: 9 -> 9; matrix products, arithmetic and copies ran while one was open for 5% -> 1% of each run, Pallas kernels for 20% -> 26%
where the time goes in v2:
time: 90.2 us; the launch traced here: 89.8 us
  Pallas kernels  35.8 us (40%)
  waiting for transfers between devices  22.8 us (25%)
  starting transfers between devices  21.9 us (24%)
  local copies, waits for them, and re-layouts  8.53 us (9%)
    pallas_call x2, Pallas kernels, attention(): call(functools.partial(attention_kernel, len(kv), far), long_rows, 'svv'...  10 us
    ppermute x3, waiting for transfers between devices, seq_ring(): lax.ppermute(array, 'seq', [(i, (i + 2) % seq_size) for i in range(seq_si...  9.9 us
    unnamed x39, local copies, waits for them, and re-layouts  8.51 us
    ppermute x5, waiting for transfers between devices, seq_swap(): return lax.ppermute(array, 'seq', [(i, i ^ 1) for i in range(seq_size)])  7.98 us
    pallas_call x1, Pallas kernels, on_device(): call(functools.partial(gather_kernel, blocks), (long_rows, short_rows), '...  6.05 us
    pallas_call x1, Pallas kernels, on_device(): call(decoder_kernel, jax.ShapeDtypeStruct(dec_queries.shape, jnp.float32)...  5.33 us
    pallas_call x1, Pallas kernels, on_device(): call(functools.partial(ffn_kernel, False, True), (long_rows, short_rows),...  5.11 us
    ppermute x3, starting transfers between devices, lane_step(): lax.ppermute(array, 'mp', [(i, (i + 2 * step) % lanes) for i in range(lan...  5.06 us
  transfers between devices with their start and end apart: 24, of which 9 were waited for; matrix products, arithmetic and copies ran while one was open for 1% of the time, Pallas kernels for 26%

profile of v2, /device:TPU:0, one launch (start us, length us, event | category | flops | bytes accessed | tf_op | source)
XLA Modules:
  0.0 89.8 jit_solution(6869697242301559067)
XLA Ops:
  0.1 1.0 %copy-done = bf16[512,2,224]{0,2,1:T(8,128)(2,1)S(1)} copy-done((bf16[512,2,224]{0,2,1:T(8,128)(2,1)S(1)}, bf16[512,2,224]{0,2,1:T(8,128)(2,1)}, u32[]{:S(2)}) %copy-start) | copy-done | bytes 458776
  1.1 1.0 %copy-done.2 = bf16[896,224]{0,1:T(8,128)(2,1)S(1)} copy-done((bf16[896,224]{0,1:T(8,128)(2,1)S(1)}, bf16[896,224]{0,1:T(8,128)(2,1)}, u32[]{:S(2)}) %copy-start.2) | copy-done | bytes 401432
  2.1 1.0 %copy-done.4 = bf16[224,896]{1,0:T(8,128)(2,1)S(1)} copy-done((bf16[224,896]{1,0:T(8,128)(2,1)S(1)}, bf16[224,896]{1,0:T(8,128)(2,1)}, u32[]{:S(2)}) %copy-start.4) | copy-done | bytes 401432
  3.1 1.2 %copy-done.6 = f32[2,128,896]{2,1,0:T(8,128)S(1)} copy-done((f32[2,128,896]{2,1,0:T(8,128)S(1)}, f32[2,128,896]{2,1,0:T(8,128)}, u32[]{:S(2)}) %copy-start.6) | copy-done | bytes 917528
  4.3 1.1 %copy-done.7 = bf16[896,448]{0,1:T(8,128)(2,1)S(1)} copy-done((bf16[896,448]{0,1:T(8,128)(2,1)S(1)}, bf16[896,448]{0,1:T(8,128)(2,1)}, u32[]{:S(2)}) %copy-start.7) | copy-done | bytes 802840
  5.4 1.1 %copy-done.9 = bf16[448,896]{1,0:T(8,128)(2,1)S(1)} copy-done((bf16[448,896]{1,0:T(8,128)(2,1)S(1)}, bf16[448,896]{1,0:T(8,128)(2,1)}, u32[]{:S(2)}) %copy-start.9) | copy-done | bytes 802840
  7.2 0.7 copy-done.14
  7.9 1.9 %prepare.1 = (bf16[2,64,896]{2,1,0:T(8,128)(2,1)S(1)}, bf16[224,896]{1,0:T(8,128)(2,1)S(1)}, bf16[448,896]{1,0:T(8,128)(2,1)S(1)}, bf16[2,240,64]{2,1,0:T(8,128)(2,1)S(1)}) custom-call(s32[2]{0:T(128)S(1)} %pad_add_fusion.place, s32[2,8]{1,0:T(2,128)S(1)} %bitcast.20, s32[2,8]{1,0:T(2,128)S(1)} %bitcast.22, f32[2,128,896]{2,1,0:T(8,128)S(1)} %copy-done.6, ...), custom_call_target="tpu_custom_call" | custom-call | flops 917504 | bytes 8000000 | tf_op jit(solution)/shard_map/prepare/pallas_call | solution.py:301
  9.8 3.0 %collective-permute-start.11 = (bf16[224,896]{1,0:T(8,128)(2,1)S(1)}, bf16[224,896]{1,0:T(8,128)(2,1)S(1)}, u32[]{:S(2)}, u32[]{:S(2)}) collective-permute-start(bf16[224,896]{1,0:T(8,128)(2,1)S(1)} %get-tuple-element.37), channel_id=1, source_target_pairs={{0,2},{1,3},{2,0},{3,1},{4,6},{5,7},{6,4},{7,5},{8,10},{9,11},{10,... | collective-permute-start | bytes 1204232 | tf_op jit(solution)/shard_map/ppermute | solution.py:274
  12.8 1.6 %collective-permute-start.1 = (bf16[2,64,896]{2,1,0:T(8,128)(2,1)S(1)}, bf16[2,64,896]{2,1,0:T(8,128)(2,1)S(1)}, u32[]{:S(2)}, u32[]{:S(2)}) collective-permute-start(bf16[2,64,896]{2,1,0:T(8,128)(2,1)S(1)} %get-tuple-element.28.refs_0_), channel_id=1, source_target_pairs={{0,8},{4,12},{8,16},{12,20},{16,24},{20,28},{24,0},{28,4},{1,9},{5... | collective-permute-start | bytes 688136 | tf_op jit(solution)/shard_map/ppermute | solution.py:283
  14.4 1.5 %collective-permute-start.3 = (bf16[2,64,896]{2,1,0:T(8,128)(2,1)S(1)}, bf16[2,64,896]{2,1,0:T(8,128)(2,1)S(1)}, u32[]{:S(2)}, u32[]{:S(2)}) collective-permute-start(bf16[2,64,896]{2,1,0:T(8,128)(2,1)S(1)} %get-tuple-element.28.refs_0_), channel_id=1, source_target_pairs={{0,4},{4,0},{8,12},{12,8},{16,20},{20,16},{24,28},{28,24},{1,5},{5... | collective-permute-start | bytes 688136 | tf_op jit(solution)/shard_map/ppermute | solution.py:277
  15.9 5.9 %collective-permute-done.1.refs_2_ = bf16[2,64,896]{2,1,0:T(8,128)(2,1)S(1)} collective-permute-done((bf16[2,64,896]{2,1,0:T(8,128)(2,1)S(1)}, bf16[2,64,896]{2,1,0:T(8,128)(2,1)S(1)}, u32[]{:S(2)}, u32[]{:S(2)}) %collective-permute-start.1) | collective-permute-done | bytes 229408 | tf_op jit(solution)/shard_map/ppermute | solution.py:283
  21.8 3.4 %collective-permute-start = (bf16[2,240,64]{2,1,0:T(8,128)(2,1)S(1)}, bf16[2,240,64]{2,1,0:T(8,128)(2,1)S(1)}, u32[]{:S(2)}, u32[]{:S(2)}) collective-permute-start(bf16[2,240,64]{2,1,0:T(8,128)(2,1)S(1)} %get-tuple-element.27), channel_id=1, source_target_pairs={{0,4},{4,8},{8,12},{12,16},{16,20},{20,24},{24,28},{1,5},{5,9},{9,... | collective-permute-start | bytes 184328 | tf_op jit(solution)/shard_map/ppermute | solution.py:286
  25.2 2.4 %collective-permute-done = bf16[2,240,64]{2,1,0:T(8,128)(2,1)S(1)} collective-permute-done((bf16[2,240,64]{2,1,0:T(8,128)(2,1)S(1)}, bf16[2,240,64]{2,1,0:T(8,128)(2,1)S(1)}, u32[]{:S(2)}, u32[]{:S(2)}) %collective-permute-start) | collective-permute-done | bytes 61472 | tf_op jit(solution)/shard_map/ppermute | solution.py:286
  28.8 1.0 %collective-permute-done.4.refs_4_ = bf16[2,64,896]{2,1,0:T(8,128)(2,1)S(1)} collective-permute-done((bf16[2,64,896]{2,1,0:T(8,128)(2,1)S(1)}, bf16[2,64,896]{2,1,0:T(8,128)(2,1)S(1)}, u32[]{:S(2)}, u32[]{:S(2)}) %collective-permute-start.4) | collective-permute-done | bytes 229408 | tf_op jit(solution)/shard_map/ppermute | solution.py:283
  29.8 3.3 %collective-permute-start.6 = (bf16[2,64,896]{2,1,0:T(8,128)(2,1)S(1)}, bf16[2,64,896]{2,1,0:T(8,128)(2,1)S(1)}, u32[]{:S(2)}, u32[]{:S(2)}) collective-permute-start(bf16[2,64,896]{2,1,0:T(8,128)(2,1)S(1)} %collective-permute-done.4.refs_4_), channel_id=1, source_target_pairs={{0,8},{4,12},{8,16},{12,20},{16,24},{20,28},{24,0},{28,4},{1,9},{5... | collective-permute-start | bytes 688136 | tf_op jit(solution)/shard_map/ppermute | solution.py:283
  33.3 2.0 %collective-permute-start.5 = (bf16[2,64,896]{2,1,0:T(8,128)(2,1)S(1)}, bf16[2,64,896]{2,1,0:T(8,128)(2,1)S(1)}, u32[]{:S(2)}, u32[]{:S(2)}) collective-permute-start(bf16[2,64,896]{2,1,0:T(8,128)(2,1)S(1)} %collective-permute-done.4.refs_4_), channel_id=1, source_target_pairs={{0,4},{4,0},{8,12},{12,8},{16,20},{20,16},{24,28},{28,24},{1,5},{5... | collective-permute-start | bytes 688136 | tf_op jit(solution)/shard_map/ppermute | solution.py:277
  35.4 3.1 %collective-permute-done.6.refs_6_ = bf16[2,64,896]{2,1,0:T(8,128)(2,1)S(1)} collective-permute-done((bf16[2,64,896]{2,1,0:T(8,128)(2,1)S(1)}, bf16[2,64,896]{2,1,0:T(8,128)(2,1)S(1)}, u32[]{:S(2)}, u32[]{:S(2)}) %collective-permute-start.6) | collective-permute-done | bytes 229408 | tf_op jit(solution)/shard_map/ppermute | solution.py:283
  39.4 2.5 %collective-permute-done.2.refs_3_ = bf16[2,64,896]{2,1,0:T(8,128)(2,1)S(1)} collective-permute-done((bf16[2,64,896]{2,1,0:T(8,128)(2,1)S(1)}, bf16[2,64,896]{2,1,0:T(8,128)(2,1)S(1)}, u32[]{:S(2)}, u32[]{:S(2)}) %collective-permute-start.2) | collective-permute-done | bytes 229408 | tf_op jit(solution)/shard_map/ppermute | solution.py:277
  42.4 3.0 %collective-permute-done.5.refs_5_ = bf16[2,64,896]{2,1,0:T(8,128)(2,1)S(1)} collective-permute-done((bf16[2,64,896]{2,1,0:T(8,128)(2,1)S(1)}, bf16[2,64,896]{2,1,0:T(8,128)(2,1)S(1)}, u32[]{:S(2)}, u32[]{:S(2)}) %collective-permute-start.5) | collective-permute-done | bytes 229408 | tf_op jit(solution)/shard_map/ppermute | solution.py:277
  45.4 2.5 %collective-permute-done.7.refs_7_ = bf16[2,64,896]{2,1,0:T(8,128)(2,1)S(1)} collective-permute-done((bf16[2,64,896]{2,1,0:T(8,128)(2,1)S(1)}, bf16[2,64,896]{2,1,0:T(8,128)(2,1)S(1)}, u32[]{:S(2)}, u32[]{:S(2)}) %collective-permute-start.7) | collective-permute-done | bytes 229408 | tf_op jit(solution)/shard_map/ppermute | solution.py:277
  47.9 1.5 %collective-permute-start.16 = (bf16[2,224,512]{2,1,0:T(8,128)(2,1)S(1)}, bf16[2,224,512]{2,1,0:T(8,128)(2,1)S(1)}, u32[]{:S(2)}, u32[]{:S(2)}) collective-permute-start(bf16[2,224,512]{2,1,0:T(8,128)(2,1)S(1)} %pad_maximum_fusion.refs_4_), channel_id=1, source_target_pairs={{0,2},{1,3},{2,0},{3,1},{4,6},{5,7},{6,4},{7,5},{8,10},{9,11},{10,... | collective-permute-start | bytes 1376264 | tf_op jit(solution)/shard_map/ppermute | solution.py:274
  49.7 1.3 %collective-permute-start.21 = (bf16[448,896]{1,0:T(8,128)(2,1)S(1)}, bf16[448,896]{1,0:T(8,128)(2,1)S(1)}, u32[]{:S(2)}, u32[]{:S(2)}) collective-permute-start(bf16[448,896]{1,0:T(8,128)(2,1)S(1)} %collective-permute-done.15.refs_1_), channel_id=1, source_target_pairs={{0,8},{4,12},{8,0},{12,4},{16,24},{20,28},{24,16},{28,20},{1,9},{5... | collective-permute-start | bytes 2408456 | tf_op jit(solution)/shard_map/ppermute | solution.py:280
  51.0 6.0 %neighbour_rows.1 = (f32[1024,896]{1,0:T(8,128)S(1)}, bf16[1024,896]{1,0:T(8,128)(2,1)S(1)}) custom-call(s32[1]{0:T(128)} %bitcast.here.seq_index.first, s32[2,8]{1,0:T(2,128)S(1)} %bitcast.21, s32[2,8]{1,0:T(2,128)S(1)} %bitcast.23, s32[2,1]{1,0:T(2,128)S(1)} %slice_add_fusion.before, f32[1,896]{1,0:T(1,128)S(1)} %reshape.16.gain, ...), custom_call_target="tpu_custom_call" | custom-call | flops 9175040 | bytes 8000000 | tf_op jit(solution)/shard_map/neighbour_rows/pallas_call | solution.py:356
  57.2 5.0 %encoder_attention.2.before = f32[1024,896]{1,0:T(8,128)S(1)} custom-call(s32[1]{0:T(128)} %bitcast.here.seq_index.first, f32[1024,896]{1,0:T(8,128)S(1)} %get-tuple-element.32.before, bf16[1024,896]{1,0:T(8,128)(2,1)S(1)} %get-tuple-element.33.normed_in, bf16[224,896]{1,0:T(8,128)(2,1)S(1)} %bitcast.16, bf16[224,896]{1,0:T(8,128)(2,1)S(1)} %copy-done.5, ...), custom_call_target="tpu_custom_call" | custom-call | flops 1644167168 | bytes 8000000 | tf_op jit(solution)/shard_map/encoder_attention/pallas_call | solution.py:370
  63.4 1.4 %collective-permute-done.14.refs_3_ = bf16[224,896]{1,0:T(8,128)(2,1)S(1)} collective-permute-done((bf16[224,896]{1,0:T(8,128)(2,1)S(1)}, bf16[224,896]{1,0:T(8,128)(2,1)S(1)}, u32[]{:S(2)}, u32[]{:S(2)}) %collective-permute-start.14) | collective-permute-done | bytes 401440 | tf_op jit(solution)/shard_map/ppermute | solution.py:271
  65.2 5.0 %encoder_attention.3.before = f32[1024,896]{1,0:T(8,128)S(1)} custom-call(s32[1]{0:T(128)} %bitcast.here.seq_index.first, f32[1024,896]{1,0:T(8,128)S(1)} %encoder_attention.2.before, bf16[1024,896]{1,0:T(8,128)(2,1)S(1)} %get-tuple-element.33.normed_in, bf16[224,896]{1,0:T(8,128)(2,1)S(1)} %collective-permute-done.11.refs_0_, ...), custom_call_target="tpu_custom_call" | custom-call | flops 1644167168 | bytes 8000000 | tf_op jit(solution)/shard_map/encoder_attention/pallas_call | solution.py:370
  70.4 5.1 %encoder_ffn_near.1 = (f32[1024,896]{1,0:T(8,128)S(1)}, bf16[1024,896]{1,0:T(8,128)(2,1)S(1)}) custom-call(f32[1,896]{1,0:T(1,128)S(1)} %reshape.17.gain, f32[1024,896]{1,0:T(8,128)S(1)} %encoder_attention.3.before, bf16[448,896]{1,0:T(8,128)(2,1)S(1)} %bitcast.19, bf16[448,896]{1,0:T(8,128)(2,1)S(1)} %copy-done.10, ...), custom_call_target="tpu_custom_call" | custom-call | flops 3288334336 | bytes 8000000 | tf_op jit(solution)/shard_map/encoder_ffn_near/pallas_call | solution.py:388
  75.6 5.0 %encoder_ffn_far.1.encoded = bf16[1024,896]{1,0:T(8,128)(2,1)S(1)} custom-call(f32[1,896]{1,0:T(1,128)S(1)} %reshape.17.gain, f32[1024,896]{1,0:T(8,128)S(1)} %get-tuple-element.45.before, bf16[1024,896]{1,0:T(8,128)(2,1)S(1)} %get-tuple-element.46.refs_0_, bf16[448,896]{1,0:T(8,128)(2,1)S(1)} %collective-permute-done.15.refs_1_, ...), custom_call_target="tpu_custom_call" | custom-call | flops 3288334336 | bytes 8000000 | tf_op jit(solution)/shard_map/encoder_ffn_far/pallas_call | solution.py:398
  81.1 2.3 %decoder_pairs.1.own_pairs = bf16[1024,1024]{1,0:T(8,128)(2,1)S(1)} custom-call(bf16[1024,896]{1,0:T(8,128)(2,1)S(1)} %encoder_ffn_far.1.encoded, bf16[896,1024]{1,0:T(8,128)(2,1)S(1)} %bitcast.10), custom_call_target="tpu_custom_call" | custom-call | flops 1879048192 | bytes 8000000 | tf_op jit(solution)/shard_map/decoder_pairs/pallas_call | solution.py:411
  83.4 1.1 %collective-permute-done.23.other = bf16[1024,896]{1,0:T(8,128)(2,1)S(1)} collective-permute-done((bf16[1024,896]{1,0:T(8,128)(2,1)S(1)}, bf16[1024,896]{1,0:T(8,128)(2,1)S(1)}, u32[]{:S(2)}, u32[]{:S(2)}) %collective-permute-start.23) | collective-permute-done | bytes 1835040 | tf_op jit(solution)/shard_map/ppermute | solution.py:271
  84.5 5.3 %decoder_attention.1 = f32[512,512]{1,0:T(8,128)} custom-call(s32[1]{0:T(128)} %bitcast.here.seq_index.first, bf16[1024,1024]{1,0:T(8,128)(2,1)S(1)} %decoder_pairs.1.own_pairs, bf16[1024,896]{1,0:T(8,128)(2,1)S(1)} %collective-permute-done.23.other, bf16[896,1024]{1,0:T(8,128)(2,1)S(1)} %bitcast.11, bf16[512,512]{1,0:T(8,128)(2,1)S(1)} %copy-done.11), custom_call_target="tpu_custom_call" | custom-call | flops 1879048192 | bytes 8000000 | tf_op jit(solution)/shard_map/decoder_attention/pallas_call | solution.py:419
  (70 shorter events, 6.2 us)
Async XLA Ops:
  7.9 20.2 %copy-start.16 = (bf16[896,2,512]{2,1,0:T(2,128)(2,1)S(1)}, bf16[896,2,512]{2,1,0:T(2,128)(2,1)}, u32[]{:S(2)}) copy-start(bf16[896,2,512]{2,1,0:T(2,128)(2,1)} %param.23) | copy-start | bytes 5505028
  9.8 17.8 %collective-permute-start.11 = (bf16[224,896]{1,0:T(8,128)(2,1)S(1)}, bf16[224,896]{1,0:T(8,128)(2,1)S(1)}, u32[]{:S(2)}, u32[]{:S(2)}) collective-permute-start(bf16[224,896]{1,0:T(8,128)(2,1)S(1)} %get-tuple-element.37), channel_id=1, source_target_pairs={{0,2},{1,3},{2,0},{3,1},{4,6},{5,7},{6,4},{7,5},{8,10},{9,11},{10,... | collective-permute-start | bytes 1204232 | tf_op jit(solution)/shard_map/ppermute | solution.py:274
  12.8 8.9 %collective-permute-start.1 = (bf16[2,64,896]{2,1,0:T(8,128)(2,1)S(1)}, bf16[2,64,896]{2,1,0:T(8,128)(2,1)S(1)}, u32[]{:S(2)}, u32[]{:S(2)}) collective-permute-start(bf16[2,64,896]{2,1,0:T(8,128)(2,1)S(1)} %get-tuple-element.28.refs_0_), channel_id=1, source_target_pairs={{0,8},{4,12},{8,16},{12,20},{16,24},{20,28},{24,0},{28,4},{1,9},{5... | collective-permute-start | bytes 688136 | tf_op jit(solution)/shard_map/ppermute | solution.py:283
  14.4 13.2 %collective-permute-start.3 = (bf16[2,64,896]{2,1,0:T(8,128)(2,1)S(1)}, bf16[2,64,896]{2,1,0:T(8,128)(2,1)S(1)}, u32[]{:S(2)}, u32[]{:S(2)}) collective-permute-start(bf16[2,64,896]{2,1,0:T(8,128)(2,1)S(1)} %get-tuple-element.28.refs_0_), channel_id=1, source_target_pairs={{0,4},{4,0},{8,12},{12,8},{16,20},{20,16},{24,28},{28,24},{1,5},{5... | collective-permute-start | bytes 688136 | tf_op jit(solution)/shard_map/ppermute | solution.py:277
  21.7 8.0 %collective-permute-start.4 = (bf16[2,64,896]{2,1,0:T(8,128)(2,1)S(1)}, bf16[2,64,896]{2,1,0:T(8,128)(2,1)S(1)}, u32[]{:S(2)}, u32[]{:S(2)}) collective-permute-start(bf16[2,64,896]{2,1,0:T(8,128)(2,1)S(1)} %collective-permute-done.1.refs_2_), channel_id=1, source_target_pairs={{0,8},{4,12},{8,16},{12,20},{16,24},{20,28},{24,0},{28,4},{1,9},{5... | collective-permute-start | bytes 688136 | tf_op jit(solution)/shard_map/ppermute | solution.py:283
  21.8 5.8 %collective-permute-start = (bf16[2,240,64]{2,1,0:T(8,128)(2,1)S(1)}, bf16[2,240,64]{2,1,0:T(8,128)(2,1)S(1)}, u32[]{:S(2)}, u32[]{:S(2)}) collective-permute-start(bf16[2,240,64]{2,1,0:T(8,128)(2,1)S(1)} %get-tuple-element.27), channel_id=1, source_target_pairs={{0,4},{4,8},{8,12},{12,16},{16,20},{20,24},{24,28},{1,5},{5,9},{9,... | collective-permute-start | bytes 184328 | tf_op jit(solution)/shard_map/ppermute | solution.py:286
  27.6 20.3 %collective-permute-start.15 = (bf16[448,896]{1,0:T(8,128)(2,1)S(1)}, bf16[448,896]{1,0:T(8,128)(2,1)S(1)}, u32[]{:S(2)}, u32[]{:S(2)}) collective-permute-start(bf16[448,896]{1,0:T(8,128)(2,1)S(1)} %get-tuple-element.40), channel_id=1, source_target_pairs={{0,2},{1,3},{2,0},{3,1},{4,6},{5,7},{6,4},{7,5},{8,10},{9,11},{10,... | collective-permute-start | bytes 2408456 | tf_op jit(solution)/shard_map/ppermute | solution.py:274
  28.1 11.0 %copy-start.1 = (bf16[512,2,224]{0,2,1:T(8,128)(2,1)S(1)}, bf16[512,2,224]{0,2,1:T(8,128)(2,1)}, u32[]{:S(2)}) copy-start(bf16[512,2,224]{0,2,1:T(8,128)(2,1)} %param.12) | copy-start | bytes 1376260
  28.1 13.8 %copy-start.3 = (bf16[896,224]{0,1:T(8,128)(2,1)S(1)}, bf16[896,224]{0,1:T(8,128)(2,1)}, u32[]{:S(2)}) copy-start(bf16[896,224]{0,1:T(8,128)(2,1)} %param.18) | copy-start | bytes 1204228
  28.1 17.3 %copy-start.5 = (bf16[224,896]{1,0:T(8,128)(2,1)S(1)}, bf16[224,896]{1,0:T(8,128)(2,1)}, u32[]{:S(2)}) copy-start(bf16[224,896]{1,0:T(8,128)(2,1)} %refs_1_.2) | copy-start | bytes 1204228
  28.1 22.9 %copy-start.13 = (s32[8,2]{0,1:T(2,128)S(1)}, s32[8,2]{0,1:T(2,128)}, u32[]{:S(2)}) copy-start(s32[8,2]{0,1:T(2,128)} %param.16) | copy-start | bytes 196
  28.1 22.9 %copy-start.15 = (s32[8,2]{0,1:T(2,128)S(1)}, s32[8,2]{0,1:T(2,128)}, u32[]{:S(2)}) copy-start(s32[8,2]{0,1:T(2,128)} %param.15) | copy-start | bytes 196
  29.8 8.7 %collective-permute-start.6 = (bf16[2,64,896]{2,1,0:T(8,128)(2,1)S(1)}, bf16[2,64,896]{2,1,0:T(8,128)(2,1)S(1)}, u32[]{:S(2)}, u32[]{:S(2)}) collective-permute-start(bf16[2,64,896]{2,1,0:T(8,128)(2,1)S(1)} %collective-permute-done.4.refs_4_), channel_id=1, source_target_pairs={{0,8},{4,12},{8,16},{12,20},{16,24},{20,28},{24,0},{28,4},{1,9},{5... | collective-permute-start | bytes 688136 | tf_op jit(solution)/shard_map/ppermute | solution.py:283
  33.2 8.6 %collective-permute-start.2 = (bf16[2,64,896]{2,1,0:T(8,128)(2,1)S(1)}, bf16[2,64,896]{2,1,0:T(8,128)(2,1)S(1)}, u32[]{:S(2)}, u32[]{:S(2)}) collective-permute-start(bf16[2,64,896]{2,1,0:T(8,128)(2,1)S(1)} %collective-permute-done.1.refs_2_), channel_id=1, source_target_pairs={{0,4},{4,0},{8,12},{12,8},{16,20},{20,16},{24,28},{28,24},{1,5},{5... | collective-permute-start | bytes 688136 | tf_op jit(solution)/shard_map/ppermute | solution.py:277
  33.3 12.1 %collective-permute-start.5 = (bf16[2,64,896]{2,1,0:T(8,128)(2,1)S(1)}, bf16[2,64,896]{2,1,0:T(8,128)(2,1)S(1)}, u32[]{:S(2)}, u32[]{:S(2)}) collective-permute-start(bf16[2,64,896]{2,1,0:T(8,128)(2,1)S(1)} %collective-permute-done.4.refs_4_), channel_id=1, source_target_pairs={{0,4},{4,0},{8,12},{12,8},{16,20},{20,16},{24,28},{28,24},{1,5},{5... | collective-permute-start | bytes 688136 | tf_op jit(solution)/shard_map/ppermute | solution.py:277
  38.5 9.3 %collective-permute-start.7 = (bf16[2,64,896]{2,1,0:T(8,128)(2,1)S(1)}, bf16[2,64,896]{2,1,0:T(8,128)(2,1)S(1)}, u32[]{:S(2)}, u32[]{:S(2)}) collective-permute-start(bf16[2,64,896]{2,1,0:T(8,128)(2,1)S(1)} %collective-permute-done.6.refs_6_), channel_id=1, source_target_pairs={{0,4},{4,0},{8,12},{12,8},{16,20},{20,16},{24,28},{28,24},{1,5},{5... | collective-permute-start | bytes 688136 | tf_op jit(solution)/shard_map/ppermute | solution.py:277
  41.8 7.8 %collective-permute-start.10 = (bf16[2,224,512]{2,1,0:T(8,128)(2,1)S(1)}, bf16[2,224,512]{2,1,0:T(8,128)(2,1)S(1)}, u32[]{:S(2)}, u32[]{:S(2)}) collective-permute-start(bf16[2,224,512]{2,1,0:T(8,128)(2,1)S(1)} %pad_maximum_fusion.refs_4_), channel_id=1, source_target_pairs={{0,1},{1,0},{2,3},{3,2},{4,5},{5,4},{6,7},{7,6},{8,9},{9,8},{10,11... | collective-permute-start | bytes 1376264 | tf_op jit(solution)/shard_map/ppermute | solution.py:271
  41.9 15.2 %collective-permute-start.8 = (bf16[224,896]{1,0:T(8,128)(2,1)S(1)}, bf16[224,896]{1,0:T(8,128)(2,1)S(1)}, u32[]{:S(2)}, u32[]{:S(2)}) collective-permute-start(bf16[224,896]{1,0:T(8,128)(2,1)S(1)} %bitcast.15), channel_id=1, source_target_pairs={{0,1},{1,0},{2,3},{3,2},{4,5},{5,4},{6,7},{7,6},{8,9},{9,8},{10,11... | collective-permute-start | bytes 1204232 | tf_op jit(solution)/shard_map/ppermute | solution.py:271
  45.4 11.8 %collective-permute-start.9 = (bf16[224,896]{1,0:T(8,128)(2,1)S(1)}, bf16[224,896]{1,0:T(8,128)(2,1)S(1)}, u32[]{:S(2)}, u32[]{:S(2)}) collective-permute-start(bf16[224,896]{1,0:T(8,128)(2,1)S(1)} %copy-done.5), channel_id=1, source_target_pairs={{0,1},{1,0},{2,3},{3,2},{4,5},{5,4},{6,7},{7,6},{8,9},{9,8},{10,11... | collective-permute-start | bytes 1204232 | tf_op jit(solution)/shard_map/ppermute | solution.py:271
  47.9 14.4 %collective-permute-start.16 = (bf16[2,224,512]{2,1,0:T(8,128)(2,1)S(1)}, bf16[2,224,512]{2,1,0:T(8,128)(2,1)S(1)}, u32[]{:S(2)}, u32[]{:S(2)}) collective-permute-start(bf16[2,224,512]{2,1,0:T(8,128)(2,1)S(1)} %pad_maximum_fusion.refs_4_), channel_id=1, source_target_pairs={{0,2},{1,3},{2,0},{3,1},{4,6},{5,7},{6,4},{7,5},{8,10},{9,11},{10,... | collective-permute-start | bytes 1376264 | tf_op jit(solution)/shard_map/ppermute | solution.py:274
  49.4 13.4 %collective-permute-start.12 = (bf16[224,896]{1,0:T(8,128)(2,1)S(1)}, bf16[224,896]{1,0:T(8,128)(2,1)S(1)}, u32[]{:S(2)}, u32[]{:S(2)}) collective-permute-start(bf16[224,896]{1,0:T(8,128)(2,1)S(1)} %collective-permute-done.11.refs_0_), channel_id=1, source_target_pairs={{0,4},{4,0},{8,12},{12,8},{16,20},{20,16},{24,28},{28,24},{1,5},{5... | collective-permute-start | bytes 1204232 | tf_op jit(solution)/shard_map/ppermute | solution.py:277
  49.7 20.5 %collective-permute-start.21 = (bf16[448,896]{1,0:T(8,128)(2,1)S(1)}, bf16[448,896]{1,0:T(8,128)(2,1)S(1)}, u32[]{:S(2)}, u32[]{:S(2)}) collective-permute-start(bf16[448,896]{1,0:T(8,128)(2,1)S(1)} %collective-permute-done.15.refs_1_), channel_id=1, source_target_pairs={{0,8},{4,12},{8,0},{12,4},{16,24},{20,28},{24,16},{28,20},{1,9},{5... | collective-permute-start | bytes 2408456 | tf_op jit(solution)/shard_map/ppermute | solution.py:280
  57.1 6.2 %collective-permute-start.13 = (bf16[224,896]{1,0:T(8,128)(2,1)S(1)}, bf16[224,896]{1,0:T(8,128)(2,1)S(1)}, u32[]{:S(2)}, u32[]{:S(2)}) collective-permute-start(bf16[224,896]{1,0:T(8,128)(2,1)S(1)} %collective-permute-done.11.refs_0_), channel_id=1, source_target_pairs={{0,1},{1,0},{2,3},{3,2},{4,5},{5,4},{6,7},{7,6},{8,9},{9,8},{10,11... | collective-permute-start | bytes 1204232 | tf_op jit(solution)/shard_map/ppermute | solution.py:271
  57.2 5.7 %copy-start.8 = (bf16[896,448]{0,1:T(8,128)(2,1)S(1)}, bf16[896,448]{0,1:T(8,128)(2,1)}, u32[]{:S(2)}) copy-start(bf16[896,448]{0,1:T(8,128)(2,1)} %param.21) | copy-start | bytes 2408452
  57.2 6.1 %copy-start.10 = (bf16[448,896]{1,0:T(8,128)(2,1)S(1)}, bf16[448,896]{1,0:T(8,128)(2,1)}, u32[]{:S(2)}) copy-start(bf16[448,896]{1,0:T(8,128)(2,1)} %refs_1_.3) | copy-start | bytes 2408452
  62.2 2.9 %collective-permute-start.17 = (bf16[2,224,512]{2,1,0:T(8,128)(2,1)S(1)}, bf16[2,224,512]{2,1,0:T(8,128)(2,1)S(1)}, u32[]{:S(2)}, u32[]{:S(2)}) collective-permute-start(bf16[2,224,512]{2,1,0:T(8,128)(2,1)S(1)} %collective-permute-done.16.refs_4_), channel_id=1, source_target_pairs={{0,1},{1,0},{2,3},{3,2},{4,5},{5,4},{6,7},{7,6},{8,9},{9,8},{10,11... | collective-permute-start | bytes 1376264 | tf_op jit(solution)/shard_map/ppermute | solution.py:271
  62.8 2.0 %collective-permute-start.14 = (bf16[224,896]{1,0:T(8,128)(2,1)S(1)}, bf16[224,896]{1,0:T(8,128)(2,1)S(1)}, u32[]{:S(2)}, u32[]{:S(2)}) collective-permute-start(bf16[224,896]{1,0:T(8,128)(2,1)S(1)} %collective-permute-done.12.refs_1_), channel_id=1, source_target_pairs={{0,1},{1,0},{2,3},{3,2},{4,5},{5,4},{6,7},{7,6},{8,9},{9,8},{10,11... | collective-permute-start | bytes 1204232 | tf_op jit(solution)/shard_map/ppermute | solution.py:271
  62.9 7.6 %collective-permute-start.18 = (bf16[448,896]{1,0:T(8,128)(2,1)S(1)}, bf16[448,896]{1,0:T(8,128)(2,1)S(1)}, u32[]{:S(2)}, u32[]{:S(2)}) collective-permute-start(bf16[448,896]{1,0:T(8,128)(2,1)S(1)} %bitcast.18), channel_id=1, source_target_pairs={{0,1},{1,0},{2,3},{3,2},{4,5},{5,4},{6,7},{7,6},{8,9},{9,8},{10,11... | collective-permute-start | bytes 2408456 | tf_op jit(solution)/shard_map/ppermute | solution.py:271
  63.3 7.1 %collective-permute-start.19 = (bf16[448,896]{1,0:T(8,128)(2,1)S(1)}, bf16[448,896]{1,0:T(8,128)(2,1)S(1)}, u32[]{:S(2)}, u32[]{:S(2)}) collective-permute-start(bf16[448,896]{1,0:T(8,128)(2,1)S(1)} %copy-done.10), channel_id=1, source_target_pairs={{0,1},{1,0},{2,3},{3,2},{4,5},{5,4},{6,7},{7,6},{8,9},{9,8},{10,11... | collective-permute-start | bytes 2408456 | tf_op jit(solution)/shard_map/ppermute | solution.py:271
  64.8 10.8 %collective-permute-start.20 = (bf16[448,896]{1,0:T(8,128)(2,1)S(1)}, bf16[448,896]{1,0:T(8,128)(2,1)S(1)}, u32[]{:S(2)}, u32[]{:S(2)}) collective-permute-start(bf16[448,896]{1,0:T(8,128)(2,1)S(1)} %collective-permute-done.15.refs_1_), channel_id=1, source_target_pairs={{0,1},{1,0},{2,3},{3,2},{4,5},{5,4},{6,7},{7,6},{8,9},{9,8},{10,11... | collective-permute-start | bytes 2408456 | tf_op jit(solution)/shard_map/ppermute | solution.py:271
  70.2 5.3 %collective-permute-start.22 = (bf16[448,896]{1,0:T(8,128)(2,1)S(1)}, bf16[448,896]{1,0:T(8,128)(2,1)S(1)}, u32[]{:S(2)}, u32[]{:S(2)}) collective-permute-start(bf16[448,896]{1,0:T(8,128)(2,1)S(1)} %collective-permute-done.21.refs_3_), channel_id=1, source_target_pairs={{0,1},{1,0},{2,3},{3,2},{4,5},{5,4},{6,7},{7,6},{8,9},{9,8},{10,11... | collective-permute-start | bytes 2408456 | tf_op jit(solution)/shard_map/ppermute | solution.py:271
  80.6 3.9 %collective-permute-start.23 = (bf16[1024,896]{1,0:T(8,128)(2,1)S(1)}, bf16[1024,896]{1,0:T(8,128)(2,1)S(1)}, u32[]{:S(2)}, u32[]{:S(2)}) collective-permute-start(bf16[1024,896]{1,0:T(8,128)(2,1)S(1)} %encoder_ffn_far.1.encoded), channel_id=1, source_target_pairs={{0,1},{1,0},{2,3},{3,2},{4,5},{5,4},{6,7},{7,6},{8,9},{9,8},{10,11... | collective-permute-start | bytes 5505032 | tf_op jit(solution)/shard_map/ppermute | solution.py:271
  (11 other events, 13.1 us)

commit v3 on v2

--- a/solution.py
+++ b/solution.py
@@ -33,10 +33,10 @@
     return jnp.concatenate([chunk[:, SPAN:], chunk[:, :SPAN]], axis=1)
 
 
-def prepare_kernel(place, host, index, database, query_t, enc_out, up_t, down, kv_t, *refs):
+def prepare_kernel(here, lane_here, host, index, database, query_t, enc_out, up_t, down, kv_t, *refs):
     db_half, attention_half, ffn_half, packet, db_in, kv_in, sems = refs
     per_host, half_rows, width = db_half.shape
-    seq, lane = place[0], place[1]
+    seq, lane = here[0], lane_here[0]
     copies = [
         pltpu.make_async_copy(
             database.at[:, pl.ds(pl.multiple_of(lane % HALVES * half_rows, half_rows), half_rows)],
@@ -73,11 +73,10 @@
 
 
 def gather_kernel(blocks, here, host, index, before, gain, *refs):
-    *db_refs, values_out, normed_out, nbrs, sems = refs
+    *db_refs, rows_out, normed_out = refs
     per_host, part_rows, width = db_refs[0].shape
     seq = here[0]
-    copies = []
-    for i in range(nbrs.shape[0]):
+    for i in range(CH_DEV * NEIGH):
         span, k = i // NEIGH, i % NEIGH
         if span == 0:
             of_host, place = before[k, 0] // per_host, before[k, 0] % per_host
@@ -88,15 +87,10 @@
 
             @pl.when(block == b)
             def _(b=b, place=place, i=i):
-                pltpu.make_async_copy(db_refs[b].at[place], nbrs.at[i], sems.at[i]).start()
-
-        copies.append(pltpu.make_async_copy(db_refs[0].at[0], nbrs.at[i], sems.at[i]))
-    for i in range(nbrs.shape[0]):
-        copies[i].wait()
-        values = nbrs[i].astype(jnp.float32)
-        at = slice(i * part_rows, (i + 1) * part_rows)
-        values_out[at, :] = values
-        normed_out[at, :] = rms_scale(values, gain[...]).astype(jnp.bfloat16)
+                rows_out[i * part_rows : (i + 1) * part_rows, :] = db_refs[b][place]
+
+    values = rows_out[...].astype(jnp.float32)
+    normed_out[...] = rms_scale(values, gain[...]).astype(jnp.bfloat16)
 
 
 def attention_kernel(pieces, far, seq_index, before, normed_in, *refs):
@@ -162,7 +156,7 @@
                     heads.append((mixed[:, :HEAD_DIM] / mixed[:, HEAD_DIM:]).astype(jnp.bfloat16))
                 attended.append(jnp.concatenate(heads, axis=1))
             so_far = before if p == 0 else result
-            result[block, :] = so_far[block, :] + mxu(jnp.concatenate(attended, axis=0), out_w, NN)
+            result[block, :] = so_far[block, :].astype(jnp.float32) + mxu(jnp.concatenate(attended, axis=0), out_w, NN)
 
 
 def ffn_kernel(far, first, gain, before, *refs):
@@ -294,7 +288,7 @@
     kept = tokens - SPAN
 
     here = seq_index.reshape(1).astype(jnp.int32)
-    place = jnp.stack([seq_index, lane_index]).astype(jnp.int32)
+    lane_here = lane_index.reshape(1).astype(jnp.int32)
     host, index = nbr_host.T, nbr_index.T
     dma = pltpu.SemaphoreType.DMA
     short = functools.partial(jax.ShapeDtypeStruct, dtype=jnp.bfloat16)
@@ -306,16 +300,16 @@
             short(ffn_down.shape),
             short((2, kv_rows + 16, SPAN)),
         ),
-        "sss" + "h" * 6,
+        "ssss" + "h" * 6,
         "prepare",
         rows * width,
-        8,
+        60,
         scratch=[
             pltpu.VMEM((entries_here, half_rows, width), jnp.float32),
             pltpu.VMEM((2, kv_rows, 2 * SPAN), jnp.bfloat16),
             dma((6,)),
         ],
-    )(place, host, index, database, query_t, enc_out, up_t, ffn_down, kv_t)
+    )(here, lane_here, host, index, database, query_t, enc_out, up_t, ffn_down, kv_t)
 
     attention_far = [lane_step(attention_half, n + 1) for n in range(far_lanes)]
     packet = next_seq(packet)
@@ -335,7 +329,7 @@
 
     near_step = database_ring[min(1, blocks - 1)]
     ffn_far = [
-        lane_step(after(ffn_half, packet, near_step, database_blocks[1], *attention_far), n + 1)
+        lane_step(after(ffn_half, near_step, database_blocks[1], *attention_far), n + 1)
         for n in range(far_lanes)
     ]
     attention_core = tuple(core_swap(a) for a in after((query_t, enc_out), database_ring[-1]))
@@ -355,15 +349,11 @@
     short_rows = short((rows, width))
     values, normed = call(
         functools.partial(gather_kernel, blocks),
-        (long_rows, short_rows),
-        "ssssv" + "h" * 2 * blocks,
+        (short_rows, short_rows),
+        "ssss" + "v" * (1 + 2 * blocks),
         "neighbour_rows",
         10 * rows * width,
-        16,
-        scratch=[
-            pltpu.VMEM((CH_DEV * NEIGH, half_rows, width), jnp.bfloat16),
-            dma((CH_DEV * NEIGH,)),
-        ],
+        16 + (8 * blocks * database_half.size >> 20),
     )(here, host, index, before, enc_gain, *database_blocks)
 
     def attention(so_far, weights, kv, far):

time: 90.2 us -> 79.1 us (0.88)
  local copies, waits for them, and re-layouts: 8.53 us -> 0.68 us
  Pallas kernels: 35.8 us -> 33.8 us
  waiting for transfers between devices: 22.8 us -> 21.6 us
    unnamed x39 -> x25, local copies, waits for them, and re-layouts: 8.51 us -> 0.67 us
    pallas_call x1, Pallas kernels: 6.05 us -> 2.5 us  [on_device(): call(functools.partial(gather_kernel, blocks), (short_rows, short_rows),...]
    ppermute x3, starting transfers between devices: 4.91 us -> 1.58 us  [seq_ring(): lax.ppermute(array, 'seq', [(i, (i + 2) % seq_size) for i in range(seq_si...]
    ppermute x5, starting transfers between devices: 4.48 us -> 7.6 us  [seq_swap(): return lax.ppermute(array, 'seq', [(i, i ^ 1) for i in range(seq_size)])]
    ppermute x3, waiting for transfers between devices: 9.9 us -> 12.4 us  [seq_ring(): lax.ppermute(array, 'seq', [(i, (i + 2) % seq_size) for i in range(seq_si...]
    ppermute x1, waiting for transfers between devices: 2.42 us -> 0.22 us  [next_seq(): return lax.ppermute(array, 'seq', [(i, i + 1) for i in range(seq_size - 1)])]
    ppermute x5, waiting for transfers between devices: 7.98 us -> 6.11 us  [seq_swap(): return lax.ppermute(array, 'seq', [(i, i ^ 1) for i in range(seq_size)])]
    pallas_call x1, Pallas kernels: 1.87 us -> 3.44 us  [on_device(): call(prepare_kernel, (short((entries_here, half_rows, width)), short(enc_...]
  transfers between devices with their start and end apart: 24 -> 24, of which waited for: 9 -> 11; matrix products, arithmetic and copies ran while one was open for 1% -> 1% of each run, Pallas kernels for 26% -> 25%
where the time goes in v3:
time: 79.1 us; the launch traced here: 78.9 us
  Pallas kernels  33.8 us (43%)
  starting transfers between devices  22.1 us (28%)
  waiting for transfers between devices  21.6 us (27%)
    ppermute x3, waiting for transfers between devices, seq_ring(): lax.ppermute(array, 'seq', [(i, (i + 2) % seq_size) for i in range(seq_si...  12.4 us
    pallas_call x2, Pallas kernels, attention(): call(functools.partial(attention_kernel, len(kv), far), long_rows, 'svv'...  10.1 us
    ppermute x5, starting transfers between devices, seq_swap(): return lax.ppermute(array, 'seq', [(i, i ^ 1) for i in range(seq_size)])  7.6 us
    ppermute x5, waiting for transfers between devices, seq_swap(): return lax.ppermute(array, 'seq', [(i, i ^ 1) for i in range(seq_size)])  6.11 us
    pallas_call x1, Pallas kernels, on_device(): call(decoder_kernel, jax.ShapeDtypeStruct(dec_queries.shape, jnp.float32)...  5.33 us
    ppermute x3, starting transfers between devices, lane_step(): lax.ppermute(array, 'mp', [(i, (i + 2 * step) % lanes) for i in range(lan...  5.28 us
    pallas_call x1, Pallas kernels, on_device(): call(functools.partial(ffn_kernel, False, True), (long_rows, short_rows),...  5.1 us
    pallas_call x1, Pallas kernels, on_device(): call(functools.partial(ffn_kernel, True, False), short_rows, 'vvv' + 'v'...  5.06 us
  transfers between devices with their start and end apart: 24, of which 11 were waited for; matrix products, arithmetic and copies ran while one was open for 1% of the time, Pallas kernels for 25%

profile of v3, /device:TPU:0, one launch (start us, length us, event | category | flops | bytes accessed | tf_op | source)
XLA Modules:
  0.0 78.9 jit_solution(5324686550825872367)
XLA Ops:
  0.0 3.4 %prepare.1 = (bf16[2,64,896]{2,1,0:T(8,128)(2,1)}, bf16[224,896]{1,0:T(8,128)(2,1)}, bf16[448,896]{1,0:T(8,128)(2,1)}, bf16[2,240,64]{2,1,0:T(8,128)(2,1)}) custom-call(s32[1]{0:T(128)} %bitcast.here.seq_index.first, s32[1]{0:T(128)} %bitcast.1.lane_here, s32[2,8]{1,0:T(2,128)} %bitcast.18, s32[2,8]{1,0:T(2,128)} %bitcast.20, f32[2,128,896]{2,1,0:T(8,128)} %database.1, ...), custom_call_target="tpu_custom_call" | custom-call | flops 917504 | bytes 8000000 | tf_op jit(solution)/shard_map/prepare/pallas_call | solution.py:295
  3.5 3.0 %collective-permute-start.11 = (bf16[224,896]{1,0:T(8,128)(2,1)}, bf16[224,896]{1,0:T(8,128)(2,1)S(1)}, u32[]{:S(2)}, u32[]{:S(2)}) collective-permute-start(bf16[224,896]{1,0:T(8,128)(2,1)} %get-tuple-element.37), channel_id=1, source_target_pairs={{0,2},{1,3},{2,0},{3,1},{4,6},{5,7},{6,4},{7,5},{8,10},{9,11},{10,... | collective-permute-start | bytes 1204232 | tf_op jit(solution)/shard_map/ppermute | solution.py:268
  6.5 1.6 %collective-permute-start.1 = (bf16[2,64,896]{2,1,0:T(8,128)(2,1)}, bf16[2,64,896]{2,1,0:T(8,128)(2,1)S(1)}, u32[]{:S(2)}, u32[]{:S(2)}) collective-permute-start(bf16[2,64,896]{2,1,0:T(8,128)(2,1)} %get-tuple-element.28.refs_0_), channel_id=1, source_target_pairs={{0,8},{4,12},{8,16},{12,20},{16,24},{20,28},{24,0},{28,4},{1,9},{5... | collective-permute-start | bytes 688136 | tf_op jit(solution)/shard_map/ppermute | solution.py:277
  8.1 1.5 %collective-permute-start.3 = (bf16[2,64,896]{2,1,0:T(8,128)(2,1)}, bf16[2,64,896]{2,1,0:T(8,128)(2,1)S(1)}, u32[]{:S(2)}, u32[]{:S(2)}) collective-permute-start(bf16[2,64,896]{2,1,0:T(8,128)(2,1)} %get-tuple-element.28.refs_0_), channel_id=1, source_target_pairs={{0,4},{4,0},{8,12},{12,8},{16,20},{20,16},{24,28},{28,24},{1,5},{5... | collective-permute-start | bytes 688136 | tf_op jit(solution)/shard_map/ppermute | solution.py:271
  9.6 6.1 %collective-permute-done.1.refs_2_ = bf16[2,64,896]{2,1,0:T(8,128)(2,1)S(1)} collective-permute-done((bf16[2,64,896]{2,1,0:T(8,128)(2,1)}, bf16[2,64,896]{2,1,0:T(8,128)(2,1)S(1)}, u32[]{:S(2)}, u32[]{:S(2)}) %collective-permute-start.1) | collective-permute-done | bytes 229408 | tf_op jit(solution)/shard_map/ppermute | solution.py:277
  15.6 0.4 collective-permute-done.11.refs_0_
  16.0 1.7 %collective-permute-start.15 = (bf16[448,896]{1,0:T(8,128)(2,1)}, bf16[448,896]{1,0:T(8,128)(2,1)S(1)}, u32[]{:S(2)}, u32[]{:S(2)}) collective-permute-start(bf16[448,896]{1,0:T(8,128)(2,1)} %get-tuple-element.40), channel_id=1, source_target_pairs={{0,2},{1,3},{2,0},{3,1},{4,6},{5,7},{6,4},{7,5},{8,10},{9,11},{10,... | collective-permute-start | bytes 2408456 | tf_op jit(solution)/shard_map/ppermute | solution.py:268
  17.7 3.4 %collective-permute-start = (bf16[2,240,64]{2,1,0:T(8,128)(2,1)}, bf16[2,240,64]{2,1,0:T(8,128)(2,1)S(1)}, u32[]{:S(2)}, u32[]{:S(2)}) collective-permute-start(bf16[2,240,64]{2,1,0:T(8,128)(2,1)} %get-tuple-element.27), channel_id=1, source_target_pairs={{0,4},{4,8},{8,12},{12,16},{16,20},{20,24},{24,28},{1,5},{5,9},{9,... | collective-permute-start | bytes 184328 | tf_op jit(solution)/shard_map/ppermute | solution.py:280
  21.2 0.5 copy.13
  21.8 1.8 %collective-permute-done.4.refs_4_ = bf16[2,64,896]{2,1,0:T(8,128)(2,1)S(1)} collective-permute-done((bf16[2,64,896]{2,1,0:T(8,128)(2,1)S(1)}, bf16[2,64,896]{2,1,0:T(8,128)(2,1)S(1)}, u32[]{:S(2)}, u32[]{:S(2)}) %collective-permute-start.4) | collective-permute-done | bytes 229408 | tf_op jit(solution)/shard_map/ppermute | solution.py:277
  24.0 2.8 %collective-permute-start.2 = (bf16[2,64,896]{2,1,0:T(8,128)(2,1)S(1)}, bf16[2,64,896]{2,1,0:T(8,128)(2,1)S(1)}, u32[]{:S(2)}, u32[]{:S(2)}) collective-permute-start(bf16[2,64,896]{2,1,0:T(8,128)(2,1)S(1)} %collective-permute-done.1.refs_2_), channel_id=1, source_target_pairs={{0,4},{4,0},{8,12},{12,8},{16,20},{20,16},{24,28},{28,24},{1,5},{5... | collective-permute-start | bytes 688136 | tf_op jit(solution)/shard_map/ppermute | solution.py:271
  27.0 4.5 %collective-permute-done.6.refs_6_ = bf16[2,64,896]{2,1,0:T(8,128)(2,1)S(1)} collective-permute-done((bf16[2,64,896]{2,1,0:T(8,128)(2,1)S(1)}, bf16[2,64,896]{2,1,0:T(8,128)(2,1)S(1)}, u32[]{:S(2)}, u32[]{:S(2)}) %collective-permute-start.6) | collective-permute-done | bytes 229408 | tf_op jit(solution)/shard_map/ppermute | solution.py:277
  31.5 1.5 %collective-permute-start.7 = (bf16[2,64,896]{2,1,0:T(8,128)(2,1)S(1)}, bf16[2,64,896]{2,1,0:T(8,128)(2,1)S(1)}, u32[]{:S(2)}, u32[]{:S(2)}) collective-permute-start(bf16[2,64,896]{2,1,0:T(8,128)(2,1)S(1)} %collective-permute-done.6.refs_6_), channel_id=1, source_target_pairs={{0,4},{4,0},{8,12},{12,8},{16,20},{20,16},{24,28},{28,24},{1,5},{5... | collective-permute-start | bytes 688136 | tf_op jit(solution)/shard_map/ppermute | solution.py:271
  33.3 0.5 collective-permute-start.8
  33.8 3.5 %collective-permute-done.5.refs_5_ = bf16[2,64,896]{2,1,0:T(8,128)(2,1)S(1)} collective-permute-done((bf16[2,64,896]{2,1,0:T(8,128)(2,1)S(1)}, bf16[2,64,896]{2,1,0:T(8,128)(2,1)S(1)}, u32[]{:S(2)}, u32[]{:S(2)}) %collective-permute-start.5) | collective-permute-done | bytes 229408 | tf_op jit(solution)/shard_map/ppermute | solution.py:271
  37.4 2.5 %collective-permute-done.7.refs_7_ = bf16[2,64,896]{2,1,0:T(8,128)(2,1)S(1)} collective-permute-done((bf16[2,64,896]{2,1,0:T(8,128)(2,1)S(1)}, bf16[2,64,896]{2,1,0:T(8,128)(2,1)S(1)}, u32[]{:S(2)}, u32[]{:S(2)}) %collective-permute-start.7) | collective-permute-done | bytes 229408 | tf_op jit(solution)/shard_map/ppermute | solution.py:271
  39.8 0.5 collective-permute-start.16
  40.3 1.7 %collective-permute-start.12 = (bf16[224,896]{1,0:T(8,128)(2,1)S(1)}, bf16[224,896]{1,0:T(8,128)(2,1)S(1)}, u32[]{:S(2)}, u32[]{:S(2)}) collective-permute-start(bf16[224,896]{1,0:T(8,128)(2,1)S(1)} %collective-permute-done.11.refs_0_), channel_id=1, source_target_pairs={{0,4},{4,0},{8,12},{12,8},{16,20},{20,16},{24,28},{28,24},{1,5},{5... | collective-permute-start | bytes 1204232 | tf_op jit(solution)/shard_map/ppermute | solution.py:271
  42.1 1.6 %collective-permute-start.21 = (bf16[448,896]{1,0:T(8,128)(2,1)S(1)}, bf16[448,896]{1,0:T(8,128)(2,1)S(1)}, u32[]{:S(2)}, u32[]{:S(2)}) collective-permute-start(bf16[448,896]{1,0:T(8,128)(2,1)S(1)} %collective-permute-done.15.refs_1_), channel_id=1, source_target_pairs={{0,8},{4,12},{8,0},{12,4},{16,24},{20,28},{24,16},{28,20},{1,9},{5... | collective-permute-start | bytes 2408456 | tf_op jit(solution)/shard_map/ppermute | solution.py:274
  43.7 2.5 %neighbour_rows.1 = (bf16[1024,896]{1,0:T(8,128)(2,1)S(1)}, bf16[1024,896]{1,0:T(8,128)(2,1)S(1)}) custom-call(s32[1]{0:T(128)} %bitcast.here.seq_index.first, s32[2,8]{1,0:T(2,128)S(1)} %bitcast.19, s32[2,8]{1,0:T(2,128)S(1)} %bitcast.21, s32[2,1]{1,0:T(2,128)S(1)} %slice_add_fusion.before, f32[1,896]{1,0:T(1,128)S(1)} %reshape.20.gain, ...), custom_call_target="tpu_custom_call" | custom-call | flops 9175040 | bytes 8000000 | tf_op jit(solution)/shard_map/neighbour_rows/pallas_call | solution.py:350
  46.3 5.0 %encoder_attention.2.before = f32[1024,896]{1,0:T(8,128)S(1)} custom-call(s32[1]{0:T(128)} %bitcast.here.seq_index.first, bf16[1024,896]{1,0:T(8,128)(2,1)S(1)} %get-tuple-element.32.before, bf16[1024,896]{1,0:T(8,128)(2,1)S(1)} %get-tuple-element.33.normed_in, bf16[224,896]{1,0:T(8,128)(2,1)S(1)} %bitcast.14, bf16[224,896]{1,0:T(8,128)(2,1)S(1)} %copy-done.1, ...), custom_call_target="tpu_custom_call" | custom-call | flops 1644167168 | bytes 8000000 | tf_op jit(solution)/shard_map/encoder_attention/pallas_call | solution.py:360
  51.3 0.5 collective-permute-start.17
  52.0 0.4 collective-permute-start.18
  52.5 1.4 %collective-permute-done.14.refs_3_ = bf16[224,896]{1,0:T(8,128)(2,1)S(1)} collective-permute-done((bf16[224,896]{1,0:T(8,128)(2,1)S(1)}, bf16[224,896]{1,0:T(8,128)(2,1)S(1)}, u32[]{:S(2)}, u32[]{:S(2)}) %collective-permute-start.14) | collective-permute-done | bytes 401440 | tf_op jit(solution)/shard_map/ppermute | solution.py:265
  53.9 0.4 collective-permute-start.20
  54.3 5.0 %encoder_attention.3.before = f32[1024,896]{1,0:T(8,128)S(1)} custom-call(s32[1]{0:T(128)} %bitcast.here.seq_index.first, f32[1024,896]{1,0:T(8,128)S(1)} %encoder_attention.2.before, bf16[1024,896]{1,0:T(8,128)(2,1)S(1)} %get-tuple-element.33.normed_in, bf16[224,896]{1,0:T(8,128)(2,1)S(1)} %collective-permute-done.11.refs_0_, ...), custom_call_target="tpu_custom_call" | custom-call | flops 1644167168 | bytes 8000000 | tf_op jit(solution)/shard_map/encoder_attention/pallas_call | solution.py:360
  59.5 5.1 %encoder_ffn_near.1 = (f32[1024,896]{1,0:T(8,128)S(1)}, bf16[1024,896]{1,0:T(8,128)(2,1)S(1)}) custom-call(f32[1,896]{1,0:T(1,128)S(1)} %reshape.21.gain, f32[1024,896]{1,0:T(8,128)S(1)} %encoder_attention.3.before, bf16[448,896]{1,0:T(8,128)(2,1)S(1)} %bitcast.17, bf16[448,896]{1,0:T(8,128)(2,1)S(1)} %copy-done.3, ...), custom_call_target="tpu_custom_call" | custom-call | flops 3288334336 | bytes 8000000 | tf_op jit(solution)/shard_map/encoder_ffn_near/pallas_call | solution.py:378
  64.7 5.1 %encoder_ffn_far.1.encoded = bf16[1024,896]{1,0:T(8,128)(2,1)S(1)} custom-call(f32[1,896]{1,0:T(1,128)S(1)} %reshape.21.gain, f32[1024,896]{1,0:T(8,128)S(1)} %get-tuple-element.45.before, bf16[1024,896]{1,0:T(8,128)(2,1)S(1)} %get-tuple-element.46.refs_0_, bf16[448,896]{1,0:T(8,128)(2,1)S(1)} %collective-permute-done.15.refs_1_, ...), custom_call_target="tpu_custom_call" | custom-call | flops 3288334336 | bytes 8000000 | tf_op jit(solution)/shard_map/encoder_ffn_far/pallas_call | solution.py:388
  69.7 0.4 collective-permute-start.23
  70.2 2.3 %decoder_pairs.1.own_pairs = bf16[1024,1024]{1,0:T(8,128)(2,1)S(1)} custom-call(bf16[1024,896]{1,0:T(8,128)(2,1)S(1)} %encoder_ffn_far.1.encoded, bf16[896,1024]{1,0:T(8,128)(2,1)S(1)} %bitcast.10), custom_call_target="tpu_custom_call" | custom-call | flops 1879048192 | bytes 8000000 | tf_op jit(solution)/shard_map/decoder_pairs/pallas_call | solution.py:401
  72.5 1.1 %collective-permute-done.23.other = bf16[1024,896]{1,0:T(8,128)(2,1)S(1)} collective-permute-done((bf16[1024,896]{1,0:T(8,128)(2,1)S(1)}, bf16[1024,896]{1,0:T(8,128)(2,1)S(1)}, u32[]{:S(2)}, u32[]{:S(2)}) %collective-permute-start.23) | collective-permute-done | bytes 1835040 | tf_op jit(solution)/shard_map/ppermute | solution.py:265
  73.6 5.3 %decoder_attention.1 = f32[512,512]{1,0:T(8,128)} custom-call(s32[1]{0:T(128)} %bitcast.here.seq_index.first, bf16[1024,1024]{1,0:T(8,128)(2,1)S(1)} %decoder_pairs.1.own_pairs, bf16[1024,896]{1,0:T(8,128)(2,1)S(1)} %collective-permute-done.23.other, bf16[896,1024]{1,0:T(8,128)(2,1)S(1)} %bitcast.11, bf16[512,512]{1,0:T(8,128)(2,1)S(1)} %copy-done.4), custom_call_target="tpu_custom_call" | custom-call | flops 1879048192 | bytes 8000000 | tf_op jit(solution)/shard_map/decoder_attention/pallas_call | solution.py:409
  (55 shorter events, 1.6 us)
Async XLA Ops:
  0.0 21.1 %copy-start.8 = (bf16[896,2,512]{2,1,0:T(2,128)(2,1)S(1)}, bf16[896,2,512]{2,1,0:T(2,128)(2,1)}, u32[]{:S(2)}) copy-start(bf16[896,2,512]{2,1,0:T(2,128)(2,1)} %param.23) | copy-start | bytes 5505028
  3.5 12.5 %collective-permute-start.11 = (bf16[224,896]{1,0:T(8,128)(2,1)}, bf16[224,896]{1,0:T(8,128)(2,1)S(1)}, u32[]{:S(2)}, u32[]{:S(2)}) collective-permute-start(bf16[224,896]{1,0:T(8,128)(2,1)} %get-tuple-element.37), channel_id=1, source_target_pairs={{0,2},{1,3},{2,0},{3,1},{4,6},{5,7},{6,4},{7,5},{8,10},{9,11},{10,... | collective-permute-start | bytes 1204232 | tf_op jit(solution)/shard_map/ppermute | solution.py:268
  6.5 9.1 %collective-permute-start.1 = (bf16[2,64,896]{2,1,0:T(8,128)(2,1)}, bf16[2,64,896]{2,1,0:T(8,128)(2,1)S(1)}, u32[]{:S(2)}, u32[]{:S(2)}) collective-permute-start(bf16[2,64,896]{2,1,0:T(8,128)(2,1)} %get-tuple-element.28.refs_0_), channel_id=1, source_target_pairs={{0,8},{4,12},{8,16},{12,20},{16,24},{20,28},{24,0},{28,4},{1,9},{5... | collective-permute-start | bytes 688136 | tf_op jit(solution)/shard_map/ppermute | solution.py:277
  8.1 7.6 %collective-permute-start.3 = (bf16[2,64,896]{2,1,0:T(8,128)(2,1)}, bf16[2,64,896]{2,1,0:T(8,128)(2,1)S(1)}, u32[]{:S(2)}, u32[]{:S(2)}) collective-permute-start(bf16[2,64,896]{2,1,0:T(8,128)(2,1)} %get-tuple-element.28.refs_0_), channel_id=1, source_target_pairs={{0,4},{4,0},{8,12},{12,8},{16,20},{20,16},{24,28},{28,24},{1,5},{5... | collective-permute-start | bytes 688136 | tf_op jit(solution)/shard_map/ppermute | solution.py:271
  15.6 8.0 %collective-permute-start.4 = (bf16[2,64,896]{2,1,0:T(8,128)(2,1)S(1)}, bf16[2,64,896]{2,1,0:T(8,128)(2,1)S(1)}, u32[]{:S(2)}, u32[]{:S(2)}) collective-permute-start(bf16[2,64,896]{2,1,0:T(8,128)(2,1)S(1)} %collective-permute-done.1.refs_2_), channel_id=1, source_target_pairs={{0,8},{4,12},{8,16},{12,20},{16,24},{20,28},{24,0},{28,4},{1,9},{5... | collective-permute-start | bytes 688136 | tf_op jit(solution)/shard_map/ppermute | solution.py:277
  16.0 23.8 %collective-permute-start.15 = (bf16[448,896]{1,0:T(8,128)(2,1)}, bf16[448,896]{1,0:T(8,128)(2,1)S(1)}, u32[]{:S(2)}, u32[]{:S(2)}) collective-permute-start(bf16[448,896]{1,0:T(8,128)(2,1)} %get-tuple-element.40), channel_id=1, source_target_pairs={{0,2},{1,3},{2,0},{3,1},{4,6},{5,7},{6,4},{7,5},{8,10},{9,11},{10,... | collective-permute-start | bytes 2408456 | tf_op jit(solution)/shard_map/ppermute | solution.py:268
  17.7 6.1 %collective-permute-start = (bf16[2,240,64]{2,1,0:T(8,128)(2,1)}, bf16[2,240,64]{2,1,0:T(8,128)(2,1)S(1)}, u32[]{:S(2)}, u32[]{:S(2)}) collective-permute-start(bf16[2,240,64]{2,1,0:T(8,128)(2,1)} %get-tuple-element.27), channel_id=1, source_target_pairs={{0,4},{4,8},{8,12},{12,16},{16,20},{20,24},{24,28},{1,5},{5,9},{9,... | collective-permute-start | bytes 184328 | tf_op jit(solution)/shard_map/ppermute | solution.py:280
  21.2 11.8 %copy-start.9 = (bf16[512,2,224]{0,2,1:T(8,128)(2,1)S(1)}, bf16[512,2,224]{0,2,1:T(8,128)(2,1)}, u32[]{:S(2)}) copy-start(bf16[512,2,224]{0,2,1:T(8,128)(2,1)} %param.12) | copy-start | bytes 1376260
  21.2 12.2 %copy-start = (bf16[896,224]{0,1:T(8,128)(2,1)S(1)}, bf16[896,224]{0,1:T(8,128)(2,1)}, u32[]{:S(2)}) copy-start(bf16[896,224]{0,1:T(8,128)(2,1)} %param.18) | copy-start | bytes 1204228
  21.2 16.2 %copy-start.1 = (bf16[224,896]{1,0:T(8,128)(2,1)S(1)}, bf16[224,896]{1,0:T(8,128)(2,1)}, u32[]{:S(2)}) copy-start(bf16[224,896]{1,0:T(8,128)(2,1)} %refs_1_.2) | copy-start | bytes 1204228
  21.2 22.5 %copy-start.5 = (bf16[2,64,896]{2,1,0:T(8,128)(2,1)S(1)}, bf16[2,64,896]{2,1,0:T(8,128)(2,1)}, u32[]{:S(2)}) copy-start(bf16[2,64,896]{2,1,0:T(8,128)(2,1)} %get-tuple-element.28.refs_0_) | copy-start | bytes 688132
  21.2 22.5 %copy-start.6 = (s32[8,2]{0,1:T(2,128)S(1)}, s32[8,2]{0,1:T(2,128)}, u32[]{:S(2)}) copy-start(s32[8,2]{0,1:T(2,128)} %param.16) | copy-start | bytes 196
  21.2 22.5 %copy-start.7 = (s32[8,2]{0,1:T(2,128)S(1)}, s32[8,2]{0,1:T(2,128)}, u32[]{:S(2)}) copy-start(s32[8,2]{0,1:T(2,128)} %param.15) | copy-start | bytes 196
  23.6 7.8 %collective-permute-start.6 = (bf16[2,64,896]{2,1,0:T(8,128)(2,1)S(1)}, bf16[2,64,896]{2,1,0:T(8,128)(2,1)S(1)}, u32[]{:S(2)}, u32[]{:S(2)}) collective-permute-start(bf16[2,64,896]{2,1,0:T(8,128)(2,1)S(1)} %collective-permute-done.4.refs_4_), channel_id=1, source_target_pairs={{0,8},{4,12},{8,16},{12,20},{16,24},{20,28},{24,0},{28,4},{1,9},{5... | collective-permute-start | bytes 688136 | tf_op jit(solution)/shard_map/ppermute | solution.py:277
  24.0 9.3 %collective-permute-start.2 = (bf16[2,64,896]{2,1,0:T(8,128)(2,1)S(1)}, bf16[2,64,896]{2,1,0:T(8,128)(2,1)S(1)}, u32[]{:S(2)}, u32[]{:S(2)}) collective-permute-start(bf16[2,64,896]{2,1,0:T(8,128)(2,1)S(1)} %collective-permute-done.1.refs_2_), channel_id=1, source_target_pairs={{0,4},{4,0},{8,12},{12,8},{16,20},{20,16},{24,28},{28,24},{1,5},{5... | collective-permute-start | bytes 688136 | tf_op jit(solution)/shard_map/ppermute | solution.py:271
  26.8 10.6 %collective-permute-start.5 = (bf16[2,64,896]{2,1,0:T(8,128)(2,1)S(1)}, bf16[2,64,896]{2,1,0:T(8,128)(2,1)S(1)}, u32[]{:S(2)}, u32[]{:S(2)}) collective-permute-start(bf16[2,64,896]{2,1,0:T(8,128)(2,1)S(1)} %collective-permute-done.4.refs_4_), channel_id=1, source_target_pairs={{0,4},{4,0},{8,12},{12,8},{16,20},{20,16},{24,28},{28,24},{1,5},{5... | collective-permute-start | bytes 688136 | tf_op jit(solution)/shard_map/ppermute | solution.py:271
  31.5 8.4 %collective-permute-start.7 = (bf16[2,64,896]{2,1,0:T(8,128)(2,1)S(1)}, bf16[2,64,896]{2,1,0:T(8,128)(2,1)S(1)}, u32[]{:S(2)}, u32[]{:S(2)}) collective-permute-start(bf16[2,64,896]{2,1,0:T(8,128)(2,1)S(1)} %collective-permute-done.6.refs_6_), channel_id=1, source_target_pairs={{0,4},{4,0},{8,12},{12,8},{16,20},{20,16},{24,28},{28,24},{1,5},{5... | collective-permute-start | bytes 688136 | tf_op jit(solution)/shard_map/ppermute | solution.py:271
  33.3 8.8 %collective-permute-start.10 = (bf16[2,224,512]{2,1,0:T(8,128)(2,1)S(1)}, bf16[2,224,512]{2,1,0:T(8,128)(2,1)S(1)}, u32[]{:S(2)}, u32[]{:S(2)}) collective-permute-start(bf16[2,224,512]{2,1,0:T(8,128)(2,1)S(1)} %pad_maximum_fusion.refs_4_), channel_id=1, source_target_pairs={{0,1},{1,0},{2,3},{3,2},{4,5},{5,4},{6,7},{7,6},{8,9},{9,8},{10,11... | collective-permute-start | bytes 1376264 | tf_op jit(solution)/shard_map/ppermute | solution.py:265
  33.3 12.9 %collective-permute-start.8 = (bf16[224,896]{1,0:T(8,128)(2,1)S(1)}, bf16[224,896]{1,0:T(8,128)(2,1)S(1)}, u32[]{:S(2)}, u32[]{:S(2)}) collective-permute-start(bf16[224,896]{1,0:T(8,128)(2,1)S(1)} %bitcast.13), channel_id=1, source_target_pairs={{0,1},{1,0},{2,3},{3,2},{4,5},{5,4},{6,7},{7,6},{8,9},{9,8},{10,11... | collective-permute-start | bytes 1204232 | tf_op jit(solution)/shard_map/ppermute | solution.py:265
  37.4 8.9 %collective-permute-start.9 = (bf16[224,896]{1,0:T(8,128)(2,1)S(1)}, bf16[224,896]{1,0:T(8,128)(2,1)S(1)}, u32[]{:S(2)}, u32[]{:S(2)}) collective-permute-start(bf16[224,896]{1,0:T(8,128)(2,1)S(1)} %copy-done.1), channel_id=1, source_target_pairs={{0,1},{1,0},{2,3},{3,2},{4,5},{5,4},{6,7},{7,6},{8,9},{9,8},{10,11... | collective-permute-start | bytes 1204232 | tf_op jit(solution)/shard_map/ppermute | solution.py:265
  39.8 11.5 %collective-permute-start.16 = (bf16[2,224,512]{2,1,0:T(8,128)(2,1)S(1)}, bf16[2,224,512]{2,1,0:T(8,128)(2,1)S(1)}, u32[]{:S(2)}, u32[]{:S(2)}) collective-permute-start(bf16[2,224,512]{2,1,0:T(8,128)(2,1)S(1)} %pad_maximum_fusion.refs_4_), channel_id=1, source_target_pairs={{0,2},{1,3},{2,0},{3,1},{4,6},{5,7},{6,4},{7,5},{8,10},{9,11},{10,... | collective-permute-start | bytes 1376264 | tf_op jit(solution)/shard_map/ppermute | solution.py:268
  40.3 11.5 %collective-permute-start.12 = (bf16[224,896]{1,0:T(8,128)(2,1)S(1)}, bf16[224,896]{1,0:T(8,128)(2,1)S(1)}, u32[]{:S(2)}, u32[]{:S(2)}) collective-permute-start(bf16[224,896]{1,0:T(8,128)(2,1)S(1)} %collective-permute-done.11.refs_0_), channel_id=1, source_target_pairs={{0,4},{4,0},{8,12},{12,8},{16,20},{20,16},{24,28},{28,24},{1,5},{5... | collective-permute-start | bytes 1204232 | tf_op jit(solution)/shard_map/ppermute | solution.py:271
  42.1 17.3 %collective-permute-start.21 = (bf16[448,896]{1,0:T(8,128)(2,1)S(1)}, bf16[448,896]{1,0:T(8,128)(2,1)S(1)}, u32[]{:S(2)}, u32[]{:S(2)}) collective-permute-start(bf16[448,896]{1,0:T(8,128)(2,1)S(1)} %collective-permute-done.15.refs_1_), channel_id=1, source_target_pairs={{0,8},{4,12},{8,0},{12,4},{16,24},{20,28},{24,16},{28,20},{1,9},{5... | collective-permute-start | bytes 2408456 | tf_op jit(solution)/shard_map/ppermute | solution.py:274
  46.2 6.2 %collective-permute-start.13 = (bf16[224,896]{1,0:T(8,128)(2,1)S(1)}, bf16[224,896]{1,0:T(8,128)(2,1)S(1)}, u32[]{:S(2)}, u32[]{:S(2)}) collective-permute-start(bf16[224,896]{1,0:T(8,128)(2,1)S(1)} %collective-permute-done.11.refs_0_), channel_id=1, source_target_pairs={{0,1},{1,0},{2,3},{3,2},{4,5},{5,4},{6,7},{7,6},{8,9},{9,8},{10,11... | collective-permute-start | bytes 1204232 | tf_op jit(solution)/shard_map/ppermute | solution.py:265
  46.3 6.1 %copy-start.3 = (bf16[448,896]{1,0:T(8,128)(2,1)S(1)}, bf16[448,896]{1,0:T(8,128)(2,1)}, u32[]{:S(2)}) copy-start(bf16[448,896]{1,0:T(8,128)(2,1)} %refs_1_.3) | copy-start | bytes 2408452
  51.3 2.9 %collective-permute-start.17 = (bf16[2,224,512]{2,1,0:T(8,128)(2,1)S(1)}, bf16[2,224,512]{2,1,0:T(8,128)(2,1)S(1)}, u32[]{:S(2)}, u32[]{:S(2)}) collective-permute-start(bf16[2,224,512]{2,1,0:T(8,128)(2,1)S(1)} %collective-permute-done.16.refs_4_), channel_id=1, source_target_pairs={{0,1},{1,0},{2,3},{3,2},{4,5},{5,4},{6,7},{7,6},{8,9},{9,8},{10,11... | collective-permute-start | bytes 1376264 | tf_op jit(solution)/shard_map/ppermute | solution.py:265
  51.9 2.0 %collective-permute-start.14 = (bf16[224,896]{1,0:T(8,128)(2,1)S(1)}, bf16[224,896]{1,0:T(8,128)(2,1)S(1)}, u32[]{:S(2)}, u32[]{:S(2)}) collective-permute-start(bf16[224,896]{1,0:T(8,128)(2,1)S(1)} %collective-permute-done.12.refs_1_), channel_id=1, source_target_pairs={{0,1},{1,0},{2,3},{3,2},{4,5},{5,4},{6,7},{7,6},{8,9},{9,8},{10,11... | collective-permute-start | bytes 1204232 | tf_op jit(solution)/shard_map/ppermute | solution.py:265
  52.0 7.6 %collective-permute-start.18 = (bf16[448,896]{1,0:T(8,128)(2,1)S(1)}, bf16[448,896]{1,0:T(8,128)(2,1)S(1)}, u32[]{:S(2)}, u32[]{:S(2)}) collective-permute-start(bf16[448,896]{1,0:T(8,128)(2,1)S(1)} %bitcast.16), channel_id=1, source_target_pairs={{0,1},{1,0},{2,3},{3,2},{4,5},{5,4},{6,7},{7,6},{8,9},{9,8},{10,11... | collective-permute-start | bytes 2408456 | tf_op jit(solution)/shard_map/ppermute | solution.py:265
  52.4 7.1 %collective-permute-start.19 = (bf16[448,896]{1,0:T(8,128)(2,1)S(1)}, bf16[448,896]{1,0:T(8,128)(2,1)S(1)}, u32[]{:S(2)}, u32[]{:S(2)}) collective-permute-start(bf16[448,896]{1,0:T(8,128)(2,1)S(1)} %copy-done.3), channel_id=1, source_target_pairs={{0,1},{1,0},{2,3},{3,2},{4,5},{5,4},{6,7},{7,6},{8,9},{9,8},{10,11... | collective-permute-start | bytes 2408456 | tf_op jit(solution)/shard_map/ppermute | solution.py:265
  53.9 10.8 %collective-permute-start.20 = (bf16[448,896]{1,0:T(8,128)(2,1)S(1)}, bf16[448,896]{1,0:T(8,128)(2,1)S(1)}, u32[]{:S(2)}, u32[]{:S(2)}) collective-permute-start(bf16[448,896]{1,0:T(8,128)(2,1)S(1)} %collective-permute-done.15.refs_1_), channel_id=1, source_target_pairs={{0,1},{1,0},{2,3},{3,2},{4,5},{5,4},{6,7},{7,6},{8,9},{9,8},{10,11... | collective-permute-start | bytes 2408456 | tf_op jit(solution)/shard_map/ppermute | solution.py:265
  59.4 5.3 %collective-permute-start.22 = (bf16[448,896]{1,0:T(8,128)(2,1)S(1)}, bf16[448,896]{1,0:T(8,128)(2,1)S(1)}, u32[]{:S(2)}, u32[]{:S(2)}) collective-permute-start(bf16[448,896]{1,0:T(8,128)(2,1)S(1)} %collective-permute-done.21.refs_3_), channel_id=1, source_target_pairs={{0,1},{1,0},{2,3},{3,2},{4,5},{5,4},{6,7},{7,6},{8,9},{9,8},{10,11... | collective-permute-start | bytes 2408456 | tf_op jit(solution)/shard_map/ppermute | solution.py:265
  69.7 3.9 %collective-permute-start.23 = (bf16[1024,896]{1,0:T(8,128)(2,1)S(1)}, bf16[1024,896]{1,0:T(8,128)(2,1)S(1)}, u32[]{:S(2)}, u32[]{:S(2)}) collective-permute-start(bf16[1024,896]{1,0:T(8,128)(2,1)S(1)} %encoder_ffn_far.1.encoded), channel_id=1, source_target_pairs={{0,1},{1,0},{2,3},{3,2},{4,5},{5,4},{6,7},{7,6},{8,9},{9,8},{10,11... | collective-permute-start | bytes 5505032 | tf_op jit(solution)/shard_map/ppermute | solution.py:265
  (4 other events, 11.0 us)

commit v4 on v3

--- a/solution.py
+++ b/solution.py
@@ -201,6 +201,7 @@
             axis=0,
         )
 
+    ones = jnp.ones((2 * part, HEAD_DIM), jnp.bfloat16)
     for head in range(width // HEAD_DIM):
         col = head * HEAD_DIM
         query = (queries[:, col : col + HEAD_DIM].astype(jnp.float32) * scale).astype(jnp.bfloat16)
@@ -211,13 +212,11 @@
             ],
             axis=0,
         )
-        weights_f = jnp.exp(scores - jnp.max(scores, axis=1, keepdims=True))
-        weights_f = weights_f / jnp.sum(weights_f, axis=1, keepdims=True)
-        weights_b = weights_f.astype(jnp.bfloat16)
+        weights_b = jnp.exp(scores - jnp.max(scores, axis=1, keepdims=True)).astype(jnp.bfloat16)
         for span in range(CH_DEV):
-            result = mxu(
-                weights_b[span * SPAN : (span + 1) * SPAN], span_pairs_of(span, width + col), NN
-            )
+            vals = jnp.concatenate([span_pairs_of(span, width + col), ones], axis=1)
+            result = mxu(weights_b[span * SPAN : (span + 1) * SPAN], vals, NN)
+            result = result[:, :HEAD_DIM] / result[:, HEAD_DIM:]
             if span == 0:
                 result = jnp.where(first[0] == 0, jnp.zeros_like(result), result)
             out[span * SPAN : (span + 1) * SPAN, col : col + HEAD_DIM] = result
@@ -273,8 +272,8 @@
     def seq_cross(array):
         return lax.ppermute(array, "seq", [(i, i ^ 2) for i in range(seq_size)])
 
-    def seq_ring(array):
-        return lax.ppermute(array, "seq", [(i, (i + 2) % seq_size) for i in range(seq_size)])
+    def seq_ring(array, way):
+        return lax.ppermute(array, "seq", [(i, (i + 2 * way) % seq_size) for i in range(seq_size)])
 
     def next_seq(array):
         return lax.ppermute(array, "seq", [(i, i + 1) for i in range(seq_size - 1)])
@@ -312,13 +311,17 @@
     )(here, lane_here, host, index, database, query_t, enc_out, up_t, ffn_down, kv_t)
 
     attention_far = [lane_step(attention_half, n + 1) for n in range(far_lanes)]
-    packet = next_seq(packet)
-    database_ring = [database_half]
-    for _ in range(blocks - 1):
-        database_ring.append(seq_ring(database_ring[-1]))
+    database_far = [database_half] + [None] * (blocks - 1)
+    for step in range(1, blocks // 2 + 1):
+        database_far[step] = seq_ring(database_far[step - 1], 1)
+        if blocks - step > blocks // 2:
+            database_far[blocks - step] = seq_ring(database_far[(blocks - step + 1) % blocks], -1)
     database_blocks = []
-    for block in database_ring:
+    for block in database_far:
         database_blocks += [block, seq_swap(block)]
+    packet = next_seq(after(packet, database_blocks[1], database_far[1]))
+    ffn_half = after(ffn_half, *attention_far)
+    ffn_far = [lane_step(ffn_half, n + 1) for n in range(far_lanes)]
 
     dec_width = dec_kv.shape[2]
     kv_weights = dec_kv.reshape(width, 2 * dec_width)
@@ -327,21 +330,16 @@
     before = before[:, :1] * DIGIT + before[:, 1:]
     kv_t = jnp.concatenate([packet[:, :kv_rows], kv_t[:, :, :kept]], axis=2)
 
-    near_step = database_ring[min(1, blocks - 1)]
-    ffn_far = [
-        lane_step(after(ffn_half, near_step, database_blocks[1], *attention_far), n + 1)
-        for n in range(far_lanes)
-    ]
-    attention_core = tuple(core_swap(a) for a in after((query_t, enc_out), database_ring[-1]))
-    attention_cross = [seq_swap(after(a, *database_blocks)) for a in attention_far]
+    attention_core = tuple(core_swap(a) for a in after((query_t, enc_out), database_blocks[3]))
+    attention_cross = [seq_swap(after(a, database_blocks[-1])) for a in attention_far]
     kv_t, kv_weights, enc_gain, ffn_gain, before, *_ = lax.optimization_barrier(
-        (kv_t, kv_weights, enc_gain, ffn_gain, before, database_blocks[min(3, 2 * blocks - 1)])
+        (kv_t, kv_weights, enc_gain, ffn_gain, before, database_blocks[3], database_blocks[-1])
     )
     kv_core = core_swap(kv_t)
-    kv_send = after(kv_t, *ffn_far, *database_blocks)
+    kv_send = after(kv_t, *ffn_far)
     kv_far = [lane_step(kv_send, n + 1) for n in range(far_lanes)]
     ffn_cross = [seq_cross(a) for a in ffn_far]
-    up_send, down_send = after((up_t, ffn_down), *attention_cross)
+    up_send, down_send = after((up_t, ffn_down), database_blocks[3])
     ffn_core = (core_swap(up_send), core_swap(down_send))
 
     gemm = 2 * rows * width * width

time: 79.1 us -> 81.9 us (1.035)
  starting transfers between devices: 22.1 us -> 26.7 us
  waiting for transfers between devices: 21.6 us -> 20 us
    ppermute x3, waiting for transfers between devices: 12.4 us -> 0.01 us  [seq_ring(): lax.ppermute(array, 'seq', [(i, (i + 2 * way) % seq_size) for i in range(...]
    ppermute x5, waiting for transfers between devices: 6.11 us -> 11.8 us  [seq_swap(): return lax.ppermute(array, 'seq', [(i, i ^ 1) for i in range(seq_size)])]
    ppermute x3, starting transfers between devices: 1.58 us -> 6.35 us  [seq_ring(): lax.ppermute(array, 'seq', [(i, (i + 2 * way) % seq_size) for i in range(...]
    ppermute x3, waiting for transfers between devices: 0.37 us -> 4.19 us  [lane_step(): lax.ppermute(array, 'mp', [(i, (i + 2 * step) % lanes) for i in range(lan...]
    ppermute x1, waiting for transfers between devices: 0.06 us -> 1.5 us  [seq_cross(): return lax.ppermute(array, 'seq', [(i, i ^ 2) for i in range(seq_size)])]
  transfers between devices with their start and end apart: 24 -> 24, of which waited for: 11 -> 7; matrix products, arithmetic and copies ran while one was open for 1% -> 1% of each run, Pallas kernels for 25% -> 24%
where the time goes in v4:
time: 81.9 us; the launch traced here: 81.7 us
  Pallas kernels  33.5 us (41%)
  starting transfers between devices  26.7 us (33%)
  waiting for transfers between devices  20 us (24%)
    ppermute x5, waiting for transfers between devices, seq_swap(): return lax.ppermute(array, 'seq', [(i, i ^ 1) for i in range(seq_size)])  11.8 us
    pallas_call x2, Pallas kernels, attention(): call(functools.partial(attention_kernel, len(kv), far), long_rows, 'svv'...  10.1 us
    ppermute x5, starting transfers between devices, seq_swap(): return lax.ppermute(array, 'seq', [(i, i ^ 1) for i in range(seq_size)])  7.38 us
    ppermute x3, starting transfers between devices, seq_ring(): lax.ppermute(array, 'seq', [(i, (i + 2 * way) % seq_size) for i in range(...  6.35 us
    ppermute x3, starting transfers between devices, lane_step(): lax.ppermute(array, 'mp', [(i, (i + 2 * step) % lanes) for i in range(lan...  5.34 us
    pallas_call x1, Pallas kernels, on_device(): call(functools.partial(ffn_kernel, False, True), (long_rows, short_rows),...  5.1 us
    pallas_call x1, Pallas kernels, on_device(): call(functools.partial(ffn_kernel, True, False), short_rows, 'vvv' + 'v'...  5.05 us
    pallas_call x1, Pallas kernels, on_device(): call(decoder_kernel, jax.ShapeDtypeStruct(dec_queries.shape, jnp.float32)...  5.01 us
  transfers between devices with their start and end apart: 24, of which 7 were waited for; matrix products, arithmetic and copies ran while one was open for 1% of the time, Pallas kernels for 24%

profile of v4, /device:TPU:0, one launch (start us, length us, event | category | flops | bytes accessed | tf_op | source)
XLA Modules:
  0.0 81.7 jit_solution(7251325324150257273)
XLA Ops:
  0.0 3.4 %prepare.1 = (bf16[2,64,896]{2,1,0:T(8,128)(2,1)}, bf16[224,896]{1,0:T(8,128)(2,1)}, bf16[448,896]{1,0:T(8,128)(2,1)}, bf16[2,240,64]{2,1,0:T(8,128)(2,1)}) custom-call(s32[1]{0:T(128)} %bitcast.here.seq_index.first, s32[1]{0:T(128)} %bitcast.1.lane_here, s32[2,8]{1,0:T(2,128)} %bitcast.18, s32[2,8]{1,0:T(2,128)} %bitcast.20, f32[2,128,896]{2,1,0:T(8,128)} %database.1, ...), custom_call_target="tpu_custom_call" | custom-call | flops 917504 | bytes 8000000 | tf_op jit(solution)/shard_map/prepare/pallas_call | solution.py:294
  3.5 3.0 %collective-permute-start.11 = (bf16[224,896]{1,0:T(8,128)(2,1)}, bf16[224,896]{1,0:T(8,128)(2,1)S(1)}, u32[]{:S(2)}, u32[]{:S(2)}) collective-permute-start(bf16[224,896]{1,0:T(8,128)(2,1)} %get-tuple-element.39), channel_id=1, source_target_pairs={{0,2},{1,3},{2,0},{3,1},{4,6},{5,7},{6,4},{7,5},{8,10},{9,11},{10,... | collective-permute-start | bytes 1204232 | tf_op jit(solution)/shard_map/ppermute | solution.py:267
  6.5 1.6 %collective-permute-start.1 = (bf16[2,64,896]{2,1,0:T(8,128)(2,1)}, bf16[2,64,896]{2,1,0:T(8,128)(2,1)S(1)}, u32[]{:S(2)}, u32[]{:S(2)}) collective-permute-start(bf16[2,64,896]{2,1,0:T(8,128)(2,1)} %get-tuple-element.29.refs_0_), channel_id=1, source_target_pairs={{0,8},{4,12},{8,16},{12,20},{16,24},{20,28},{24,0},{28,4},{1,9},{5... | collective-permute-start | bytes 688136 | tf_op jit(solution)/shard_map/ppermute | solution.py:276
  8.1 1.5 %collective-permute-start = (bf16[2,64,896]{2,1,0:T(8,128)(2,1)}, bf16[2,64,896]{2,1,0:T(8,128)(2,1)S(1)}, u32[]{:S(2)}, u32[]{:S(2)}) collective-permute-start(bf16[2,64,896]{2,1,0:T(8,128)(2,1)} %get-tuple-element.29.refs_0_), channel_id=1, source_target_pairs={{0,4},{4,0},{8,12},{12,8},{16,20},{20,16},{24,28},{28,24},{1,5},{5... | collective-permute-start | bytes 688136 | tf_op jit(solution)/shard_map/ppermute | solution.py:270
  9.6 2.2 %collective-permute-start.4 = (bf16[2,64,896]{2,1,0:T(8,128)(2,1)}, bf16[2,64,896]{2,1,0:T(8,128)(2,1)S(1)}, u32[]{:S(2)}, u32[]{:S(2)}) collective-permute-start(bf16[2,64,896]{2,1,0:T(8,128)(2,1)} %get-tuple-element.29.refs_0_), channel_id=1, source_target_pairs={{0,24},{4,28},{8,0},{12,4},{16,8},{20,12},{24,16},{28,20},{1,25},{... | collective-permute-start | bytes 688136 | tf_op jit(solution)/shard_map/ppermute | solution.py:276
  11.8 4.2 %collective-permute-done.11.refs_0_ = bf16[224,896]{1,0:T(8,128)(2,1)S(1)} collective-permute-done((bf16[224,896]{1,0:T(8,128)(2,1)}, bf16[224,896]{1,0:T(8,128)(2,1)S(1)}, u32[]{:S(2)}, u32[]{:S(2)}) %collective-permute-start.11) | collective-permute-done | bytes 401440 | tf_op jit(solution)/shard_map/ppermute | solution.py:267
  16.0 1.7 %collective-permute-start.15 = (bf16[448,896]{1,0:T(8,128)(2,1)}, bf16[448,896]{1,0:T(8,128)(2,1)S(1)}, u32[]{:S(2)}, u32[]{:S(2)}) collective-permute-start(bf16[448,896]{1,0:T(8,128)(2,1)} %get-tuple-element.42), channel_id=1, source_target_pairs={{0,2},{1,3},{2,0},{3,1},{4,6},{5,7},{6,4},{7,5},{8,10},{9,11},{10,... | collective-permute-start | bytes 2408456 | tf_op jit(solution)/shard_map/ppermute | solution.py:267
  17.7 3.4 %collective-permute-start.2 = (bf16[2,240,64]{2,1,0:T(8,128)(2,1)}, bf16[2,240,64]{2,1,0:T(8,128)(2,1)S(1)}, u32[]{:S(2)}, u32[]{:S(2)}) collective-permute-start(bf16[2,240,64]{2,1,0:T(8,128)(2,1)} %get-tuple-element.30), channel_id=1, source_target_pairs={{0,4},{4,8},{8,12},{12,16},{16,20},{20,24},{24,28},{1,5},{5,9},{9,... | collective-permute-start | bytes 184328 | tf_op jit(solution)/shard_map/ppermute | solution.py:279
  21.2 0.5 copy.13
  21.9 1.6 %collective-permute-start.3 = (bf16[2,64,896]{2,1,0:T(8,128)(2,1)S(1)}, bf16[2,64,896]{2,1,0:T(8,128)(2,1)S(1)}, u32[]{:S(2)}, u32[]{:S(2)}) collective-permute-start(bf16[2,64,896]{2,1,0:T(8,128)(2,1)S(1)} %collective-permute-done.1.refs_2_), channel_id=1, source_target_pairs={{0,4},{4,0},{8,12},{12,8},{16,20},{20,16},{24,28},{28,24},{1,5},{5... | collective-permute-start | bytes 688136 | tf_op jit(solution)/shard_map/ppermute | solution.py:270
  23.5 2.5 %collective-permute-start.6 = (bf16[2,64,896]{2,1,0:T(8,128)(2,1)S(1)}, bf16[2,64,896]{2,1,0:T(8,128)(2,1)S(1)}, u32[]{:S(2)}, u32[]{:S(2)}) collective-permute-start(bf16[2,64,896]{2,1,0:T(8,128)(2,1)S(1)} %collective-permute-done.1.refs_2_), channel_id=1, source_target_pairs={{0,8},{4,12},{8,16},{12,20},{16,24},{20,28},{24,0},{28,4},{1,9},{5... | collective-permute-start | bytes 688136 | tf_op jit(solution)/shard_map/ppermute | solution.py:276
  26.5 3.8 %collective-permute-done.3.refs_3_ = bf16[2,64,896]{2,1,0:T(8,128)(2,1)S(1)} collective-permute-done((bf16[2,64,896]{2,1,0:T(8,128)(2,1)S(1)}, bf16[2,64,896]{2,1,0:T(8,128)(2,1)S(1)}, u32[]{:S(2)}, u32[]{:S(2)}) %collective-permute-start.3) | collective-permute-done | bytes 229408 | tf_op jit(solution)/shard_map/ppermute | solution.py:270
  30.4 2.7 %collective-permute-done.5.refs_7_ = bf16[2,64,896]{2,1,0:T(8,128)(2,1)S(1)} collective-permute-done((bf16[2,64,896]{2,1,0:T(8,128)(2,1)S(1)}, bf16[2,64,896]{2,1,0:T(8,128)(2,1)S(1)}, u32[]{:S(2)}, u32[]{:S(2)}) %collective-permute-start.5) | collective-permute-done | bytes 229408 | tf_op jit(solution)/shard_map/ppermute | solution.py:270
  33.1 0.5 collective-permute-start.8
  33.6 2.5 %collective-permute-start.7 = (bf16[2,64,896]{2,1,0:T(8,128)(2,1)S(1)}, bf16[2,64,896]{2,1,0:T(8,128)(2,1)S(1)}, u32[]{:S(2)}, u32[]{:S(2)}) collective-permute-start(bf16[2,64,896]{2,1,0:T(8,128)(2,1)S(1)} %collective-permute-done.6.refs_4_), channel_id=1, source_target_pairs={{0,4},{4,0},{8,12},{12,8},{16,20},{20,16},{24,28},{28,24},{1,5},{5... | collective-permute-start | bytes 688136 | tf_op jit(solution)/shard_map/ppermute | solution.py:270
  36.1 0.6 collective-permute-start.16
  36.7 5.3 %collective-permute-done.7.refs_5_ = bf16[2,64,896]{2,1,0:T(8,128)(2,1)S(1)} collective-permute-done((bf16[2,64,896]{2,1,0:T(8,128)(2,1)S(1)}, bf16[2,64,896]{2,1,0:T(8,128)(2,1)S(1)}, u32[]{:S(2)}, u32[]{:S(2)}) %collective-permute-start.7) | collective-permute-done | bytes 229408 | tf_op jit(solution)/shard_map/ppermute | solution.py:270
  42.0 1.7 %collective-permute-start.12 = (bf16[224,896]{1,0:T(8,128)(2,1)S(1)}, bf16[224,896]{1,0:T(8,128)(2,1)S(1)}, u32[]{:S(2)}, u32[]{:S(2)}) collective-permute-start(bf16[224,896]{1,0:T(8,128)(2,1)S(1)} %collective-permute-done.11.refs_0_), channel_id=1, source_target_pairs={{0,4},{4,0},{8,12},{12,8},{16,20},{20,16},{24,28},{28,24},{1,5},{5... | collective-permute-start | bytes 1204232 | tf_op jit(solution)/shard_map/ppermute | solution.py:270
  43.7 1.6 %collective-permute-start.21 = (bf16[448,896]{1,0:T(8,128)(2,1)S(1)}, bf16[448,896]{1,0:T(8,128)(2,1)S(1)}, u32[]{:S(2)}, u32[]{:S(2)}) collective-permute-start(bf16[448,896]{1,0:T(8,128)(2,1)S(1)} %collective-permute-done.15.refs_1_), channel_id=1, source_target_pairs={{0,8},{4,12},{8,0},{12,4},{16,24},{20,28},{24,16},{28,20},{1,9},{5... | collective-permute-start | bytes 2408456 | tf_op jit(solution)/shard_map/ppermute | solution.py:273
  45.3 2.5 %neighbour_rows.1 = (bf16[1024,896]{1,0:T(8,128)(2,1)S(1)}, bf16[1024,896]{1,0:T(8,128)(2,1)S(1)}) custom-call(s32[1]{0:T(128)} %bitcast.here.seq_index.first, s32[2,8]{1,0:T(2,128)S(1)} %bitcast.19, s32[2,8]{1,0:T(2,128)S(1)} %bitcast.21, s32[2,1]{1,0:T(2,128)S(1)} %slice_add_fusion.before, f32[1,896]{1,0:T(1,128)S(1)} %reshape.20.gain, ...), custom_call_target="tpu_custom_call" | custom-call | flops 9175040 | bytes 8000000 | tf_op jit(solution)/shard_map/neighbour_rows/pallas_call | solution.py:348
  47.9 5.0 %encoder_attention.2.before = f32[1024,896]{1,0:T(8,128)S(1)} custom-call(s32[1]{0:T(128)} %bitcast.here.seq_index.first, bf16[1024,896]{1,0:T(8,128)(2,1)S(1)} %get-tuple-element.34.before, bf16[1024,896]{1,0:T(8,128)(2,1)S(1)} %get-tuple-element.35.normed_in, bf16[224,896]{1,0:T(8,128)(2,1)S(1)} %bitcast.14, bf16[224,896]{1,0:T(8,128)(2,1)S(1)} %copy-done.1, ...), custom_call_target="tpu_custom_call" | custom-call | flops 1644167168 | bytes 8000000 | tf_op jit(solution)/shard_map/encoder_attention/pallas_call | solution.py:358
  53.0 0.5 collective-permute-start.17
  53.6 0.4 collective-permute-start.18
  54.1 1.4 %collective-permute-done.14.refs_3_ = bf16[224,896]{1,0:T(8,128)(2,1)S(1)} collective-permute-done((bf16[224,896]{1,0:T(8,128)(2,1)S(1)}, bf16[224,896]{1,0:T(8,128)(2,1)S(1)}, u32[]{:S(2)}, u32[]{:S(2)}) %collective-permute-start.14) | collective-permute-done | bytes 401440 | tf_op jit(solution)/shard_map/ppermute | solution.py:264
  55.9 5.0 %encoder_attention.3.before = f32[1024,896]{1,0:T(8,128)S(1)} custom-call(s32[1]{0:T(128)} %bitcast.here.seq_index.first, f32[1024,896]{1,0:T(8,128)S(1)} %encoder_attention.2.before, bf16[1024,896]{1,0:T(8,128)(2,1)S(1)} %get-tuple-element.35.normed_in, bf16[224,896]{1,0:T(8,128)(2,1)S(1)} %collective-permute-done.11.refs_0_, ...), custom_call_target="tpu_custom_call" | custom-call | flops 1644167168 | bytes 8000000 | tf_op jit(solution)/shard_map/encoder_attention/pallas_call | solution.py:358
  60.9 1.5 %collective-permute-done.21.refs_3_ = bf16[448,896]{1,0:T(8,128)(2,1)S(1)} collective-permute-done((bf16[448,896]{1,0:T(8,128)(2,1)S(1)}, bf16[448,896]{1,0:T(8,128)(2,1)S(1)}, u32[]{:S(2)}, u32[]{:S(2)}) %collective-permute-start.21) | collective-permute-done | bytes 802848 | tf_op jit(solution)/shard_map/ppermute | solution.py:273
  62.5 5.1 %encoder_ffn_near.1 = (f32[1024,896]{1,0:T(8,128)S(1)}, bf16[1024,896]{1,0:T(8,128)(2,1)S(1)}) custom-call(f32[1,896]{1,0:T(1,128)S(1)} %reshape.21.gain, f32[1024,896]{1,0:T(8,128)S(1)} %encoder_attention.3.before, bf16[448,896]{1,0:T(8,128)(2,1)S(1)} %bitcast.17, bf16[448,896]{1,0:T(8,128)(2,1)S(1)} %copy-done.3, ...), custom_call_target="tpu_custom_call" | custom-call | flops 3288334336 | bytes 8000000 | tf_op jit(solution)/shard_map/encoder_ffn_near/pallas_call | solution.py:376
  67.6 5.0 %encoder_ffn_far.1.encoded = bf16[1024,896]{1,0:T(8,128)(2,1)S(1)} custom-call(f32[1,896]{1,0:T(1,128)S(1)} %reshape.21.gain, f32[1024,896]{1,0:T(8,128)S(1)} %get-tuple-element.47.before, bf16[1024,896]{1,0:T(8,128)(2,1)S(1)} %get-tuple-element.48.refs_0_, bf16[448,896]{1,0:T(8,128)(2,1)S(1)} %collective-permute-done.15.refs_1_, ...), custom_call_target="tpu_custom_call" | custom-call | flops 3288334336 | bytes 8000000 | tf_op jit(solution)/shard_map/encoder_ffn_far/pallas_call | solution.py:386
  72.7 0.6 collective-permute-start.23
  73.2 2.3 %decoder_pairs.1.own_pairs = bf16[1024,1024]{1,0:T(8,128)(2,1)S(1)} custom-call(bf16[1024,896]{1,0:T(8,128)(2,1)S(1)} %encoder_ffn_far.1.encoded, bf16[896,1024]{1,0:T(8,128)(2,1)S(1)} %bitcast.10), custom_call_target="tpu_custom_call" | custom-call | flops 1879048192 | bytes 8000000 | tf_op jit(solution)/shard_map/decoder_pairs/pallas_call | solution.py:399
  75.6 1.1 %collective-permute-done.23.other = bf16[1024,896]{1,0:T(8,128)(2,1)S(1)} collective-permute-done((bf16[1024,896]{1,0:T(8,128)(2,1)S(1)}, bf16[1024,896]{1,0:T(8,128)(2,1)S(1)}, u32[]{:S(2)}, u32[]{:S(2)}) %collective-permute-start.23) | collective-permute-done | bytes 1835040 | tf_op jit(solution)/shard_map/ppermute | solution.py:264
  76.7 5.0 %decoder_attention.1 = f32[512,512]{1,0:T(8,128)} custom-call(s32[1]{0:T(128)} %bitcast.here.seq_index.first, bf16[1024,1024]{1,0:T(8,128)(2,1)S(1)} %decoder_pairs.1.own_pairs, bf16[1024,896]{1,0:T(8,128)(2,1)S(1)} %collective-permute-done.23.other, bf16[896,1024]{1,0:T(8,128)(2,1)S(1)} %bitcast.11, bf16[512,512]{1,0:T(8,128)(2,1)S(1)} %copy-done.4), custom_call_target="tpu_custom_call" | custom-call | flops 1879048192 | bytes 8000000 | tf_op jit(solution)/shard_map/decoder_attention/pallas_call | solution.py:407
  (55 shorter events, 1.4 us)
Async XLA Ops:
  0.0 21.1 %copy-start.8 = (bf16[896,2,512]{2,1,0:T(2,128)(2,1)S(1)}, bf16[896,2,512]{2,1,0:T(2,128)(2,1)}, u32[]{:S(2)}) copy-start(bf16[896,2,512]{2,1,0:T(2,128)(2,1)} %param.23) | copy-start | bytes 5505028
  3.5 12.5 %collective-permute-start.11 = (bf16[224,896]{1,0:T(8,128)(2,1)}, bf16[224,896]{1,0:T(8,128)(2,1)S(1)}, u32[]{:S(2)}, u32[]{:S(2)}) collective-permute-start(bf16[224,896]{1,0:T(8,128)(2,1)} %get-tuple-element.39), channel_id=1, source_target_pairs={{0,2},{1,3},{2,0},{3,1},{4,6},{5,7},{6,4},{7,5},{8,10},{9,11},{10,... | collective-permute-start | bytes 1204232 | tf_op jit(solution)/shard_map/ppermute | solution.py:267
  6.5 11.2 %collective-permute-start.1 = (bf16[2,64,896]{2,1,0:T(8,128)(2,1)}, bf16[2,64,896]{2,1,0:T(8,128)(2,1)S(1)}, u32[]{:S(2)}, u32[]{:S(2)}) collective-permute-start(bf16[2,64,896]{2,1,0:T(8,128)(2,1)} %get-tuple-element.29.refs_0_), channel_id=1, source_target_pairs={{0,8},{4,12},{8,16},{12,20},{16,24},{20,28},{24,0},{28,4},{1,9},{5... | collective-permute-start | bytes 688136 | tf_op jit(solution)/shard_map/ppermute | solution.py:276
  8.1 9.7 %collective-permute-start = (bf16[2,64,896]{2,1,0:T(8,128)(2,1)}, bf16[2,64,896]{2,1,0:T(8,128)(2,1)S(1)}, u32[]{:S(2)}, u32[]{:S(2)}) collective-permute-start(bf16[2,64,896]{2,1,0:T(8,128)(2,1)} %get-tuple-element.29.refs_0_), channel_id=1, source_target_pairs={{0,4},{4,0},{8,12},{12,8},{16,20},{20,16},{24,28},{28,24},{1,5},{5... | collective-permute-start | bytes 688136 | tf_op jit(solution)/shard_map/ppermute | solution.py:270
  9.6 16.4 %collective-permute-start.4 = (bf16[2,64,896]{2,1,0:T(8,128)(2,1)}, bf16[2,64,896]{2,1,0:T(8,128)(2,1)S(1)}, u32[]{:S(2)}, u32[]{:S(2)}) collective-permute-start(bf16[2,64,896]{2,1,0:T(8,128)(2,1)} %get-tuple-element.29.refs_0_), channel_id=1, source_target_pairs={{0,24},{4,28},{8,0},{12,4},{16,8},{20,12},{24,16},{28,20},{1,25},{... | collective-permute-start | bytes 688136 | tf_op jit(solution)/shard_map/ppermute | solution.py:276
  16.0 20.1 %collective-permute-start.15 = (bf16[448,896]{1,0:T(8,128)(2,1)}, bf16[448,896]{1,0:T(8,128)(2,1)S(1)}, u32[]{:S(2)}, u32[]{:S(2)}) collective-permute-start(bf16[448,896]{1,0:T(8,128)(2,1)} %get-tuple-element.42), channel_id=1, source_target_pairs={{0,2},{1,3},{2,0},{3,1},{4,6},{5,7},{6,4},{7,5},{8,10},{9,11},{10,... | collective-permute-start | bytes 2408456 | tf_op jit(solution)/shard_map/ppermute | solution.py:267
  17.7 8.3 %collective-permute-start.2 = (bf16[2,240,64]{2,1,0:T(8,128)(2,1)}, bf16[2,240,64]{2,1,0:T(8,128)(2,1)S(1)}, u32[]{:S(2)}, u32[]{:S(2)}) collective-permute-start(bf16[2,240,64]{2,1,0:T(8,128)(2,1)} %get-tuple-element.30), channel_id=1, source_target_pairs={{0,4},{4,8},{8,12},{12,16},{16,20},{20,24},{24,28},{1,5},{5,9},{9,... | collective-permute-start | bytes 184328 | tf_op jit(solution)/shard_map/ppermute | solution.py:279
  21.2 11.9 %copy-start = (bf16[896,224]{0,1:T(8,128)(2,1)S(1)}, bf16[896,224]{0,1:T(8,128)(2,1)}, u32[]{:S(2)}) copy-start(bf16[896,224]{0,1:T(8,128)(2,1)} %param.18) | copy-start | bytes 1204228
  21.2 14.9 %copy-start.1 = (bf16[224,896]{1,0:T(8,128)(2,1)S(1)}, bf16[224,896]{1,0:T(8,128)(2,1)}, u32[]{:S(2)}) copy-start(bf16[224,896]{1,0:T(8,128)(2,1)} %refs_1_.2) | copy-start | bytes 1204228
  21.2 24.1 %copy-start.5 = (bf16[2,64,896]{2,1,0:T(8,128)(2,1)S(1)}, bf16[2,64,896]{2,1,0:T(8,128)(2,1)}, u32[]{:S(2)}) copy-start(bf16[2,64,896]{2,1,0:T(8,128)(2,1)} %get-tuple-element.29.refs_0_) | copy-start | bytes 688132
  21.2 24.1 %copy-start.6 = (s32[8,2]{0,1:T(2,128)S(1)}, s32[8,2]{0,1:T(2,128)}, u32[]{:S(2)}) copy-start(s32[8,2]{0,1:T(2,128)} %param.16) | copy-start | bytes 196
  21.2 24.1 %copy-start.7 = (s32[8,2]{0,1:T(2,128)S(1)}, s32[8,2]{0,1:T(2,128)}, u32[]{:S(2)}) copy-start(s32[8,2]{0,1:T(2,128)} %param.15) | copy-start | bytes 196
  21.9 8.5 %collective-permute-start.3 = (bf16[2,64,896]{2,1,0:T(8,128)(2,1)S(1)}, bf16[2,64,896]{2,1,0:T(8,128)(2,1)S(1)}, u32[]{:S(2)}, u32[]{:S(2)}) collective-permute-start(bf16[2,64,896]{2,1,0:T(8,128)(2,1)S(1)} %collective-permute-done.1.refs_2_), channel_id=1, source_target_pairs={{0,4},{4,0},{8,12},{12,8},{16,20},{20,16},{24,28},{28,24},{1,5},{5... | collective-permute-start | bytes 688136 | tf_op jit(solution)/shard_map/ppermute | solution.py:270
  23.5 10.2 %collective-permute-start.6 = (bf16[2,64,896]{2,1,0:T(8,128)(2,1)S(1)}, bf16[2,64,896]{2,1,0:T(8,128)(2,1)S(1)}, u32[]{:S(2)}, u32[]{:S(2)}) collective-permute-start(bf16[2,64,896]{2,1,0:T(8,128)(2,1)S(1)} %collective-permute-done.1.refs_2_), channel_id=1, source_target_pairs={{0,8},{4,12},{8,16},{12,20},{16,24},{20,28},{24,0},{28,4},{1,9},{5... | collective-permute-start | bytes 688136 | tf_op jit(solution)/shard_map/ppermute | solution.py:276
  26.0 7.1 %collective-permute-start.5 = (bf16[2,64,896]{2,1,0:T(8,128)(2,1)S(1)}, bf16[2,64,896]{2,1,0:T(8,128)(2,1)S(1)}, u32[]{:S(2)}, u32[]{:S(2)}) collective-permute-start(bf16[2,64,896]{2,1,0:T(8,128)(2,1)S(1)} %collective-permute-done.4.refs_6_), channel_id=1, source_target_pairs={{0,4},{4,0},{8,12},{12,8},{16,20},{20,16},{24,28},{28,24},{1,5},{5... | collective-permute-start | bytes 688136 | tf_op jit(solution)/shard_map/ppermute | solution.py:270
  33.1 14.8 %collective-permute-start.10 = (bf16[2,224,512]{2,1,0:T(8,128)(2,1)S(1)}, bf16[2,224,512]{2,1,0:T(8,128)(2,1)S(1)}, u32[]{:S(2)}, u32[]{:S(2)}) collective-permute-start(bf16[2,224,512]{2,1,0:T(8,128)(2,1)S(1)} %pad_maximum_fusion.refs_4_), channel_id=1, source_target_pairs={{0,1},{1,0},{2,3},{3,2},{4,5},{5,4},{6,7},{7,6},{8,9},{9,8},{10,11... | collective-permute-start | bytes 1376264 | tf_op jit(solution)/shard_map/ppermute | solution.py:264
  33.1 10.6 %collective-permute-start.8 = (bf16[224,896]{1,0:T(8,128)(2,1)S(1)}, bf16[224,896]{1,0:T(8,128)(2,1)S(1)}, u32[]{:S(2)}, u32[]{:S(2)}) collective-permute-start(bf16[224,896]{1,0:T(8,128)(2,1)S(1)} %bitcast.13), channel_id=1, source_target_pairs={{0,1},{1,0},{2,3},{3,2},{4,5},{5,4},{6,7},{7,6},{8,9},{9,8},{10,11... | collective-permute-start | bytes 1204232 | tf_op jit(solution)/shard_map/ppermute | solution.py:264
  33.6 8.3 %collective-permute-start.7 = (bf16[2,64,896]{2,1,0:T(8,128)(2,1)S(1)}, bf16[2,64,896]{2,1,0:T(8,128)(2,1)S(1)}, u32[]{:S(2)}, u32[]{:S(2)}) collective-permute-start(bf16[2,64,896]{2,1,0:T(8,128)(2,1)S(1)} %collective-permute-done.6.refs_4_), channel_id=1, source_target_pairs={{0,4},{4,0},{8,12},{12,8},{16,20},{20,16},{24,28},{28,24},{1,5},{5... | collective-permute-start | bytes 688136 | tf_op jit(solution)/shard_map/ppermute | solution.py:270
  36.1 11.7 %collective-permute-start.9 = (bf16[224,896]{1,0:T(8,128)(2,1)S(1)}, bf16[224,896]{1,0:T(8,128)(2,1)S(1)}, u32[]{:S(2)}, u32[]{:S(2)}) collective-permute-start(bf16[224,896]{1,0:T(8,128)(2,1)S(1)} %copy-done.1), channel_id=1, source_target_pairs={{0,1},{1,0},{2,3},{3,2},{4,5},{5,4},{6,7},{7,6},{8,9},{9,8},{10,11... | collective-permute-start | bytes 1204232 | tf_op jit(solution)/shard_map/ppermute | solution.py:264
  36.1 16.8 %collective-permute-start.16 = (bf16[2,224,512]{2,1,0:T(8,128)(2,1)S(1)}, bf16[2,224,512]{2,1,0:T(8,128)(2,1)S(1)}, u32[]{:S(2)}, u32[]{:S(2)}) collective-permute-start(bf16[2,224,512]{2,1,0:T(8,128)(2,1)S(1)} %pad_maximum_fusion.refs_4_), channel_id=1, source_target_pairs={{0,2},{1,3},{2,0},{3,1},{4,6},{5,7},{6,4},{7,5},{8,10},{9,11},{10,... | collective-permute-start | bytes 1376264 | tf_op jit(solution)/shard_map/ppermute | solution.py:267
  42.0 11.5 %collective-permute-start.12 = (bf16[224,896]{1,0:T(8,128)(2,1)S(1)}, bf16[224,896]{1,0:T(8,128)(2,1)S(1)}, u32[]{:S(2)}, u32[]{:S(2)}) collective-permute-start(bf16[224,896]{1,0:T(8,128)(2,1)S(1)} %collective-permute-done.11.refs_0_), channel_id=1, source_target_pairs={{0,4},{4,0},{8,12},{12,8},{16,20},{20,16},{24,28},{28,24},{1,5},{5... | collective-permute-start | bytes 1204232 | tf_op jit(solution)/shard_map/ppermute | solution.py:270
  43.7 18.7 %collective-permute-start.21 = (bf16[448,896]{1,0:T(8,128)(2,1)S(1)}, bf16[448,896]{1,0:T(8,128)(2,1)S(1)}, u32[]{:S(2)}, u32[]{:S(2)}) collective-permute-start(bf16[448,896]{1,0:T(8,128)(2,1)S(1)} %collective-permute-done.15.refs_1_), channel_id=1, source_target_pairs={{0,8},{4,12},{8,0},{12,4},{16,24},{20,28},{24,16},{28,20},{1,9},{5... | collective-permute-start | bytes 2408456 | tf_op jit(solution)/shard_map/ppermute | solution.py:273
  47.8 6.2 %collective-permute-start.13 = (bf16[224,896]{1,0:T(8,128)(2,1)S(1)}, bf16[224,896]{1,0:T(8,128)(2,1)S(1)}, u32[]{:S(2)}, u32[]{:S(2)}) collective-permute-start(bf16[224,896]{1,0:T(8,128)(2,1)S(1)} %collective-permute-done.11.refs_0_), channel_id=1, source_target_pairs={{0,1},{1,0},{2,3},{3,2},{4,5},{5,4},{6,7},{7,6},{8,9},{9,8},{10,11... | collective-permute-start | bytes 1204232 | tf_op jit(solution)/shard_map/ppermute | solution.py:264
  47.9 5.7 %copy-start.2 = (bf16[896,448]{0,1:T(8,128)(2,1)S(1)}, bf16[896,448]{0,1:T(8,128)(2,1)}, u32[]{:S(2)}) copy-start(bf16[896,448]{0,1:T(8,128)(2,1)} %param.21) | copy-start | bytes 2408452
  47.9 6.1 %copy-start.3 = (bf16[448,896]{1,0:T(8,128)(2,1)S(1)}, bf16[448,896]{1,0:T(8,128)(2,1)}, u32[]{:S(2)}) copy-start(bf16[448,896]{1,0:T(8,128)(2,1)} %refs_1_.3) | copy-start | bytes 2408452
  53.0 2.9 %collective-permute-start.17 = (bf16[2,224,512]{2,1,0:T(8,128)(2,1)S(1)}, bf16[2,224,512]{2,1,0:T(8,128)(2,1)S(1)}, u32[]{:S(2)}, u32[]{:S(2)}) collective-permute-start(bf16[2,224,512]{2,1,0:T(8,128)(2,1)S(1)} %collective-permute-done.16.refs_4_), channel_id=1, source_target_pairs={{0,1},{1,0},{2,3},{3,2},{4,5},{5,4},{6,7},{7,6},{8,9},{9,8},{10,11... | collective-permute-start | bytes 1376264 | tf_op jit(solution)/shard_map/ppermute | solution.py:264
  53.5 2.0 %collective-permute-start.14 = (bf16[224,896]{1,0:T(8,128)(2,1)S(1)}, bf16[224,896]{1,0:T(8,128)(2,1)S(1)}, u32[]{:S(2)}, u32[]{:S(2)}) collective-permute-start(bf16[224,896]{1,0:T(8,128)(2,1)S(1)} %collective-permute-done.12.refs_1_), channel_id=1, source_target_pairs={{0,1},{1,0},{2,3},{3,2},{4,5},{5,4},{6,7},{7,6},{8,9},{9,8},{10,11... | collective-permute-start | bytes 1204232 | tf_op jit(solution)/shard_map/ppermute | solution.py:264
  53.6 8.9 %collective-permute-start.18 = (bf16[448,896]{1,0:T(8,128)(2,1)S(1)}, bf16[448,896]{1,0:T(8,128)(2,1)S(1)}, u32[]{:S(2)}, u32[]{:S(2)}) collective-permute-start(bf16[448,896]{1,0:T(8,128)(2,1)S(1)} %bitcast.16), channel_id=1, source_target_pairs={{0,1},{1,0},{2,3},{3,2},{4,5},{5,4},{6,7},{7,6},{8,9},{9,8},{10,11... | collective-permute-start | bytes 2408456 | tf_op jit(solution)/shard_map/ppermute | solution.py:264
  54.0 8.4 %collective-permute-start.19 = (bf16[448,896]{1,0:T(8,128)(2,1)S(1)}, bf16[448,896]{1,0:T(8,128)(2,1)S(1)}, u32[]{:S(2)}, u32[]{:S(2)}) collective-permute-start(bf16[448,896]{1,0:T(8,128)(2,1)S(1)} %copy-done.3), channel_id=1, source_target_pairs={{0,1},{1,0},{2,3},{3,2},{4,5},{5,4},{6,7},{7,6},{8,9},{9,8},{10,11... | collective-permute-start | bytes 2408456 | tf_op jit(solution)/shard_map/ppermute | solution.py:264
  55.5 12.0 %collective-permute-start.20 = (bf16[448,896]{1,0:T(8,128)(2,1)S(1)}, bf16[448,896]{1,0:T(8,128)(2,1)S(1)}, u32[]{:S(2)}, u32[]{:S(2)}) collective-permute-start(bf16[448,896]{1,0:T(8,128)(2,1)S(1)} %collective-permute-done.15.refs_1_), channel_id=1, source_target_pairs={{0,1},{1,0},{2,3},{3,2},{4,5},{5,4},{6,7},{7,6},{8,9},{9,8},{10,11... | collective-permute-start | bytes 2408456 | tf_op jit(solution)/shard_map/ppermute | solution.py:264
  62.4 5.1 %collective-permute-start.22 = (bf16[448,896]{1,0:T(8,128)(2,1)S(1)}, bf16[448,896]{1,0:T(8,128)(2,1)S(1)}, u32[]{:S(2)}, u32[]{:S(2)}) collective-permute-start(bf16[448,896]{1,0:T(8,128)(2,1)S(1)} %collective-permute-done.21.refs_3_), channel_id=1, source_target_pairs={{0,1},{1,0},{2,3},{3,2},{4,5},{5,4},{6,7},{7,6},{8,9},{9,8},{10,11... | collective-permute-start | bytes 2408456 | tf_op jit(solution)/shard_map/ppermute | solution.py:264
  72.7 4.0 %collective-permute-start.23 = (bf16[1024,896]{1,0:T(8,128)(2,1)S(1)}, bf16[1024,896]{1,0:T(8,128)(2,1)S(1)}, u32[]{:S(2)}, u32[]{:S(2)}) collective-permute-start(bf16[1024,896]{1,0:T(8,128)(2,1)S(1)} %encoder_ffn_far.1.encoded), channel_id=1, source_target_pairs={{0,1},{1,0},{2,3},{3,2},{4,5},{5,4},{6,7},{7,6},{8,9},{9,8},{10,11... | collective-permute-start | bytes 5505032 | tf_op jit(solution)/shard_map/ppermute | solution.py:264
  (4 other events, 10.3 us)

commit v5 on v4

--- a/solution.py
+++ b/solution.py
@@ -16,6 +16,23 @@
 HALVES = 2
 BLOCK = 512
 DIGIT = 128
+
+ORDER = {
+    "pk": ("x0",),
+    "xp": ("xn",),
+    "xa": ("xm",),
+    "ca": ("xn",),
+    "cf": ("xn",),
+    "keys": ("xp",),
+    "yk": ("yf", "xm",),
+    "cya": ("yf",),
+    "cyf": ("far",),
+    "cyk": ("near",),
+    "czf": ("far",),
+    "near": ("yf",),
+    "wk": ("ya",),
+    "gains": ("zn",),
+}
 
 NT = (((1,), (1,)), ((), ()))
 NN = (((1,), (0,)), ((), ()))
@@ -258,7 +275,6 @@
     half_rows = block_rows // HALVES
     rows = CH_DEV * NEIGH * half_rows
     blocks = seq_size // 2
-    far_lanes = lanes // 2 - 1
 
     def core_swap(array):
         return lax.ppermute(array, "mp", [(i, i ^ 1) for i in range(lanes)])
@@ -277,9 +293,6 @@
 
     def next_seq(array):
         return lax.ppermute(array, "seq", [(i, i + 1) for i in range(seq_size - 1)])
-
-    def after(array, *others):
-        return lax.optimization_barrier((array, *others))[0]
 
     query_t, up_t = enc_query.T, ffn_up.T
     kv_t = jnp.transpose(span_pairs, (1, 2, 0))
@@ -310,41 +323,71 @@
         ],
     )(here, lane_here, host, index, database, query_t, enc_out, up_t, ffn_down, kv_t)
 
-    attention_far = [lane_step(attention_half, n + 1) for n in range(far_lanes)]
-    database_far = [database_half] + [None] * (blocks - 1)
-    for step in range(1, blocks // 2 + 1):
-        database_far[step] = seq_ring(database_far[step - 1], 1)
-        if blocks - step > blocks // 2:
-            database_far[blocks - step] = seq_ring(database_far[(blocks - step + 1) % blocks], -1)
-    database_blocks = []
-    for block in database_far:
-        database_blocks += [block, seq_swap(block)]
-    packet = next_seq(after(packet, database_blocks[1], database_far[1]))
-    ffn_half = after(ffn_half, *attention_far)
-    ffn_far = [lane_step(ffn_half, n + 1) for n in range(far_lanes)]
-
     dec_width = dec_kv.shape[2]
-    kv_weights = dec_kv.reshape(width, 2 * dec_width)
+    middle, last = blocks // 2, blocks - 1
+    names = {"0": 0, "n": 1, "p": last, "m": middle}
+    short_name = {place: name for name, place in names.items()}
+    arrived = {}
+
+    def got(name):
+        if name not in arrived:
+            arrived[name] = makers[name]()
+        return arrived[name]
+
+    def ready(name, array):
+        others = [got(other) for other in ORDER.get(name, ())]
+        return lax.optimization_barrier((array, others))[0] if others else array
+
+    def database(place):
+        if place == 0:
+            return database_half
+        way = 1 if place <= middle else -1
+        source = database_at((place - way) % blocks)
+        return seq_ring(ready(f"z{short_name.get(place, place)}", source), way)
+
+    def database_at(place):
+        return got(f"z{short_name.get(place, place)}")
+
+    def swapped_at(place):
+        return got(f"x{short_name.get(place, place)}")
+
+    def received_keys():
+        return jnp.concatenate([got("pk")[:, :kv_rows], kv_t[:, :, :kept]], axis=2)
+
+    def both_cores(name, arrays):
+        return tuple(core_swap(a) for a in ready(name, arrays))
+
+    makers = {
+        "ya": lambda: lane_step(ready("ya", attention_half), 1),
+        "yf": lambda: lane_step(ready("yf", ffn_half), 1),
+        "yk": lambda: lane_step(ready("yk", got("keys")), 1),
+        "pk": lambda: next_seq(ready("pk", packet)),
+        "keys": lambda: ready("keys", received_keys()),
+        "xa": lambda: seq_swap(ready("xa", got("ya"))),
+        "zf": lambda: seq_cross(ready("zf", got("yf"))),
+        "ca": lambda: both_cores("ca", (query_t, enc_out)),
+        "cf": lambda: both_cores("cf", (up_t, ffn_down)),
+        "ck": lambda: core_swap(ready("ck", got("keys"))),
+        "cya": lambda: core_swap(ready("cya", got("ya"))),
+        "cyk": lambda: core_swap(ready("cyk", got("yk"))),
+        "cyf": lambda: core_swap(ready("cyf", got("yf"))),
+        "cxa": lambda: core_swap(ready("cxa", got("xa"))),
+        "czf": lambda: core_swap(ready("czf", got("zf"))),
+        "wk": lambda: ready("wk", dec_kv.reshape(width, 2 * dec_width)),
+    }
+    for place in range(blocks):
+        name = short_name.get(place, place)
+        makers[f"z{name}"] = functools.partial(database, place)
+        makers[f"x{name}"] = lambda place=place, name=name: seq_swap(ready(f"x{name}", database_at(place)))
     enc_gain, ffn_gain = enc_gain.reshape(1, width), ffn_gain.reshape(1, width)
-    before = packet[:, kv_rows : kv_rows + 2, 0].astype(jnp.int32)
-    before = before[:, :1] * DIGIT + before[:, 1:]
-    kv_t = jnp.concatenate([packet[:, :kv_rows], kv_t[:, :, :kept]], axis=2)
-
-    attention_core = tuple(core_swap(a) for a in after((query_t, enc_out), database_blocks[3]))
-    attention_cross = [seq_swap(after(a, database_blocks[-1])) for a in attention_far]
-    kv_t, kv_weights, enc_gain, ffn_gain, before, *_ = lax.optimization_barrier(
-        (kv_t, kv_weights, enc_gain, ffn_gain, before, database_blocks[3], database_blocks[-1])
-    )
-    kv_core = core_swap(kv_t)
-    kv_send = after(kv_t, *ffn_far)
-    kv_far = [lane_step(kv_send, n + 1) for n in range(far_lanes)]
-    ffn_cross = [seq_cross(a) for a in ffn_far]
-    up_send, down_send = after((up_t, ffn_down), database_blocks[3])
-    ffn_core = (core_swap(up_send), core_swap(down_send))
+    enc_gain, ffn_gain = ready("gains", (enc_gain, ffn_gain))
 
     gemm = 2 * rows * width * width
     long_rows = jax.ShapeDtypeStruct((rows, width), jnp.float32)
     short_rows = short((rows, width))
+    before = got("pk")[:, kv_rows : kv_rows + 2, 0].astype(jnp.int32)
+    before = before[:, :1] * DIGIT + before[:, 1:]
+    database_blocks = [a for place in range(blocks) for a in (database_at(place), swapped_at(place))]
     values, normed = call(
         functools.partial(gather_kernel, blocks),
         (short_rows, short_rows),
@@ -352,7 +395,7 @@
         "neighbour_rows",
         10 * rows * width,
         16 + (8 * blocks * database_half.size >> 20),
-    )(here, host, index, before, enc_gain, *database_blocks)
+    )(ready("gather", here), host, index, before, enc_gain, *database_blocks)
 
     def attention(so_far, weights, kv, far):
         return call(
@@ -364,15 +407,14 @@
             24,
         )(here, so_far, normed, *weights, *kv)
 
-    partial_rows = attention(values, (query_t, enc_out, *attention_core), (kv_t, kv_core), False)
-    far_weights, far_kv = [], []
-    kv_forward = after(tuple(kv_far), partial_rows)
-    for straight, crossed, kv, forward in zip(attention_far, attention_cross, kv_far, kv_forward):
-        far_weights += [straight, crossed, core_swap(straight), core_swap(crossed)]
-        far_kv += [kv, core_swap(forward)]
-    resid = attention(partial_rows, far_weights, far_kv, True)
-
-    near_units = (up_t, ffn_down, *ffn_core)
+    arrived["near"] = attention(
+        ready("near", values), (query_t, enc_out, *got("ca")), (got("keys"), got("ck")), False
+    )
+    far_weights = (got("ya"), got("xa"), got("cya"), got("cxa"))
+    resid = attention(got("near"), far_weights, (got("yk"), got("cyk")), True)
+    arrived["far"] = resid
+
+    near_units = (up_t, ffn_down, *got("cf"))
     partial_rows, normed = call(
         functools.partial(ffn_kernel, False, True),
         (long_rows, short_rows),
@@ -381,8 +423,8 @@
         2 * gemm,
         30,
     )(ffn_gain, resid, *near_units)
-    ffn_cross = after(tuple(ffn_cross), resid)
-    far_units = [p for piece in [*ffn_far, *ffn_cross] for p in (piece, core_swap(piece))]
+    arrived["units"] = partial_rows
+    far_units = [got(name) for name in ("yf", "cyf", "zf", "czf")]
     encoded = call(
         functools.partial(ffn_kernel, True, False),
         short_rows,
@@ -403,7 +445,7 @@
         "decoder_pairs",
         pairs_flops,
         20,
-    )(encoded, kv_weights)
+    )(encoded, got("wk"))
     return call(
         decoder_kernel,
         jax.ShapeDtypeStruct(dec_queries.shape, jnp.float32),
@@ -412,7 +454,7 @@
         pairs_flops,
         28,
         scratch=[pltpu.VMEM(pairs_shape, jnp.bfloat16)],
-    )(here, own_pairs, other, kv_weights, dec_queries)
+    )(here, own_pairs, other, got("wk"), dec_queries)
 
 
 def solution(mesh):

time: 81.9 us -> 76.7 us (0.937)
  waiting for transfers between devices: 20 us -> 15.8 us
  starting transfers between devices: 26.7 us -> 24.3 us
  local copies, waits for them, and re-layouts: 0.68 us -> 1.5 us
    ppermute x5, waiting for transfers between devices: 11.8 us -> 6.54 us  [seq_swap(): return lax.ppermute(array, 'seq', [(i, i ^ 1) for i in range(seq_size)])]
    ppermute x3, waiting for transfers between devices: 0.01 us -> 4.87 us  [seq_ring(): lax.ppermute(array, 'seq', [(i, (i + 2 * way) % seq_size) for i in range(...]
    ppermute x3, waiting for transfers between devices: 4.19 us -> 0.49 us  [lane_step(): lax.ppermute(array, 'mp', [(i, (i + 2 * step) % lanes) for i in range(lan...]
    ppermute x1, starting transfers between devices: 3.39 us -> 2.14 us  [next_seq(): return lax.ppermute(array, 'seq', [(i, i + 1) for i in range(seq_size - 1)])]
    ppermute x5, starting transfers between devices: 7.38 us -> 8.54 us  [seq_swap(): return lax.ppermute(array, 'seq', [(i, i ^ 1) for i in range(seq_size)])]
    ppermute x3, starting transfers between devices: 6.35 us -> 5.34 us  [seq_ring(): lax.ppermute(array, 'seq', [(i, (i + 2 * way) % seq_size) for i in range(...]
  transfers between devices with their start and end apart: 24 -> 24, of which waited for: 7 -> 10; matrix products, arithmetic and copies ran while one was open for 1% -> 1% of each run, Pallas kernels for 24% -> 26%
where the time goes in v5:
time: 76.7 us; the launch traced here: 75.8 us
  Pallas kernels  33.5 us (44%)
  starting transfers between devices  24.3 us (32%)
  waiting for transfers between devices  15.8 us (21%)
  local copies, waits for them, and re-layouts  1.5 us (2%)
    pallas_call x2, Pallas kernels, attention(): call(functools.partial(attention_kernel, len(kv), far), long_rows, 'svv'...  10.1 us
    ppermute x5, starting transfers between devices, seq_swap(): return lax.ppermute(array, 'seq', [(i, i ^ 1) for i in range(seq_size)])  8.54 us
    ppermute x5, waiting for transfers between devices, seq_swap(): return lax.ppermute(array, 'seq', [(i, i ^ 1) for i in range(seq_size)])  6.54 us
    ppermute x3, starting transfers between devices, seq_ring(): lax.ppermute(array, 'seq', [(i, (i + 2 * way) % seq_size) for i in range(...  5.34 us
    pallas_call x1, Pallas kernels, on_device(): call(functools.partial(ffn_kernel, False, True), (long_rows, short_rows),...  5.1 us
    pallas_call x1, Pallas kernels, on_device(): call(functools.partial(ffn_kernel, True, False), short_rows, 'vvv' + 'v'...  5.06 us
    pallas_call x1, Pallas kernels, on_device(): call(decoder_kernel, jax.ShapeDtypeStruct(dec_queries.shape, jnp.float32)...  5.01 us
    ppermute x3, starting transfers between devices, lane_step(): lax.ppermute(array, 'mp', [(i, (i + 2 * step) % lanes) for i in range(lan...  4.91 us
  transfers between devices with their start and end apart: 24, of which 10 were waited for; matrix products, arithmetic and copies ran while one was open for 1% of the time, Pallas kernels for 26%

profile of v5, /device:TPU:0, one launch (start us, length us, event | category | flops | bytes accessed | tf_op | source)
XLA Modules:
  0.0 75.8 jit_solution(2139448365895954004)
XLA Ops:
  0.0 3.4 %prepare.1 = (bf16[2,64,896]{2,1,0:T(8,128)(2,1)}, bf16[224,896]{1,0:T(8,128)(2,1)}, bf16[448,896]{1,0:T(8,128)(2,1)}, bf16[2,240,64]{2,1,0:T(8,128)(2,1)}) custom-call(s32[1]{0:T(128)} %bitcast.here.seq_index.first, s32[1]{0:T(128)} %bitcast.1.lane_here, s32[2,8]{1,0:T(2,128)} %bitcast.18, s32[2,8]{1,0:T(2,128)} %bitcast.20, f32[2,128,896]{2,1,0:T(8,128)} %database.1, ...), custom_call_target="tpu_custom_call" | custom-call | flops 917504 | bytes 8000000 | tf_op jit(solution)/shard_map/prepare/pallas_call | solution.py:307
  3.5 3.1 %collective-permute-start = (bf16[2,64,896]{2,1,0:T(8,128)(2,1)}, bf16[2,64,896]{2,1,0:T(8,128)(2,1)S(1)}, u32[]{:S(2)}, u32[]{:S(2)}) collective-permute-start(bf16[2,64,896]{2,1,0:T(8,128)(2,1)} %get-tuple-element.30.refs_0_), channel_id=1, source_target_pairs={{0,8},{4,12},{8,16},{12,20},{16,24},{20,28},{24,0},{28,4},{1,9},{5... | collective-permute-start | bytes 688136 | tf_op jit(solution)/shard_map/ppermute | solution.py:292
  6.6 1.5 %collective-permute-start.8 = (bf16[448,896]{1,0:T(8,128)(2,1)}, bf16[448,896]{1,0:T(8,128)(2,1)S(1)}, u32[]{:S(2)}, u32[]{:S(2)}) collective-permute-start(bf16[448,896]{1,0:T(8,128)(2,1)} %get-tuple-element.37), channel_id=1, source_target_pairs={{0,2},{1,3},{2,0},{3,1},{4,6},{5,7},{6,4},{7,5},{8,10},{9,11},{10,... | collective-permute-start | bytes 2408456 | tf_op jit(solution)/shard_map/ppermute | solution.py:283
  8.1 1.5 %collective-permute-start.1 = (bf16[2,64,896]{2,1,0:T(8,128)(2,1)}, bf16[2,64,896]{2,1,0:T(8,128)(2,1)S(1)}, u32[]{:S(2)}, u32[]{:S(2)}) collective-permute-start(bf16[2,64,896]{2,1,0:T(8,128)(2,1)} %get-tuple-element.30.refs_0_), channel_id=1, source_target_pairs={{0,4},{4,0},{8,12},{12,8},{16,20},{20,16},{24,28},{28,24},{1,5},{5... | collective-permute-start | bytes 688136 | tf_op jit(solution)/shard_map/ppermute | solution.py:286
  9.6 2.2 %collective-permute-start.6 = (bf16[2,64,896]{2,1,0:T(8,128)(2,1)}, bf16[2,64,896]{2,1,0:T(8,128)(2,1)S(1)}, u32[]{:S(2)}, u32[]{:S(2)}) collective-permute-start(bf16[2,64,896]{2,1,0:T(8,128)(2,1)} %get-tuple-element.30.refs_0_), channel_id=1, source_target_pairs={{0,24},{4,28},{8,0},{12,4},{16,8},{20,12},{24,16},{28,20},{1,25},{... | collective-permute-start | bytes 688136 | tf_op jit(solution)/shard_map/ppermute | solution.py:292
  11.8 3.4 %collective-permute-done.refs_2_ = bf16[2,64,896]{2,1,0:T(8,128)(2,1)S(1)} collective-permute-done((bf16[2,64,896]{2,1,0:T(8,128)(2,1)}, bf16[2,64,896]{2,1,0:T(8,128)(2,1)S(1)}, u32[]{:S(2)}, u32[]{:S(2)}) %collective-permute-start) | collective-permute-done | bytes 229408 | tf_op jit(solution)/shard_map/ppermute | solution.py:292
  15.2 1.8 %collective-permute-start.3 = (bf16[2,64,896]{2,1,0:T(8,128)(2,1)S(1)}, bf16[2,64,896]{2,1,0:T(8,128)(2,1)S(1)}, u32[]{:S(2)}, u32[]{:S(2)}) collective-permute-start(bf16[2,64,896]{2,1,0:T(8,128)(2,1)S(1)} %collective-permute-done.refs_2_), channel_id=1, source_target_pairs={{0,4},{4,0},{8,12},{12,8},{16,20},{20,16},{24,28},{28,24},{1,5},{5... | collective-permute-start | bytes 688136 | tf_op jit(solution)/shard_map/ppermute | solution.py:286
  17.0 2.1 %collective-permute-start.2 = (bf16[2,240,64]{2,1,0:T(8,128)(2,1)}, bf16[2,240,64]{2,1,0:T(8,128)(2,1)S(1)}, u32[]{:S(2)}, u32[]{:S(2)}) collective-permute-start(bf16[2,240,64]{2,1,0:T(8,128)(2,1)} %get-tuple-element.33), channel_id=1, source_target_pairs={{0,4},{4,8},{8,12},{12,16},{16,20},{20,24},{24,28},{1,5},{5,9},{9,... | collective-permute-start | bytes 184328 | tf_op jit(solution)/shard_map/ppermute | solution.py:295
  19.5 1.9 %collective-permute-done.3.refs_3_ = bf16[2,64,896]{2,1,0:T(8,128)(2,1)S(1)} collective-permute-done((bf16[2,64,896]{2,1,0:T(8,128)(2,1)S(1)}, bf16[2,64,896]{2,1,0:T(8,128)(2,1)S(1)}, u32[]{:S(2)}, u32[]{:S(2)}) %collective-permute-start.3) | collective-permute-done | bytes 229408 | tf_op jit(solution)/shard_map/ppermute | solution.py:286
  21.4 3.0 %collective-permute-start.7 = (bf16[2,64,896]{2,1,0:T(8,128)(2,1)S(1)}, bf16[2,64,896]{2,1,0:T(8,128)(2,1)S(1)}, u32[]{:S(2)}, u32[]{:S(2)}) collective-permute-start(bf16[2,64,896]{2,1,0:T(8,128)(2,1)S(1)} %collective-permute-done.6.refs_6_), channel_id=1, source_target_pairs={{0,4},{4,0},{8,12},{12,8},{16,20},{20,16},{24,28},{28,24},{1,5},{5... | collective-permute-start | bytes 688136 | tf_op jit(solution)/shard_map/ppermute | solution.py:286
  24.5 1.2 %collective-permute-done.4.refs_4_ = bf16[2,64,896]{2,1,0:T(8,128)(2,1)S(1)} collective-permute-done((bf16[2,64,896]{2,1,0:T(8,128)(2,1)S(1)}, bf16[2,64,896]{2,1,0:T(8,128)(2,1)S(1)}, u32[]{:S(2)}, u32[]{:S(2)}) %collective-permute-start.4) | collective-permute-done | bytes 229408 | tf_op jit(solution)/shard_map/ppermute | solution.py:292
  25.8 1.9 %collective-permute-start.12 = (bf16[224,896]{1,0:T(8,128)(2,1)}, bf16[224,896]{1,0:T(8,128)(2,1)S(1)}, u32[]{:S(2)}, u32[]{:S(2)}) collective-permute-start(bf16[224,896]{1,0:T(8,128)(2,1)} %get-tuple-element.43), channel_id=1, source_target_pairs={{0,2},{1,3},{2,0},{3,1},{4,6},{5,7},{6,4},{7,5},{8,10},{9,11},{10,... | collective-permute-start | bytes 1204232 | tf_op jit(solution)/shard_map/ppermute | solution.py:283
  28.0 2.1 %collective-permute-done.7.refs_7_ = bf16[2,64,896]{2,1,0:T(8,128)(2,1)S(1)} collective-permute-done((bf16[2,64,896]{2,1,0:T(8,128)(2,1)S(1)}, bf16[2,64,896]{2,1,0:T(8,128)(2,1)S(1)}, u32[]{:S(2)}, u32[]{:S(2)}) %collective-permute-start.7) | collective-permute-done | bytes 229408 | tf_op jit(solution)/shard_map/ppermute | solution.py:286
  30.1 2.5 %collective-permute-done.5.refs_5_ = bf16[2,64,896]{2,1,0:T(8,128)(2,1)S(1)} collective-permute-done((bf16[2,64,896]{2,1,0:T(8,128)(2,1)S(1)}, bf16[2,64,896]{2,1,0:T(8,128)(2,1)S(1)}, u32[]{:S(2)}, u32[]{:S(2)}) %collective-permute-start.5) | collective-permute-done | bytes 229408 | tf_op jit(solution)/shard_map/ppermute | solution.py:286
  32.6 1.5 %collective-permute-start.16 = (bf16[2,224,512]{2,1,0:T(8,128)(2,1)S(1)}, bf16[2,224,512]{2,1,0:T(8,128)(2,1)S(1)}, u32[]{:S(2)}, u32[]{:S(2)}) collective-permute-start(bf16[2,224,512]{2,1,0:T(8,128)(2,1)S(1)} %pad_maximum_fusion.refs_4_), channel_id=1, source_target_pairs={{0,2},{1,3},{2,0},{3,1},{4,6},{5,7},{6,4},{7,5},{8,10},{9,11},{10,... | collective-permute-start | bytes 1376264 | tf_op jit(solution)/shard_map/ppermute | solution.py:283
  34.3 0.5 collective-permute-done.12.refs_0_
  34.7 2.1 %collective-permute-start.13 = (bf16[224,896]{1,0:T(8,128)(2,1)S(1)}, bf16[224,896]{1,0:T(8,128)(2,1)S(1)}, u32[]{:S(2)}, u32[]{:S(2)}) collective-permute-start(bf16[224,896]{1,0:T(8,128)(2,1)S(1)} %collective-permute-done.12.refs_0_), channel_id=1, source_target_pairs={{0,4},{4,0},{8,12},{12,8},{16,20},{20,16},{24,28},{28,24},{1,5},{5... | collective-permute-start | bytes 1204232 | tf_op jit(solution)/shard_map/ppermute | solution.py:286
  36.8 1.1 %collective-permute-start.21 = (bf16[448,896]{1,0:T(8,128)(2,1)S(1)}, bf16[448,896]{1,0:T(8,128)(2,1)S(1)}, u32[]{:S(2)}, u32[]{:S(2)}) collective-permute-start(bf16[448,896]{1,0:T(8,128)(2,1)S(1)} %collective-permute-done.8.refs_1_), channel_id=1, source_target_pairs={{0,8},{4,12},{8,0},{12,4},{16,24},{20,28},{24,16},{28,20},{1,9},{5... | collective-permute-start | bytes 2408456 | tf_op jit(solution)/shard_map/ppermute | solution.py:289
  38.0 0.9 %copy-done.5 = bf16[2,64,896]{2,1,0:T(8,128)(2,1)S(1)} copy-done((bf16[2,64,896]{2,1,0:T(8,128)(2,1)S(1)}, bf16[2,64,896]{2,1,0:T(8,128)(2,1)}, u32[]{:S(2)}) %copy-start.5) | copy-done | bytes 229400
  39.0 2.5 %neighbour_rows.1 = (bf16[1024,896]{1,0:T(8,128)(2,1)S(1)}, bf16[1024,896]{1,0:T(8,128)(2,1)S(1)}) custom-call(s32[1]{0:T(128)} %bitcast.here.seq_index.first, s32[2,8]{1,0:T(2,128)S(1)} %bitcast.19, s32[2,8]{1,0:T(2,128)S(1)} %bitcast.21, s32[2,1]{1,0:T(2,128)S(1)} %slice_add_fusion.before, f32[1,896]{1,0:T(1,128)S(1)} %reshape.18.gain, ...), custom_call_target="tpu_custom_call" | custom-call | flops 9175040 | bytes 8000000 | tf_op jit(solution)/shard_map/neighbour_rows/pallas_call | solution.py:391
  41.6 5.0 %encoder_attention.2.before = f32[1024,896]{1,0:T(8,128)S(1)} custom-call(s32[1]{0:T(128)} %bitcast.here.seq_index.first, bf16[1024,896]{1,0:T(8,128)(2,1)S(1)} %get-tuple-element.38.before, bf16[1024,896]{1,0:T(8,128)(2,1)S(1)} %get-tuple-element.39.normed_in, bf16[224,896]{1,0:T(8,128)(2,1)S(1)} %bitcast.14, bf16[224,896]{1,0:T(8,128)(2,1)S(1)} %copy-done.1, ...), custom_call_target="tpu_custom_call" | custom-call | flops 1644167168 | bytes 8000000 | tf_op jit(solution)/shard_map/encoder_attention/pallas_call | solution.py:401
  46.6 0.5 collective-permute-start.17
  47.8 1.4 %collective-permute-done.15.refs_3_ = bf16[224,896]{1,0:T(8,128)(2,1)S(1)} collective-permute-done((bf16[224,896]{1,0:T(8,128)(2,1)S(1)}, bf16[224,896]{1,0:T(8,128)(2,1)S(1)}, u32[]{:S(2)}, u32[]{:S(2)}) %collective-permute-start.15) | collective-permute-done | bytes 401440 | tf_op jit(solution)/shard_map/ppermute | solution.py:280
  49.2 5.0 %encoder_attention.3.before = f32[1024,896]{1,0:T(8,128)S(1)} custom-call(s32[1]{0:T(128)} %bitcast.here.seq_index.first, f32[1024,896]{1,0:T(8,128)S(1)} %encoder_attention.2.before, bf16[1024,896]{1,0:T(8,128)(2,1)S(1)} %get-tuple-element.39.normed_in, bf16[224,896]{1,0:T(8,128)(2,1)S(1)} %collective-permute-done.12.refs_0_, ...), custom_call_target="tpu_custom_call" | custom-call | flops 1644167168 | bytes 8000000 | tf_op jit(solution)/shard_map/encoder_attention/pallas_call | solution.py:401
  54.7 1.9 %collective-permute-done.21.refs_3_ = bf16[448,896]{1,0:T(8,128)(2,1)S(1)} collective-permute-done((bf16[448,896]{1,0:T(8,128)(2,1)S(1)}, bf16[448,896]{1,0:T(8,128)(2,1)S(1)}, u32[]{:S(2)}, u32[]{:S(2)}) %collective-permute-start.21) | collective-permute-done | bytes 802848 | tf_op jit(solution)/shard_map/ppermute | solution.py:289
  56.6 5.1 %encoder_ffn_near.1 = (f32[1024,896]{1,0:T(8,128)S(1)}, bf16[1024,896]{1,0:T(8,128)(2,1)S(1)}) custom-call(f32[1,896]{1,0:T(1,128)S(1)} %reshape.19.gain, f32[1024,896]{1,0:T(8,128)S(1)} %encoder_attention.3.before, bf16[448,896]{1,0:T(8,128)(2,1)S(1)} %bitcast.17, bf16[448,896]{1,0:T(8,128)(2,1)S(1)} %copy-done.3, ...), custom_call_target="tpu_custom_call" | custom-call | flops 3288334336 | bytes 8000000 | tf_op jit(solution)/shard_map/encoder_ffn_near/pallas_call | solution.py:418
  61.7 5.1 %encoder_ffn_far.1.encoded = bf16[1024,896]{1,0:T(8,128)(2,1)S(1)} custom-call(f32[1,896]{1,0:T(1,128)S(1)} %reshape.19.gain, f32[1024,896]{1,0:T(8,128)S(1)} %get-tuple-element.50.before, bf16[1024,896]{1,0:T(8,128)(2,1)S(1)} %get-tuple-element.51.refs_0_, bf16[448,896]{1,0:T(8,128)(2,1)S(1)} %collective-permute-done.8.refs_1_, ...), custom_call_target="tpu_custom_call" | custom-call | flops 3288334336 | bytes 8000000 | tf_op jit(solution)/shard_map/encoder_ffn_far/pallas_call | solution.py:428
  66.8 0.6 collective-permute-start.23
  67.3 0.5 copy.13
  67.9 2.3 %decoder_pairs.1.own_pairs = bf16[1024,1024]{1,0:T(8,128)(2,1)S(1)} custom-call(bf16[1024,896]{1,0:T(8,128)(2,1)S(1)} %encoder_ffn_far.1.encoded, bf16[896,1024]{1,0:T(8,128)(2,1)S(1)} %bitcast.10), custom_call_target="tpu_custom_call" | custom-call | flops 1879048192 | bytes 8000000 | tf_op jit(solution)/shard_map/decoder_pairs/pallas_call | solution.py:441
  70.2 0.6 collective-permute-done.23.other
  70.8 5.0 %decoder_attention.1 = f32[512,512]{1,0:T(8,128)} custom-call(s32[1]{0:T(128)} %bitcast.here.seq_index.first, bf16[1024,1024]{1,0:T(8,128)(2,1)S(1)} %decoder_pairs.1.own_pairs, bf16[1024,896]{1,0:T(8,128)(2,1)S(1)} %collective-permute-done.23.other, bf16[896,1024]{1,0:T(8,128)(2,1)S(1)} %bitcast.11, bf16[512,512]{1,0:T(8,128)(2,1)S(1)} %copy-done.4), custom_call_target="tpu_custom_call" | custom-call | flops 1879048192 | bytes 8000000 | tf_op jit(solution)/shard_map/decoder_attention/pallas_call | solution.py:449
  (55 shorter events, 2.2 us)
Async XLA Ops:
  0.0 27.7 %copy-start = (bf16[896,224]{0,1:T(8,128)(2,1)S(1)}, bf16[896,224]{0,1:T(8,128)(2,1)}, u32[]{:S(2)}) copy-start(bf16[896,224]{0,1:T(8,128)(2,1)} %param.18) | copy-start | bytes 1204228
  0.0 27.7 %copy-start.9 = (bf16[512,2,224]{0,2,1:T(8,128)(2,1)S(1)}, bf16[512,2,224]{0,2,1:T(8,128)(2,1)}, u32[]{:S(2)}) copy-start(bf16[512,2,224]{0,2,1:T(8,128)(2,1)} %param.12) | copy-start | bytes 1376260
  0.0 32.6 %copy-start.1 = (bf16[224,896]{1,0:T(8,128)(2,1)S(1)}, bf16[224,896]{1,0:T(8,128)(2,1)}, u32[]{:S(2)}) copy-start(bf16[224,896]{1,0:T(8,128)(2,1)} %refs_1_.2) | copy-start | bytes 1204228
  0.0 32.6 %copy-start.10 = (f32[896]{0:T(1024)S(1)}, f32[896]{0:T(1024)}, u32[]{:S(2)}) copy-start(f32[896]{0:T(1024)} %param.17) | copy-start | bytes 10756
  0.0 32.6 %copy-start.11 = (f32[896]{0:T(1024)S(1)}, f32[896]{0:T(1024)}, u32[]{:S(2)}) copy-start(f32[896]{0:T(1024)} %param.20) | copy-start | bytes 10756
  0.0 38.0 %copy-start.6 = (s32[8,2]{0,1:T(2,128)S(1)}, s32[8,2]{0,1:T(2,128)}, u32[]{:S(2)}) copy-start(s32[8,2]{0,1:T(2,128)} %param.16) | copy-start | bytes 196
  0.0 38.0 %copy-start.7 = (s32[8,2]{0,1:T(2,128)S(1)}, s32[8,2]{0,1:T(2,128)}, u32[]{:S(2)}) copy-start(s32[8,2]{0,1:T(2,128)} %param.15) | copy-start | bytes 196
  3.5 11.8 %collective-permute-start = (bf16[2,64,896]{2,1,0:T(8,128)(2,1)}, bf16[2,64,896]{2,1,0:T(8,128)(2,1)S(1)}, u32[]{:S(2)}, u32[]{:S(2)}) collective-permute-start(bf16[2,64,896]{2,1,0:T(8,128)(2,1)} %get-tuple-element.30.refs_0_), channel_id=1, source_target_pairs={{0,8},{4,12},{8,16},{12,20},{16,24},{20,28},{24,0},{28,4},{1,9},{5... | collective-permute-start | bytes 688136 | tf_op jit(solution)/shard_map/ppermute | solution.py:292
  6.6 26.0 %collective-permute-start.8 = (bf16[448,896]{1,0:T(8,128)(2,1)}, bf16[448,896]{1,0:T(8,128)(2,1)S(1)}, u32[]{:S(2)}, u32[]{:S(2)}) collective-permute-start(bf16[448,896]{1,0:T(8,128)(2,1)} %get-tuple-element.37), channel_id=1, source_target_pairs={{0,2},{1,3},{2,0},{3,1},{4,6},{5,7},{6,4},{7,5},{8,10},{9,11},{10,... | collective-permute-start | bytes 2408456 | tf_op jit(solution)/shard_map/ppermute | solution.py:283
  8.1 8.9 %collective-permute-start.1 = (bf16[2,64,896]{2,1,0:T(8,128)(2,1)}, bf16[2,64,896]{2,1,0:T(8,128)(2,1)S(1)}, u32[]{:S(2)}, u32[]{:S(2)}) collective-permute-start(bf16[2,64,896]{2,1,0:T(8,128)(2,1)} %get-tuple-element.30.refs_0_), channel_id=1, source_target_pairs={{0,4},{4,0},{8,12},{12,8},{16,20},{20,16},{24,28},{28,24},{1,5},{5... | collective-permute-start | bytes 688136 | tf_op jit(solution)/shard_map/ppermute | solution.py:286
  9.6 9.9 %collective-permute-start.6 = (bf16[2,64,896]{2,1,0:T(8,128)(2,1)}, bf16[2,64,896]{2,1,0:T(8,128)(2,1)S(1)}, u32[]{:S(2)}, u32[]{:S(2)}) collective-permute-start(bf16[2,64,896]{2,1,0:T(8,128)(2,1)} %get-tuple-element.30.refs_0_), channel_id=1, source_target_pairs={{0,24},{4,28},{8,0},{12,4},{16,8},{20,12},{24,16},{28,20},{1,25},{... | collective-permute-start | bytes 688136 | tf_op jit(solution)/shard_map/ppermute | solution.py:292
  15.2 6.2 %collective-permute-start.3 = (bf16[2,64,896]{2,1,0:T(8,128)(2,1)S(1)}, bf16[2,64,896]{2,1,0:T(8,128)(2,1)S(1)}, u32[]{:S(2)}, u32[]{:S(2)}) collective-permute-start(bf16[2,64,896]{2,1,0:T(8,128)(2,1)S(1)} %collective-permute-done.refs_2_), channel_id=1, source_target_pairs={{0,4},{4,0},{8,12},{12,8},{16,20},{20,16},{24,28},{28,24},{1,5},{5... | collective-permute-start | bytes 688136 | tf_op jit(solution)/shard_map/ppermute | solution.py:286
  17.0 8.6 %collective-permute-start.4 = (bf16[2,64,896]{2,1,0:T(8,128)(2,1)S(1)}, bf16[2,64,896]{2,1,0:T(8,128)(2,1)S(1)}, u32[]{:S(2)}, u32[]{:S(2)}) collective-permute-start(bf16[2,64,896]{2,1,0:T(8,128)(2,1)S(1)} %collective-permute-done.refs_2_), channel_id=1, source_target_pairs={{0,8},{4,12},{8,16},{12,20},{16,24},{20,28},{24,0},{28,4},{1,9},{5... | collective-permute-start | bytes 688136 | tf_op jit(solution)/shard_map/ppermute | solution.py:292
  17.0 10.7 %collective-permute-start.2 = (bf16[2,240,64]{2,1,0:T(8,128)(2,1)}, bf16[2,240,64]{2,1,0:T(8,128)(2,1)S(1)}, u32[]{:S(2)}, u32[]{:S(2)}) collective-permute-start(bf16[2,240,64]{2,1,0:T(8,128)(2,1)} %get-tuple-element.33), channel_id=1, source_target_pairs={{0,4},{4,8},{8,12},{12,16},{16,20},{20,24},{24,28},{1,5},{5,9},{9,... | collective-permute-start | bytes 184328 | tf_op jit(solution)/shard_map/ppermute | solution.py:295
  21.4 8.7 %collective-permute-start.7 = (bf16[2,64,896]{2,1,0:T(8,128)(2,1)S(1)}, bf16[2,64,896]{2,1,0:T(8,128)(2,1)S(1)}, u32[]{:S(2)}, u32[]{:S(2)}) collective-permute-start(bf16[2,64,896]{2,1,0:T(8,128)(2,1)S(1)} %collective-permute-done.6.refs_6_), channel_id=1, source_target_pairs={{0,4},{4,0},{8,12},{12,8},{16,20},{20,16},{24,28},{28,24},{1,5},{5... | collective-permute-start | bytes 688136 | tf_op jit(solution)/shard_map/ppermute | solution.py:286
  25.6 6.9 %collective-permute-start.5 = (bf16[2,64,896]{2,1,0:T(8,128)(2,1)S(1)}, bf16[2,64,896]{2,1,0:T(8,128)(2,1)S(1)}, u32[]{:S(2)}, u32[]{:S(2)}) collective-permute-start(bf16[2,64,896]{2,1,0:T(8,128)(2,1)S(1)} %collective-permute-done.4.refs_4_), channel_id=1, source_target_pairs={{0,4},{4,0},{8,12},{12,8},{16,20},{20,16},{24,28},{28,24},{1,5},{5... | collective-permute-start | bytes 688136 | tf_op jit(solution)/shard_map/ppermute | solution.py:286
  25.8 9.0 %collective-permute-start.12 = (bf16[224,896]{1,0:T(8,128)(2,1)}, bf16[224,896]{1,0:T(8,128)(2,1)S(1)}, u32[]{:S(2)}, u32[]{:S(2)}) collective-permute-start(bf16[224,896]{1,0:T(8,128)(2,1)} %get-tuple-element.43), channel_id=1, source_target_pairs={{0,2},{1,3},{2,0},{3,1},{4,6},{5,7},{6,4},{7,5},{8,10},{9,11},{10,... | collective-permute-start | bytes 1204232 | tf_op jit(solution)/shard_map/ppermute | solution.py:283
  27.7 9.1 %collective-permute-start.9 = (bf16[224,896]{1,0:T(8,128)(2,1)S(1)}, bf16[224,896]{1,0:T(8,128)(2,1)S(1)}, u32[]{:S(2)}, u32[]{:S(2)}) collective-permute-start(bf16[224,896]{1,0:T(8,128)(2,1)S(1)} %bitcast.13), channel_id=1, source_target_pairs={{0,1},{1,0},{2,3},{3,2},{4,5},{5,4},{6,7},{7,6},{8,9},{9,8},{10,11... | collective-permute-start | bytes 1204232 | tf_op jit(solution)/shard_map/ppermute | solution.py:280
  30.1 11.4 %collective-permute-start.11 = (bf16[2,224,512]{2,1,0:T(8,128)(2,1)S(1)}, bf16[2,224,512]{2,1,0:T(8,128)(2,1)S(1)}, u32[]{:S(2)}, u32[]{:S(2)}) collective-permute-start(bf16[2,224,512]{2,1,0:T(8,128)(2,1)S(1)} %pad_maximum_fusion.refs_4_), channel_id=1, source_target_pairs={{0,1},{1,0},{2,3},{3,2},{4,5},{5,4},{6,7},{7,6},{8,9},{9,8},{10,11... | collective-permute-start | bytes 1376264 | tf_op jit(solution)/shard_map/ppermute | solution.py:280
  32.6 8.9 %collective-permute-start.10 = (bf16[224,896]{1,0:T(8,128)(2,1)S(1)}, bf16[224,896]{1,0:T(8,128)(2,1)S(1)}, u32[]{:S(2)}, u32[]{:S(2)}) collective-permute-start(bf16[224,896]{1,0:T(8,128)(2,1)S(1)} %copy-done.1), channel_id=1, source_target_pairs={{0,1},{1,0},{2,3},{3,2},{4,5},{5,4},{6,7},{7,6},{8,9},{9,8},{10,11... | collective-permute-start | bytes 1204232 | tf_op jit(solution)/shard_map/ppermute | solution.py:280
  32.6 14.0 %collective-permute-start.16 = (bf16[2,224,512]{2,1,0:T(8,128)(2,1)S(1)}, bf16[2,224,512]{2,1,0:T(8,128)(2,1)S(1)}, u32[]{:S(2)}, u32[]{:S(2)}) collective-permute-start(bf16[2,224,512]{2,1,0:T(8,128)(2,1)S(1)} %pad_maximum_fusion.refs_4_), channel_id=1, source_target_pairs={{0,2},{1,3},{2,0},{3,1},{4,6},{5,7},{6,4},{7,5},{8,10},{9,11},{10,... | collective-permute-start | bytes 1376264 | tf_op jit(solution)/shard_map/ppermute | solution.py:283
  34.7 12.4 %collective-permute-start.13 = (bf16[224,896]{1,0:T(8,128)(2,1)S(1)}, bf16[224,896]{1,0:T(8,128)(2,1)S(1)}, u32[]{:S(2)}, u32[]{:S(2)}) collective-permute-start(bf16[224,896]{1,0:T(8,128)(2,1)S(1)} %collective-permute-done.12.refs_0_), channel_id=1, source_target_pairs={{0,4},{4,0},{8,12},{12,8},{16,20},{20,16},{24,28},{28,24},{1,5},{5... | collective-permute-start | bytes 1204232 | tf_op jit(solution)/shard_map/ppermute | solution.py:286
  36.8 19.7 %collective-permute-start.21 = (bf16[448,896]{1,0:T(8,128)(2,1)S(1)}, bf16[448,896]{1,0:T(8,128)(2,1)S(1)}, u32[]{:S(2)}, u32[]{:S(2)}) collective-permute-start(bf16[448,896]{1,0:T(8,128)(2,1)S(1)} %collective-permute-done.8.refs_1_), channel_id=1, source_target_pairs={{0,8},{4,12},{8,0},{12,4},{16,24},{20,28},{24,16},{28,20},{1,9},{5... | collective-permute-start | bytes 2408456 | tf_op jit(solution)/shard_map/ppermute | solution.py:289
  41.5 6.2 %collective-permute-start.14 = (bf16[224,896]{1,0:T(8,128)(2,1)S(1)}, bf16[224,896]{1,0:T(8,128)(2,1)S(1)}, u32[]{:S(2)}, u32[]{:S(2)}) collective-permute-start(bf16[224,896]{1,0:T(8,128)(2,1)S(1)} %collective-permute-done.12.refs_0_), channel_id=1, source_target_pairs={{0,1},{1,0},{2,3},{3,2},{4,5},{5,4},{6,7},{7,6},{8,9},{9,8},{10,11... | collective-permute-start | bytes 1204232 | tf_op jit(solution)/shard_map/ppermute | solution.py:280
  41.6 6.1 %copy-start.3 = (bf16[448,896]{1,0:T(8,128)(2,1)S(1)}, bf16[448,896]{1,0:T(8,128)(2,1)}, u32[]{:S(2)}) copy-start(bf16[448,896]{1,0:T(8,128)(2,1)} %refs_1_.3) | copy-start | bytes 2408452
  46.6 2.6 %collective-permute-start.17 = (bf16[2,224,512]{2,1,0:T(8,128)(2,1)S(1)}, bf16[2,224,512]{2,1,0:T(8,128)(2,1)S(1)}, u32[]{:S(2)}, u32[]{:S(2)}) collective-permute-start(bf16[2,224,512]{2,1,0:T(8,128)(2,1)S(1)} %collective-permute-done.16.refs_4_), channel_id=1, source_target_pairs={{0,1},{1,0},{2,3},{3,2},{4,5},{5,4},{6,7},{7,6},{8,9},{9,8},{10,11... | collective-permute-start | bytes 1376264 | tf_op jit(solution)/shard_map/ppermute | solution.py:280
  47.2 2.0 %collective-permute-start.15 = (bf16[224,896]{1,0:T(8,128)(2,1)S(1)}, bf16[224,896]{1,0:T(8,128)(2,1)S(1)}, u32[]{:S(2)}, u32[]{:S(2)}) collective-permute-start(bf16[224,896]{1,0:T(8,128)(2,1)S(1)} %collective-permute-done.13.refs_1_), channel_id=1, source_target_pairs={{0,1},{1,0},{2,3},{3,2},{4,5},{5,4},{6,7},{7,6},{8,9},{9,8},{10,11... | collective-permute-start | bytes 1204232 | tf_op jit(solution)/shard_map/ppermute | solution.py:280
  47.3 9.3 %collective-permute-start.18 = (bf16[448,896]{1,0:T(8,128)(2,1)S(1)}, bf16[448,896]{1,0:T(8,128)(2,1)S(1)}, u32[]{:S(2)}, u32[]{:S(2)}) collective-permute-start(bf16[448,896]{1,0:T(8,128)(2,1)S(1)} %bitcast.16), channel_id=1, source_target_pairs={{0,1},{1,0},{2,3},{3,2},{4,5},{5,4},{6,7},{7,6},{8,9},{9,8},{10,11... | collective-permute-start | bytes 2408456 | tf_op jit(solution)/shard_map/ppermute | solution.py:280
  47.7 8.9 %collective-permute-start.19 = (bf16[448,896]{1,0:T(8,128)(2,1)S(1)}, bf16[448,896]{1,0:T(8,128)(2,1)S(1)}, u32[]{:S(2)}, u32[]{:S(2)}) collective-permute-start(bf16[448,896]{1,0:T(8,128)(2,1)S(1)} %copy-done.3), channel_id=1, source_target_pairs={{0,1},{1,0},{2,3},{3,2},{4,5},{5,4},{6,7},{7,6},{8,9},{9,8},{10,11... | collective-permute-start | bytes 2408456 | tf_op jit(solution)/shard_map/ppermute | solution.py:280
  54.2 7.4 %collective-permute-start.20 = (bf16[448,896]{1,0:T(8,128)(2,1)S(1)}, bf16[448,896]{1,0:T(8,128)(2,1)S(1)}, u32[]{:S(2)}, u32[]{:S(2)}) collective-permute-start(bf16[448,896]{1,0:T(8,128)(2,1)S(1)} %collective-permute-done.8.refs_1_), channel_id=1, source_target_pairs={{0,1},{1,0},{2,3},{3,2},{4,5},{5,4},{6,7},{7,6},{8,9},{9,8},{10,11... | collective-permute-start | bytes 2408456 | tf_op jit(solution)/shard_map/ppermute | solution.py:280
  56.6 5.1 %collective-permute-start.22 = (bf16[448,896]{1,0:T(8,128)(2,1)S(1)}, bf16[448,896]{1,0:T(8,128)(2,1)S(1)}, u32[]{:S(2)}, u32[]{:S(2)}) collective-permute-start(bf16[448,896]{1,0:T(8,128)(2,1)S(1)} %collective-permute-done.21.refs_3_), channel_id=1, source_target_pairs={{0,1},{1,0},{2,3},{3,2},{4,5},{5,4},{6,7},{7,6},{8,9},{9,8},{10,11... | collective-permute-start | bytes 2408456 | tf_op jit(solution)/shard_map/ppermute | solution.py:280
  66.8 4.0 %collective-permute-start.23 = (bf16[1024,896]{1,0:T(8,128)(2,1)S(1)}, bf16[1024,896]{1,0:T(8,128)(2,1)S(1)}, u32[]{:S(2)}, u32[]{:S(2)}) collective-permute-start(bf16[1024,896]{1,0:T(8,128)(2,1)S(1)} %encoder_ffn_far.1.encoded), channel_id=1, source_target_pairs={{0,1},{1,0},{2,3},{3,2},{4,5},{5,4},{6,7},{7,6},{8,9},{9,8},{10,11... | collective-permute-start | bytes 5505032 | tf_op jit(solution)/shard_map/ppermute | solution.py:280
  (4 other events, 15.2 us)

commit v6 on v5

--- a/solution.py
+++ b/solution.py
@@ -51,7 +51,8 @@
 
 
 def prepare_kernel(here, lane_here, host, index, database, query_t, enc_out, up_t, down, kv_t, *refs):
-    db_half, attention_half, ffn_half, packet, db_in, kv_in, sems = refs
+    db_half, attention_half, ffn_half, packet = refs[:4]
+    db_in, db_out, kv_in, packet_out, attention_out, ffn_out, sems = refs[4:]
     per_host, half_rows, width = db_half.shape
     seq, lane = here[0], lane_here[0]
     copies = [
@@ -62,8 +63,8 @@
         ),
         pltpu.make_async_copy(kv_t.at[:, :, pl.ds(kv_t.shape[2] - 2 * SPAN, 2 * SPAN)], kv_in, sems.at[1]),
     ]
-    halves = ((query_t, attention_half, 0, seq % 2), (enc_out, attention_half, 1, seq % 2))
-    halves += ((up_t, ffn_half, 0, seq // 2 % 2), (down, ffn_half, 1, seq // 2 % 2))
+    halves = ((up_t, ffn_out, 0, seq // 2 % 2), (down, ffn_out, 1, seq // 2 % 2))
+    halves += ((query_t, attention_out, 0, seq % 2), (enc_out, attention_out, 1, seq % 2))
     for i, (source, target, spot, parity) in enumerate(halves):
         count = source.shape[0] // 2
         copies.append(
@@ -75,17 +76,31 @@
         )
     for copy in copies:
         copy.start()
+    backs = []
+
+    def back(source, target):
+        backs.append(pltpu.make_async_copy(source, target, sems.at[6 + len(backs)]))
+        backs[-1].start()
+
     copies[0].wait()
-    db_half[...] = db_in[...].astype(jnp.bfloat16)
+    db_out[...] = db_in[...].astype(jnp.bfloat16)
+    back(db_out, db_half)
     copies[1].wait()
     kv_rows = kv_in.shape[1]
     row = lax.broadcasted_iota(jnp.int32, (packet.shape[1] - kv_rows, SPAN), 0)
     for k in range(NEIGH):
         entry = host[k, CH_DEV - 1] * per_host + index[k, CH_DEV - 1]
         digits = jnp.where(row == 0, entry // DIGIT, jnp.where(row == 1, entry % DIGIT, 0))
-        packet[k, :kv_rows, :] = kv_in[k][:, SPAN:]
-        packet[k, kv_rows:, :] = digits.astype(jnp.float32).astype(jnp.bfloat16)
-    for copy in copies[2:]:
+        packet_out[k, :kv_rows, :] = kv_in[k][:, SPAN:]
+        packet_out[k, kv_rows:, :] = digits.astype(jnp.float32).astype(jnp.bfloat16)
+    back(packet_out, packet)
+    for copy in copies[2:4]:
+        copy.wait()
+    back(ffn_out, ffn_half)
+    for copy in copies[4:]:
+        copy.wait()
+    back(attention_out, attention_half)
+    for copy in backs:
         copy.wait()
 
 
@@ -125,6 +140,7 @@
     empty = jnp.zeros((HEAD_DIM, 2 * SPAN), jnp.bfloat16)
     ones = jnp.ones((2 * HEAD_DIM - EHEAD_DIM, 2 * SPAN), jnp.bfloat16)
     weight_rest = jnp.zeros((pad, width), jnp.bfloat16)
+    q_parts, out_parts = [], []
     for p in range(pieces):
         first, second = weight_refs[2 * p][...], weight_refs[2 * p + 1][...]
         if far:
@@ -132,16 +148,18 @@
                 jnp.where(odd == 0, first, second),
                 jnp.where(odd == 0, second, first),
             )
-            q_parts = (first[:EHEAD_DIM], second[:EHEAD_DIM])
-            out_parts = (first[EHEAD_DIM:], second[EHEAD_DIM:])
+            q_parts += [first[:EHEAD_DIM], weight_rest, second[:EHEAD_DIM], weight_rest]
+            out_parts += [first[EHEAD_DIM:], weight_rest, second[EHEAD_DIM:], weight_rest]
         else:
-            q_parts = (first[:EHEAD_DIM], first[EHEAD_DIM:])
-            out_parts = (second[:EHEAD_DIM], second[EHEAD_DIM:])
-        q_w = jnp.concatenate([q_parts[0], weight_rest, q_parts[1], weight_rest], axis=0)
-        out_w = jnp.concatenate([out_parts[0], weight_rest, out_parts[1], weight_rest], axis=0)
-        for start in range(0, rows, BLOCK):
-            block = slice(start, start + BLOCK)
-            query = (mxu(normed_in[block, :], q_w, NT) * scale).astype(jnp.bfloat16)
+            q_parts += [first[:EHEAD_DIM], weight_rest, first[EHEAD_DIM:], weight_rest]
+            out_parts += [second[:EHEAD_DIM], weight_rest, second[EHEAD_DIM:], weight_rest]
+    q_w, out_w = jnp.concatenate(q_parts, axis=0), jnp.concatenate(out_parts, axis=0)
+    left = lax.broadcasted_iota(jnp.int32, (BLOCK, 2 * SPAN), 1) < SPAN
+    for start in range(0, rows, BLOCK):
+        block = slice(start, start + BLOCK)
+        query = (mxu(normed_in[block, :], q_w, NT) * scale).astype(jnp.bfloat16)
+        attended = []
+        for p in range(pieces):
             scores = []
             for at in range(0, BLOCK, pair_rows):
                 tok = (start + at) // pair_rows * 2 * SPAN
@@ -153,52 +171,49 @@
                     ],
                     axis=1,
                 )
-                both = mxu(query[at : at + pair_rows], keys, NN)
+                of_piece = query[at : at + pair_rows, 2 * HEAD_DIM * p : 2 * HEAD_DIM * (p + 1)]
+                both = mxu(of_piece, keys, NN)
                 scores.append(jnp.where(own_lanes, both[:, : 2 * SPAN], both[:, 2 * SPAN :]))
             scores = jnp.concatenate(scores, axis=0)
-            left = lax.broadcasted_iota(jnp.int32, scores.shape, 1) < SPAN
             low = jnp.max(jnp.where(left, scores, -jnp.inf), axis=1, keepdims=True)
             high = jnp.max(jnp.where(left, -jnp.inf, scores), axis=1, keepdims=True)
             weights = jnp.exp(scores - jnp.where(left, low, high)).astype(jnp.bfloat16)
-            attended = []
+            of_heads = [[], []]
             for at in range(0, BLOCK, pair_rows):
                 tok = (start + at) // pair_rows * 2 * SPAN
                 part = weights[at : at + pair_rows]
                 vals = kv_refs[p][1, :, tok : tok + 2 * SPAN]
-                heads = []
                 for head in range(2):
                     picked = jnp.where(own_lanes if head == 0 else ~own_lanes, part, jnp.zeros_like(part))
                     of_head = vals[:EHEAD_DIM] if head == 0 else turned(vals[EHEAD_DIM:])
                     mixed = mxu(picked, jnp.concatenate([of_head, ones], axis=0), NT)
-                    heads.append((mixed[:, :HEAD_DIM] / mixed[:, HEAD_DIM:]).astype(jnp.bfloat16))
-                attended.append(jnp.concatenate(heads, axis=1))
-            so_far = before if p == 0 else result
-            result[block, :] = so_far[block, :].astype(jnp.float32) + mxu(jnp.concatenate(attended, axis=0), out_w, NN)
+                    of_heads[head].append((mixed[:, :HEAD_DIM] / mixed[:, HEAD_DIM:]).astype(jnp.bfloat16))
+            attended += [jnp.concatenate(parts, axis=0) for parts in of_heads]
+        added = mxu(jnp.concatenate(attended, axis=1), out_w, NN)
+        result[block, :] = before[block, :].astype(jnp.float32) + added
 
 
 def ffn_kernel(far, first, gain, before, *refs):
     if first:
-        *group_refs, total, normed = refs
-        normed[...] = rms_scale(before[...], gain[...]).astype(jnp.bfloat16)
-        result = total
+        *group_refs, result, normed = refs
     else:
-        normed, *group_refs, result, total = refs
+        normed, *group_refs, result = refs
     if far:
         half = group_refs[0].shape[0] // 2
-        groups = [(r.at[pl.ds(0, half)], r.at[pl.ds(half, half)]) for r in group_refs]
+        ups, downs = [r[:half] for r in group_refs], [r[half:] for r in group_refs]
     else:
-        groups = list(zip(group_refs[::2], group_refs[1::2]))
-    ahead = mxu(normed[...], groups[0][0][...], NT)
-    for g in range(len(groups)):
-        units = ahead
-        if g + 1 < len(groups):
-            ahead = mxu(normed[...], groups[g + 1][0][...], NT)
-        added = mxu(jax.nn.gelu(units).astype(jnp.bfloat16), groups[g][1][...], NN)
-        added = (before if g == 0 else total)[...] + added
-        if g + 1 < len(groups):
-            total[...] = added
-        else:
-            result[...] = added.astype(result.dtype)
+        ups, downs = [r[...] for r in group_refs[::2]], [r[...] for r in group_refs[1::2]]
+    up, down = jnp.concatenate(ups, axis=0), jnp.concatenate(downs, axis=0)
+    raised = []
+    for start in range(0, before.shape[0], BLOCK):
+        block = slice(start, start + BLOCK)
+        if first:
+            normed[block, :] = rms_scale(before[block, :], gain[...]).astype(jnp.bfloat16)
+        raised.append(mxu(normed[block, :], up, NT).astype(jnp.bfloat16))
+    for i, units in enumerate(raised):
+        block = slice(i * BLOCK, (i + 1) * BLOCK)
+        added = before[block, :] + mxu(jax.nn.gelu(units), down, NN)
+        result[block, :] = added.astype(result.dtype)
 
 
 def pairs_kernel(encoded, weights, pairs):
@@ -239,13 +254,13 @@
             out[span * SPAN : (span + 1) * SPAN, col : col + HEAD_DIM] = result
 
 
-def call(body, out_shape, in_specs, name, flops, vmem_mib, scratch=()):
+def call(body, out_shape, in_specs, name, flops, vmem_mib, scratch=(), out="v"):
     spaces = {"s": pltpu.SMEM, "v": pltpu.VMEM, "h": pl.ANY}
     return pl.pallas_call(
         body,
         out_shape=out_shape,
         in_specs=[pl.BlockSpec(memory_space=spaces[c]) for c in in_specs],
-        out_specs=jax.tree.map(lambda _: pl.BlockSpec(memory_space=pltpu.VMEM), out_shape),
+        out_specs=jax.tree.map(lambda _: pl.BlockSpec(memory_space=spaces[out]), out_shape),
         scratch_shapes=list(scratch),
         compiler_params=pltpu.CompilerParams(vmem_limit_bytes=vmem_mib * 1024 * 1024),
         cost_estimate=pl.CostEstimate(flops=flops, bytes_accessed=8_000_000, transcendentals=0),
@@ -318,9 +333,14 @@
         60,
         scratch=[
             pltpu.VMEM((entries_here, half_rows, width), jnp.float32),
+            pltpu.VMEM((entries_here, half_rows, width), jnp.bfloat16),
             pltpu.VMEM((2, kv_rows, 2 * SPAN), jnp.bfloat16),
-            dma((6,)),
+            pltpu.VMEM((2, kv_rows + 16, SPAN), jnp.bfloat16),
+            pltpu.VMEM(enc_out.shape, jnp.bfloat16),
+            pltpu.VMEM(ffn_down.shape, jnp.bfloat16),
+            dma((10,)),
         ],
+        out="h",
     )(here, lane_here, host, index, database, query_t, enc_out, up_t, ffn_down, kv_t)
 
     dec_width = dec_kv.shape[2]
@@ -432,7 +452,6 @@
         "encoder_ffn_far",
         2 * gemm,
         30,
-        scratch=[pltpu.VMEM((rows, width), jnp.float32)],
     )(ffn_gain, partial_rows, normed, *far_units)
 
     other = core_swap(encoded)

time: 76.7 us -> 75.7 us (0.987)
  Pallas kernels: 33.5 us -> 30.7 us
  waiting for transfers between devices: 15.8 us -> 17.6 us
    pallas_call x2, Pallas kernels: 10.1 us -> 8.27 us  [attention(): call(functools.partial(attention_kernel, len(kv), far), long_rows, 'svv'...]
    ppermute x1, waiting for transfers between devices: 1.88 us -> 3.67 us  [seq_cross(): return lax.ppermute(array, 'seq', [(i, i ^ 2) for i in range(seq_size)])]
  transfers between devices with their start and end apart: 24 -> 24, of which waited for: 10 -> 11; matrix products, arithmetic and copies ran while one was open for 1% -> 1% of each run, Pallas kernels for 26% -> 24%
where the time goes in v6:
time: 75.7 us; the launch traced here: 74.7 us
  Pallas kernels  30.7 us (41%)
  starting transfers between devices  24.3 us (32%)
  waiting for transfers between devices  17.6 us (23%)
  local copies, waits for them, and re-layouts  1.5 us (2%)
    ppermute x5, starting transfers between devices, seq_swap(): return lax.ppermute(array, 'seq', [(i, i ^ 1) for i in range(seq_size)])  8.54 us
    pallas_call x2, Pallas kernels, attention(): call(functools.partial(attention_kernel, len(kv), far), long_rows, 'svv'...  8.27 us
    ppermute x5, waiting for transfers between devices, seq_swap(): return lax.ppermute(array, 'seq', [(i, i ^ 1) for i in range(seq_size)])  6.76 us
    ppermute x3, starting transfers between devices, seq_ring(): lax.ppermute(array, 'seq', [(i, (i + 2 * way) % seq_size) for i in range(...  5.34 us
    pallas_call x1, Pallas kernels, on_device(): call(decoder_kernel, jax.ShapeDtypeStruct(dec_queries.shape, jnp.float32)...  5.01 us
    ppermute x3, starting transfers between devices, lane_step(): lax.ppermute(array, 'mp', [(i, (i + 2 * step) % lanes) for i in range(lan...  4.91 us
    ppermute x3, waiting for transfers between devices, seq_ring(): lax.ppermute(array, 'seq', [(i, (i + 2 * way) % seq_size) for i in range(...  4.87 us
    pallas_call x1, Pallas kernels, on_device(): call(functools.partial(ffn_kernel, False, True), (long_rows, short_rows),...  4.85 us
  transfers between devices with their start and end apart: 24, of which 11 were waited for; matrix products, arithmetic and copies ran while one was open for 1% of the time, Pallas kernels for 24%

profile of v6, /device:TPU:0, one launch (start us, length us, event | category | flops | bytes accessed | tf_op | source)
XLA Modules:
  0.0 74.7 jit_solution(18221115037222792050)
XLA Ops:
  0.0 3.3 %prepare.1 = (bf16[2,64,896]{2,1,0:T(8,128)(2,1)}, bf16[224,896]{1,0:T(8,128)(2,1)}, bf16[448,896]{1,0:T(8,128)(2,1)}, bf16[2,240,64]{2,1,0:T(8,128)(2,1)}) custom-call(s32[1]{0:T(128)} %bitcast.here.seq_index.first, s32[1]{0:T(128)} %bitcast.1.lane_here, s32[2,8]{1,0:T(2,128)} %bitcast.18, s32[2,8]{1,0:T(2,128)} %bitcast.20, f32[2,128,896]{2,1,0:T(8,128)} %database.1, ...), custom_call_target="tpu_custom_call" | custom-call | flops 917504 | bytes 8000000 | tf_op jit(solution)/shard_map/prepare/pallas_call | solution.py:322
  3.3 3.1 %collective-permute-start = (bf16[2,64,896]{2,1,0:T(8,128)(2,1)}, bf16[2,64,896]{2,1,0:T(8,128)(2,1)S(1)}, u32[]{:S(2)}, u32[]{:S(2)}) collective-permute-start(bf16[2,64,896]{2,1,0:T(8,128)(2,1)} %get-tuple-element.30.refs_0_), channel_id=1, source_target_pairs={{0,8},{4,12},{8,16},{12,20},{16,24},{20,28},{24,0},{28,4},{1,9},{5... | collective-permute-start | bytes 688136 | tf_op jit(solution)/shard_map/ppermute | solution.py:307
  6.4 1.5 %collective-permute-start.8 = (bf16[448,896]{1,0:T(8,128)(2,1)}, bf16[448,896]{1,0:T(8,128)(2,1)S(1)}, u32[]{:S(2)}, u32[]{:S(2)}) collective-permute-start(bf16[448,896]{1,0:T(8,128)(2,1)} %get-tuple-element.37), channel_id=1, source_target_pairs={{0,2},{1,3},{2,0},{3,1},{4,6},{5,7},{6,4},{7,5},{8,10},{9,11},{10,... | collective-permute-start | bytes 2408456 | tf_op jit(solution)/shard_map/ppermute | solution.py:298
  7.9 1.5 %collective-permute-start.1 = (bf16[2,64,896]{2,1,0:T(8,128)(2,1)}, bf16[2,64,896]{2,1,0:T(8,128)(2,1)S(1)}, u32[]{:S(2)}, u32[]{:S(2)}) collective-permute-start(bf16[2,64,896]{2,1,0:T(8,128)(2,1)} %get-tuple-element.30.refs_0_), channel_id=1, source_target_pairs={{0,4},{4,0},{8,12},{12,8},{16,20},{20,16},{24,28},{28,24},{1,5},{5... | collective-permute-start | bytes 688136 | tf_op jit(solution)/shard_map/ppermute | solution.py:301
  9.4 2.2 %collective-permute-start.6 = (bf16[2,64,896]{2,1,0:T(8,128)(2,1)}, bf16[2,64,896]{2,1,0:T(8,128)(2,1)S(1)}, u32[]{:S(2)}, u32[]{:S(2)}) collective-permute-start(bf16[2,64,896]{2,1,0:T(8,128)(2,1)} %get-tuple-element.30.refs_0_), channel_id=1, source_target_pairs={{0,24},{4,28},{8,0},{12,4},{16,8},{20,12},{24,16},{28,20},{1,25},{... | collective-permute-start | bytes 688136 | tf_op jit(solution)/shard_map/ppermute | solution.py:307
  11.7 3.4 %collective-permute-done.refs_2_ = bf16[2,64,896]{2,1,0:T(8,128)(2,1)S(1)} collective-permute-done((bf16[2,64,896]{2,1,0:T(8,128)(2,1)}, bf16[2,64,896]{2,1,0:T(8,128)(2,1)S(1)}, u32[]{:S(2)}, u32[]{:S(2)}) %collective-permute-start) | collective-permute-done | bytes 229408 | tf_op jit(solution)/shard_map/ppermute | solution.py:307
  15.1 1.8 %collective-permute-start.3 = (bf16[2,64,896]{2,1,0:T(8,128)(2,1)S(1)}, bf16[2,64,896]{2,1,0:T(8,128)(2,1)S(1)}, u32[]{:S(2)}, u32[]{:S(2)}) collective-permute-start(bf16[2,64,896]{2,1,0:T(8,128)(2,1)S(1)} %collective-permute-done.refs_2_), channel_id=1, source_target_pairs={{0,4},{4,0},{8,12},{12,8},{16,20},{20,16},{24,28},{28,24},{1,5},{5... | collective-permute-start | bytes 688136 | tf_op jit(solution)/shard_map/ppermute | solution.py:301
  16.8 2.1 %collective-permute-start.2 = (bf16[2,240,64]{2,1,0:T(8,128)(2,1)}, bf16[2,240,64]{2,1,0:T(8,128)(2,1)S(1)}, u32[]{:S(2)}, u32[]{:S(2)}) collective-permute-start(bf16[2,240,64]{2,1,0:T(8,128)(2,1)} %get-tuple-element.33), channel_id=1, source_target_pairs={{0,4},{4,8},{8,12},{12,16},{16,20},{20,24},{24,28},{1,5},{5,9},{9,... | collective-permute-start | bytes 184328 | tf_op jit(solution)/shard_map/ppermute | solution.py:310
  19.3 1.9 %collective-permute-done.3.refs_3_ = bf16[2,64,896]{2,1,0:T(8,128)(2,1)S(1)} collective-permute-done((bf16[2,64,896]{2,1,0:T(8,128)(2,1)S(1)}, bf16[2,64,896]{2,1,0:T(8,128)(2,1)S(1)}, u32[]{:S(2)}, u32[]{:S(2)}) %collective-permute-start.3) | collective-permute-done | bytes 229408 | tf_op jit(solution)/shard_map/ppermute | solution.py:301
  21.2 3.0 %collective-permute-start.7 = (bf16[2,64,896]{2,1,0:T(8,128)(2,1)S(1)}, bf16[2,64,896]{2,1,0:T(8,128)(2,1)S(1)}, u32[]{:S(2)}, u32[]{:S(2)}) collective-permute-start(bf16[2,64,896]{2,1,0:T(8,128)(2,1)S(1)} %collective-permute-done.6.refs_6_), channel_id=1, source_target_pairs={{0,4},{4,0},{8,12},{12,8},{16,20},{20,16},{24,28},{28,24},{1,5},{5... | collective-permute-start | bytes 688136 | tf_op jit(solution)/shard_map/ppermute | solution.py:301
  24.3 1.2 %collective-permute-done.4.refs_4_ = bf16[2,64,896]{2,1,0:T(8,128)(2,1)S(1)} collective-permute-done((bf16[2,64,896]{2,1,0:T(8,128)(2,1)S(1)}, bf16[2,64,896]{2,1,0:T(8,128)(2,1)S(1)}, u32[]{:S(2)}, u32[]{:S(2)}) %collective-permute-start.4) | collective-permute-done | bytes 229408 | tf_op jit(solution)/shard_map/ppermute | solution.py:307
  25.6 1.9 %collective-permute-start.12 = (bf16[224,896]{1,0:T(8,128)(2,1)}, bf16[224,896]{1,0:T(8,128)(2,1)S(1)}, u32[]{:S(2)}, u32[]{:S(2)}) collective-permute-start(bf16[224,896]{1,0:T(8,128)(2,1)} %get-tuple-element.43), channel_id=1, source_target_pairs={{0,2},{1,3},{2,0},{3,1},{4,6},{5,7},{6,4},{7,5},{8,10},{9,11},{10,... | collective-permute-start | bytes 1204232 | tf_op jit(solution)/shard_map/ppermute | solution.py:298
  27.8 2.1 %collective-permute-done.7.refs_7_ = bf16[2,64,896]{2,1,0:T(8,128)(2,1)S(1)} collective-permute-done((bf16[2,64,896]{2,1,0:T(8,128)(2,1)S(1)}, bf16[2,64,896]{2,1,0:T(8,128)(2,1)S(1)}, u32[]{:S(2)}, u32[]{:S(2)}) %collective-permute-start.7) | collective-permute-done | bytes 229408 | tf_op jit(solution)/shard_map/ppermute | solution.py:301
  29.9 2.5 %collective-permute-done.5.refs_5_ = bf16[2,64,896]{2,1,0:T(8,128)(2,1)S(1)} collective-permute-done((bf16[2,64,896]{2,1,0:T(8,128)(2,1)S(1)}, bf16[2,64,896]{2,1,0:T(8,128)(2,1)S(1)}, u32[]{:S(2)}, u32[]{:S(2)}) %collective-permute-start.5) | collective-permute-done | bytes 229408 | tf_op jit(solution)/shard_map/ppermute | solution.py:301
  32.4 1.5 %collective-permute-start.16 = (bf16[2,224,512]{2,1,0:T(8,128)(2,1)S(1)}, bf16[2,224,512]{2,1,0:T(8,128)(2,1)S(1)}, u32[]{:S(2)}, u32[]{:S(2)}) collective-permute-start(bf16[2,224,512]{2,1,0:T(8,128)(2,1)S(1)} %pad_maximum_fusion.refs_4_), channel_id=1, source_target_pairs={{0,2},{1,3},{2,0},{3,1},{4,6},{5,7},{6,4},{7,5},{8,10},{9,11},{10,... | collective-permute-start | bytes 1376264 | tf_op jit(solution)/shard_map/ppermute | solution.py:298
  34.1 0.5 collective-permute-done.12.refs_0_
  34.6 2.1 %collective-permute-start.13 = (bf16[224,896]{1,0:T(8,128)(2,1)S(1)}, bf16[224,896]{1,0:T(8,128)(2,1)S(1)}, u32[]{:S(2)}, u32[]{:S(2)}) collective-permute-start(bf16[224,896]{1,0:T(8,128)(2,1)S(1)} %collective-permute-done.12.refs_0_), channel_id=1, source_target_pairs={{0,4},{4,0},{8,12},{12,8},{16,20},{20,16},{24,28},{28,24},{1,5},{5... | collective-permute-start | bytes 1204232 | tf_op jit(solution)/shard_map/ppermute | solution.py:301
  36.6 1.1 %collective-permute-start.21 = (bf16[448,896]{1,0:T(8,128)(2,1)S(1)}, bf16[448,896]{1,0:T(8,128)(2,1)S(1)}, u32[]{:S(2)}, u32[]{:S(2)}) collective-permute-start(bf16[448,896]{1,0:T(8,128)(2,1)S(1)} %collective-permute-done.8.refs_1_), channel_id=1, source_target_pairs={{0,8},{4,12},{8,0},{12,4},{16,24},{20,28},{24,16},{28,20},{1,9},{5... | collective-permute-start | bytes 2408456 | tf_op jit(solution)/shard_map/ppermute | solution.py:304
  37.8 0.9 %copy-done.5 = bf16[2,64,896]{2,1,0:T(8,128)(2,1)S(1)} copy-done((bf16[2,64,896]{2,1,0:T(8,128)(2,1)S(1)}, bf16[2,64,896]{2,1,0:T(8,128)(2,1)}, u32[]{:S(2)}) %copy-start.5) | copy-done | bytes 229400
  38.8 2.5 %neighbour_rows.1 = (bf16[1024,896]{1,0:T(8,128)(2,1)S(1)}, bf16[1024,896]{1,0:T(8,128)(2,1)S(1)}) custom-call(s32[1]{0:T(128)} %bitcast.here.seq_index.first, s32[2,8]{1,0:T(2,128)S(1)} %bitcast.19, s32[2,8]{1,0:T(2,128)S(1)} %bitcast.21, s32[2,1]{1,0:T(2,128)S(1)} %slice_add_fusion.before, f32[1,896]{1,0:T(1,128)S(1)} %reshape.18.gain, ...), custom_call_target="tpu_custom_call" | custom-call | flops 9175040 | bytes 8000000 | tf_op jit(solution)/shard_map/neighbour_rows/pallas_call | solution.py:411
  41.4 4.1 %encoder_attention.2.before = f32[1024,896]{1,0:T(8,128)S(1)} custom-call(s32[1]{0:T(128)} %bitcast.here.seq_index.first, bf16[1024,896]{1,0:T(8,128)(2,1)S(1)} %get-tuple-element.38.before, bf16[1024,896]{1,0:T(8,128)(2,1)S(1)} %get-tuple-element.39.normed_in, bf16[224,896]{1,0:T(8,128)(2,1)S(1)} %bitcast.14, bf16[224,896]{1,0:T(8,128)(2,1)S(1)} %copy-done.1, ...), custom_call_target="tpu_custom_call" | custom-call | flops 1644167168 | bytes 8000000 | tf_op jit(solution)/shard_map/encoder_attention/pallas_call | solution.py:421
  45.5 0.5 collective-permute-start.17
  46.3 0.5 collective-permute-start.18
  46.9 1.2 %collective-permute-done.15.refs_3_ = bf16[224,896]{1,0:T(8,128)(2,1)S(1)} collective-permute-done((bf16[224,896]{1,0:T(8,128)(2,1)S(1)}, bf16[224,896]{1,0:T(8,128)(2,1)S(1)}, u32[]{:S(2)}, u32[]{:S(2)}) %collective-permute-start.15) | collective-permute-done | bytes 401440 | tf_op jit(solution)/shard_map/ppermute | solution.py:295
  48.1 4.1 %encoder_attention.3.before = f32[1024,896]{1,0:T(8,128)S(1)} custom-call(s32[1]{0:T(128)} %bitcast.here.seq_index.first, f32[1024,896]{1,0:T(8,128)S(1)} %encoder_attention.2.before, bf16[1024,896]{1,0:T(8,128)(2,1)S(1)} %get-tuple-element.39.normed_in, bf16[224,896]{1,0:T(8,128)(2,1)S(1)} %collective-permute-done.12.refs_0_, ...), custom_call_target="tpu_custom_call" | custom-call | flops 1644167168 | bytes 8000000 | tf_op jit(solution)/shard_map/encoder_attention/pallas_call | solution.py:421
  52.7 3.7 %collective-permute-done.21.refs_3_ = bf16[448,896]{1,0:T(8,128)(2,1)S(1)} collective-permute-done((bf16[448,896]{1,0:T(8,128)(2,1)S(1)}, bf16[448,896]{1,0:T(8,128)(2,1)S(1)}, u32[]{:S(2)}, u32[]{:S(2)}) %collective-permute-start.21) | collective-permute-done | bytes 802848 | tf_op jit(solution)/shard_map/ppermute | solution.py:304
  56.4 4.8 %encoder_ffn_near.1 = (f32[1024,896]{1,0:T(8,128)S(1)}, bf16[1024,896]{1,0:T(8,128)(2,1)S(1)}) custom-call(f32[1,896]{1,0:T(1,128)S(1)} %reshape.19.gain, f32[1024,896]{1,0:T(8,128)S(1)} %encoder_attention.3.before, bf16[448,896]{1,0:T(8,128)(2,1)S(1)} %bitcast.17, bf16[448,896]{1,0:T(8,128)(2,1)S(1)} %copy-done.3, ...), custom_call_target="tpu_custom_call" | custom-call | flops 3288334336 | bytes 8000000 | tf_op jit(solution)/shard_map/encoder_ffn_near/pallas_call | solution.py:438
  61.3 4.5 %encoder_ffn_far.1.encoded = bf16[1024,896]{1,0:T(8,128)(2,1)S(1)} custom-call(f32[1,896]{1,0:T(1,128)S(1)} %reshape.19.gain, f32[1024,896]{1,0:T(8,128)S(1)} %get-tuple-element.50.before, bf16[1024,896]{1,0:T(8,128)(2,1)S(1)} %get-tuple-element.51.refs_0_, bf16[448,896]{1,0:T(8,128)(2,1)S(1)} %collective-permute-done.8.refs_1_, ...), custom_call_target="tpu_custom_call" | custom-call | flops 3288334336 | bytes 8000000 | tf_op jit(solution)/shard_map/encoder_ffn_far/pallas_call | solution.py:448
  65.7 0.6 collective-permute-start.23
  66.8 2.3 %decoder_pairs.1.own_pairs = bf16[1024,1024]{1,0:T(8,128)(2,1)S(1)} custom-call(bf16[1024,896]{1,0:T(8,128)(2,1)S(1)} %encoder_ffn_far.1.encoded, bf16[896,1024]{1,0:T(8,128)(2,1)S(1)} %bitcast.10), custom_call_target="tpu_custom_call" | custom-call | flops 1879048192 | bytes 8000000 | tf_op jit(solution)/shard_map/decoder_pairs/pallas_call | solution.py:460
  69.2 0.6 collective-permute-done.23.other
  69.7 5.0 %decoder_attention.1 = f32[512,512]{1,0:T(8,128)} custom-call(s32[1]{0:T(128)} %bitcast.here.seq_index.first, bf16[1024,1024]{1,0:T(8,128)(2,1)S(1)} %decoder_pairs.1.own_pairs, bf16[1024,896]{1,0:T(8,128)(2,1)S(1)} %collective-permute-done.23.other, bf16[896,1024]{1,0:T(8,128)(2,1)S(1)} %bitcast.11, bf16[512,512]{1,0:T(8,128)(2,1)S(1)} %copy-done.4), custom_call_target="tpu_custom_call" | custom-call | flops 1879048192 | bytes 8000000 | tf_op jit(solution)/shard_map/decoder_attention/pallas_call | solution.py:468
  (55 shorter events, 2.3 us)
Async XLA Ops:
  0.0 27.5 %copy-start = (bf16[896,224]{0,1:T(8,128)(2,1)S(1)}, bf16[896,224]{0,1:T(8,128)(2,1)}, u32[]{:S(2)}) copy-start(bf16[896,224]{0,1:T(8,128)(2,1)} %param.18) | copy-start | bytes 1204228
  0.0 27.5 %copy-start.9 = (bf16[512,2,224]{0,2,1:T(8,128)(2,1)S(1)}, bf16[512,2,224]{0,2,1:T(8,128)(2,1)}, u32[]{:S(2)}) copy-start(bf16[512,2,224]{0,2,1:T(8,128)(2,1)} %param.12) | copy-start | bytes 1376260
  0.0 32.4 %copy-start.1 = (bf16[224,896]{1,0:T(8,128)(2,1)S(1)}, bf16[224,896]{1,0:T(8,128)(2,1)}, u32[]{:S(2)}) copy-start(bf16[224,896]{1,0:T(8,128)(2,1)} %refs_1_.2) | copy-start | bytes 1204228
  0.0 32.4 %copy-start.10 = (f32[896]{0:T(1024)S(1)}, f32[896]{0:T(1024)}, u32[]{:S(2)}) copy-start(f32[896]{0:T(1024)} %param.17) | copy-start | bytes 10756
  0.0 32.4 %copy-start.11 = (f32[896]{0:T(1024)S(1)}, f32[896]{0:T(1024)}, u32[]{:S(2)}) copy-start(f32[896]{0:T(1024)} %param.20) | copy-start | bytes 10756
  0.0 37.8 %copy-start.6 = (s32[8,2]{0,1:T(2,128)S(1)}, s32[8,2]{0,1:T(2,128)}, u32[]{:S(2)}) copy-start(s32[8,2]{0,1:T(2,128)} %param.16) | copy-start | bytes 196
  0.0 37.8 %copy-start.7 = (s32[8,2]{0,1:T(2,128)S(1)}, s32[8,2]{0,1:T(2,128)}, u32[]{:S(2)}) copy-start(s32[8,2]{0,1:T(2,128)} %param.15) | copy-start | bytes 196
  3.3 11.8 %collective-permute-start = (bf16[2,64,896]{2,1,0:T(8,128)(2,1)}, bf16[2,64,896]{2,1,0:T(8,128)(2,1)S(1)}, u32[]{:S(2)}, u32[]{:S(2)}) collective-permute-start(bf16[2,64,896]{2,1,0:T(8,128)(2,1)} %get-tuple-element.30.refs_0_), channel_id=1, source_target_pairs={{0,8},{4,12},{8,16},{12,20},{16,24},{20,28},{24,0},{28,4},{1,9},{5... | collective-permute-start | bytes 688136 | tf_op jit(solution)/shard_map/ppermute | solution.py:307
  6.4 26.0 %collective-permute-start.8 = (bf16[448,896]{1,0:T(8,128)(2,1)}, bf16[448,896]{1,0:T(8,128)(2,1)S(1)}, u32[]{:S(2)}, u32[]{:S(2)}) collective-permute-start(bf16[448,896]{1,0:T(8,128)(2,1)} %get-tuple-element.37), channel_id=1, source_target_pairs={{0,2},{1,3},{2,0},{3,1},{4,6},{5,7},{6,4},{7,5},{8,10},{9,11},{10,... | collective-permute-start | bytes 2408456 | tf_op jit(solution)/shard_map/ppermute | solution.py:298
  7.9 8.9 %collective-permute-start.1 = (bf16[2,64,896]{2,1,0:T(8,128)(2,1)}, bf16[2,64,896]{2,1,0:T(8,128)(2,1)S(1)}, u32[]{:S(2)}, u32[]{:S(2)}) collective-permute-start(bf16[2,64,896]{2,1,0:T(8,128)(2,1)} %get-tuple-element.30.refs_0_), channel_id=1, source_target_pairs={{0,4},{4,0},{8,12},{12,8},{16,20},{20,16},{24,28},{28,24},{1,5},{5... | collective-permute-start | bytes 688136 | tf_op jit(solution)/shard_map/ppermute | solution.py:301
  9.4 9.9 %collective-permute-start.6 = (bf16[2,64,896]{2,1,0:T(8,128)(2,1)}, bf16[2,64,896]{2,1,0:T(8,128)(2,1)S(1)}, u32[]{:S(2)}, u32[]{:S(2)}) collective-permute-start(bf16[2,64,896]{2,1,0:T(8,128)(2,1)} %get-tuple-element.30.refs_0_), channel_id=1, source_target_pairs={{0,24},{4,28},{8,0},{12,4},{16,8},{20,12},{24,16},{28,20},{1,25},{... | collective-permute-start | bytes 688136 | tf_op jit(solution)/shard_map/ppermute | solution.py:307
  15.1 6.2 %collective-permute-start.3 = (bf16[2,64,896]{2,1,0:T(8,128)(2,1)S(1)}, bf16[2,64,896]{2,1,0:T(8,128)(2,1)S(1)}, u32[]{:S(2)}, u32[]{:S(2)}) collective-permute-start(bf16[2,64,896]{2,1,0:T(8,128)(2,1)S(1)} %collective-permute-done.refs_2_), channel_id=1, source_target_pairs={{0,4},{4,0},{8,12},{12,8},{16,20},{20,16},{24,28},{28,24},{1,5},{5... | collective-permute-start | bytes 688136 | tf_op jit(solution)/shard_map/ppermute | solution.py:301
  16.8 8.6 %collective-permute-start.4 = (bf16[2,64,896]{2,1,0:T(8,128)(2,1)S(1)}, bf16[2,64,896]{2,1,0:T(8,128)(2,1)S(1)}, u32[]{:S(2)}, u32[]{:S(2)}) collective-permute-start(bf16[2,64,896]{2,1,0:T(8,128)(2,1)S(1)} %collective-permute-done.refs_2_), channel_id=1, source_target_pairs={{0,8},{4,12},{8,16},{12,20},{16,24},{20,28},{24,0},{28,4},{1,9},{5... | collective-permute-start | bytes 688136 | tf_op jit(solution)/shard_map/ppermute | solution.py:307
  16.8 10.7 %collective-permute-start.2 = (bf16[2,240,64]{2,1,0:T(8,128)(2,1)}, bf16[2,240,64]{2,1,0:T(8,128)(2,1)S(1)}, u32[]{:S(2)}, u32[]{:S(2)}) collective-permute-start(bf16[2,240,64]{2,1,0:T(8,128)(2,1)} %get-tuple-element.33), channel_id=1, source_target_pairs={{0,4},{4,8},{8,12},{12,16},{16,20},{20,24},{24,28},{1,5},{5,9},{9,... | collective-permute-start | bytes 184328 | tf_op jit(solution)/shard_map/ppermute | solution.py:310
  21.2 8.7 %collective-permute-start.7 = (bf16[2,64,896]{2,1,0:T(8,128)(2,1)S(1)}, bf16[2,64,896]{2,1,0:T(8,128)(2,1)S(1)}, u32[]{:S(2)}, u32[]{:S(2)}) collective-permute-start(bf16[2,64,896]{2,1,0:T(8,128)(2,1)S(1)} %collective-permute-done.6.refs_6_), channel_id=1, source_target_pairs={{0,4},{4,0},{8,12},{12,8},{16,20},{20,16},{24,28},{28,24},{1,5},{5... | collective-permute-start | bytes 688136 | tf_op jit(solution)/shard_map/ppermute | solution.py:301
  25.4 6.9 %collective-permute-start.5 = (bf16[2,64,896]{2,1,0:T(8,128)(2,1)S(1)}, bf16[2,64,896]{2,1,0:T(8,128)(2,1)S(1)}, u32[]{:S(2)}, u32[]{:S(2)}) collective-permute-start(bf16[2,64,896]{2,1,0:T(8,128)(2,1)S(1)} %collective-permute-done.4.refs_4_), channel_id=1, source_target_pairs={{0,4},{4,0},{8,12},{12,8},{16,20},{20,16},{24,28},{28,24},{1,5},{5... | collective-permute-start | bytes 688136 | tf_op jit(solution)/shard_map/ppermute | solution.py:301
  25.6 9.0 %collective-permute-start.12 = (bf16[224,896]{1,0:T(8,128)(2,1)}, bf16[224,896]{1,0:T(8,128)(2,1)S(1)}, u32[]{:S(2)}, u32[]{:S(2)}) collective-permute-start(bf16[224,896]{1,0:T(8,128)(2,1)} %get-tuple-element.43), channel_id=1, source_target_pairs={{0,2},{1,3},{2,0},{3,1},{4,6},{5,7},{6,4},{7,5},{8,10},{9,11},{10,... | collective-permute-start | bytes 1204232 | tf_op jit(solution)/shard_map/ppermute | solution.py:298
  27.5 9.1 %collective-permute-start.9 = (bf16[224,896]{1,0:T(8,128)(2,1)S(1)}, bf16[224,896]{1,0:T(8,128)(2,1)S(1)}, u32[]{:S(2)}, u32[]{:S(2)}) collective-permute-start(bf16[224,896]{1,0:T(8,128)(2,1)S(1)} %bitcast.13), channel_id=1, source_target_pairs={{0,1},{1,0},{2,3},{3,2},{4,5},{5,4},{6,7},{7,6},{8,9},{9,8},{10,11... | collective-permute-start | bytes 1204232 | tf_op jit(solution)/shard_map/ppermute | solution.py:295
  29.9 11.4 %collective-permute-start.11 = (bf16[2,224,512]{2,1,0:T(8,128)(2,1)S(1)}, bf16[2,224,512]{2,1,0:T(8,128)(2,1)S(1)}, u32[]{:S(2)}, u32[]{:S(2)}) collective-permute-start(bf16[2,224,512]{2,1,0:T(8,128)(2,1)S(1)} %pad_maximum_fusion.refs_4_), channel_id=1, source_target_pairs={{0,1},{1,0},{2,3},{3,2},{4,5},{5,4},{6,7},{7,6},{8,9},{9,8},{10,11... | collective-permute-start | bytes 1376264 | tf_op jit(solution)/shard_map/ppermute | solution.py:295
  32.4 8.9 %collective-permute-start.10 = (bf16[224,896]{1,0:T(8,128)(2,1)S(1)}, bf16[224,896]{1,0:T(8,128)(2,1)S(1)}, u32[]{:S(2)}, u32[]{:S(2)}) collective-permute-start(bf16[224,896]{1,0:T(8,128)(2,1)S(1)} %copy-done.1), channel_id=1, source_target_pairs={{0,1},{1,0},{2,3},{3,2},{4,5},{5,4},{6,7},{7,6},{8,9},{9,8},{10,11... | collective-permute-start | bytes 1204232 | tf_op jit(solution)/shard_map/ppermute | solution.py:295
  32.4 13.1 %collective-permute-start.16 = (bf16[2,224,512]{2,1,0:T(8,128)(2,1)S(1)}, bf16[2,224,512]{2,1,0:T(8,128)(2,1)S(1)}, u32[]{:S(2)}, u32[]{:S(2)}) collective-permute-start(bf16[2,224,512]{2,1,0:T(8,128)(2,1)S(1)} %pad_maximum_fusion.refs_4_), channel_id=1, source_target_pairs={{0,2},{1,3},{2,0},{3,1},{4,6},{5,7},{6,4},{7,5},{8,10},{9,11},{10,... | collective-permute-start | bytes 1376264 | tf_op jit(solution)/shard_map/ppermute | solution.py:298
  34.6 11.7 %collective-permute-start.13 = (bf16[224,896]{1,0:T(8,128)(2,1)S(1)}, bf16[224,896]{1,0:T(8,128)(2,1)S(1)}, u32[]{:S(2)}, u32[]{:S(2)}) collective-permute-start(bf16[224,896]{1,0:T(8,128)(2,1)S(1)} %collective-permute-done.12.refs_0_), channel_id=1, source_target_pairs={{0,4},{4,0},{8,12},{12,8},{16,20},{20,16},{24,28},{28,24},{1,5},{5... | collective-permute-start | bytes 1204232 | tf_op jit(solution)/shard_map/ppermute | solution.py:301
  36.6 19.7 %collective-permute-start.21 = (bf16[448,896]{1,0:T(8,128)(2,1)S(1)}, bf16[448,896]{1,0:T(8,128)(2,1)S(1)}, u32[]{:S(2)}, u32[]{:S(2)}) collective-permute-start(bf16[448,896]{1,0:T(8,128)(2,1)S(1)} %collective-permute-done.8.refs_1_), channel_id=1, source_target_pairs={{0,8},{4,12},{8,0},{12,4},{16,24},{20,28},{24,16},{28,20},{1,9},{5... | collective-permute-start | bytes 2408456 | tf_op jit(solution)/shard_map/ppermute | solution.py:304
  41.3 5.5 %collective-permute-start.14 = (bf16[224,896]{1,0:T(8,128)(2,1)S(1)}, bf16[224,896]{1,0:T(8,128)(2,1)S(1)}, u32[]{:S(2)}, u32[]{:S(2)}) collective-permute-start(bf16[224,896]{1,0:T(8,128)(2,1)S(1)} %collective-permute-done.12.refs_0_), channel_id=1, source_target_pairs={{0,1},{1,0},{2,3},{3,2},{4,5},{5,4},{6,7},{7,6},{8,9},{9,8},{10,11... | collective-permute-start | bytes 1204232 | tf_op jit(solution)/shard_map/ppermute | solution.py:295
  41.4 5.4 %copy-start.3 = (bf16[448,896]{1,0:T(8,128)(2,1)S(1)}, bf16[448,896]{1,0:T(8,128)(2,1)}, u32[]{:S(2)}) copy-start(bf16[448,896]{1,0:T(8,128)(2,1)} %refs_1_.3) | copy-start | bytes 2408452
  45.5 2.6 %collective-permute-start.17 = (bf16[2,224,512]{2,1,0:T(8,128)(2,1)S(1)}, bf16[2,224,512]{2,1,0:T(8,128)(2,1)S(1)}, u32[]{:S(2)}, u32[]{:S(2)}) collective-permute-start(bf16[2,224,512]{2,1,0:T(8,128)(2,1)S(1)} %collective-permute-done.16.refs_4_), channel_id=1, source_target_pairs={{0,1},{1,0},{2,3},{3,2},{4,5},{5,4},{6,7},{7,6},{8,9},{9,8},{10,11... | collective-permute-start | bytes 1376264 | tf_op jit(solution)/shard_map/ppermute | solution.py:295
  46.3 1.8 %collective-permute-start.15 = (bf16[224,896]{1,0:T(8,128)(2,1)S(1)}, bf16[224,896]{1,0:T(8,128)(2,1)S(1)}, u32[]{:S(2)}, u32[]{:S(2)}) collective-permute-start(bf16[224,896]{1,0:T(8,128)(2,1)S(1)} %collective-permute-done.13.refs_1_), channel_id=1, source_target_pairs={{0,1},{1,0},{2,3},{3,2},{4,5},{5,4},{6,7},{7,6},{8,9},{9,8},{10,11... | collective-permute-start | bytes 1204232 | tf_op jit(solution)/shard_map/ppermute | solution.py:295
  46.3 10.1 %collective-permute-start.18 = (bf16[448,896]{1,0:T(8,128)(2,1)S(1)}, bf16[448,896]{1,0:T(8,128)(2,1)S(1)}, u32[]{:S(2)}, u32[]{:S(2)}) collective-permute-start(bf16[448,896]{1,0:T(8,128)(2,1)S(1)} %bitcast.16), channel_id=1, source_target_pairs={{0,1},{1,0},{2,3},{3,2},{4,5},{5,4},{6,7},{7,6},{8,9},{9,8},{10,11... | collective-permute-start | bytes 2408456 | tf_op jit(solution)/shard_map/ppermute | solution.py:295
  46.8 9.6 %collective-permute-start.19 = (bf16[448,896]{1,0:T(8,128)(2,1)S(1)}, bf16[448,896]{1,0:T(8,128)(2,1)S(1)}, u32[]{:S(2)}, u32[]{:S(2)}) collective-permute-start(bf16[448,896]{1,0:T(8,128)(2,1)S(1)} %copy-done.3), channel_id=1, source_target_pairs={{0,1},{1,0},{2,3},{3,2},{4,5},{5,4},{6,7},{7,6},{8,9},{9,8},{10,11... | collective-permute-start | bytes 2408456 | tf_op jit(solution)/shard_map/ppermute | solution.py:295
  52.3 9.0 %collective-permute-start.20 = (bf16[448,896]{1,0:T(8,128)(2,1)S(1)}, bf16[448,896]{1,0:T(8,128)(2,1)S(1)}, u32[]{:S(2)}, u32[]{:S(2)}) collective-permute-start(bf16[448,896]{1,0:T(8,128)(2,1)S(1)} %collective-permute-done.8.refs_1_), channel_id=1, source_target_pairs={{0,1},{1,0},{2,3},{3,2},{4,5},{5,4},{6,7},{7,6},{8,9},{9,8},{10,11... | collective-permute-start | bytes 2408456 | tf_op jit(solution)/shard_map/ppermute | solution.py:295
  56.4 4.9 %collective-permute-start.22 = (bf16[448,896]{1,0:T(8,128)(2,1)S(1)}, bf16[448,896]{1,0:T(8,128)(2,1)S(1)}, u32[]{:S(2)}, u32[]{:S(2)}) collective-permute-start(bf16[448,896]{1,0:T(8,128)(2,1)S(1)} %collective-permute-done.21.refs_3_), channel_id=1, source_target_pairs={{0,1},{1,0},{2,3},{3,2},{4,5},{5,4},{6,7},{7,6},{8,9},{9,8},{10,11... | collective-permute-start | bytes 2408456 | tf_op jit(solution)/shard_map/ppermute | solution.py:295
  65.7 4.0 %collective-permute-start.23 = (bf16[1024,896]{1,0:T(8,128)(2,1)S(1)}, bf16[1024,896]{1,0:T(8,128)(2,1)S(1)}, u32[]{:S(2)}, u32[]{:S(2)}) collective-permute-start(bf16[1024,896]{1,0:T(8,128)(2,1)S(1)} %encoder_ffn_far.1.encoded), channel_id=1, source_target_pairs={{0,1},{1,0},{2,3},{3,2},{4,5},{5,4},{6,7},{7,6},{8,9},{9,8},{10,11... | collective-permute-start | bytes 5505032 | tf_op jit(solution)/shard_map/ppermute | solution.py:295
  (4 other events, 13.8 us)

commit v7 on v6

--- a/solution.py
+++ b/solution.py
@@ -29,7 +29,7 @@
     "cyf": ("far",),
     "cyk": ("near",),
     "czf": ("far",),
-    "near": ("yf",),
+    "near": ("yf", "wk"),
     "wk": ("ya",),
     "gains": ("zn",),
 }
@@ -220,7 +220,7 @@
     pairs[...] = mxu(encoded[...], weights[...], NN).astype(jnp.bfloat16)
 
 
-def decoder_kernel(first, own_pairs, other, weights, queries, out, other_pairs):
+def decoder_kernel(first, own_pairs, other, weights, queries, out, other_pairs, held, sems):
     rows = other.shape[0]
     part = rows // CH_DEV
     width = queries.shape[1]
@@ -234,6 +234,7 @@
         )
 
     ones = jnp.ones((2 * part, HEAD_DIM), jnp.bfloat16)
+    copies = []
     for head in range(width // HEAD_DIM):
         col = head * HEAD_DIM
         query = (queries[:, col : col + HEAD_DIM].astype(jnp.float32) * scale).astype(jnp.bfloat16)
@@ -251,7 +252,13 @@
             result = result[:, :HEAD_DIM] / result[:, HEAD_DIM:]
             if span == 0:
                 result = jnp.where(first[0] == 0, jnp.zeros_like(result), result)
-            out[span * SPAN : (span + 1) * SPAN, col : col + HEAD_DIM] = result
+            held[head, span * SPAN : (span + 1) * SPAN, :] = result
+        copies.append(
+            pltpu.make_async_copy(held.at[head], out.at[:, pl.ds(col, HEAD_DIM)], sems.at[head])
+        )
+        copies[-1].start()
+    for copy in copies:
+        copy.wait()
 
 
 def call(body, out_shape, in_specs, name, flops, vmem_mib, scratch=(), out="v"):
@@ -330,7 +337,7 @@
         "ssss" + "h" * 6,
         "prepare",
         rows * width,
-        60,
+        53,
         scratch=[
             pltpu.VMEM((entries_here, half_rows, width), jnp.float32),
             pltpu.VMEM((entries_here, half_rows, width), jnp.bfloat16),
@@ -472,7 +479,12 @@
         "decoder_attention",
         pairs_flops,
         28,
-        scratch=[pltpu.VMEM(pairs_shape, jnp.bfloat16)],
+        scratch=[
+            pltpu.VMEM(pairs_shape, jnp.bfloat16),
+            pltpu.VMEM((dec_width // HEAD_DIM, dec_queries.shape[0], HEAD_DIM), jnp.float32),
+            dma((dec_width // HEAD_DIM,)),
+        ],
+        out="h",
     )(here, own_pairs, other, got("wk"), dec_queries)
 
 

time: 75.7 us -> 77.5 us (1.024)
  waiting for transfers between devices: 17.6 us -> 19.1 us
    ppermute x11, starting transfers between devices: 2.22 us -> 1.44 us  [core_swap(): return lax.ppermute(array, 'mp', [(i, i ^ 1) for i in range(lanes)])]
    unnamed x25 -> x23, local copies, waits for them, and re-layouts: 1.48 us -> 1.89 us
  transfers between devices with their start and end apart: 24 -> 24, of which waited for: 11 -> 12; matrix products, arithmetic and copies ran while one was open for 1% -> 1% of each run, Pallas kernels for 24% -> 23%
where the time goes in v7:
time: 77.5 us; the launch traced here: 76.5 us
  Pallas kernels  30.7 us (40%)
  starting transfers between devices  24 us (31%)
  waiting for transfers between devices  19.1 us (25%)
  local copies, waits for them, and re-layouts  1.9 us (2%)
    ppermute x5, starting transfers between devices, seq_swap(): return lax.ppermute(array, 'seq', [(i, i ^ 1) for i in range(seq_size)])  8.94 us
    pallas_call x2, Pallas kernels, attention(): call(functools.partial(attention_kernel, len(kv), far), long_rows, 'svv'...  8.27 us
    ppermute x5, waiting for transfers between devices, seq_swap(): return lax.ppermute(array, 'seq', [(i, i ^ 1) for i in range(seq_size)])  7.3 us
    ppermute x3, starting transfers between devices, seq_ring(): lax.ppermute(array, 'seq', [(i, (i + 2 * way) % seq_size) for i in range(...  5.33 us
    ppermute x3, starting transfers between devices, lane_step(): lax.ppermute(array, 'mp', [(i, (i + 2 * step) % lanes) for i in range(lan...  5.01 us
    pallas_call x1, Pallas kernels, on_device(): call(functools.partial(ffn_kernel, False, True), (long_rows, short_rows),...  4.83 us
    pallas_call x1, Pallas kernels, on_device(): call(decoder_kernel, jax.ShapeDtypeStruct(dec_queries.shape, jnp.float32)...  4.8 us
    ppermute x3, waiting for transfers between devices, seq_ring(): lax.ppermute(array, 'seq', [(i, (i + 2 * way) % seq_size) for i in range(...  4.66 us
  transfers between devices with their start and end apart: 24, of which 12 were waited for; matrix products, arithmetic and copies ran while one was open for 1% of the time, Pallas kernels for 23%

profile of v7, /device:TPU:0, one launch (start us, length us, event | category | flops | bytes accessed | tf_op | source)
XLA Modules:
  0.0 76.5 jit_solution(982430276684894357)
XLA Ops:
  0.0 0.7 copy-done.5
  0.7 0.7 copy-done.6
  1.4 3.5 %prepare.1 = (bf16[2,64,896]{2,1,0:T(8,128)(2,1)S(1)}, bf16[224,896]{1,0:T(8,128)(2,1)S(1)}, bf16[448,896]{1,0:T(8,128)(2,1)}, bf16[2,240,64]{2,1,0:T(8,128)(2,1)S(1)}) custom-call(s32[1]{0:T(128)} %bitcast.here.seq_index.first, s32[1]{0:T(128)} %bitcast.1.lane_here, s32[2,8]{1,0:T(2,128)S(1)} %bitcast.18, s32[2,8]{1,0:T(2,128)S(1)} %bitcast.20, ...), custom_call_target="tpu_custom_call" | custom-call | flops 917504 | bytes 8000000 | tf_op jit(solution)/shard_map/prepare/pallas_call | solution.py:329
  4.9 3.1 %collective-permute-start = (bf16[2,64,896]{2,1,0:T(8,128)(2,1)S(1)}, bf16[2,64,896]{2,1,0:T(8,128)(2,1)S(1)}, u32[]{:S(2)}, u32[]{:S(2)}) collective-permute-start(bf16[2,64,896]{2,1,0:T(8,128)(2,1)S(1)} %get-tuple-element.30.refs_0_), channel_id=1, source_target_pairs={{0,8},{4,12},{8,16},{12,20},{16,24},{20,28},{24,0},{28,4},{1,9},{5... | collective-permute-start | bytes 688136 | tf_op jit(solution)/shard_map/ppermute | solution.py:314
  8.0 1.5 %collective-permute-start.8 = (bf16[448,896]{1,0:T(8,128)(2,1)}, bf16[448,896]{1,0:T(8,128)(2,1)S(1)}, u32[]{:S(2)}, u32[]{:S(2)}) collective-permute-start(bf16[448,896]{1,0:T(8,128)(2,1)} %get-tuple-element.37), channel_id=1, source_target_pairs={{0,2},{1,3},{2,0},{3,1},{4,6},{5,7},{6,4},{7,5},{8,10},{9,11},{10,... | collective-permute-start | bytes 2408456 | tf_op jit(solution)/shard_map/ppermute | solution.py:305
  9.5 1.5 %collective-permute-start.1 = (bf16[2,64,896]{2,1,0:T(8,128)(2,1)S(1)}, bf16[2,64,896]{2,1,0:T(8,128)(2,1)S(1)}, u32[]{:S(2)}, u32[]{:S(2)}) collective-permute-start(bf16[2,64,896]{2,1,0:T(8,128)(2,1)S(1)} %get-tuple-element.30.refs_0_), channel_id=1, source_target_pairs={{0,4},{4,0},{8,12},{12,8},{16,20},{20,16},{24,28},{28,24},{1,5},{5... | collective-permute-start | bytes 688136 | tf_op jit(solution)/shard_map/ppermute | solution.py:308
  11.0 2.2 %collective-permute-start.6 = (bf16[2,64,896]{2,1,0:T(8,128)(2,1)S(1)}, bf16[2,64,896]{2,1,0:T(8,128)(2,1)S(1)}, u32[]{:S(2)}, u32[]{:S(2)}) collective-permute-start(bf16[2,64,896]{2,1,0:T(8,128)(2,1)S(1)} %get-tuple-element.30.refs_0_), channel_id=1, source_target_pairs={{0,24},{4,28},{8,0},{12,4},{16,8},{20,12},{24,16},{28,20},{1,25},{... | collective-permute-start | bytes 688136 | tf_op jit(solution)/shard_map/ppermute | solution.py:314
  13.2 3.2 %collective-permute-done.refs_2_ = bf16[2,64,896]{2,1,0:T(8,128)(2,1)S(1)} collective-permute-done((bf16[2,64,896]{2,1,0:T(8,128)(2,1)S(1)}, bf16[2,64,896]{2,1,0:T(8,128)(2,1)S(1)}, u32[]{:S(2)}, u32[]{:S(2)}) %collective-permute-start) | collective-permute-done | bytes 229408 | tf_op jit(solution)/shard_map/ppermute | solution.py:314
  16.4 1.8 %collective-permute-start.3 = (bf16[2,64,896]{2,1,0:T(8,128)(2,1)S(1)}, bf16[2,64,896]{2,1,0:T(8,128)(2,1)S(1)}, u32[]{:S(2)}, u32[]{:S(2)}) collective-permute-start(bf16[2,64,896]{2,1,0:T(8,128)(2,1)S(1)} %collective-permute-done.refs_2_), channel_id=1, source_target_pairs={{0,4},{4,0},{8,12},{12,8},{16,20},{20,16},{24,28},{28,24},{1,5},{5... | collective-permute-start | bytes 688136 | tf_op jit(solution)/shard_map/ppermute | solution.py:308
  18.2 2.1 %collective-permute-start.2 = (bf16[2,240,64]{2,1,0:T(8,128)(2,1)S(1)}, bf16[2,240,64]{2,1,0:T(8,128)(2,1)S(1)}, u32[]{:S(2)}, u32[]{:S(2)}) collective-permute-start(bf16[2,240,64]{2,1,0:T(8,128)(2,1)S(1)} %get-tuple-element.33), channel_id=1, source_target_pairs={{0,4},{4,8},{8,12},{12,16},{16,20},{20,24},{24,28},{1,5},{5,9},{9,... | collective-permute-start | bytes 184328 | tf_op jit(solution)/shard_map/ppermute | solution.py:317
  20.7 1.8 %collective-permute-done.3.refs_3_ = bf16[2,64,896]{2,1,0:T(8,128)(2,1)S(1)} collective-permute-done((bf16[2,64,896]{2,1,0:T(8,128)(2,1)S(1)}, bf16[2,64,896]{2,1,0:T(8,128)(2,1)S(1)}, u32[]{:S(2)}, u32[]{:S(2)}) %collective-permute-start.3) | collective-permute-done | bytes 229408 | tf_op jit(solution)/shard_map/ppermute | solution.py:308
  22.5 3.1 %collective-permute-start.7 = (bf16[2,64,896]{2,1,0:T(8,128)(2,1)S(1)}, bf16[2,64,896]{2,1,0:T(8,128)(2,1)S(1)}, u32[]{:S(2)}, u32[]{:S(2)}) collective-permute-start(bf16[2,64,896]{2,1,0:T(8,128)(2,1)S(1)} %collective-permute-done.6.refs_6_), channel_id=1, source_target_pairs={{0,4},{4,0},{8,12},{12,8},{16,20},{20,16},{24,28},{28,24},{1,5},{5... | collective-permute-start | bytes 688136 | tf_op jit(solution)/shard_map/ppermute | solution.py:308
  25.6 1.2 %collective-permute-done.4.refs_4_ = bf16[2,64,896]{2,1,0:T(8,128)(2,1)S(1)} collective-permute-done((bf16[2,64,896]{2,1,0:T(8,128)(2,1)S(1)}, bf16[2,64,896]{2,1,0:T(8,128)(2,1)S(1)}, u32[]{:S(2)}, u32[]{:S(2)}) %collective-permute-start.4) | collective-permute-done | bytes 229408 | tf_op jit(solution)/shard_map/ppermute | solution.py:314
  26.9 1.9 %collective-permute-start.9 = (bf16[224,896]{1,0:T(8,128)(2,1)S(1)}, bf16[224,896]{1,0:T(8,128)(2,1)S(1)}, u32[]{:S(2)}, u32[]{:S(2)}) collective-permute-start(bf16[224,896]{1,0:T(8,128)(2,1)S(1)} %get-tuple-element.38), channel_id=1, source_target_pairs={{0,2},{1,3},{2,0},{3,1},{4,6},{5,7},{6,4},{7,5},{8,10},{9,11},{10,... | collective-permute-start | bytes 1204232 | tf_op jit(solution)/shard_map/ppermute | solution.py:305
  29.1 2.0 %collective-permute-done.7.refs_7_ = bf16[2,64,896]{2,1,0:T(8,128)(2,1)S(1)} collective-permute-done((bf16[2,64,896]{2,1,0:T(8,128)(2,1)S(1)}, bf16[2,64,896]{2,1,0:T(8,128)(2,1)S(1)}, u32[]{:S(2)}, u32[]{:S(2)}) %collective-permute-start.7) | collective-permute-done | bytes 229408 | tf_op jit(solution)/shard_map/ppermute | solution.py:308
  31.2 2.5 %collective-permute-done.5.refs_5_ = bf16[2,64,896]{2,1,0:T(8,128)(2,1)S(1)} collective-permute-done((bf16[2,64,896]{2,1,0:T(8,128)(2,1)S(1)}, bf16[2,64,896]{2,1,0:T(8,128)(2,1)S(1)}, u32[]{:S(2)}, u32[]{:S(2)}) %collective-permute-start.5) | collective-permute-done | bytes 229408 | tf_op jit(solution)/shard_map/ppermute | solution.py:308
  34.2 1.6 %collective-permute-start.16 = (bf16[2,224,512]{2,1,0:T(8,128)(2,1)S(1)}, bf16[2,224,512]{2,1,0:T(8,128)(2,1)S(1)}, u32[]{:S(2)}, u32[]{:S(2)}) collective-permute-start(bf16[2,224,512]{2,1,0:T(8,128)(2,1)S(1)} %pad_maximum_fusion.refs_4_), channel_id=1, source_target_pairs={{0,2},{1,3},{2,0},{3,1},{4,6},{5,7},{6,4},{7,5},{8,10},{9,11},{10,... | collective-permute-start | bytes 1376264 | tf_op jit(solution)/shard_map/ppermute | solution.py:305
  36.1 2.4 %collective-permute-start.13 = (bf16[224,896]{1,0:T(8,128)(2,1)S(1)}, bf16[224,896]{1,0:T(8,128)(2,1)S(1)}, u32[]{:S(2)}, u32[]{:S(2)}) collective-permute-start(bf16[224,896]{1,0:T(8,128)(2,1)S(1)} %collective-permute-done.9.refs_0_), channel_id=1, source_target_pairs={{0,4},{4,0},{8,12},{12,8},{16,20},{20,16},{24,28},{28,24},{1,5},{5... | collective-permute-start | bytes 1204232 | tf_op jit(solution)/shard_map/ppermute | solution.py:308
  38.5 1.1 %collective-permute-start.21 = (bf16[448,896]{1,0:T(8,128)(2,1)S(1)}, bf16[448,896]{1,0:T(8,128)(2,1)S(1)}, u32[]{:S(2)}, u32[]{:S(2)}) collective-permute-start(bf16[448,896]{1,0:T(8,128)(2,1)S(1)} %collective-permute-done.8.refs_1_), channel_id=1, source_target_pairs={{0,8},{4,12},{8,0},{12,4},{16,24},{20,28},{24,16},{28,20},{1,9},{5... | collective-permute-start | bytes 2408456 | tf_op jit(solution)/shard_map/ppermute | solution.py:311
  39.7 2.5 %neighbour_rows.1 = (bf16[1024,896]{1,0:T(8,128)(2,1)S(1)}, bf16[1024,896]{1,0:T(8,128)(2,1)S(1)}) custom-call(s32[1]{0:T(128)} %bitcast.here.seq_index.first, s32[2,8]{1,0:T(2,128)S(1)} %bitcast.19, s32[2,8]{1,0:T(2,128)S(1)} %bitcast.21, s32[2,1]{1,0:T(2,128)S(1)} %slice_add_fusion.before, f32[1,896]{1,0:T(1,128)S(1)} %reshape.18.gain, ...), custom_call_target="tpu_custom_call" | custom-call | flops 9175040 | bytes 8000000 | tf_op jit(solution)/shard_map/neighbour_rows/pallas_call | solution.py:418
  42.3 4.1 %encoder_attention.2.before = f32[1024,896]{1,0:T(8,128)S(1)} custom-call(s32[1]{0:T(128)} %bitcast.here.seq_index.first, bf16[1024,896]{1,0:T(8,128)(2,1)S(1)} %get-tuple-element.40.before, bf16[1024,896]{1,0:T(8,128)(2,1)S(1)} %get-tuple-element.41.normed_in, bf16[224,896]{1,0:T(8,128)(2,1)S(1)} %bitcast.14, bf16[224,896]{1,0:T(8,128)(2,1)S(1)} %copy-done.1, ...), custom_call_target="tpu_custom_call" | custom-call | flops 1644167168 | bytes 8000000 | tf_op jit(solution)/shard_map/encoder_attention/pallas_call | solution.py:428
  46.5 0.7 collective-permute-done.16.refs_4_
  47.2 1.0 %collective-permute-done.13.refs_1_ = bf16[224,896]{1,0:T(8,128)(2,1)S(1)} collective-permute-done((bf16[224,896]{1,0:T(8,128)(2,1)S(1)}, bf16[224,896]{1,0:T(8,128)(2,1)S(1)}, u32[]{:S(2)}, u32[]{:S(2)}) %collective-permute-start.13) | collective-permute-done | bytes 401440 | tf_op jit(solution)/shard_map/ppermute | solution.py:308
  48.8 1.1 %collective-permute-done.15.refs_3_ = bf16[224,896]{1,0:T(8,128)(2,1)S(1)} collective-permute-done((bf16[224,896]{1,0:T(8,128)(2,1)S(1)}, bf16[224,896]{1,0:T(8,128)(2,1)S(1)}, u32[]{:S(2)}, u32[]{:S(2)}) %collective-permute-start.15) | collective-permute-done | bytes 401440 | tf_op jit(solution)/shard_map/ppermute | solution.py:302
  49.9 4.1 %encoder_attention.3.before = f32[1024,896]{1,0:T(8,128)S(1)} custom-call(s32[1]{0:T(128)} %bitcast.here.seq_index.first, f32[1024,896]{1,0:T(8,128)S(1)} %encoder_attention.2.before, bf16[1024,896]{1,0:T(8,128)(2,1)S(1)} %get-tuple-element.41.normed_in, bf16[224,896]{1,0:T(8,128)(2,1)S(1)} %collective-permute-done.9.refs_0_, ...), custom_call_target="tpu_custom_call" | custom-call | flops 1644167168 | bytes 8000000 | tf_op jit(solution)/shard_map/encoder_attention/pallas_call | solution.py:428
  54.3 4.0 %collective-permute-done.21.refs_3_ = bf16[448,896]{1,0:T(8,128)(2,1)S(1)} collective-permute-done((bf16[448,896]{1,0:T(8,128)(2,1)S(1)}, bf16[448,896]{1,0:T(8,128)(2,1)S(1)}, u32[]{:S(2)}, u32[]{:S(2)}) %collective-permute-start.21) | collective-permute-done | bytes 802848 | tf_op jit(solution)/shard_map/ppermute | solution.py:311
  58.2 4.8 %encoder_ffn_near.1 = (f32[1024,896]{1,0:T(8,128)S(1)}, bf16[1024,896]{1,0:T(8,128)(2,1)S(1)}) custom-call(f32[1,896]{1,0:T(1,128)S(1)} %reshape.19.gain, f32[1024,896]{1,0:T(8,128)S(1)} %encoder_attention.3.before, bf16[448,896]{1,0:T(8,128)(2,1)S(1)} %bitcast.17, bf16[448,896]{1,0:T(8,128)(2,1)S(1)} %copy-done.3, ...), custom_call_target="tpu_custom_call" | custom-call | flops 3288334336 | bytes 8000000 | tf_op jit(solution)/shard_map/encoder_ffn_near/pallas_call | solution.py:445
  63.1 4.5 %encoder_ffn_far.1.encoded = bf16[1024,896]{1,0:T(8,128)(2,1)S(1)} custom-call(f32[1,896]{1,0:T(1,128)S(1)} %reshape.19.gain, f32[1024,896]{1,0:T(8,128)S(1)} %get-tuple-element.51.before, bf16[1024,896]{1,0:T(8,128)(2,1)S(1)} %get-tuple-element.52.refs_0_, bf16[448,896]{1,0:T(8,128)(2,1)S(1)} %collective-permute-done.8.refs_1_, ...), custom_call_target="tpu_custom_call" | custom-call | flops 3288334336 | bytes 8000000 | tf_op jit(solution)/shard_map/encoder_ffn_far/pallas_call | solution.py:455
  67.6 0.6 collective-permute-start.23
  68.1 2.3 %decoder_pairs.1.own_pairs = bf16[1024,1024]{1,0:T(8,128)(2,1)S(1)} custom-call(bf16[1024,896]{1,0:T(8,128)(2,1)S(1)} %encoder_ffn_far.1.encoded, bf16[896,1024]{1,0:T(8,128)(2,1)S(1)} %bitcast.10), custom_call_target="tpu_custom_call" | custom-call | flops 1879048192 | bytes 8000000 | tf_op jit(solution)/shard_map/decoder_pairs/pallas_call | solution.py:467
  70.5 1.1 %collective-permute-done.23.other = bf16[1024,896]{1,0:T(8,128)(2,1)S(1)} collective-permute-done((bf16[1024,896]{1,0:T(8,128)(2,1)S(1)}, bf16[1024,896]{1,0:T(8,128)(2,1)S(1)}, u32[]{:S(2)}, u32[]{:S(2)}) %collective-permute-start.23) | collective-permute-done | bytes 1835040 | tf_op jit(solution)/shard_map/ppermute | solution.py:302
  71.6 4.8 %decoder_attention.1 = f32[512,512]{1,0:T(8,128)} custom-call(s32[1]{0:T(128)} %bitcast.here.seq_index.first, bf16[1024,1024]{1,0:T(8,128)(2,1)S(1)} %decoder_pairs.1.own_pairs, bf16[1024,896]{1,0:T(8,128)(2,1)S(1)} %collective-permute-done.23.other, bf16[896,1024]{1,0:T(8,128)(2,1)S(1)} %bitcast.11, bf16[512,512]{1,0:T(8,128)(2,1)S(1)} %copy-done.4), custom_call_target="tpu_custom_call" | custom-call | flops 1879048192 | bytes 8000000 | tf_op jit(solution)/shard_map/decoder_attention/pallas_call | solution.py:475
  (53 shorter events, 2.6 us)
Async XLA Ops:
  1.4 27.5 %copy-start = (bf16[896,224]{0,1:T(8,128)(2,1)S(1)}, bf16[896,224]{0,1:T(8,128)(2,1)}, u32[]{:S(2)}) copy-start(bf16[896,224]{0,1:T(8,128)(2,1)} %param.18) | copy-start | bytes 1204228
  1.4 27.5 %copy-start.8 = (bf16[512,2,224]{0,2,1:T(8,128)(2,1)S(1)}, bf16[512,2,224]{0,2,1:T(8,128)(2,1)}, u32[]{:S(2)}) copy-start(bf16[512,2,224]{0,2,1:T(8,128)(2,1)} %param.12) | copy-start | bytes 1376260
  1.4 32.3 %copy-start.1 = (bf16[224,896]{1,0:T(8,128)(2,1)S(1)}, bf16[224,896]{1,0:T(8,128)(2,1)}, u32[]{:S(2)}) copy-start(bf16[224,896]{1,0:T(8,128)(2,1)} %refs_1_.2) | copy-start | bytes 1204228
  1.4 32.3 %copy-start.9 = (f32[896]{0:T(1024)S(1)}, f32[896]{0:T(1024)}, u32[]{:S(2)}) copy-start(f32[896]{0:T(1024)} %param.17) | copy-start | bytes 10756
  1.4 32.3 %copy-start.10 = (f32[896]{0:T(1024)S(1)}, f32[896]{0:T(1024)}, u32[]{:S(2)}) copy-start(f32[896]{0:T(1024)} %param.20) | copy-start | bytes 10756
  1.4 32.3 %copy-start.7 = (bf16[896,2,512]{2,1,0:T(2,128)(2,1)S(1)}, bf16[896,2,512]{2,1,0:T(2,128)(2,1)}, u32[]{:S(2)}) copy-start(bf16[896,2,512]{2,1,0:T(2,128)(2,1)} %param.23) | copy-start | bytes 5505028
  4.9 11.5 %collective-permute-start = (bf16[2,64,896]{2,1,0:T(8,128)(2,1)S(1)}, bf16[2,64,896]{2,1,0:T(8,128)(2,1)S(1)}, u32[]{:S(2)}, u32[]{:S(2)}) collective-permute-start(bf16[2,64,896]{2,1,0:T(8,128)(2,1)S(1)} %get-tuple-element.30.refs_0_), channel_id=1, source_target_pairs={{0,8},{4,12},{8,16},{12,20},{16,24},{20,28},{24,0},{28,4},{1,9},{5... | collective-permute-start | bytes 688136 | tf_op jit(solution)/shard_map/ppermute | solution.py:314
  8.0 26.2 %collective-permute-start.8 = (bf16[448,896]{1,0:T(8,128)(2,1)}, bf16[448,896]{1,0:T(8,128)(2,1)S(1)}, u32[]{:S(2)}, u32[]{:S(2)}) collective-permute-start(bf16[448,896]{1,0:T(8,128)(2,1)} %get-tuple-element.37), channel_id=1, source_target_pairs={{0,2},{1,3},{2,0},{3,1},{4,6},{5,7},{6,4},{7,5},{8,10},{9,11},{10,... | collective-permute-start | bytes 2408456 | tf_op jit(solution)/shard_map/ppermute | solution.py:305
  9.5 8.7 %collective-permute-start.1 = (bf16[2,64,896]{2,1,0:T(8,128)(2,1)S(1)}, bf16[2,64,896]{2,1,0:T(8,128)(2,1)S(1)}, u32[]{:S(2)}, u32[]{:S(2)}) collective-permute-start(bf16[2,64,896]{2,1,0:T(8,128)(2,1)S(1)} %get-tuple-element.30.refs_0_), channel_id=1, source_target_pairs={{0,4},{4,0},{8,12},{12,8},{16,20},{20,16},{24,28},{28,24},{1,5},{5... | collective-permute-start | bytes 688136 | tf_op jit(solution)/shard_map/ppermute | solution.py:308
  11.0 9.7 %collective-permute-start.6 = (bf16[2,64,896]{2,1,0:T(8,128)(2,1)S(1)}, bf16[2,64,896]{2,1,0:T(8,128)(2,1)S(1)}, u32[]{:S(2)}, u32[]{:S(2)}) collective-permute-start(bf16[2,64,896]{2,1,0:T(8,128)(2,1)S(1)} %get-tuple-element.30.refs_0_), channel_id=1, source_target_pairs={{0,24},{4,28},{8,0},{12,4},{16,8},{20,12},{24,16},{28,20},{1,25},{... | collective-permute-start | bytes 688136 | tf_op jit(solution)/shard_map/ppermute | solution.py:314
  16.4 6.1 %collective-permute-start.3 = (bf16[2,64,896]{2,1,0:T(8,128)(2,1)S(1)}, bf16[2,64,896]{2,1,0:T(8,128)(2,1)S(1)}, u32[]{:S(2)}, u32[]{:S(2)}) collective-permute-start(bf16[2,64,896]{2,1,0:T(8,128)(2,1)S(1)} %collective-permute-done.refs_2_), channel_id=1, source_target_pairs={{0,4},{4,0},{8,12},{12,8},{16,20},{20,16},{24,28},{28,24},{1,5},{5... | collective-permute-start | bytes 688136 | tf_op jit(solution)/shard_map/ppermute | solution.py:308
  18.2 8.6 %collective-permute-start.4 = (bf16[2,64,896]{2,1,0:T(8,128)(2,1)S(1)}, bf16[2,64,896]{2,1,0:T(8,128)(2,1)S(1)}, u32[]{:S(2)}, u32[]{:S(2)}) collective-permute-start(bf16[2,64,896]{2,1,0:T(8,128)(2,1)S(1)} %collective-permute-done.refs_2_), channel_id=1, source_target_pairs={{0,8},{4,12},{8,16},{12,20},{16,24},{20,28},{24,0},{28,4},{1,9},{5... | collective-permute-start | bytes 688136 | tf_op jit(solution)/shard_map/ppermute | solution.py:314
  18.2 10.7 %collective-permute-start.2 = (bf16[2,240,64]{2,1,0:T(8,128)(2,1)S(1)}, bf16[2,240,64]{2,1,0:T(8,128)(2,1)S(1)}, u32[]{:S(2)}, u32[]{:S(2)}) collective-permute-start(bf16[2,240,64]{2,1,0:T(8,128)(2,1)S(1)} %get-tuple-element.33), channel_id=1, source_target_pairs={{0,4},{4,8},{8,12},{12,16},{16,20},{20,24},{24,28},{1,5},{5,9},{9,... | collective-permute-start | bytes 184328 | tf_op jit(solution)/shard_map/ppermute | solution.py:317
  22.5 8.7 %collective-permute-start.7 = (bf16[2,64,896]{2,1,0:T(8,128)(2,1)S(1)}, bf16[2,64,896]{2,1,0:T(8,128)(2,1)S(1)}, u32[]{:S(2)}, u32[]{:S(2)}) collective-permute-start(bf16[2,64,896]{2,1,0:T(8,128)(2,1)S(1)} %collective-permute-done.6.refs_6_), channel_id=1, source_target_pairs={{0,4},{4,0},{8,12},{12,8},{16,20},{20,16},{24,28},{28,24},{1,5},{5... | collective-permute-start | bytes 688136 | tf_op jit(solution)/shard_map/ppermute | solution.py:308
  26.8 6.8 %collective-permute-start.5 = (bf16[2,64,896]{2,1,0:T(8,128)(2,1)S(1)}, bf16[2,64,896]{2,1,0:T(8,128)(2,1)S(1)}, u32[]{:S(2)}, u32[]{:S(2)}) collective-permute-start(bf16[2,64,896]{2,1,0:T(8,128)(2,1)S(1)} %collective-permute-done.4.refs_4_), channel_id=1, source_target_pairs={{0,4},{4,0},{8,12},{12,8},{16,20},{20,16},{24,28},{28,24},{1,5},{5... | collective-permute-start | bytes 688136 | tf_op jit(solution)/shard_map/ppermute | solution.py:308
  26.9 9.2 %collective-permute-start.9 = (bf16[224,896]{1,0:T(8,128)(2,1)S(1)}, bf16[224,896]{1,0:T(8,128)(2,1)S(1)}, u32[]{:S(2)}, u32[]{:S(2)}) collective-permute-start(bf16[224,896]{1,0:T(8,128)(2,1)S(1)} %get-tuple-element.38), channel_id=1, source_target_pairs={{0,2},{1,3},{2,0},{3,1},{4,6},{5,7},{6,4},{7,5},{8,10},{9,11},{10,... | collective-permute-start | bytes 1204232 | tf_op jit(solution)/shard_map/ppermute | solution.py:305
  28.9 9.6 %collective-permute-start.10 = (bf16[224,896]{1,0:T(8,128)(2,1)S(1)}, bf16[224,896]{1,0:T(8,128)(2,1)S(1)}, u32[]{:S(2)}, u32[]{:S(2)}) collective-permute-start(bf16[224,896]{1,0:T(8,128)(2,1)S(1)} %bitcast.13), channel_id=1, source_target_pairs={{0,1},{1,0},{2,3},{3,2},{4,5},{5,4},{6,7},{7,6},{8,9},{9,8},{10,11... | collective-permute-start | bytes 1204232 | tf_op jit(solution)/shard_map/ppermute | solution.py:302
  31.2 11.1 %collective-permute-start.12 = (bf16[2,224,512]{2,1,0:T(8,128)(2,1)S(1)}, bf16[2,224,512]{2,1,0:T(8,128)(2,1)S(1)}, u32[]{:S(2)}, u32[]{:S(2)}) collective-permute-start(bf16[2,224,512]{2,1,0:T(8,128)(2,1)S(1)} %pad_maximum_fusion.refs_4_), channel_id=1, source_target_pairs={{0,1},{1,0},{2,3},{3,2},{4,5},{5,4},{6,7},{7,6},{8,9},{9,8},{10,11... | collective-permute-start | bytes 1376264 | tf_op jit(solution)/shard_map/ppermute | solution.py:302
  33.6 8.6 %collective-permute-start.11 = (bf16[224,896]{1,0:T(8,128)(2,1)S(1)}, bf16[224,896]{1,0:T(8,128)(2,1)S(1)}, u32[]{:S(2)}, u32[]{:S(2)}) collective-permute-start(bf16[224,896]{1,0:T(8,128)(2,1)S(1)} %copy-done.1), channel_id=1, source_target_pairs={{0,1},{1,0},{2,3},{3,2},{4,5},{5,4},{6,7},{7,6},{8,9},{9,8},{10,11... | collective-permute-start | bytes 1204232 | tf_op jit(solution)/shard_map/ppermute | solution.py:302
  34.2 13.0 %collective-permute-start.16 = (bf16[2,224,512]{2,1,0:T(8,128)(2,1)S(1)}, bf16[2,224,512]{2,1,0:T(8,128)(2,1)S(1)}, u32[]{:S(2)}, u32[]{:S(2)}) collective-permute-start(bf16[2,224,512]{2,1,0:T(8,128)(2,1)S(1)} %pad_maximum_fusion.refs_4_), channel_id=1, source_target_pairs={{0,2},{1,3},{2,0},{3,1},{4,6},{5,7},{6,4},{7,5},{8,10},{9,11},{10,... | collective-permute-start | bytes 1376264 | tf_op jit(solution)/shard_map/ppermute | solution.py:305
  36.1 12.0 %collective-permute-start.13 = (bf16[224,896]{1,0:T(8,128)(2,1)S(1)}, bf16[224,896]{1,0:T(8,128)(2,1)S(1)}, u32[]{:S(2)}, u32[]{:S(2)}) collective-permute-start(bf16[224,896]{1,0:T(8,128)(2,1)S(1)} %collective-permute-done.9.refs_0_), channel_id=1, source_target_pairs={{0,4},{4,0},{8,12},{12,8},{16,20},{20,16},{24,28},{28,24},{1,5},{5... | collective-permute-start | bytes 1204232 | tf_op jit(solution)/shard_map/ppermute | solution.py:308
  38.5 19.7 %collective-permute-start.21 = (bf16[448,896]{1,0:T(8,128)(2,1)S(1)}, bf16[448,896]{1,0:T(8,128)(2,1)S(1)}, u32[]{:S(2)}, u32[]{:S(2)}) collective-permute-start(bf16[448,896]{1,0:T(8,128)(2,1)S(1)} %collective-permute-done.8.refs_1_), channel_id=1, source_target_pairs={{0,8},{4,12},{8,0},{12,4},{16,24},{20,28},{24,16},{28,20},{1,9},{5... | collective-permute-start | bytes 2408456 | tf_op jit(solution)/shard_map/ppermute | solution.py:311
  42.2 6.5 %collective-permute-start.14 = (bf16[224,896]{1,0:T(8,128)(2,1)S(1)}, bf16[224,896]{1,0:T(8,128)(2,1)S(1)}, u32[]{:S(2)}, u32[]{:S(2)}) collective-permute-start(bf16[224,896]{1,0:T(8,128)(2,1)S(1)} %collective-permute-done.9.refs_0_), channel_id=1, source_target_pairs={{0,1},{1,0},{2,3},{3,2},{4,5},{5,4},{6,7},{7,6},{8,9},{9,8},{10,11... | collective-permute-start | bytes 1204232 | tf_op jit(solution)/shard_map/ppermute | solution.py:302
  42.3 5.9 %copy-start.2 = (bf16[896,448]{0,1:T(8,128)(2,1)S(1)}, bf16[896,448]{0,1:T(8,128)(2,1)}, u32[]{:S(2)}) copy-start(bf16[896,448]{0,1:T(8,128)(2,1)} %param.21) | copy-start | bytes 2408452
  42.3 6.4 %copy-start.3 = (bf16[448,896]{1,0:T(8,128)(2,1)S(1)}, bf16[448,896]{1,0:T(8,128)(2,1)}, u32[]{:S(2)}) copy-start(bf16[448,896]{1,0:T(8,128)(2,1)} %refs_1_.3) | copy-start | bytes 2408452
  47.2 2.7 %collective-permute-start.17 = (bf16[2,224,512]{2,1,0:T(8,128)(2,1)S(1)}, bf16[2,224,512]{2,1,0:T(8,128)(2,1)S(1)}, u32[]{:S(2)}, u32[]{:S(2)}) collective-permute-start(bf16[2,224,512]{2,1,0:T(8,128)(2,1)S(1)} %collective-permute-done.16.refs_4_), channel_id=1, source_target_pairs={{0,1},{1,0},{2,3},{3,2},{4,5},{5,4},{6,7},{7,6},{8,9},{9,8},{10,11... | collective-permute-start | bytes 1376264 | tf_op jit(solution)/shard_map/ppermute | solution.py:302
  48.2 1.7 %collective-permute-start.15 = (bf16[224,896]{1,0:T(8,128)(2,1)S(1)}, bf16[224,896]{1,0:T(8,128)(2,1)S(1)}, u32[]{:S(2)}, u32[]{:S(2)}) collective-permute-start(bf16[224,896]{1,0:T(8,128)(2,1)S(1)} %collective-permute-done.13.refs_1_), channel_id=1, source_target_pairs={{0,1},{1,0},{2,3},{3,2},{4,5},{5,4},{6,7},{7,6},{8,9},{9,8},{10,11... | collective-permute-start | bytes 1204232 | tf_op jit(solution)/shard_map/ppermute | solution.py:302
  48.2 10.1 %collective-permute-start.18 = (bf16[448,896]{1,0:T(8,128)(2,1)S(1)}, bf16[448,896]{1,0:T(8,128)(2,1)S(1)}, u32[]{:S(2)}, u32[]{:S(2)}) collective-permute-start(bf16[448,896]{1,0:T(8,128)(2,1)S(1)} %bitcast.16), channel_id=1, source_target_pairs={{0,1},{1,0},{2,3},{3,2},{4,5},{5,4},{6,7},{7,6},{8,9},{9,8},{10,11... | collective-permute-start | bytes 2408456 | tf_op jit(solution)/shard_map/ppermute | solution.py:302
  48.7 9.6 %collective-permute-start.19 = (bf16[448,896]{1,0:T(8,128)(2,1)S(1)}, bf16[448,896]{1,0:T(8,128)(2,1)S(1)}, u32[]{:S(2)}, u32[]{:S(2)}) collective-permute-start(bf16[448,896]{1,0:T(8,128)(2,1)S(1)} %copy-done.3), channel_id=1, source_target_pairs={{0,1},{1,0},{2,3},{3,2},{4,5},{5,4},{6,7},{7,6},{8,9},{9,8},{10,11... | collective-permute-start | bytes 2408456 | tf_op jit(solution)/shard_map/ppermute | solution.py:302
  54.1 9.0 %collective-permute-start.20 = (bf16[448,896]{1,0:T(8,128)(2,1)S(1)}, bf16[448,896]{1,0:T(8,128)(2,1)S(1)}, u32[]{:S(2)}, u32[]{:S(2)}) collective-permute-start(bf16[448,896]{1,0:T(8,128)(2,1)S(1)} %collective-permute-done.8.refs_1_), channel_id=1, source_target_pairs={{0,1},{1,0},{2,3},{3,2},{4,5},{5,4},{6,7},{7,6},{8,9},{9,8},{10,11... | collective-permute-start | bytes 2408456 | tf_op jit(solution)/shard_map/ppermute | solution.py:302
  58.2 4.9 %collective-permute-start.22 = (bf16[448,896]{1,0:T(8,128)(2,1)S(1)}, bf16[448,896]{1,0:T(8,128)(2,1)S(1)}, u32[]{:S(2)}, u32[]{:S(2)}) collective-permute-start(bf16[448,896]{1,0:T(8,128)(2,1)S(1)} %collective-permute-done.21.refs_3_), channel_id=1, source_target_pairs={{0,1},{1,0},{2,3},{3,2},{4,5},{5,4},{6,7},{7,6},{8,9},{9,8},{10,11... | collective-permute-start | bytes 2408456 | tf_op jit(solution)/shard_map/ppermute | solution.py:302
  67.6 4.0 %collective-permute-start.23 = (bf16[1024,896]{1,0:T(8,128)(2,1)S(1)}, bf16[1024,896]{1,0:T(8,128)(2,1)S(1)}, u32[]{:S(2)}, u32[]{:S(2)}) collective-permute-start(bf16[1024,896]{1,0:T(8,128)(2,1)S(1)} %encoder_ffn_far.1.encoded), channel_id=1, source_target_pairs={{0,1},{1,0},{2,3},{3,2},{4,5},{5,4},{6,7},{7,6},{8,9},{9,8},{10,11... | collective-permute-start | bytes 5505032 | tf_op jit(solution)/shard_map/ppermute | solution.py:302
  (3 other events, 5.3 us)

commit v8 on v7

--- a/solution.py
+++ b/solution.py
@@ -15,6 +15,7 @@
 CH_DEV = 8
 HALVES = 2
 BLOCK = 512
+NORM_BLOCK = 64
 DIGIT = 128
 
 ORDER = {
@@ -29,7 +30,7 @@
     "cyf": ("far",),
     "cyk": ("near",),
     "czf": ("far",),
-    "near": ("yf", "wk"),
+    "near": ("yf",),
     "wk": ("ya",),
     "gains": ("zn",),
 }
@@ -121,8 +122,9 @@
             def _(b=b, place=place, i=i):
                 rows_out[i * part_rows : (i + 1) * part_rows, :] = db_refs[b][place]
 
-    values = rows_out[...].astype(jnp.float32)
-    normed_out[...] = rms_scale(values, gain[...]).astype(jnp.bfloat16)
+    for at in range(0, rows_out.shape[0], NORM_BLOCK):
+        values = rows_out[at : at + NORM_BLOCK, :].astype(jnp.float32)
+        normed_out[at : at + NORM_BLOCK, :] = rms_scale(values, gain[...]).astype(jnp.bfloat16)
 
 
 def attention_kernel(pieces, far, seq_index, before, normed_in, *refs):
@@ -208,7 +210,9 @@
     for start in range(0, before.shape[0], BLOCK):
         block = slice(start, start + BLOCK)
         if first:
-            normed[block, :] = rms_scale(before[block, :], gain[...]).astype(jnp.bfloat16)
+            for at in range(start, start + BLOCK, NORM_BLOCK):
+                values = rms_scale(before[at : at + NORM_BLOCK, :], gain[...])
+                normed[at : at + NORM_BLOCK, :] = values.astype(jnp.bfloat16)
         raised.append(mxu(normed[block, :], up, NT).astype(jnp.bfloat16))
     for i, units in enumerate(raised):
         block = slice(i * BLOCK, (i + 1) * BLOCK)
@@ -337,7 +341,7 @@
         "ssss" + "h" * 6,
         "prepare",
         rows * width,
-        53,
+        60,
         scratch=[
             pltpu.VMEM((entries_here, half_rows, width), jnp.float32),
             pltpu.VMEM((entries_here, half_rows, width), jnp.bfloat16),

time: 77.5 us -> 75.6 us (0.975)
  waiting for transfers between devices: 19.1 us -> 17.6 us
    unnamed x23 -> x25, local copies, waits for them, and re-layouts: 1.89 us -> 1.48 us
  transfers between devices with their start and end apart: 24 -> 24, of which waited for: 12 -> 11; matrix products, arithmetic and copies ran while one was open for 1% -> 1% of each run, Pallas kernels for 23% -> 24%
where the time goes in v8:
time: 75.6 us; the launch traced here: 74.7 us
  Pallas kernels  30.5 us (40%)
  starting transfers between devices  24.3 us (32%)
  waiting for transfers between devices  17.6 us (23%)
  local copies, waits for them, and re-layouts  1.5 us (2%)
    ppermute x5, starting transfers between devices, seq_swap(): return lax.ppermute(array, 'seq', [(i, i ^ 1) for i in range(seq_size)])  8.54 us
    pallas_call x2, Pallas kernels, attention(): call(functools.partial(attention_kernel, len(kv), far), long_rows, 'svv'...  8.27 us
    ppermute x5, waiting for transfers between devices, seq_swap(): return lax.ppermute(array, 'seq', [(i, i ^ 1) for i in range(seq_size)])  6.76 us
    ppermute x3, starting transfers between devices, seq_ring(): lax.ppermute(array, 'seq', [(i, (i + 2 * way) % seq_size) for i in range(...  5.34 us
    ppermute x3, starting transfers between devices, lane_step(): lax.ppermute(array, 'mp', [(i, (i + 2 * step) % lanes) for i in range(lan...  4.91 us
    ppermute x3, waiting for transfers between devices, seq_ring(): lax.ppermute(array, 'seq', [(i, (i + 2 * way) % seq_size) for i in range(...  4.87 us
    pallas_call x1, Pallas kernels, on_device(): call(functools.partial(ffn_kernel, False, True), (long_rows, short_rows),...  4.85 us
    pallas_call x1, Pallas kernels, on_device(): call(decoder_kernel, jax.ShapeDtypeStruct(dec_queries.shape, jnp.float32)...  4.8 us
  transfers between devices with their start and end apart: 24, of which 11 were waited for; matrix products, arithmetic and copies ran while one was open for 1% of the time, Pallas kernels for 24%

profile of v8, /device:TPU:0, one launch (start us, length us, event | category | flops | bytes accessed | tf_op | source)
XLA Modules:
  0.0 74.7 jit_solution(9692067213404595658)
XLA Ops:
  0.0 3.3 %prepare.1 = (bf16[2,64,896]{2,1,0:T(8,128)(2,1)}, bf16[224,896]{1,0:T(8,128)(2,1)}, bf16[448,896]{1,0:T(8,128)(2,1)}, bf16[2,240,64]{2,1,0:T(8,128)(2,1)}) custom-call(s32[1]{0:T(128)} %bitcast.here.seq_index.first, s32[1]{0:T(128)} %bitcast.1.lane_here, s32[2,8]{1,0:T(2,128)} %bitcast.18, s32[2,8]{1,0:T(2,128)} %bitcast.20, f32[2,128,896]{2,1,0:T(8,128)} %database.1, ...), custom_call_target="tpu_custom_call" | custom-call | flops 917504 | bytes 8000000 | tf_op jit(solution)/shard_map/prepare/pallas_call | solution.py:333
  3.3 3.1 %collective-permute-start = (bf16[2,64,896]{2,1,0:T(8,128)(2,1)}, bf16[2,64,896]{2,1,0:T(8,128)(2,1)S(1)}, u32[]{:S(2)}, u32[]{:S(2)}) collective-permute-start(bf16[2,64,896]{2,1,0:T(8,128)(2,1)} %get-tuple-element.30.refs_0_), channel_id=1, source_target_pairs={{0,8},{4,12},{8,16},{12,20},{16,24},{20,28},{24,0},{28,4},{1,9},{5... | collective-permute-start | bytes 688136 | tf_op jit(solution)/shard_map/ppermute | solution.py:318
  6.4 1.5 %collective-permute-start.8 = (bf16[448,896]{1,0:T(8,128)(2,1)}, bf16[448,896]{1,0:T(8,128)(2,1)S(1)}, u32[]{:S(2)}, u32[]{:S(2)}) collective-permute-start(bf16[448,896]{1,0:T(8,128)(2,1)} %get-tuple-element.37), channel_id=1, source_target_pairs={{0,2},{1,3},{2,0},{3,1},{4,6},{5,7},{6,4},{7,5},{8,10},{9,11},{10,... | collective-permute-start | bytes 2408456 | tf_op jit(solution)/shard_map/ppermute | solution.py:309
  7.9 1.5 %collective-permute-start.1 = (bf16[2,64,896]{2,1,0:T(8,128)(2,1)}, bf16[2,64,896]{2,1,0:T(8,128)(2,1)S(1)}, u32[]{:S(2)}, u32[]{:S(2)}) collective-permute-start(bf16[2,64,896]{2,1,0:T(8,128)(2,1)} %get-tuple-element.30.refs_0_), channel_id=1, source_target_pairs={{0,4},{4,0},{8,12},{12,8},{16,20},{20,16},{24,28},{28,24},{1,5},{5... | collective-permute-start | bytes 688136 | tf_op jit(solution)/shard_map/ppermute | solution.py:312
  9.4 2.2 %collective-permute-start.6 = (bf16[2,64,896]{2,1,0:T(8,128)(2,1)}, bf16[2,64,896]{2,1,0:T(8,128)(2,1)S(1)}, u32[]{:S(2)}, u32[]{:S(2)}) collective-permute-start(bf16[2,64,896]{2,1,0:T(8,128)(2,1)} %get-tuple-element.30.refs_0_), channel_id=1, source_target_pairs={{0,24},{4,28},{8,0},{12,4},{16,8},{20,12},{24,16},{28,20},{1,25},{... | collective-permute-start | bytes 688136 | tf_op jit(solution)/shard_map/ppermute | solution.py:318
  11.7 3.4 %collective-permute-done.refs_2_ = bf16[2,64,896]{2,1,0:T(8,128)(2,1)S(1)} collective-permute-done((bf16[2,64,896]{2,1,0:T(8,128)(2,1)}, bf16[2,64,896]{2,1,0:T(8,128)(2,1)S(1)}, u32[]{:S(2)}, u32[]{:S(2)}) %collective-permute-start) | collective-permute-done | bytes 229408 | tf_op jit(solution)/shard_map/ppermute | solution.py:318
  15.1 1.8 %collective-permute-start.3 = (bf16[2,64,896]{2,1,0:T(8,128)(2,1)S(1)}, bf16[2,64,896]{2,1,0:T(8,128)(2,1)S(1)}, u32[]{:S(2)}, u32[]{:S(2)}) collective-permute-start(bf16[2,64,896]{2,1,0:T(8,128)(2,1)S(1)} %collective-permute-done.refs_2_), channel_id=1, source_target_pairs={{0,4},{4,0},{8,12},{12,8},{16,20},{20,16},{24,28},{28,24},{1,5},{5... | collective-permute-start | bytes 688136 | tf_op jit(solution)/shard_map/ppermute | solution.py:312
  16.8 2.1 %collective-permute-start.2 = (bf16[2,240,64]{2,1,0:T(8,128)(2,1)}, bf16[2,240,64]{2,1,0:T(8,128)(2,1)S(1)}, u32[]{:S(2)}, u32[]{:S(2)}) collective-permute-start(bf16[2,240,64]{2,1,0:T(8,128)(2,1)} %get-tuple-element.33), channel_id=1, source_target_pairs={{0,4},{4,8},{8,12},{12,16},{16,20},{20,24},{24,28},{1,5},{5,9},{9,... | collective-permute-start | bytes 184328 | tf_op jit(solution)/shard_map/ppermute | solution.py:321
  19.3 1.9 %collective-permute-done.3.refs_3_ = bf16[2,64,896]{2,1,0:T(8,128)(2,1)S(1)} collective-permute-done((bf16[2,64,896]{2,1,0:T(8,128)(2,1)S(1)}, bf16[2,64,896]{2,1,0:T(8,128)(2,1)S(1)}, u32[]{:S(2)}, u32[]{:S(2)}) %collective-permute-start.3) | collective-permute-done | bytes 229408 | tf_op jit(solution)/shard_map/ppermute | solution.py:312
  21.2 3.0 %collective-permute-start.7 = (bf16[2,64,896]{2,1,0:T(8,128)(2,1)S(1)}, bf16[2,64,896]{2,1,0:T(8,128)(2,1)S(1)}, u32[]{:S(2)}, u32[]{:S(2)}) collective-permute-start(bf16[2,64,896]{2,1,0:T(8,128)(2,1)S(1)} %collective-permute-done.6.refs_6_), channel_id=1, source_target_pairs={{0,4},{4,0},{8,12},{12,8},{16,20},{20,16},{24,28},{28,24},{1,5},{5... | collective-permute-start | bytes 688136 | tf_op jit(solution)/shard_map/ppermute | solution.py:312
  24.3 1.2 %collective-permute-done.4.refs_4_ = bf16[2,64,896]{2,1,0:T(8,128)(2,1)S(1)} collective-permute-done((bf16[2,64,896]{2,1,0:T(8,128)(2,1)S(1)}, bf16[2,64,896]{2,1,0:T(8,128)(2,1)S(1)}, u32[]{:S(2)}, u32[]{:S(2)}) %collective-permute-start.4) | collective-permute-done | bytes 229408 | tf_op jit(solution)/shard_map/ppermute | solution.py:318
  25.6 1.9 %collective-permute-start.12 = (bf16[224,896]{1,0:T(8,128)(2,1)}, bf16[224,896]{1,0:T(8,128)(2,1)S(1)}, u32[]{:S(2)}, u32[]{:S(2)}) collective-permute-start(bf16[224,896]{1,0:T(8,128)(2,1)} %get-tuple-element.43), channel_id=1, source_target_pairs={{0,2},{1,3},{2,0},{3,1},{4,6},{5,7},{6,4},{7,5},{8,10},{9,11},{10,... | collective-permute-start | bytes 1204232 | tf_op jit(solution)/shard_map/ppermute | solution.py:309
  27.8 2.1 %collective-permute-done.7.refs_7_ = bf16[2,64,896]{2,1,0:T(8,128)(2,1)S(1)} collective-permute-done((bf16[2,64,896]{2,1,0:T(8,128)(2,1)S(1)}, bf16[2,64,896]{2,1,0:T(8,128)(2,1)S(1)}, u32[]{:S(2)}, u32[]{:S(2)}) %collective-permute-start.7) | collective-permute-done | bytes 229408 | tf_op jit(solution)/shard_map/ppermute | solution.py:312
  29.9 2.5 %collective-permute-done.5.refs_5_ = bf16[2,64,896]{2,1,0:T(8,128)(2,1)S(1)} collective-permute-done((bf16[2,64,896]{2,1,0:T(8,128)(2,1)S(1)}, bf16[2,64,896]{2,1,0:T(8,128)(2,1)S(1)}, u32[]{:S(2)}, u32[]{:S(2)}) %collective-permute-start.5) | collective-permute-done | bytes 229408 | tf_op jit(solution)/shard_map/ppermute | solution.py:312
  32.4 1.5 %collective-permute-start.16 = (bf16[2,224,512]{2,1,0:T(8,128)(2,1)S(1)}, bf16[2,224,512]{2,1,0:T(8,128)(2,1)S(1)}, u32[]{:S(2)}, u32[]{:S(2)}) collective-permute-start(bf16[2,224,512]{2,1,0:T(8,128)(2,1)S(1)} %pad_maximum_fusion.refs_4_), channel_id=1, source_target_pairs={{0,2},{1,3},{2,0},{3,1},{4,6},{5,7},{6,4},{7,5},{8,10},{9,11},{10,... | collective-permute-start | bytes 1376264 | tf_op jit(solution)/shard_map/ppermute | solution.py:309
  34.1 0.5 collective-permute-done.12.refs_0_
  34.6 2.1 %collective-permute-start.13 = (bf16[224,896]{1,0:T(8,128)(2,1)S(1)}, bf16[224,896]{1,0:T(8,128)(2,1)S(1)}, u32[]{:S(2)}, u32[]{:S(2)}) collective-permute-start(bf16[224,896]{1,0:T(8,128)(2,1)S(1)} %collective-permute-done.12.refs_0_), channel_id=1, source_target_pairs={{0,4},{4,0},{8,12},{12,8},{16,20},{20,16},{24,28},{28,24},{1,5},{5... | collective-permute-start | bytes 1204232 | tf_op jit(solution)/shard_map/ppermute | solution.py:312
  36.6 1.1 %collective-permute-start.21 = (bf16[448,896]{1,0:T(8,128)(2,1)S(1)}, bf16[448,896]{1,0:T(8,128)(2,1)S(1)}, u32[]{:S(2)}, u32[]{:S(2)}) collective-permute-start(bf16[448,896]{1,0:T(8,128)(2,1)S(1)} %collective-permute-done.8.refs_1_), channel_id=1, source_target_pairs={{0,8},{4,12},{8,0},{12,4},{16,24},{20,28},{24,16},{28,20},{1,9},{5... | collective-permute-start | bytes 2408456 | tf_op jit(solution)/shard_map/ppermute | solution.py:315
  37.8 0.9 %copy-done.5 = bf16[2,64,896]{2,1,0:T(8,128)(2,1)S(1)} copy-done((bf16[2,64,896]{2,1,0:T(8,128)(2,1)S(1)}, bf16[2,64,896]{2,1,0:T(8,128)(2,1)}, u32[]{:S(2)}) %copy-start.5) | copy-done | bytes 229400
  38.8 2.5 %neighbour_rows.1 = (bf16[1024,896]{1,0:T(8,128)(2,1)S(1)}, bf16[1024,896]{1,0:T(8,128)(2,1)S(1)}) custom-call(s32[1]{0:T(128)} %bitcast.here.seq_index.first, s32[2,8]{1,0:T(2,128)S(1)} %bitcast.19, s32[2,8]{1,0:T(2,128)S(1)} %bitcast.21, s32[2,1]{1,0:T(2,128)S(1)} %slice_add_fusion.before, f32[1,896]{1,0:T(1,128)S(1)} %reshape.18.gain, ...), custom_call_target="tpu_custom_call" | custom-call | flops 9175040 | bytes 8000000 | tf_op jit(solution)/shard_map/neighbour_rows/pallas_call | solution.py:422
  41.4 4.1 %encoder_attention.2.before = f32[1024,896]{1,0:T(8,128)S(1)} custom-call(s32[1]{0:T(128)} %bitcast.here.seq_index.first, bf16[1024,896]{1,0:T(8,128)(2,1)S(1)} %get-tuple-element.38.before, bf16[1024,896]{1,0:T(8,128)(2,1)S(1)} %get-tuple-element.39.normed_in, bf16[224,896]{1,0:T(8,128)(2,1)S(1)} %bitcast.14, bf16[224,896]{1,0:T(8,128)(2,1)S(1)} %copy-done.1, ...), custom_call_target="tpu_custom_call" | custom-call | flops 1644167168 | bytes 8000000 | tf_op jit(solution)/shard_map/encoder_attention/pallas_call | solution.py:432
  45.5 0.5 collective-permute-start.17
  46.3 0.5 collective-permute-start.18
  46.9 1.2 %collective-permute-done.15.refs_3_ = bf16[224,896]{1,0:T(8,128)(2,1)S(1)} collective-permute-done((bf16[224,896]{1,0:T(8,128)(2,1)S(1)}, bf16[224,896]{1,0:T(8,128)(2,1)S(1)}, u32[]{:S(2)}, u32[]{:S(2)}) %collective-permute-start.15) | collective-permute-done | bytes 401440 | tf_op jit(solution)/shard_map/ppermute | solution.py:306
  48.1 4.1 %encoder_attention.3.before = f32[1024,896]{1,0:T(8,128)S(1)} custom-call(s32[1]{0:T(128)} %bitcast.here.seq_index.first, f32[1024,896]{1,0:T(8,128)S(1)} %encoder_attention.2.before, bf16[1024,896]{1,0:T(8,128)(2,1)S(1)} %get-tuple-element.39.normed_in, bf16[224,896]{1,0:T(8,128)(2,1)S(1)} %collective-permute-done.12.refs_0_, ...), custom_call_target="tpu_custom_call" | custom-call | flops 1644167168 | bytes 8000000 | tf_op jit(solution)/shard_map/encoder_attention/pallas_call | solution.py:432
  52.7 3.7 %collective-permute-done.21.refs_3_ = bf16[448,896]{1,0:T(8,128)(2,1)S(1)} collective-permute-done((bf16[448,896]{1,0:T(8,128)(2,1)S(1)}, bf16[448,896]{1,0:T(8,128)(2,1)S(1)}, u32[]{:S(2)}, u32[]{:S(2)}) %collective-permute-start.21) | collective-permute-done | bytes 802848 | tf_op jit(solution)/shard_map/ppermute | solution.py:315
  56.4 4.9 %encoder_ffn_near.1 = (f32[1024,896]{1,0:T(8,128)S(1)}, bf16[1024,896]{1,0:T(8,128)(2,1)S(1)}) custom-call(f32[1,896]{1,0:T(1,128)S(1)} %reshape.19.gain, f32[1024,896]{1,0:T(8,128)S(1)} %encoder_attention.3.before, bf16[448,896]{1,0:T(8,128)(2,1)S(1)} %bitcast.17, bf16[448,896]{1,0:T(8,128)(2,1)S(1)} %copy-done.3, ...), custom_call_target="tpu_custom_call" | custom-call | flops 3288334336 | bytes 8000000 | tf_op jit(solution)/shard_map/encoder_ffn_near/pallas_call | solution.py:449
  61.3 4.5 %encoder_ffn_far.1.encoded = bf16[1024,896]{1,0:T(8,128)(2,1)S(1)} custom-call(f32[1,896]{1,0:T(1,128)S(1)} %reshape.19.gain, f32[1024,896]{1,0:T(8,128)S(1)} %get-tuple-element.50.before, bf16[1024,896]{1,0:T(8,128)(2,1)S(1)} %get-tuple-element.51.refs_0_, bf16[448,896]{1,0:T(8,128)(2,1)S(1)} %collective-permute-done.8.refs_1_, ...), custom_call_target="tpu_custom_call" | custom-call | flops 3288334336 | bytes 8000000 | tf_op jit(solution)/shard_map/encoder_ffn_far/pallas_call | solution.py:459
  65.7 0.6 collective-permute-start.23
  66.8 2.3 %decoder_pairs.1.own_pairs = bf16[1024,1024]{1,0:T(8,128)(2,1)S(1)} custom-call(bf16[1024,896]{1,0:T(8,128)(2,1)S(1)} %encoder_ffn_far.1.encoded, bf16[896,1024]{1,0:T(8,128)(2,1)S(1)} %bitcast.10), custom_call_target="tpu_custom_call" | custom-call | flops 1879048192 | bytes 8000000 | tf_op jit(solution)/shard_map/decoder_pairs/pallas_call | solution.py:471
  69.2 0.6 collective-permute-done.23.other
  69.7 4.8 %decoder_attention.1 = f32[512,512]{1,0:T(8,128)} custom-call(s32[1]{0:T(128)} %bitcast.here.seq_index.first, bf16[1024,1024]{1,0:T(8,128)(2,1)S(1)} %decoder_pairs.1.own_pairs, bf16[1024,896]{1,0:T(8,128)(2,1)S(1)} %collective-permute-done.23.other, bf16[896,1024]{1,0:T(8,128)(2,1)S(1)} %bitcast.11, bf16[512,512]{1,0:T(8,128)(2,1)S(1)} %copy-done.4), custom_call_target="tpu_custom_call" | custom-call | flops 1879048192 | bytes 8000000 | tf_op jit(solution)/shard_map/decoder_attention/pallas_call | solution.py:479
  (55 shorter events, 2.3 us)
Async XLA Ops:
  0.0 27.5 %copy-start = (bf16[896,224]{0,1:T(8,128)(2,1)S(1)}, bf16[896,224]{0,1:T(8,128)(2,1)}, u32[]{:S(2)}) copy-start(bf16[896,224]{0,1:T(8,128)(2,1)} %param.18) | copy-start | bytes 1204228
  0.0 27.5 %copy-start.9 = (bf16[512,2,224]{0,2,1:T(8,128)(2,1)S(1)}, bf16[512,2,224]{0,2,1:T(8,128)(2,1)}, u32[]{:S(2)}) copy-start(bf16[512,2,224]{0,2,1:T(8,128)(2,1)} %param.12) | copy-start | bytes 1376260
  0.0 32.4 %copy-start.1 = (bf16[224,896]{1,0:T(8,128)(2,1)S(1)}, bf16[224,896]{1,0:T(8,128)(2,1)}, u32[]{:S(2)}) copy-start(bf16[224,896]{1,0:T(8,128)(2,1)} %refs_1_.2) | copy-start | bytes 1204228
  0.0 32.4 %copy-start.10 = (f32[896]{0:T(1024)S(1)}, f32[896]{0:T(1024)}, u32[]{:S(2)}) copy-start(f32[896]{0:T(1024)} %param.17) | copy-start | bytes 10756
  0.0 32.4 %copy-start.11 = (f32[896]{0:T(1024)S(1)}, f32[896]{0:T(1024)}, u32[]{:S(2)}) copy-start(f32[896]{0:T(1024)} %param.20) | copy-start | bytes 10756
  0.0 37.8 %copy-start.6 = (s32[8,2]{0,1:T(2,128)S(1)}, s32[8,2]{0,1:T(2,128)}, u32[]{:S(2)}) copy-start(s32[8,2]{0,1:T(2,128)} %param.16) | copy-start | bytes 196
  0.0 37.8 %copy-start.7 = (s32[8,2]{0,1:T(2,128)S(1)}, s32[8,2]{0,1:T(2,128)}, u32[]{:S(2)}) copy-start(s32[8,2]{0,1:T(2,128)} %param.15) | copy-start | bytes 196
  3.3 11.8 %collective-permute-start = (bf16[2,64,896]{2,1,0:T(8,128)(2,1)}, bf16[2,64,896]{2,1,0:T(8,128)(2,1)S(1)}, u32[]{:S(2)}, u32[]{:S(2)}) collective-permute-start(bf16[2,64,896]{2,1,0:T(8,128)(2,1)} %get-tuple-element.30.refs_0_), channel_id=1, source_target_pairs={{0,8},{4,12},{8,16},{12,20},{16,24},{20,28},{24,0},{28,4},{1,9},{5... | collective-permute-start | bytes 688136 | tf_op jit(solution)/shard_map/ppermute | solution.py:318
  6.4 26.0 %collective-permute-start.8 = (bf16[448,896]{1,0:T(8,128)(2,1)}, bf16[448,896]{1,0:T(8,128)(2,1)S(1)}, u32[]{:S(2)}, u32[]{:S(2)}) collective-permute-start(bf16[448,896]{1,0:T(8,128)(2,1)} %get-tuple-element.37), channel_id=1, source_target_pairs={{0,2},{1,3},{2,0},{3,1},{4,6},{5,7},{6,4},{7,5},{8,10},{9,11},{10,... | collective-permute-start | bytes 2408456 | tf_op jit(solution)/shard_map/ppermute | solution.py:309
  7.9 8.9 %collective-permute-start.1 = (bf16[2,64,896]{2,1,0:T(8,128)(2,1)}, bf16[2,64,896]{2,1,0:T(8,128)(2,1)S(1)}, u32[]{:S(2)}, u32[]{:S(2)}) collective-permute-start(bf16[2,64,896]{2,1,0:T(8,128)(2,1)} %get-tuple-element.30.refs_0_), channel_id=1, source_target_pairs={{0,4},{4,0},{8,12},{12,8},{16,20},{20,16},{24,28},{28,24},{1,5},{5... | collective-permute-start | bytes 688136 | tf_op jit(solution)/shard_map/ppermute | solution.py:312
  9.4 9.9 %collective-permute-start.6 = (bf16[2,64,896]{2,1,0:T(8,128)(2,1)}, bf16[2,64,896]{2,1,0:T(8,128)(2,1)S(1)}, u32[]{:S(2)}, u32[]{:S(2)}) collective-permute-start(bf16[2,64,896]{2,1,0:T(8,128)(2,1)} %get-tuple-element.30.refs_0_), channel_id=1, source_target_pairs={{0,24},{4,28},{8,0},{12,4},{16,8},{20,12},{24,16},{28,20},{1,25},{... | collective-permute-start | bytes 688136 | tf_op jit(solution)/shard_map/ppermute | solution.py:318
  15.1 6.2 %collective-permute-start.3 = (bf16[2,64,896]{2,1,0:T(8,128)(2,1)S(1)}, bf16[2,64,896]{2,1,0:T(8,128)(2,1)S(1)}, u32[]{:S(2)}, u32[]{:S(2)}) collective-permute-start(bf16[2,64,896]{2,1,0:T(8,128)(2,1)S(1)} %collective-permute-done.refs_2_), channel_id=1, source_target_pairs={{0,4},{4,0},{8,12},{12,8},{16,20},{20,16},{24,28},{28,24},{1,5},{5... | collective-permute-start | bytes 688136 | tf_op jit(solution)/shard_map/ppermute | solution.py:312
  16.8 8.6 %collective-permute-start.4 = (bf16[2,64,896]{2,1,0:T(8,128)(2,1)S(1)}, bf16[2,64,896]{2,1,0:T(8,128)(2,1)S(1)}, u32[]{:S(2)}, u32[]{:S(2)}) collective-permute-start(bf16[2,64,896]{2,1,0:T(8,128)(2,1)S(1)} %collective-permute-done.refs_2_), channel_id=1, source_target_pairs={{0,8},{4,12},{8,16},{12,20},{16,24},{20,28},{24,0},{28,4},{1,9},{5... | collective-permute-start | bytes 688136 | tf_op jit(solution)/shard_map/ppermute | solution.py:318
  16.8 10.7 %collective-permute-start.2 = (bf16[2,240,64]{2,1,0:T(8,128)(2,1)}, bf16[2,240,64]{2,1,0:T(8,128)(2,1)S(1)}, u32[]{:S(2)}, u32[]{:S(2)}) collective-permute-start(bf16[2,240,64]{2,1,0:T(8,128)(2,1)} %get-tuple-element.33), channel_id=1, source_target_pairs={{0,4},{4,8},{8,12},{12,16},{16,20},{20,24},{24,28},{1,5},{5,9},{9,... | collective-permute-start | bytes 184328 | tf_op jit(solution)/shard_map/ppermute | solution.py:321
  21.2 8.7 %collective-permute-start.7 = (bf16[2,64,896]{2,1,0:T(8,128)(2,1)S(1)}, bf16[2,64,896]{2,1,0:T(8,128)(2,1)S(1)}, u32[]{:S(2)}, u32[]{:S(2)}) collective-permute-start(bf16[2,64,896]{2,1,0:T(8,128)(2,1)S(1)} %collective-permute-done.6.refs_6_), channel_id=1, source_target_pairs={{0,4},{4,0},{8,12},{12,8},{16,20},{20,16},{24,28},{28,24},{1,5},{5... | collective-permute-start | bytes 688136 | tf_op jit(solution)/shard_map/ppermute | solution.py:312
  25.4 6.9 %collective-permute-start.5 = (bf16[2,64,896]{2,1,0:T(8,128)(2,1)S(1)}, bf16[2,64,896]{2,1,0:T(8,128)(2,1)S(1)}, u32[]{:S(2)}, u32[]{:S(2)}) collective-permute-start(bf16[2,64,896]{2,1,0:T(8,128)(2,1)S(1)} %collective-permute-done.4.refs_4_), channel_id=1, source_target_pairs={{0,4},{4,0},{8,12},{12,8},{16,20},{20,16},{24,28},{28,24},{1,5},{5... | collective-permute-start | bytes 688136 | tf_op jit(solution)/shard_map/ppermute | solution.py:312
  25.6 9.0 %collective-permute-start.12 = (bf16[224,896]{1,0:T(8,128)(2,1)}, bf16[224,896]{1,0:T(8,128)(2,1)S(1)}, u32[]{:S(2)}, u32[]{:S(2)}) collective-permute-start(bf16[224,896]{1,0:T(8,128)(2,1)} %get-tuple-element.43), channel_id=1, source_target_pairs={{0,2},{1,3},{2,0},{3,1},{4,6},{5,7},{6,4},{7,5},{8,10},{9,11},{10,... | collective-permute-start | bytes 1204232 | tf_op jit(solution)/shard_map/ppermute | solution.py:309
  27.5 9.1 %collective-permute-start.9 = (bf16[224,896]{1,0:T(8,128)(2,1)S(1)}, bf16[224,896]{1,0:T(8,128)(2,1)S(1)}, u32[]{:S(2)}, u32[]{:S(2)}) collective-permute-start(bf16[224,896]{1,0:T(8,128)(2,1)S(1)} %bitcast.13), channel_id=1, source_target_pairs={{0,1},{1,0},{2,3},{3,2},{4,5},{5,4},{6,7},{7,6},{8,9},{9,8},{10,11... | collective-permute-start | bytes 1204232 | tf_op jit(solution)/shard_map/ppermute | solution.py:306
  29.9 11.4 %collective-permute-start.11 = (bf16[2,224,512]{2,1,0:T(8,128)(2,1)S(1)}, bf16[2,224,512]{2,1,0:T(8,128)(2,1)S(1)}, u32[]{:S(2)}, u32[]{:S(2)}) collective-permute-start(bf16[2,224,512]{2,1,0:T(8,128)(2,1)S(1)} %pad_maximum_fusion.refs_4_), channel_id=1, source_target_pairs={{0,1},{1,0},{2,3},{3,2},{4,5},{5,4},{6,7},{7,6},{8,9},{9,8},{10,11... | collective-permute-start | bytes 1376264 | tf_op jit(solution)/shard_map/ppermute | solution.py:306
  32.4 8.9 %collective-permute-start.10 = (bf16[224,896]{1,0:T(8,128)(2,1)S(1)}, bf16[224,896]{1,0:T(8,128)(2,1)S(1)}, u32[]{:S(2)}, u32[]{:S(2)}) collective-permute-start(bf16[224,896]{1,0:T(8,128)(2,1)S(1)} %copy-done.1), channel_id=1, source_target_pairs={{0,1},{1,0},{2,3},{3,2},{4,5},{5,4},{6,7},{7,6},{8,9},{9,8},{10,11... | collective-permute-start | bytes 1204232 | tf_op jit(solution)/shard_map/ppermute | solution.py:306
  32.4 13.1 %collective-permute-start.16 = (bf16[2,224,512]{2,1,0:T(8,128)(2,1)S(1)}, bf16[2,224,512]{2,1,0:T(8,128)(2,1)S(1)}, u32[]{:S(2)}, u32[]{:S(2)}) collective-permute-start(bf16[2,224,512]{2,1,0:T(8,128)(2,1)S(1)} %pad_maximum_fusion.refs_4_), channel_id=1, source_target_pairs={{0,2},{1,3},{2,0},{3,1},{4,6},{5,7},{6,4},{7,5},{8,10},{9,11},{10,... | collective-permute-start | bytes 1376264 | tf_op jit(solution)/shard_map/ppermute | solution.py:309
  34.6 11.7 %collective-permute-start.13 = (bf16[224,896]{1,0:T(8,128)(2,1)S(1)}, bf16[224,896]{1,0:T(8,128)(2,1)S(1)}, u32[]{:S(2)}, u32[]{:S(2)}) collective-permute-start(bf16[224,896]{1,0:T(8,128)(2,1)S(1)} %collective-permute-done.12.refs_0_), channel_id=1, source_target_pairs={{0,4},{4,0},{8,12},{12,8},{16,20},{20,16},{24,28},{28,24},{1,5},{5... | collective-permute-start | bytes 1204232 | tf_op jit(solution)/shard_map/ppermute | solution.py:312
  36.6 19.7 %collective-permute-start.21 = (bf16[448,896]{1,0:T(8,128)(2,1)S(1)}, bf16[448,896]{1,0:T(8,128)(2,1)S(1)}, u32[]{:S(2)}, u32[]{:S(2)}) collective-permute-start(bf16[448,896]{1,0:T(8,128)(2,1)S(1)} %collective-permute-done.8.refs_1_), channel_id=1, source_target_pairs={{0,8},{4,12},{8,0},{12,4},{16,24},{20,28},{24,16},{28,20},{1,9},{5... | collective-permute-start | bytes 2408456 | tf_op jit(solution)/shard_map/ppermute | solution.py:315
  41.3 5.5 %collective-permute-start.14 = (bf16[224,896]{1,0:T(8,128)(2,1)S(1)}, bf16[224,896]{1,0:T(8,128)(2,1)S(1)}, u32[]{:S(2)}, u32[]{:S(2)}) collective-permute-start(bf16[224,896]{1,0:T(8,128)(2,1)S(1)} %collective-permute-done.12.refs_0_), channel_id=1, source_target_pairs={{0,1},{1,0},{2,3},{3,2},{4,5},{5,4},{6,7},{7,6},{8,9},{9,8},{10,11... | collective-permute-start | bytes 1204232 | tf_op jit(solution)/shard_map/ppermute | solution.py:306
  41.4 5.4 %copy-start.3 = (bf16[448,896]{1,0:T(8,128)(2,1)S(1)}, bf16[448,896]{1,0:T(8,128)(2,1)}, u32[]{:S(2)}) copy-start(bf16[448,896]{1,0:T(8,128)(2,1)} %refs_1_.3) | copy-start | bytes 2408452
  45.5 2.6 %collective-permute-start.17 = (bf16[2,224,512]{2,1,0:T(8,128)(2,1)S(1)}, bf16[2,224,512]{2,1,0:T(8,128)(2,1)S(1)}, u32[]{:S(2)}, u32[]{:S(2)}) collective-permute-start(bf16[2,224,512]{2,1,0:T(8,128)(2,1)S(1)} %collective-permute-done.16.refs_4_), channel_id=1, source_target_pairs={{0,1},{1,0},{2,3},{3,2},{4,5},{5,4},{6,7},{7,6},{8,9},{9,8},{10,11... | collective-permute-start | bytes 1376264 | tf_op jit(solution)/shard_map/ppermute | solution.py:306
  46.3 1.8 %collective-permute-start.15 = (bf16[224,896]{1,0:T(8,128)(2,1)S(1)}, bf16[224,896]{1,0:T(8,128)(2,1)S(1)}, u32[]{:S(2)}, u32[]{:S(2)}) collective-permute-start(bf16[224,896]{1,0:T(8,128)(2,1)S(1)} %collective-permute-done.13.refs_1_), channel_id=1, source_target_pairs={{0,1},{1,0},{2,3},{3,2},{4,5},{5,4},{6,7},{7,6},{8,9},{9,8},{10,11... | collective-permute-start | bytes 1204232 | tf_op jit(solution)/shard_map/ppermute | solution.py:306
  46.3 10.1 %collective-permute-start.18 = (bf16[448,896]{1,0:T(8,128)(2,1)S(1)}, bf16[448,896]{1,0:T(8,128)(2,1)S(1)}, u32[]{:S(2)}, u32[]{:S(2)}) collective-permute-start(bf16[448,896]{1,0:T(8,128)(2,1)S(1)} %bitcast.16), channel_id=1, source_target_pairs={{0,1},{1,0},{2,3},{3,2},{4,5},{5,4},{6,7},{7,6},{8,9},{9,8},{10,11... | collective-permute-start | bytes 2408456 | tf_op jit(solution)/shard_map/ppermute | solution.py:306
  46.8 9.6 %collective-permute-start.19 = (bf16[448,896]{1,0:T(8,128)(2,1)S(1)}, bf16[448,896]{1,0:T(8,128)(2,1)S(1)}, u32[]{:S(2)}, u32[]{:S(2)}) collective-permute-start(bf16[448,896]{1,0:T(8,128)(2,1)S(1)} %copy-done.3), channel_id=1, source_target_pairs={{0,1},{1,0},{2,3},{3,2},{4,5},{5,4},{6,7},{7,6},{8,9},{9,8},{10,11... | collective-permute-start | bytes 2408456 | tf_op jit(solution)/shard_map/ppermute | solution.py:306
  52.3 9.0 %collective-permute-start.20 = (bf16[448,896]{1,0:T(8,128)(2,1)S(1)}, bf16[448,896]{1,0:T(8,128)(2,1)S(1)}, u32[]{:S(2)}, u32[]{:S(2)}) collective-permute-start(bf16[448,896]{1,0:T(8,128)(2,1)S(1)} %collective-permute-done.8.refs_1_), channel_id=1, source_target_pairs={{0,1},{1,0},{2,3},{3,2},{4,5},{5,4},{6,7},{7,6},{8,9},{9,8},{10,11... | collective-permute-start | bytes 2408456 | tf_op jit(solution)/shard_map/ppermute | solution.py:306
  56.4 4.9 %collective-permute-start.22 = (bf16[448,896]{1,0:T(8,128)(2,1)S(1)}, bf16[448,896]{1,0:T(8,128)(2,1)S(1)}, u32[]{:S(2)}, u32[]{:S(2)}) collective-permute-start(bf16[448,896]{1,0:T(8,128)(2,1)S(1)} %collective-permute-done.21.refs_3_), channel_id=1, source_target_pairs={{0,1},{1,0},{2,3},{3,2},{4,5},{5,4},{6,7},{7,6},{8,9},{9,8},{10,11... | collective-permute-start | bytes 2408456 | tf_op jit(solution)/shard_map/ppermute | solution.py:306
  65.7 4.0 %collective-permute-start.23 = (bf16[1024,896]{1,0:T(8,128)(2,1)S(1)}, bf16[1024,896]{1,0:T(8,128)(2,1)S(1)}, u32[]{:S(2)}, u32[]{:S(2)}) collective-permute-start(bf16[1024,896]{1,0:T(8,128)(2,1)S(1)} %encoder_ffn_far.1.encoded), channel_id=1, source_target_pairs={{0,1},{1,0},{2,3},{3,2},{4,5},{5,4},{6,7},{7,6},{8,9},{9,8},{10,11... | collective-permute-start | bytes 5505032 | tf_op jit(solution)/shard_map/ppermute | solution.py:306
  (4 other events, 13.8 us)

commit v9 on v8

--- a/solution.py
+++ b/solution.py
@@ -21,7 +21,8 @@
 ORDER = {
     "pk": ("x0",),
     "xp": ("xn",),
-    "xa": ("xm",),
+    "xa": ("xm", "ca"),
+    "zm": ("x0",),
     "ca": ("xn",),
     "cf": ("xn",),
     "keys": ("xp",),

time: 75.6 us -> 76.1 us (level)
  starting transfers between devices: 24.3 us -> 25.7 us
  waiting for transfers between devices: 17.6 us -> 16.5 us
    ppermute x1, starting transfers between devices: 1.12 us -> 5.51 us  [seq_cross(): return lax.ppermute(array, 'seq', [(i, i ^ 2) for i in range(seq_size)])]
    ppermute x1, waiting for transfers between devices: 0.01 us -> 4.04 us  [next_seq(): return lax.ppermute(array, 'seq', [(i, i + 1) for i in range(seq_size - 1)])]
    ppermute x1, waiting for transfers between devices: 3.67 us -> 0.3 us  [seq_cross(): return lax.ppermute(array, 'seq', [(i, i ^ 2) for i in range(seq_size)])]
    ppermute x5, waiting for transfers between devices: 6.76 us -> 3.4 us  [seq_swap(): return lax.ppermute(array, 'seq', [(i, i ^ 1) for i in range(seq_size)])]
    ppermute x5, starting transfers between devices: 8.54 us -> 5.66 us  [seq_swap(): return lax.ppermute(array, 'seq', [(i, i ^ 1) for i in range(seq_size)])]
    ppermute x3, waiting for transfers between devices: 4.87 us -> 6.3 us  [seq_ring(): lax.ppermute(array, 'seq', [(i, (i + 2 * way) % seq_size) for i in range(...]
where the time goes in v9:
time: 76.1 us; the launch traced here: 75.1 us
  Pallas kernels  30.5 us (40%)
  starting transfers between devices  25.7 us (34%)
  waiting for transfers between devices  16.5 us (22%)
  local copies, waits for them, and re-layouts  1.5 us (2%)
    pallas_call x2, Pallas kernels, attention(): call(functools.partial(attention_kernel, len(kv), far), long_rows, 'svv'...  8.28 us
    ppermute x3, waiting for transfers between devices, seq_ring(): lax.ppermute(array, 'seq', [(i, (i + 2 * way) % seq_size) for i in range(...  6.3 us
    ppermute x5, starting transfers between devices, seq_swap(): return lax.ppermute(array, 'seq', [(i, i ^ 1) for i in range(seq_size)])  5.66 us
    ppermute x1, starting transfers between devices, seq_cross(): return lax.ppermute(array, 'seq', [(i, i ^ 2) for i in range(seq_size)])  5.51 us
    ppermute x3, starting transfers between devices, seq_ring(): lax.ppermute(array, 'seq', [(i, (i + 2 * way) % seq_size) for i in range(...  5.34 us
    pallas_call x1, Pallas kernels, on_device(): call(functools.partial(ffn_kernel, False, True), (long_rows, short_rows),...  4.85 us
    pallas_call x1, Pallas kernels, on_device(): call(decoder_kernel, jax.ShapeDtypeStruct(dec_queries.shape, jnp.float32)...  4.8 us
    pallas_call x1, Pallas kernels, on_device(): call(functools.partial(ffn_kernel, True, False), short_rows, 'vvv' + 'v'...  4.48 us
  transfers between devices with their start and end apart: 24, of which 11 were waited for; matrix products, arithmetic and copies ran while one was open for 1% of the time, Pallas kernels for 24%

profile of v9, /device:TPU:0, one launch (start us, length us, event | category | flops | bytes accessed | tf_op | source)
XLA Modules:
  0.0 75.1 jit_solution(6908917179145203512)
XLA Ops:
  0.0 3.3 %prepare.1 = (bf16[2,64,896]{2,1,0:T(8,128)(2,1)}, bf16[224,896]{1,0:T(8,128)(2,1)}, bf16[448,896]{1,0:T(8,128)(2,1)}, bf16[2,240,64]{2,1,0:T(8,128)(2,1)}) custom-call(s32[1]{0:T(128)} %bitcast.here.seq_index.first, s32[1]{0:T(128)} %bitcast.1.lane_here, s32[2,8]{1,0:T(2,128)} %bitcast.18, s32[2,8]{1,0:T(2,128)} %bitcast.20, f32[2,128,896]{2,1,0:T(8,128)} %database.1, ...), custom_call_target="tpu_custom_call" | custom-call | flops 917504 | bytes 8000000 | tf_op jit(solution)/shard_map/prepare/pallas_call | solution.py:334
  3.3 3.1 %collective-permute-start = (bf16[2,64,896]{2,1,0:T(8,128)(2,1)}, bf16[2,64,896]{2,1,0:T(8,128)(2,1)S(1)}, u32[]{:S(2)}, u32[]{:S(2)}) collective-permute-start(bf16[2,64,896]{2,1,0:T(8,128)(2,1)} %get-tuple-element.31.refs_0_), channel_id=1, source_target_pairs={{0,8},{4,12},{8,16},{12,20},{16,24},{20,28},{24,0},{28,4},{1,9},{5... | collective-permute-start | bytes 688136 | tf_op jit(solution)/shard_map/ppermute | solution.py:319
  6.4 1.5 %collective-permute-start.1 = (bf16[2,64,896]{2,1,0:T(8,128)(2,1)}, bf16[2,64,896]{2,1,0:T(8,128)(2,1)S(1)}, u32[]{:S(2)}, u32[]{:S(2)}) collective-permute-start(bf16[2,64,896]{2,1,0:T(8,128)(2,1)} %get-tuple-element.31.refs_0_), channel_id=1, source_target_pairs={{0,4},{4,0},{8,12},{12,8},{16,20},{20,16},{24,28},{28,24},{1,5},{5... | collective-permute-start | bytes 688136 | tf_op jit(solution)/shard_map/ppermute | solution.py:313
  7.9 1.5 %collective-permute-start.8 = (bf16[448,896]{1,0:T(8,128)(2,1)}, bf16[448,896]{1,0:T(8,128)(2,1)S(1)}, u32[]{:S(2)}, u32[]{:S(2)}) collective-permute-start(bf16[448,896]{1,0:T(8,128)(2,1)} %get-tuple-element.39), channel_id=1, source_target_pairs={{0,2},{1,3},{2,0},{3,1},{4,6},{5,7},{6,4},{7,5},{8,10},{9,11},{10,... | collective-permute-start | bytes 2408456 | tf_op jit(solution)/shard_map/ppermute | solution.py:310
  9.4 2.2 %collective-permute-start.6 = (bf16[2,64,896]{2,1,0:T(8,128)(2,1)}, bf16[2,64,896]{2,1,0:T(8,128)(2,1)S(1)}, u32[]{:S(2)}, u32[]{:S(2)}) collective-permute-start(bf16[2,64,896]{2,1,0:T(8,128)(2,1)} %get-tuple-element.31.refs_0_), channel_id=1, source_target_pairs={{0,24},{4,28},{8,0},{12,4},{16,8},{20,12},{24,16},{28,20},{1,25},{... | collective-permute-start | bytes 688136 | tf_op jit(solution)/shard_map/ppermute | solution.py:319
  11.7 3.4 %collective-permute-done.refs_2_ = bf16[2,64,896]{2,1,0:T(8,128)(2,1)S(1)} collective-permute-done((bf16[2,64,896]{2,1,0:T(8,128)(2,1)}, bf16[2,64,896]{2,1,0:T(8,128)(2,1)S(1)}, u32[]{:S(2)}, u32[]{:S(2)}) %collective-permute-start) | collective-permute-done | bytes 229408 | tf_op jit(solution)/shard_map/ppermute | solution.py:319
  15.1 1.8 %collective-permute-start.3 = (bf16[2,64,896]{2,1,0:T(8,128)(2,1)S(1)}, bf16[2,64,896]{2,1,0:T(8,128)(2,1)S(1)}, u32[]{:S(2)}, u32[]{:S(2)}) collective-permute-start(bf16[2,64,896]{2,1,0:T(8,128)(2,1)S(1)} %collective-permute-done.refs_2_), channel_id=1, source_target_pairs={{0,4},{4,0},{8,12},{12,8},{16,20},{20,16},{24,28},{28,24},{1,5},{5... | collective-permute-start | bytes 688136 | tf_op jit(solution)/shard_map/ppermute | solution.py:313
  16.8 2.5 %collective-permute-done.6.refs_6_ = bf16[2,64,896]{2,1,0:T(8,128)(2,1)S(1)} collective-permute-done((bf16[2,64,896]{2,1,0:T(8,128)(2,1)}, bf16[2,64,896]{2,1,0:T(8,128)(2,1)S(1)}, u32[]{:S(2)}, u32[]{:S(2)}) %collective-permute-start.6) | collective-permute-done | bytes 229408 | tf_op jit(solution)/shard_map/ppermute | solution.py:319
  19.3 1.8 %collective-permute-done.3.refs_3_ = bf16[2,64,896]{2,1,0:T(8,128)(2,1)S(1)} collective-permute-done((bf16[2,64,896]{2,1,0:T(8,128)(2,1)S(1)}, bf16[2,64,896]{2,1,0:T(8,128)(2,1)S(1)}, u32[]{:S(2)}, u32[]{:S(2)}) %collective-permute-start.3) | collective-permute-done | bytes 229408 | tf_op jit(solution)/shard_map/ppermute | solution.py:313
  21.1 1.8 %collective-permute-start.7 = (bf16[2,64,896]{2,1,0:T(8,128)(2,1)S(1)}, bf16[2,64,896]{2,1,0:T(8,128)(2,1)S(1)}, u32[]{:S(2)}, u32[]{:S(2)}) collective-permute-start(bf16[2,64,896]{2,1,0:T(8,128)(2,1)S(1)} %collective-permute-done.6.refs_6_), channel_id=1, source_target_pairs={{0,4},{4,0},{8,12},{12,8},{16,20},{20,16},{24,28},{28,24},{1,5},{5... | collective-permute-start | bytes 688136 | tf_op jit(solution)/shard_map/ppermute | solution.py:313
  22.9 2.1 %collective-permute-start.2 = (bf16[2,240,64]{2,1,0:T(8,128)(2,1)}, bf16[2,240,64]{2,1,0:T(8,128)(2,1)S(1)}, u32[]{:S(2)}, u32[]{:S(2)}) collective-permute-start(bf16[2,240,64]{2,1,0:T(8,128)(2,1)} %get-tuple-element.34), channel_id=1, source_target_pairs={{0,4},{4,8},{8,12},{12,16},{16,20},{20,24},{24,28},{1,5},{5,9},{9,... | collective-permute-start | bytes 184328 | tf_op jit(solution)/shard_map/ppermute | solution.py:322
  25.4 0.6 collective-permute-start.5
  26.0 1.5 %collective-permute-start.12 = (bf16[224,896]{1,0:T(8,128)(2,1)}, bf16[224,896]{1,0:T(8,128)(2,1)S(1)}, u32[]{:S(2)}, u32[]{:S(2)}) collective-permute-start(bf16[224,896]{1,0:T(8,128)(2,1)} %get-tuple-element.45), channel_id=1, source_target_pairs={{0,2},{1,3},{2,0},{3,1},{4,6},{5,7},{6,4},{7,5},{8,10},{9,11},{10,... | collective-permute-start | bytes 1204232 | tf_op jit(solution)/shard_map/ppermute | solution.py:310
  27.6 4.0 %collective-permute-done.2 = bf16[2,240,64]{2,1,0:T(8,128)(2,1)S(1)} collective-permute-done((bf16[2,240,64]{2,1,0:T(8,128)(2,1)}, bf16[2,240,64]{2,1,0:T(8,128)(2,1)S(1)}, u32[]{:S(2)}, u32[]{:S(2)}) %collective-permute-start.2) | collective-permute-done | bytes 61472 | tf_op jit(solution)/shard_map/ppermute | solution.py:322
  31.6 0.5 collective-permute-start.10
  32.4 1.6 %collective-permute-done.5.refs_5_ = bf16[2,64,896]{2,1,0:T(8,128)(2,1)S(1)} collective-permute-done((bf16[2,64,896]{2,1,0:T(8,128)(2,1)S(1)}, bf16[2,64,896]{2,1,0:T(8,128)(2,1)S(1)}, u32[]{:S(2)}, u32[]{:S(2)}) %collective-permute-start.5) | collective-permute-done | bytes 229408 | tf_op jit(solution)/shard_map/ppermute | solution.py:313
  34.0 1.4 %collective-permute-start.16 = (bf16[2,224,512]{2,1,0:T(8,128)(2,1)S(1)}, bf16[2,224,512]{2,1,0:T(8,128)(2,1)S(1)}, u32[]{:S(2)}, u32[]{:S(2)}) collective-permute-start(bf16[2,224,512]{2,1,0:T(8,128)(2,1)S(1)} %pad_maximum_fusion.refs_4_), channel_id=1, source_target_pairs={{0,2},{1,3},{2,0},{3,1},{4,6},{5,7},{6,4},{7,5},{8,10},{9,11},{10,... | collective-permute-start | bytes 1376264 | tf_op jit(solution)/shard_map/ppermute | solution.py:310
  35.5 0.5 collective-permute-done.12.refs_0_
  36.0 5.5 %collective-permute-start.21 = (bf16[448,896]{1,0:T(8,128)(2,1)S(1)}, bf16[448,896]{1,0:T(8,128)(2,1)S(1)}, u32[]{:S(2)}, u32[]{:S(2)}) collective-permute-start(bf16[448,896]{1,0:T(8,128)(2,1)S(1)} %collective-permute-done.8.refs_1_), channel_id=1, source_target_pairs={{0,8},{4,12},{8,0},{12,4},{16,24},{20,28},{24,16},{28,20},{1,9},{5... | collective-permute-start | bytes 2408456 | tf_op jit(solution)/shard_map/ppermute | solution.py:316
  41.7 0.9 %copy-done.5 = bf16[2,64,896]{2,1,0:T(8,128)(2,1)S(1)} copy-done((bf16[2,64,896]{2,1,0:T(8,128)(2,1)S(1)}, bf16[2,64,896]{2,1,0:T(8,128)(2,1)}, u32[]{:S(2)}) %copy-start.5) | copy-done | bytes 229400
  42.6 2.5 %neighbour_rows.1 = (bf16[1024,896]{1,0:T(8,128)(2,1)S(1)}, bf16[1024,896]{1,0:T(8,128)(2,1)S(1)}) custom-call(s32[1]{0:T(128)} %bitcast.here.seq_index.first, s32[2,8]{1,0:T(2,128)S(1)} %bitcast.19, s32[2,8]{1,0:T(2,128)S(1)} %bitcast.21, s32[2,1]{1,0:T(2,128)S(1)} %slice_add_fusion.before, f32[1,896]{1,0:T(1,128)S(1)} %reshape.18.gain, ...), custom_call_target="tpu_custom_call" | custom-call | flops 9175040 | bytes 8000000 | tf_op jit(solution)/shard_map/neighbour_rows/pallas_call | solution.py:423
  45.2 4.1 %encoder_attention.2.before = f32[1024,896]{1,0:T(8,128)S(1)} custom-call(s32[1]{0:T(128)} %bitcast.here.seq_index.first, bf16[1024,896]{1,0:T(8,128)(2,1)S(1)} %get-tuple-element.40.before, bf16[1024,896]{1,0:T(8,128)(2,1)S(1)} %get-tuple-element.41.normed_in, bf16[224,896]{1,0:T(8,128)(2,1)S(1)} %bitcast.14, bf16[224,896]{1,0:T(8,128)(2,1)S(1)} %copy-done.1, ...), custom_call_target="tpu_custom_call" | custom-call | flops 1644167168 | bytes 8000000 | tf_op jit(solution)/shard_map/encoder_attention/pallas_call | solution.py:433
  49.4 0.5 collective-permute-start.17
  50.5 1.4 %collective-permute-done.15.refs_3_ = bf16[224,896]{1,0:T(8,128)(2,1)S(1)} collective-permute-done((bf16[224,896]{1,0:T(8,128)(2,1)S(1)}, bf16[224,896]{1,0:T(8,128)(2,1)S(1)}, u32[]{:S(2)}, u32[]{:S(2)}) %collective-permute-start.15) | collective-permute-done | bytes 401440 | tf_op jit(solution)/shard_map/ppermute | solution.py:307
  51.9 4.2 %encoder_attention.3.before = f32[1024,896]{1,0:T(8,128)S(1)} custom-call(s32[1]{0:T(128)} %bitcast.here.seq_index.first, f32[1024,896]{1,0:T(8,128)S(1)} %encoder_attention.2.before, bf16[1024,896]{1,0:T(8,128)(2,1)S(1)} %get-tuple-element.41.normed_in, bf16[224,896]{1,0:T(8,128)(2,1)S(1)} %collective-permute-done.12.refs_0_, ...), custom_call_target="tpu_custom_call" | custom-call | flops 1644167168 | bytes 8000000 | tf_op jit(solution)/shard_map/encoder_attention/pallas_call | solution.py:433
  56.8 4.8 %encoder_ffn_near.1 = (f32[1024,896]{1,0:T(8,128)S(1)}, bf16[1024,896]{1,0:T(8,128)(2,1)S(1)}) custom-call(f32[1,896]{1,0:T(1,128)S(1)} %reshape.19.gain, f32[1024,896]{1,0:T(8,128)S(1)} %encoder_attention.3.before, bf16[448,896]{1,0:T(8,128)(2,1)S(1)} %bitcast.17, bf16[448,896]{1,0:T(8,128)(2,1)S(1)} %copy-done.3, ...), custom_call_target="tpu_custom_call" | custom-call | flops 3288334336 | bytes 8000000 | tf_op jit(solution)/shard_map/encoder_ffn_near/pallas_call | solution.py:450
  61.7 4.5 %encoder_ffn_far.1.encoded = bf16[1024,896]{1,0:T(8,128)(2,1)S(1)} custom-call(f32[1,896]{1,0:T(1,128)S(1)} %reshape.19.gain, f32[1024,896]{1,0:T(8,128)S(1)} %get-tuple-element.52.before, bf16[1024,896]{1,0:T(8,128)(2,1)S(1)} %get-tuple-element.53.refs_0_, bf16[448,896]{1,0:T(8,128)(2,1)S(1)} %collective-permute-done.8.refs_1_, ...), custom_call_target="tpu_custom_call" | custom-call | flops 3288334336 | bytes 8000000 | tf_op jit(solution)/shard_map/encoder_ffn_far/pallas_call | solution.py:460
  66.2 0.6 collective-permute-start.23
  66.8 0.5 copy.13
  67.3 2.3 %decoder_pairs.1.own_pairs = bf16[1024,1024]{1,0:T(8,128)(2,1)S(1)} custom-call(bf16[1024,896]{1,0:T(8,128)(2,1)S(1)} %encoder_ffn_far.1.encoded, bf16[896,1024]{1,0:T(8,128)(2,1)S(1)} %bitcast.10), custom_call_target="tpu_custom_call" | custom-call | flops 1879048192 | bytes 8000000 | tf_op jit(solution)/shard_map/decoder_pairs/pallas_call | solution.py:472
  69.6 0.6 collective-permute-done.23.other
  70.2 4.8 %decoder_attention.1 = f32[512,512]{1,0:T(8,128)} custom-call(s32[1]{0:T(128)} %bitcast.here.seq_index.first, bf16[1024,1024]{1,0:T(8,128)(2,1)S(1)} %decoder_pairs.1.own_pairs, bf16[1024,896]{1,0:T(8,128)(2,1)S(1)} %collective-permute-done.23.other, bf16[896,1024]{1,0:T(8,128)(2,1)S(1)} %bitcast.11, bf16[512,512]{1,0:T(8,128)(2,1)S(1)} %copy-done.4), custom_call_target="tpu_custom_call" | custom-call | flops 1879048192 | bytes 8000000 | tf_op jit(solution)/shard_map/decoder_attention/pallas_call | solution.py:480
  (55 shorter events, 2.5 us)
Async XLA Ops:
  0.0 31.6 %copy-start = (bf16[896,224]{0,1:T(8,128)(2,1)S(1)}, bf16[896,224]{0,1:T(8,128)(2,1)}, u32[]{:S(2)}) copy-start(bf16[896,224]{0,1:T(8,128)(2,1)} %param.18) | copy-start | bytes 1204228
  0.0 31.6 %copy-start.1 = (bf16[224,896]{1,0:T(8,128)(2,1)S(1)}, bf16[224,896]{1,0:T(8,128)(2,1)}, u32[]{:S(2)}) copy-start(bf16[224,896]{1,0:T(8,128)(2,1)} %refs_1_.2) | copy-start | bytes 1204228
  0.0 32.1 %copy-start.9 = (bf16[512,2,224]{0,2,1:T(8,128)(2,1)S(1)}, bf16[512,2,224]{0,2,1:T(8,128)(2,1)}, u32[]{:S(2)}) copy-start(bf16[512,2,224]{0,2,1:T(8,128)(2,1)} %param.12) | copy-start | bytes 1376260
  0.0 34.0 %copy-start.10 = (f32[896]{0:T(1024)S(1)}, f32[896]{0:T(1024)}, u32[]{:S(2)}) copy-start(f32[896]{0:T(1024)} %param.17) | copy-start | bytes 10756
  0.0 34.0 %copy-start.11 = (f32[896]{0:T(1024)S(1)}, f32[896]{0:T(1024)}, u32[]{:S(2)}) copy-start(f32[896]{0:T(1024)} %param.20) | copy-start | bytes 10756
  0.0 41.6 %copy-start.6 = (s32[8,2]{0,1:T(2,128)S(1)}, s32[8,2]{0,1:T(2,128)}, u32[]{:S(2)}) copy-start(s32[8,2]{0,1:T(2,128)} %param.16) | copy-start | bytes 196
  0.0 41.6 %copy-start.7 = (s32[8,2]{0,1:T(2,128)S(1)}, s32[8,2]{0,1:T(2,128)}, u32[]{:S(2)}) copy-start(s32[8,2]{0,1:T(2,128)} %param.15) | copy-start | bytes 196
  3.3 11.8 %collective-permute-start = (bf16[2,64,896]{2,1,0:T(8,128)(2,1)}, bf16[2,64,896]{2,1,0:T(8,128)(2,1)S(1)}, u32[]{:S(2)}, u32[]{:S(2)}) collective-permute-start(bf16[2,64,896]{2,1,0:T(8,128)(2,1)} %get-tuple-element.31.refs_0_), channel_id=1, source_target_pairs={{0,8},{4,12},{8,16},{12,20},{16,24},{20,28},{24,0},{28,4},{1,9},{5... | collective-permute-start | bytes 688136 | tf_op jit(solution)/shard_map/ppermute | solution.py:319
  6.4 10.5 %collective-permute-start.1 = (bf16[2,64,896]{2,1,0:T(8,128)(2,1)}, bf16[2,64,896]{2,1,0:T(8,128)(2,1)S(1)}, u32[]{:S(2)}, u32[]{:S(2)}) collective-permute-start(bf16[2,64,896]{2,1,0:T(8,128)(2,1)} %get-tuple-element.31.refs_0_), channel_id=1, source_target_pairs={{0,4},{4,0},{8,12},{12,8},{16,20},{20,16},{24,28},{28,24},{1,5},{5... | collective-permute-start | bytes 688136 | tf_op jit(solution)/shard_map/ppermute | solution.py:313
  7.9 26.1 %collective-permute-start.8 = (bf16[448,896]{1,0:T(8,128)(2,1)}, bf16[448,896]{1,0:T(8,128)(2,1)S(1)}, u32[]{:S(2)}, u32[]{:S(2)}) collective-permute-start(bf16[448,896]{1,0:T(8,128)(2,1)} %get-tuple-element.39), channel_id=1, source_target_pairs={{0,2},{1,3},{2,0},{3,1},{4,6},{5,7},{6,4},{7,5},{8,10},{9,11},{10,... | collective-permute-start | bytes 2408456 | tf_op jit(solution)/shard_map/ppermute | solution.py:310
  9.4 9.9 %collective-permute-start.6 = (bf16[2,64,896]{2,1,0:T(8,128)(2,1)}, bf16[2,64,896]{2,1,0:T(8,128)(2,1)S(1)}, u32[]{:S(2)}, u32[]{:S(2)}) collective-permute-start(bf16[2,64,896]{2,1,0:T(8,128)(2,1)} %get-tuple-element.31.refs_0_), channel_id=1, source_target_pairs={{0,24},{4,28},{8,0},{12,4},{16,8},{20,12},{24,16},{28,20},{1,25},{... | collective-permute-start | bytes 688136 | tf_op jit(solution)/shard_map/ppermute | solution.py:319
  15.1 6.0 %collective-permute-start.3 = (bf16[2,64,896]{2,1,0:T(8,128)(2,1)S(1)}, bf16[2,64,896]{2,1,0:T(8,128)(2,1)S(1)}, u32[]{:S(2)}, u32[]{:S(2)}) collective-permute-start(bf16[2,64,896]{2,1,0:T(8,128)(2,1)S(1)} %collective-permute-done.refs_2_), channel_id=1, source_target_pairs={{0,4},{4,0},{8,12},{12,8},{16,20},{20,16},{24,28},{28,24},{1,5},{5... | collective-permute-start | bytes 688136 | tf_op jit(solution)/shard_map/ppermute | solution.py:313
  16.8 8.6 %collective-permute-start.4 = (bf16[2,64,896]{2,1,0:T(8,128)(2,1)S(1)}, bf16[2,64,896]{2,1,0:T(8,128)(2,1)S(1)}, u32[]{:S(2)}, u32[]{:S(2)}) collective-permute-start(bf16[2,64,896]{2,1,0:T(8,128)(2,1)S(1)} %collective-permute-done.refs_2_), channel_id=1, source_target_pairs={{0,8},{4,12},{8,16},{12,20},{16,24},{20,28},{24,0},{28,4},{1,9},{5... | collective-permute-start | bytes 688136 | tf_op jit(solution)/shard_map/ppermute | solution.py:319
  21.1 10.5 %collective-permute-start.7 = (bf16[2,64,896]{2,1,0:T(8,128)(2,1)S(1)}, bf16[2,64,896]{2,1,0:T(8,128)(2,1)S(1)}, u32[]{:S(2)}, u32[]{:S(2)}) collective-permute-start(bf16[2,64,896]{2,1,0:T(8,128)(2,1)S(1)} %collective-permute-done.6.refs_6_), channel_id=1, source_target_pairs={{0,4},{4,0},{8,12},{12,8},{16,20},{20,16},{24,28},{28,24},{1,5},{5... | collective-permute-start | bytes 688136 | tf_op jit(solution)/shard_map/ppermute | solution.py:313
  22.9 8.7 %collective-permute-start.2 = (bf16[2,240,64]{2,1,0:T(8,128)(2,1)}, bf16[2,240,64]{2,1,0:T(8,128)(2,1)S(1)}, u32[]{:S(2)}, u32[]{:S(2)}) collective-permute-start(bf16[2,240,64]{2,1,0:T(8,128)(2,1)} %get-tuple-element.34), channel_id=1, source_target_pairs={{0,4},{4,8},{8,12},{12,16},{16,20},{20,24},{24,28},{1,5},{5,9},{9,... | collective-permute-start | bytes 184328 | tf_op jit(solution)/shard_map/ppermute | solution.py:322
  25.4 8.5 %collective-permute-start.5 = (bf16[2,64,896]{2,1,0:T(8,128)(2,1)S(1)}, bf16[2,64,896]{2,1,0:T(8,128)(2,1)S(1)}, u32[]{:S(2)}, u32[]{:S(2)}) collective-permute-start(bf16[2,64,896]{2,1,0:T(8,128)(2,1)S(1)} %collective-permute-done.4.refs_4_), channel_id=1, source_target_pairs={{0,4},{4,0},{8,12},{12,8},{16,20},{20,16},{24,28},{28,24},{1,5},{5... | collective-permute-start | bytes 688136 | tf_op jit(solution)/shard_map/ppermute | solution.py:313
  26.0 10.0 %collective-permute-start.12 = (bf16[224,896]{1,0:T(8,128)(2,1)}, bf16[224,896]{1,0:T(8,128)(2,1)S(1)}, u32[]{:S(2)}, u32[]{:S(2)}) collective-permute-start(bf16[224,896]{1,0:T(8,128)(2,1)} %get-tuple-element.45), channel_id=1, source_target_pairs={{0,2},{1,3},{2,0},{3,1},{4,6},{5,7},{6,4},{7,5},{8,10},{9,11},{10,... | collective-permute-start | bytes 1204232 | tf_op jit(solution)/shard_map/ppermute | solution.py:310
  31.6 10.0 %collective-permute-start.9 = (bf16[224,896]{1,0:T(8,128)(2,1)S(1)}, bf16[224,896]{1,0:T(8,128)(2,1)S(1)}, u32[]{:S(2)}, u32[]{:S(2)}) collective-permute-start(bf16[224,896]{1,0:T(8,128)(2,1)S(1)} %bitcast.13), channel_id=1, source_target_pairs={{0,1},{1,0},{2,3},{3,2},{4,5},{5,4},{6,7},{7,6},{8,9},{9,8},{10,11... | collective-permute-start | bytes 1204232 | tf_op jit(solution)/shard_map/ppermute | solution.py:307
  31.6 9.9 %collective-permute-start.10 = (bf16[224,896]{1,0:T(8,128)(2,1)S(1)}, bf16[224,896]{1,0:T(8,128)(2,1)S(1)}, u32[]{:S(2)}, u32[]{:S(2)}) collective-permute-start(bf16[224,896]{1,0:T(8,128)(2,1)S(1)} %copy-done.1), channel_id=1, source_target_pairs={{0,1},{1,0},{2,3},{3,2},{4,5},{5,4},{6,7},{7,6},{8,9},{9,8},{10,11... | collective-permute-start | bytes 1204232 | tf_op jit(solution)/shard_map/ppermute | solution.py:307
  34.0 11.2 %collective-permute-start.11 = (bf16[2,224,512]{2,1,0:T(8,128)(2,1)S(1)}, bf16[2,224,512]{2,1,0:T(8,128)(2,1)S(1)}, u32[]{:S(2)}, u32[]{:S(2)}) collective-permute-start(bf16[2,224,512]{2,1,0:T(8,128)(2,1)S(1)} %pad_maximum_fusion.refs_4_), channel_id=1, source_target_pairs={{0,1},{1,0},{2,3},{3,2},{4,5},{5,4},{6,7},{7,6},{8,9},{9,8},{10,11... | collective-permute-start | bytes 1376264 | tf_op jit(solution)/shard_map/ppermute | solution.py:307
  34.0 15.3 %collective-permute-start.16 = (bf16[2,224,512]{2,1,0:T(8,128)(2,1)S(1)}, bf16[2,224,512]{2,1,0:T(8,128)(2,1)S(1)}, u32[]{:S(2)}, u32[]{:S(2)}) collective-permute-start(bf16[2,224,512]{2,1,0:T(8,128)(2,1)S(1)} %pad_maximum_fusion.refs_4_), channel_id=1, source_target_pairs={{0,2},{1,3},{2,0},{3,1},{4,6},{5,7},{6,4},{7,5},{8,10},{9,11},{10,... | collective-permute-start | bytes 1376264 | tf_op jit(solution)/shard_map/ppermute | solution.py:310
  36.0 20.8 %collective-permute-start.21 = (bf16[448,896]{1,0:T(8,128)(2,1)S(1)}, bf16[448,896]{1,0:T(8,128)(2,1)S(1)}, u32[]{:S(2)}, u32[]{:S(2)}) collective-permute-start(bf16[448,896]{1,0:T(8,128)(2,1)S(1)} %collective-permute-done.8.refs_1_), channel_id=1, source_target_pairs={{0,8},{4,12},{8,0},{12,4},{16,24},{20,28},{24,16},{28,20},{1,9},{5... | collective-permute-start | bytes 2408456 | tf_op jit(solution)/shard_map/ppermute | solution.py:316
  41.6 8.4 %collective-permute-start.13 = (bf16[224,896]{1,0:T(8,128)(2,1)S(1)}, bf16[224,896]{1,0:T(8,128)(2,1)S(1)}, u32[]{:S(2)}, u32[]{:S(2)}) collective-permute-start(bf16[224,896]{1,0:T(8,128)(2,1)S(1)} %collective-permute-done.12.refs_0_), channel_id=1, source_target_pairs={{0,4},{4,0},{8,12},{12,8},{16,20},{20,16},{24,28},{28,24},{1,5},{5... | collective-permute-start | bytes 1204232 | tf_op jit(solution)/shard_map/ppermute | solution.py:313
  45.1 5.4 %collective-permute-start.14 = (bf16[224,896]{1,0:T(8,128)(2,1)S(1)}, bf16[224,896]{1,0:T(8,128)(2,1)S(1)}, u32[]{:S(2)}, u32[]{:S(2)}) collective-permute-start(bf16[224,896]{1,0:T(8,128)(2,1)S(1)} %collective-permute-done.12.refs_0_), channel_id=1, source_target_pairs={{0,1},{1,0},{2,3},{3,2},{4,5},{5,4},{6,7},{7,6},{8,9},{9,8},{10,11... | collective-permute-start | bytes 1204232 | tf_op jit(solution)/shard_map/ppermute | solution.py:307
  45.2 5.3 %copy-start.3 = (bf16[448,896]{1,0:T(8,128)(2,1)S(1)}, bf16[448,896]{1,0:T(8,128)(2,1)}, u32[]{:S(2)}) copy-start(bf16[448,896]{1,0:T(8,128)(2,1)} %refs_1_.3) | copy-start | bytes 2408452
  49.4 2.5 %collective-permute-start.17 = (bf16[2,224,512]{2,1,0:T(8,128)(2,1)S(1)}, bf16[2,224,512]{2,1,0:T(8,128)(2,1)S(1)}, u32[]{:S(2)}, u32[]{:S(2)}) collective-permute-start(bf16[2,224,512]{2,1,0:T(8,128)(2,1)S(1)} %collective-permute-done.16.refs_4_), channel_id=1, source_target_pairs={{0,1},{1,0},{2,3},{3,2},{4,5},{5,4},{6,7},{7,6},{8,9},{9,8},{10,11... | collective-permute-start | bytes 1376264 | tf_op jit(solution)/shard_map/ppermute | solution.py:307
  50.0 2.0 %collective-permute-start.15 = (bf16[224,896]{1,0:T(8,128)(2,1)S(1)}, bf16[224,896]{1,0:T(8,128)(2,1)S(1)}, u32[]{:S(2)}, u32[]{:S(2)}) collective-permute-start(bf16[224,896]{1,0:T(8,128)(2,1)S(1)} %collective-permute-done.13.refs_1_), channel_id=1, source_target_pairs={{0,1},{1,0},{2,3},{3,2},{4,5},{5,4},{6,7},{7,6},{8,9},{9,8},{10,11... | collective-permute-start | bytes 1204232 | tf_op jit(solution)/shard_map/ppermute | solution.py:307
  50.0 6.8 %collective-permute-start.18 = (bf16[448,896]{1,0:T(8,128)(2,1)S(1)}, bf16[448,896]{1,0:T(8,128)(2,1)S(1)}, u32[]{:S(2)}, u32[]{:S(2)}) collective-permute-start(bf16[448,896]{1,0:T(8,128)(2,1)S(1)} %bitcast.16), channel_id=1, source_target_pairs={{0,1},{1,0},{2,3},{3,2},{4,5},{5,4},{6,7},{7,6},{8,9},{9,8},{10,11... | collective-permute-start | bytes 2408456 | tf_op jit(solution)/shard_map/ppermute | solution.py:307
  50.5 6.3 %collective-permute-start.19 = (bf16[448,896]{1,0:T(8,128)(2,1)S(1)}, bf16[448,896]{1,0:T(8,128)(2,1)S(1)}, u32[]{:S(2)}, u32[]{:S(2)}) collective-permute-start(bf16[448,896]{1,0:T(8,128)(2,1)S(1)} %copy-done.3), channel_id=1, source_target_pairs={{0,1},{1,0},{2,3},{3,2},{4,5},{5,4},{6,7},{7,6},{8,9},{9,8},{10,11... | collective-permute-start | bytes 2408456 | tf_op jit(solution)/shard_map/ppermute | solution.py:307
  56.1 5.6 %collective-permute-start.20 = (bf16[448,896]{1,0:T(8,128)(2,1)S(1)}, bf16[448,896]{1,0:T(8,128)(2,1)S(1)}, u32[]{:S(2)}, u32[]{:S(2)}) collective-permute-start(bf16[448,896]{1,0:T(8,128)(2,1)S(1)} %collective-permute-done.8.refs_1_), channel_id=1, source_target_pairs={{0,1},{1,0},{2,3},{3,2},{4,5},{5,4},{6,7},{7,6},{8,9},{9,8},{10,11... | collective-permute-start | bytes 2408456 | tf_op jit(solution)/shard_map/ppermute | solution.py:307
  56.8 4.9 %collective-permute-start.22 = (bf16[448,896]{1,0:T(8,128)(2,1)S(1)}, bf16[448,896]{1,0:T(8,128)(2,1)S(1)}, u32[]{:S(2)}, u32[]{:S(2)}) collective-permute-start(bf16[448,896]{1,0:T(8,128)(2,1)S(1)} %collective-permute-done.21.refs_3_), channel_id=1, source_target_pairs={{0,1},{1,0},{2,3},{3,2},{4,5},{5,4},{6,7},{7,6},{8,9},{9,8},{10,11... | collective-permute-start | bytes 2408456 | tf_op jit(solution)/shard_map/ppermute | solution.py:307
  66.2 4.0 %collective-permute-start.23 = (bf16[1024,896]{1,0:T(8,128)(2,1)S(1)}, bf16[1024,896]{1,0:T(8,128)(2,1)S(1)}, u32[]{:S(2)}, u32[]{:S(2)}) collective-permute-start(bf16[1024,896]{1,0:T(8,128)(2,1)S(1)} %encoder_ffn_far.1.encoded), channel_id=1, source_target_pairs={{0,1},{1,0},{2,3},{3,2},{4,5},{5,4},{6,7},{7,6},{8,9},{9,8},{10,11... | collective-permute-start | bytes 5505032 | tf_op jit(solution)/shard_map/ppermute | solution.py:307
  (4 other events, 13.7 us)
